TPU v7x, 32 devices: a whole 2x2x4 slice. The times are simulated.
32 devices in a mesh: seq: 8 (over y, x, core), tp: 4 (over z).
Axes of the slice: x: 2, y: 2, z: 4, core: 2. Of those that a mesh axis runs over, the one named last changes fastest.
Arguments:
- token_ids: int32 [64, 4], replicated, may hold values from 0 to 51199
- embedding: bfloat16 [51200, 2048], P(('seq', 'tp')), may hold values from -8 to 8
- group_of: int32 [64], replicated, may hold values from 0 to 7, as said below
- prefix_len: int32 [8], replicated, may hold values from 1 to 512, as said below
- tail_len: int32 [64], replicated, may hold values from 1 to 128, as said below
- block_map: int32 [128, 2], P('seq'), may hold values from -1 to 71, as said below
- k_cache: bfloat16 [2, 16384, 2048], P(None, 'seq', 'tp'), may hold values from -100 to 100
- v_cache: bfloat16 [2, 16384, 2048], P(None, 'seq', 'tp'), may hold values from -12 to 12
- ln_gain: float32 [2, 2048], replicated, may hold values from 0.25 to 1.75
- ln_bias: float32 [2, 2048], replicated, may hold values from -1.5 to 1.5
- w_qkv: bfloat16 [2, 2048, 3, 2048], P(None, 'seq', None, 'tp'), may hold values from -0.125 to 0.125
- w_fc1: bfloat16 [2, 2048, 8192], P(None, 'seq', 'tp'), may hold values from -0.125 to 0.125
- b_fc1: float32 [2, 8192], P(None, 'tp'), may hold values from -2.5 to 2.5
- w_out: bfloat16 [2, 2048, 2048], P(None, ('tp', 'seq')), may hold values from -0.125 to 0.125
- w_fc2: bfloat16 [2, 8192, 2048], P(None, ('tp', 'seq')), may hold values from -0.0625 to 0.0625
Outputs:
- hidden_out: float32 [64, 4, 2048], replicated
Inputs may be any that keep to these rules, and one draw needn't show every extreme that they name: `group_of`: every group holds exactly 8 requests. `prefix_len`: some group's prompt is 512 long. `tail_len`: some request's tail is 128 long. `block_map`: row b gives the segment held by cache block b (slots b * 128 to b * 128 + 127): g for group g's prompt, 8 + r for request r's tail, -1 for none; and its rank within the segment. A segment of length L holds ranks 0 to ceil(L / 128) - 1, each in exactly one block; a block with segment -1 has rank 0.
All inputs are finite; a program needn't handle non-finite values.
Results may differ from a plain program's by a relative error of at most 0.04.
The roundings to bfloat16 on the way count: a program that leaves them out, or rounds other values in their place, can miss the bound.
Values may be sent and summed in bfloat16 or wider, within the bound.
No kernel may reach another device: no remote copies, remote signals or barrier semaphores. Data moves between devices by JAX's collectives and lax.ppermute only.
A program may use at most 192 MiB of HBM per device.

v0:
```python
import math

import jax
import jax.numpy as jnp
from jax import lax
from jax.sharding import PartitionSpec as P

HEADS = 32
HEAD_DIM = 64
ROT = 32
LAYERS = 2
BLOCK = 128
SPAN = 512


very_negative = -1e30


def layer_norm(values, gain_row, bias_row):
    average = jnp.mean(values, axis=-1, keepdims=True)
    centred = values - average
    variance = jnp.mean(centred * centred, axis=-1, keepdims=True)
    return centred * lax.rsqrt(variance + 1e-05) * gain_row + bias_row


def rotary(values, positions):
    half_width = ROT // 2
    frequency = jnp.exp(
        jnp.arange(half_width, dtype=jnp.float32) * (-2.0 * math.log(10000.0) / ROT)
    )
    angles = positions.astype(jnp.float32)[:, None] * frequency[None, :]
    cosine = jnp.cos(angles)[:, None, :]
    sine_part = jnp.sin(angles)[:, None, :]
    low_half = values[..., :half_width]
    high_half = values[..., half_width:ROT]
    return jnp.concatenate(
        [
            low_half * cosine - high_half * sine_part,
            high_half * cosine + low_half * sine_part,
            values[..., ROT:],
        ],
        axis=-1,
    )


def combine_parts(left_part, right_part):
    max_left, sum_left, out_left = left_part
    max_right, sum_right, out_right = right_part
    top_value = jnp.maximum(max_left, max_right)
    scale_left = jnp.exp(max_left - top_value)
    scale_right = jnp.exp(max_right - top_value)
    return (
        top_value,
        sum_left * scale_left + sum_right * scale_right,
        out_left * scale_left[..., None] + out_right * scale_right[..., None],
    )


def full_total(values):
    return lax.psum(values, ("seq", "tp"))


def per_device(
    token_ids,
    embedding,
    group_of,
    prefix_len,
    tail_len,
    block_map,
    k_cache,
    v_cache,
    ln_gain,
    ln_bias,
    w_qkv,
    w_fc1,
    b_fc1,
    w_out,
    w_fc2,
):
    tp_count = lax.axis_size("tp")
    seq_index = lax.axis_index("seq")
    tp_index = lax.axis_index("tp")
    requests = token_ids.shape[0]
    new_tokens = token_ids.shape[1]
    groups = prefix_len.shape[0]
    heads_local = HEADS // tp_count
    width_local = heads_local * HEAD_DIM
    score_scale = 1.0 / math.sqrt(HEAD_DIM)
    vocab_rows = embedding.shape[0]
    first_row = (seq_index * tp_count + tp_index) * vocab_rows
    local_ids = token_ids.reshape(-1) - first_row
    inside = (local_ids >= 0) & (local_ids < vocab_rows)
    picked = jnp.take(embedding, jnp.clip(local_ids, 0, vocab_rows - 1), axis=0).astype(jnp.float32)
    picked = jnp.where(inside[:, None], picked, 0.0)
    start_states = full_total(picked).reshape(requests, new_tokens, -1)
    group_hit = group_of[:, None] == jnp.arange(groups, dtype=jnp.int32)[None, :]
    shared_len = jnp.sum(jnp.where(group_hit, prefix_len[None, :], 0), axis=1)
    base_positions = shared_len + tail_len
    seg_len = jnp.concatenate([prefix_len, tail_len])
    seg_count = seg_len.shape[0]
    blocks_local = block_map.shape[0]
    seg_blk = block_map[:, 0]
    rank_blk = block_map[:, 1]
    seg_hit = seg_blk[:, None] == jnp.arange(seg_count, dtype=jnp.int32)[None, :]
    len_blk = jnp.sum(jnp.where(seg_hit, seg_len[None, :], 0), axis=1)
    slot_positions = rank_blk[:, None] * BLOCK + jnp.arange(BLOCK, dtype=jnp.int32)[None, :]
    live_slot = ((seg_blk[:, None] >= 0) & (slot_positions < len_blk[:, None])).reshape(-1)
    seg_slot = jnp.broadcast_to(seg_blk[:, None], (blocks_local, BLOCK)).reshape(-1)
    own_tail = seg_slot[None, :] == (groups + jnp.arange(requests, dtype=jnp.int32))[:, None]
    own_prompt = seg_slot[None, :] == group_of[:, None]
    allowed = (own_tail | own_prompt) & live_slot[None, :]
    step_count = allowed.shape[1] // SPAN
    allowed_steps = allowed.reshape(requests, step_count, SPAN).transpose(1, 0, 2)
    rows_local = w_qkv.shape[1]
    unit_count = w_fc2.shape[1]
    sub_width = w_out.shape[1]
    token_index = jnp.arange(new_tokens, dtype=jnp.int32)
    new_keys = [
        jnp.zeros((requests, new_tokens, heads_local, HEAD_DIM), jnp.bfloat16)
        for layer_index in range(LAYERS)
    ]
    new_values = [
        jnp.zeros((requests, new_tokens, heads_local, HEAD_DIM), jnp.bfloat16)
        for layer_index in range(LAYERS)
    ]
    results = []
    for token_step in range(new_tokens):
        hidden_state = start_states[:, token_step]
        positions = base_positions + token_step
        for layer_index in range(LAYERS):
            normed = layer_norm(hidden_state, ln_gain[layer_index], ln_bias[layer_index]).astype(
                jnp.bfloat16
            )
            my_rows = lax.dynamic_slice_in_dim(normed, seq_index * rows_local, rows_local, 1)
            part_proj = jnp.dot(
                my_rows,
                w_qkv[layer_index].reshape(rows_local, -1),
                preferred_element_type=jnp.float32,
            )
            part_fc1 = jnp.dot(my_rows, w_fc1[layer_index], preferred_element_type=jnp.float32)
            attention_proj, fc1_all = lax.psum((part_proj, part_fc1), "seq")
            pre_act = lax.dynamic_slice_in_dim(fc1_all, seq_index * unit_count, unit_count, 1)
            pre_act = (
                pre_act
                + lax.dynamic_slice_in_dim(
                    b_fc1[layer_index], seq_index * unit_count, unit_count, 0
                )[None, :]
            )
            activated = jax.nn.gelu(pre_act, approximate=True).astype(jnp.bfloat16)
            attention_proj = attention_proj.reshape(requests, 3, heads_local, HEAD_DIM)
            queries = rotary(attention_proj[:, 0], positions).astype(jnp.bfloat16)
            key_rows = rotary(attention_proj[:, 1], positions).astype(jnp.bfloat16)
            value_rows = attention_proj[:, 2].astype(jnp.bfloat16)
            new_keys[layer_index] = new_keys[layer_index].at[:, token_step].set(key_rows)
            new_values[layer_index] = new_values[layer_index].at[:, token_step].set(value_rows)
            key_steps = k_cache[layer_index].reshape(step_count, SPAN, heads_local, HEAD_DIM)
            value_steps = v_cache[layer_index].reshape(step_count, SPAN, heads_local, HEAD_DIM)

            def cache_step(carry, inputs):
                run_max, run_sum, run_out = carry
                key_block, value_block, allow_block = inputs
                scores = (
                    jnp.einsum(
                        "rhd,shd->hrs", queries, key_block, preferred_element_type=jnp.float32
                    )
                    * score_scale
                )
                scores = jnp.where(allow_block[None], scores, very_negative)
                next_max = jnp.maximum(run_max, jnp.max(scores, axis=2))
                weights = jnp.where(allow_block[None], jnp.exp(scores - next_max[..., None]), 0.0)
                shrink = jnp.exp(run_max - next_max)
                next_sum = run_sum * shrink + jnp.sum(weights, axis=2)
                next_out = run_out * shrink[..., None] + jnp.einsum(
                    "hrs,shd->hrd",
                    weights.astype(jnp.bfloat16),
                    value_block,
                    preferred_element_type=jnp.float32,
                )
                return ((next_max, next_sum, next_out), None)

            start_carry = (
                jnp.full((heads_local, requests), very_negative, jnp.float32),
                jnp.zeros((heads_local, requests), jnp.float32),
                jnp.zeros((heads_local, requests, HEAD_DIM), jnp.float32),
            )
            (part_max, part_sum, part_out), unused = lax.scan(
                cache_step, start_carry, (key_steps, value_steps, allowed_steps)
            )
            cache_max = lax.pmax(part_max, "seq")
            factor = jnp.exp(part_max - cache_max)
            cache_sum, cache_out = (
                lax.psum((part_sum * factor).astype(jnp.bfloat16), "seq").astype(jnp.float32),
                lax.psum((part_out * factor[..., None]).astype(jnp.bfloat16), "seq").astype(
                    jnp.float32
                ),
            )
            visible = (token_index <= token_step)[None, None, :]
            fresh_scores = (
                jnp.einsum(
                    "rhd,rjhd->hrj",
                    queries,
                    new_keys[layer_index],
                    preferred_element_type=jnp.float32,
                )
                * score_scale
            )
            fresh_scores = jnp.where(visible, fresh_scores, very_negative)
            fresh_max = jnp.max(fresh_scores, axis=2)
            fresh_weights = jnp.where(visible, jnp.exp(fresh_scores - fresh_max[..., None]), 0.0)
            fresh_sum = jnp.sum(fresh_weights, axis=2)
            fresh_out = jnp.einsum(
                "hrj,rjhd->hrd",
                fresh_weights.astype(jnp.bfloat16),
                new_values[layer_index],
                preferred_element_type=jnp.float32,
            )
            joint_max, denom_total, weighted = combine_parts(
                (cache_max, cache_sum, cache_out), (fresh_max, fresh_sum, fresh_out)
            )
            attended = (weighted / denom_total[..., None]).astype(jnp.bfloat16)
            attended = attended.transpose(1, 0, 2).reshape(requests, width_local)
            my_cols = lax.dynamic_slice_in_dim(attended, seq_index * sub_width, sub_width, 1)
            update = jnp.dot(my_cols, w_out[layer_index], preferred_element_type=jnp.float32)
            update = update + jnp.dot(
                activated, w_fc2[layer_index], preferred_element_type=jnp.float32
            )
            hidden_state = hidden_state + full_total(update)
        results.append(hidden_state)
    stacked = jnp.stack(results, axis=1)
    return stacked


def solution(mesh):
    in_specs = (
        P(),
        P(("seq", "tp"), None),
        P(),
        P(),
        P(),
        P("seq", None),
        P(None, "seq", "tp"),
        P(None, "seq", "tp"),
        P(),
        P(),
        P(None, "seq", None, "tp"),
        P(None, "seq", "tp"),
        P(None, "tp"),
        P(None, ("tp", "seq"), None),
        P(None, ("tp", "seq"), None),
    )
    out_specs = P()
    return jax.shard_map(
        per_device, mesh=mesh, in_specs=in_specs, out_specs=out_specs, check_vma=False
    )
```

profile of v0, /device:TPU:0, one launch (start us, length us, event | category | flops | bytes accessed | tf_op | source)
XLA Modules:
  0.0 1070.1 jit_solution(8516791144763793670)
XLA Ops:
  8.5 6.1 gather_fusion
  16.5 4.1 copy.71
  27.0 4.9 fusion.581
  35.1 122.2 %all-reduce.22.cloned.1.call-done = f32[64,4,2048]{2,0,1:T(8,128)} async-done(((f32[64,4,2048]{2,0,1:T(8,128)}), f32[64,4,2048]{2,0,1:T(8,128)}) %all-reduce.22.cloned.1.call-update) | async-done | bytes 2097168 | tf_op jit(solution)/shard_map/psum | solution.py:60
  173.3 3.6 reshape.1364
  176.9 4.5 copy.76
  181.5 6.2 reshape.1365
  187.7 5.5 copy.77
  194.7 70.2 %all-reduce.30.cloned.1.call-done = (f32[64,3,8,64]{3,0,2,1:T(8,128)}, f32[64,3,8,64]{3,0,2,1:T(8,128)}, f32[64,3,8,64]{3,0,2,1:T(8,128)}, f32[64,3,8,64]{3,0,2,...) async-done(((f32[64,3,8,64]{3,0,2,1:T(8,128)}, f32[64,3,8,64]{3,0,2,1:T(8,128)}, f32[64,3,8,64]{3,0,2,1:T(8,128)}, ...) | async-done | bytes 3670032 | tf_op jit(solution)/shard_map/psum | solution.py:141
  312.5 12.4 %while.142 = (s32[]{:T(128)}, f32[8,64]{1,0:T(8,128)S(1)}, f32[8,64]{1,0:T(8,128)S(1)}, f32[8,64,64]{2,1,0:T(8,128)S(1)}, pred[4,64,512]{2,1,0:T(8,128)(4,1)S(1)...) while((s32[]{:T(128)}, f32[8,64]{1,0:T(8,128)S(1)}, ...), condition=%wide.region_93.94_spmd.clone, body=%wide.region_90.93_spmd.clone.sunk | while | flops 69569024 | bytes 4718725 | solution.py:186
  324.9 12.4 %while.140 = (s32[]{:T(128)}, f32[8,64]{1,0:T(8,128)S(1)}, f32[8,64]{1,0:T(8,128)S(1)}, f32[8,64,64]{2,1,0:T(8,128)S(1)}, pred[4,64,512]{2,1,0:T(8,128)(4,1)S(1)...) while((s32[]{:T(128)}, f32[8,64]{1,0:T(8,128)S(1)}, ...), condition=%wide.region_65.66_spmd.clone, body=%wide.region_62.65_spmd.clone.sunk | while | flops 69569024 | bytes 4718725 | solution.py:186
  337.3 12.8 %while.138 = (s32[]{:T(128)}, f32[8,64]{1,0:T(8,128)S(1)}, f32[8,64]{1,0:T(8,128)S(1)}, f32[8,64,64]{2,1,0:T(8,128)S(1)}, pred[4,64,512]{2,1,0:T(8,128)(4,1)S(1)...) while((s32[]{:T(128)}, f32[8,64]{1,0:T(8,128)S(1)}, ...), condition=%wide.region_37.38_spmd.clone, body=%wide.region_34.37_spmd.clone.sunk | while | flops 69569024 | bytes 4718725 | solution.py:186
  350.1 8.8 while.136
  361.6 23.5 %all-reduce.9 = (f32[8,64]{1,0:T(8,128)S(1)}, f32[8,64]{1,0:T(8,128)S(1)}, f32[8,64]{1,0:T(8,128)S(1)}, f32[8,64]{1,0:T(8,128)S(1)}) all-reduce(f32[8,64]{1,0:T(8,128)S(1)} %get-tuple-element.568, f32[8,64]{1,0:T(8,128)S(1)} %get-tuple-element.550, f32[8,64]{1,0:T(8,128)S(1)} %get-tuple-element.556, ...), channel_id=1, replica_groups=mesh['seq'=8,'tp'=4] {'seq'}, use_global_device_ids=true, to_apply=%region_94.95 | all-reduce | flops 2048 | bytes 16384 | tf_op jit(solution)/shard_map/pmax | solution.py:189
  388.2 12.0 %all-reduce.11 = (bf16[8,64]{1,0:T(8,128)(2,1)S(1)}, bf16[8,64]{1,0:T(8,128)(2,1)S(1)}, bf16[8,64]{1,0:T(8,128)(2,1)S(1)}, bf16[8,64]{1,0:T(8,128)(2,1)S(1)}) all-reduce(bf16[8,64]{1,0:T(8,128)(2,1)S(1)} %get-tuple-element.1165, bf16[8,64]{1,0:T(8,128)(2,1)S(1)} %get-tuple-element.1163, ...), channel_id=1, replica_groups=mesh['seq'=8,'tp'=4] {'seq'}, use_global_device_ids=true, to_apply=%region_97.98 | all-reduce | flops 2048 | bytes 8192 | tf_op jit(solution)/shard_map/psum | solution.py:192
  400.4 54.6 %all-reduce.34.cloned.1.call-done = (bf16[8,64,64]{2,1,0:T(8,128)(2,1)}, bf16[8,64,64]{2,1,0:T(8,128)(2,1)}, bf16[8,64,64]{2,1,0:T(8,128)(2,1)}, bf16[8,64,64]{2,1,0:T(8,128)(2,1)}) async-done(((bf16[8,64,64]{2,1,0:T(8,128)(2,1)}, bf16[8,64,64]{2,1,0:T(8,128)(2,1)}, bf16[8,64,64]{2,1,0:T(8,128)(2,1)}, bf16[8,64,64]{2,1,0:T(8,128)(2,1)}), (bf16[8,64,64]{2,1,0:T(8,128)(2,1)}, bf16[8,64,64]{2,1,0:T(8,128)(2,1)}, ...) | async-done | bytes 262160 | tf_op jit(solution)/shard_map/psum | solution.py:193
  473.7 131.0 %all-reduce.26.cloned.1.call-done = (f32[64,2048]{1,0:T(8,128)}, f32[64,2048]{1,0:T(8,128)}, f32[64,2048]{1,0:T(8,128)}, f32[64,2048]{1,0:T(8,128)}) async-done(((f32[64,2048]{1,0:T(8,128)}, f32[64,2048]{1,0:T(8,128)}, f32[64,2048]{1,0:T(8,128)}, f32[64,2048]{1,0:T(8,128)}), (f32[64,2048]{1,0:T(8,128)}, f32[64,2048]{1,0:T(8,128)}, f32[64,2048]{1,0:T(8,128)}, ...) | async-done | bytes 2097168 | tf_op jit(solution)/shard_map/psum | solution.py:60
  621.1 3.8 reshape.1366
  624.8 4.5 copy.83
  629.4 6.2 reshape.1367
  635.6 5.5 copy.84
  642.4 70.4 %all-reduce.28.cloned.1.call-done = (f32[64,3,8,64]{3,0,2,1:T(8,128)}, f32[64,3,8,64]{3,0,2,1:T(8,128)}, f32[64,3,8,64]{3,0,2,1:T(8,128)}, f32[64,3,8,64]{3,0,2,...) async-done(((f32[64,3,8,64]{3,0,2,1:T(8,128)}, f32[64,3,8,64]{3,0,2,1:T(8,128)}, f32[64,3,8,64]{3,0,2,1:T(8,128)}, ...) | async-done | bytes 3670032 | tf_op jit(solution)/shard_map/psum | solution.py:141
  729.4 12.4 %while.137 = (s32[]{:T(128)}, f32[8,64]{1,0:T(8,128)S(1)}, f32[8,64]{1,0:T(8,128)S(1)}, f32[8,64,64]{2,1,0:T(8,128)S(1)}, pred[4,64,512]{2,1,0:T(8,128)(4,1)S(1)...) while((s32[]{:T(128)}, f32[8,64]{1,0:T(8,128)S(1)}, ...), condition=%wide.region_23.24_spmd.clone, body=%wide.region_20.23_spmd.clone.sunk | while | flops 69569024 | bytes 4718725 | solution.py:186
  754.9 12.4 %while.139 = (s32[]{:T(128)}, f32[8,64]{1,0:T(8,128)S(1)}, f32[8,64]{1,0:T(8,128)S(1)}, f32[8,64,64]{2,1,0:T(8,128)S(1)}, pred[4,64,512]{2,1,0:T(8,128)(4,1)S(1)...) while((s32[]{:T(128)}, f32[8,64]{1,0:T(8,128)S(1)}, ...), condition=%wide.region_51.52_spmd.clone, body=%wide.region_48.51_spmd.clone.sunk | while | flops 69569024 | bytes 4718725 | solution.py:186
  778.5 12.6 %while.141 = (s32[]{:T(128)}, f32[8,64]{1,0:T(8,128)S(1)}, f32[8,64]{1,0:T(8,128)S(1)}, f32[8,64,64]{2,1,0:T(8,128)S(1)}, pred[4,64,512]{2,1,0:T(8,128)(4,1)S(1)...) while((s32[]{:T(128)}, f32[8,64]{1,0:T(8,128)S(1)}, ...), condition=%wide.region_79.80_spmd.clone, body=%wide.region_76.79_spmd.clone.sunk | while | flops 69569024 | bytes 4718725 | solution.py:186
  798.3 2.6 fusion.186
  806.2 8.8 while.143
  815.4 23.4 %all-reduce.8 = (f32[8,64]{1,0:T(8,128)S(1)}, f32[8,64]{1,0:T(8,128)S(1)}, f32[8,64]{1,0:T(8,128)S(1)}, f32[8,64]{1,0:T(8,128)S(1)}) all-reduce(f32[8,64]{1,0:T(8,128)S(1)} %get-tuple-element.571, f32[8,64]{1,0:T(8,128)S(1)} %get-tuple-element.565, f32[8,64]{1,0:T(8,128)S(1)} %get-tuple-element.559, ...), channel_id=1, replica_groups=mesh['seq'=8,'tp'=4] {'seq'}, use_global_device_ids=true, to_apply=%region_108.109 | all-reduce | flops 2048 | bytes 16384 | tf_op jit(solution)/shard_map/pmax | solution.py:189
  842.0 12.0 %all-reduce.10 = (bf16[8,64]{1,0:T(8,128)(2,1)S(1)}, bf16[8,64]{1,0:T(8,128)(2,1)S(1)}, bf16[8,64]{1,0:T(8,128)(2,1)S(1)}, bf16[8,64]{1,0:T(8,128)(2,1)S(1)}) all-reduce(bf16[8,64]{1,0:T(8,128)(2,1)S(1)} %get-tuple-element.1137, bf16[8,64]{1,0:T(8,128)(2,1)S(1)} %get-tuple-element.1135, ...), channel_id=1, replica_groups=mesh['seq'=8,'tp'=4] {'seq'}, use_global_device_ids=true, to_apply=%region_111.112 | all-reduce | flops 2048 | bytes 8192 | tf_op jit(solution)/shard_map/psum | solution.py:192
  856.0 54.6 %all-reduce.32.cloned.1.call-done = (bf16[8,64,64]{2,1,0:T(8,128)(2,1)}, bf16[8,64,64]{2,1,0:T(8,128)(2,1)}, bf16[8,64,64]{2,1,0:T(8,128)(2,1)}, bf16[8,64,64]{2,1,0:T(8,128)(2,1)}) async-done(((bf16[8,64,64]{2,1,0:T(8,128)(2,1)}, bf16[8,64,64]{2,1,0:T(8,128)(2,1)}, bf16[8,64,64]{2,1,0:T(8,128)(2,1)}, bf16[8,64,64]{2,1,0:T(8,128)(2,1)}), (bf16[8,64,64]{2,1,0:T(8,128)(2,1)}, bf16[8,64,64]{2,1,0:T(8,128)(2,1)}, ...) | async-done | bytes 262160 | tf_op jit(solution)/shard_map/psum | solution.py:193
  923.8 134.1 %all-reduce.24.cloned.1.call-done = (f32[64,2048]{1,0:T(8,128)}, f32[64,2048]{1,0:T(8,128)}, f32[64,2048]{1,0:T(8,128)}, f32[64,2048]{1,0:T(8,128)}) async-done(((f32[64,2048]{1,0:T(8,128)}, f32[64,2048]{1,0:T(8,128)}, f32[64,2048]{1,0:T(8,128)}, f32[64,2048]{1,0:T(8,128)}), (f32[64,2048]{1,0:T(8,128)}, f32[64,2048]{1,0:T(8,128)}, f32[64,2048]{1,0:T(8,128)}, ...) | async-done | bytes 2097168 | tf_op jit(solution)/shard_map/psum | solution.py:60
  1060.4 2.7 copy.110
  (716 shorter events, 284.1 us)
Async XLA Ops:
  6.5 150.8 %all-reduce.22.cloned.1.call-start = ((), (), s32[]{:S(2)}) async-start(), calls=%async_computation | async-start | bytes 4194304 | tf_op jit(solution)/shard_map/psum | solution.py:60
  20.7 244.2 %all-reduce.30.cloned.1.call-start = ((), (), s32[]{:S(2)}) async-start(), calls=%async_computation.4 | async-start | bytes 10485760 | tf_op jit(solution)/shard_map/psum | solution.py:141
  22.4 289.1 %copy-start.72 = (pred[4]{0:T(512)(128)(4,1)}, pred[4]{0:T(512)(128)(4,1)S(1)}, u32[]{:S(2)}) copy-start(pred[4]{0:T(512)(128)(4,1)S(1)} %iota_compare_fusion.3) | copy-start | bytes 16
  171.8 283.3 %all-reduce.34.cloned.1.call-start = ((), (), s32[]{:S(2)}) async-start(), calls=%async_computation.6 | async-start | bytes 1048576 | tf_op jit(solution)/shard_map/psum | solution.py:193
  194.6 73.5 %copy-start.47 = (f32[64,16]{1,0:T(8,128)}, f32[64,16]{1,0:T(8,128)S(1)}, u32[]{:S(2)}) copy-start(f32[64,16]{1,0:T(8,128)S(1)} %get-tuple-element.1314) | copy-start | bytes 12292
  194.6 73.5 %copy-start.49 = (f32[64,16]{1,0:T(8,128)}, f32[64,16]{1,0:T(8,128)S(1)}, u32[]{:S(2)}) copy-start(f32[64,16]{1,0:T(8,128)S(1)} %get-tuple-element.1315) | copy-start | bytes 12292
  194.6 78.2 %copy-start.39 = (f32[64,16]{1,0:T(8,128)}, f32[64,16]{1,0:T(8,128)S(1)}, u32[]{:S(2)}) copy-start(f32[64,16]{1,0:T(8,128)S(1)} %get-tuple-element.1312) | copy-start | bytes 12292
  194.6 81.7 %copy-start.35 = (f32[64,16]{1,0:T(8,128)}, f32[64,16]{1,0:T(8,128)S(1)}, u32[]{:S(2)}) copy-start(f32[64,16]{1,0:T(8,128)S(1)} %get-tuple-element.1302) | copy-start | bytes 12292
  194.6 81.7 %copy-start.37 = (f32[64,16]{1,0:T(8,128)}, f32[64,16]{1,0:T(8,128)S(1)}, u32[]{:S(2)}) copy-start(f32[64,16]{1,0:T(8,128)S(1)} %get-tuple-element.1303) | copy-start | bytes 12292
  283.4 6.7 copy-start.60
  359.0 96.1 %copy-start.52 = (f32[8,64,1,64]{3,2,1,0:T(1,128)S(1)}, f32[8,64,1,64]{3,2,1,0:T(1,128)}, u32[]{:S(2)}) copy-start(f32[8,64,1,64]{3,2,1,0:T(1,128)} %fusion.190) | copy-start | bytes 393220
  361.6 95.6 %copy-start.51 = (f32[8,64,1,64]{3,2,1,0:T(1,128)S(1)}, f32[8,64,1,64]{3,2,1,0:T(1,128)}, u32[]{:S(2)}) copy-start(f32[8,64,1,64]{3,2,1,0:T(1,128)} %fusion.198) | copy-start | bytes 393220
  385.1 74.1 %copy-start.50 = (f32[8,64,1,64]{3,2,1,0:T(1,128)S(1)}, f32[8,64,1,64]{3,2,1,0:T(1,128)}, u32[]{:S(2)}) copy-start(f32[8,64,1,64]{3,2,1,0:T(1,128)} %fusion.206) | copy-start | bytes 393220
  387.5 72.2 %copy-start.56 = (f32[8,64,1,64]{3,2,1,0:T(1,128)S(1)}, f32[8,64,1,64]{3,2,1,0:T(1,128)}, u32[]{:S(2)}) copy-start(f32[8,64,1,64]{3,2,1,0:T(1,128)} %fusion.182) | copy-start | bytes 393220
  400.3 59.9 %copy-start.10 = (bf16[2,64,2048]{2,1,0:T(8,128)(2,1)S(1)}, bf16[2,64,2048]{2,1,0:T(8,128)(2,1)}, u32[]{:S(2)}) copy-start(bf16[2,64,2048]{2,1,0:T(8,128)(2,1)} %param.76) | copy-start | bytes 1572868
  400.4 204.4 %all-reduce.26.cloned.1.call-start = ((), (), s32[]{:S(2)}) async-start(), calls=%async_computation.2 | async-start | bytes 4194304 | tf_op jit(solution)/shard_map/psum | solution.py:60
  470.6 134.1 %copy-start.1 = (f32[64,4,2048]{2,0,1:T(8,128)S(1)}, f32[64,4,2048]{2,0,1:T(8,128)}, u32[]{:S(2)}) copy-start(f32[64,4,2048]{2,0,1:T(8,128)} %all-reduce.22.cloned.1.call-done) | copy-start | bytes 6291460
  470.6 242.1 %all-reduce.28.cloned.1.call-start = ((), (), s32[]{:S(2)}) async-start(), calls=%async_computation.3 | async-start | bytes 10485760 | tf_op jit(solution)/shard_map/psum | solution.py:141
  619.5 291.0 %all-reduce.32.cloned.1.call-start = ((), (), s32[]{:S(2)}) async-start(), calls=%async_computation.5 | async-start | bytes 1048576 | tf_op jit(solution)/shard_map/psum | solution.py:193
  635.6 80.8 %copy-start.48 = (f32[64,16]{1,0:T(8,128)S(1)}, f32[64,16]{1,0:T(8,128)}, u32[]{:S(2)}) copy-start(f32[64,16]{1,0:T(8,128)} %copy-done.47) | copy-start | bytes 12292
  806.2 8.8 copy-start.73
  815.0 39.0 %copy-start.71 = (f32[8,64]{1,0:T(8,128)S(1)}, f32[8,64]{1,0:T(8,128)}, u32[]{:S(2)}) copy-start(f32[8,64]{1,0:T(8,128)} %get-tuple-element.1284) | copy-start | bytes 6148
  815.0 39.0 %copy-start.70 = (f32[8,64]{1,0:T(8,128)S(1)}, f32[8,64]{1,0:T(8,128)}, u32[]{:S(2)}) copy-start(f32[8,64]{1,0:T(8,128)} %get-tuple-element.1282) | copy-start | bytes 6148
  838.8 17.1 %copy-start.69 = (f32[8,64]{1,0:T(8,128)S(1)}, f32[8,64]{1,0:T(8,128)}, u32[]{:S(2)}) copy-start(f32[8,64]{1,0:T(8,128)} %get-tuple-element.1280) | copy-start | bytes 6148
  838.8 71.7 %copy-start.53 = (f32[8,64,1,64]{3,2,1,0:T(1,128)S(1)}, f32[8,64,1,64]{3,2,1,0:T(1,128)}, u32[]{:S(2)}) copy-start(f32[8,64,1,64]{3,2,1,0:T(1,128)} %fusion.202) | copy-start | bytes 393220
  841.2 70.8 %copy-start.54 = (f32[8,64,1,64]{3,2,1,0:T(1,128)S(1)}, f32[8,64,1,64]{3,2,1,0:T(1,128)}, u32[]{:S(2)}) copy-start(f32[8,64,1,64]{3,2,1,0:T(1,128)} %fusion.194) | copy-start | bytes 393220
  854.1 59.4 %copy-start.55 = (f32[8,64,1,64]{3,2,1,0:T(1,128)S(1)}, f32[8,64,1,64]{3,2,1,0:T(1,128)}, u32[]{:S(2)}) copy-start(f32[8,64,1,64]{3,2,1,0:T(1,128)} %fusion.186) | copy-start | bytes 393220
  855.9 58.6 %copy-start.11 = (bf16[2,64,2048]{2,1,0:T(8,128)(2,1)S(1)}, bf16[2,64,2048]{2,1,0:T(8,128)(2,1)}, u32[]{:S(2)}) copy-start(bf16[2,64,2048]{2,1,0:T(8,128)(2,1)} %param.76) | copy-start | bytes 1572868
  855.9 202.0 %all-reduce.24.cloned.1.call-start = ((), (), s32[]{:S(2)}) async-start(), calls=%async_computation.1 | async-start | bytes 4194304 | tf_op jit(solution)/shard_map/psum | solution.py:60
  921.6 136.3 %copy-start.2 = (f32[64,4,2048]{2,0,1:T(8,128)S(1)}, f32[64,4,2048]{2,0,1:T(8,128)}, u32[]{:S(2)}) copy-start(f32[64,4,2048]{2,0,1:T(8,128)} %all-reduce.22.cloned.1.call-done) | copy-start | bytes 6291460
  921.6 136.3 %copy-start.13 = (f32[64,2048]{1,0:T(8,128)S(1)}, f32[64,2048]{1,0:T(8,128)}, u32[]{:S(2)}) copy-start(f32[64,2048]{1,0:T(8,128)} %get-tuple-element.1059) | copy-start | bytes 1572868
  921.6 136.3 %copy-start.15 = (f32[64,2048]{1,0:T(8,128)S(1)}, f32[64,2048]{1,0:T(8,128)}, u32[]{:S(2)}) copy-start(f32[64,2048]{1,0:T(8,128)} %get-tuple-element.1060) | copy-start | bytes 1572868
  (62 other events, 211.5 us)
Sparse Core Ops, SparseCore 0:
  20.8 136.4 all-reduce.21
  171.9 92.9 all-reduce.29
  400.5 54.5 all-reduce.33
  470.8 133.9 all-reduce.25
  619.6 93.0 all-reduce.27
  856.0 54.4 all-reduce.31
  923.9 133.9 all-reduce.23
where the time goes:
time: 1080 us; the launch traced here: 1070 us
  waiting for transfers between devices  637 us (59%)
  matrix products  143 us (13%)
  local copies, waits for them, and re-layouts  131 us (12%)
  blocking collectives  70.9 us (7%)
  other arithmetic  69.8 us (6%)
  between operations  15.3 us (1%)
    psum x3, waiting for transfers between devices, full_total(): return lax.psum(values, ('seq', 'tp'))  387 us
    psum x2, waiting for transfers between devices, per_device(): attention_proj, fc1_all = lax.psum((part_proj, part_fc1), 'seq')  141 us
    psum x2, waiting for transfers between devices, per_device(): lax.psum((part_out * factor[..., None]).astype(jnp.bfloat16), 'seq')  109 us
    pmax x2, blocking collectives, per_device(): cache_max = lax.pmax(part_max, 'seq')  46.8 us
    dot_general x32, matrix products, cache_step(): jnp.einsum('hrs,shd->hrd', weights.astype(jnp.bfloat16), value_block, pre...  44.8 us
    dot_general x32, matrix products, cache_step(): jnp.einsum('rhd,shd->hrs', queries, key_block, preferred_element_type=jnp...  33.1 us
    unnamed x184, local copies, waits for them, and re-layouts  30 us
    psum x2, blocking collectives, per_device(): lax.psum((part_sum * factor).astype(jnp.bfloat16), 'seq')  24 us
  transfers between devices with their start and end apart: 7, of which 7 were waited for; matrix products, arithmetic and copies ran while one was open for 6% of the time, Pallas kernels for 0%

commit v1 on v0

--- a/solution.py
+++ b/solution.py
@@ -1,8 +1,11 @@
+import functools
 import math
 
 import jax
 import jax.numpy as jnp
 from jax import lax
+from jax.experimental import pallas as pl
+from jax.experimental.pallas import tpu as pltpu
 from jax.sharding import PartitionSpec as P
 
 HEADS = 32
@@ -60,7 +63,7 @@
     return lax.psum(values, ("seq", "tp"))
 
 
-def per_device(
+def per_device_any(
     token_ids,
     embedding,
     group_of,
@@ -230,6 +233,490 @@
     return stacked
 
 
+def swap_cores(values, seq_count):
+    return lax.ppermute(values, "seq", [(i, i ^ 1) for i in range(seq_count)])
+
+
+def compiler_params(megabytes=32):
+    return pltpu.CompilerParams(vmem_limit_bytes=megabytes * 2**20)
+
+
+def whole(memory_space=pltpu.VMEM):
+    return pl.BlockSpec(memory_space=memory_space)
+
+
+def layer_block(layer_index, shape):
+    return pl.BlockSpec((1,) + shape, lambda step: (layer_index,) + (0,) * len(shape))
+
+
+def same_block(shape):
+    return pl.BlockSpec(shape, lambda step: (0,) * len(shape))
+
+
+def order_kernel(token_ref, group_ref, prefix_ref, tail_ref, rank_ref, id_ref, position_ref, count_ref):
+    requests, new_tokens = token_ref.shape
+    groups = prefix_ref.shape[0]
+    per_group = requests // groups
+    for group in range(groups):
+        count_ref[group] = 0
+
+    def place(request, unused):
+        group = group_ref[request]
+        seat = count_ref[group]
+        count_ref[group] = seat + 1
+        rank = group * per_group + seat
+        rank_ref[request] = rank
+        start = prefix_ref[group] + tail_ref[request]
+        for token in range(new_tokens):
+            id_ref[rank * new_tokens + token] = token_ref[request, token]
+            position_ref[rank * new_tokens + token] = start + token
+        return unused
+
+    lax.fori_loop(0, requests, place, 0)
+
+
+def order_requests(token_ids, group_of, prefix_len, tail_len):
+    requests, new_tokens = token_ids.shape
+    rows = requests * new_tokens
+    smem = whole(pltpu.SMEM)
+    return pl.pallas_call(
+        order_kernel,
+        out_shape=(
+            jax.ShapeDtypeStruct((requests,), jnp.int32),
+            jax.ShapeDtypeStruct((rows,), jnp.int32),
+            jax.ShapeDtypeStruct((rows,), jnp.int32),
+        ),
+        in_specs=[smem] * 4,
+        out_specs=(smem, smem, smem),
+        scratch_shapes=[pltpu.SMEM((prefix_len.shape[0],), jnp.int32)],
+        name="order_requests",
+    )(token_ids, group_of, prefix_len, tail_len)
+
+
+def state_total(part_ref, state_ref):
+    total = part_ref[0].astype(jnp.float32)
+    for source in range(1, part_ref.shape[0]):
+        total = total + part_ref[source].astype(jnp.float32)
+    if state_ref is not None:
+        total = total + state_ref[...]
+    return total
+
+
+def norm_kernel(has_state, tp_count, *refs):
+    if has_state:
+        part_ref, state_ref, gain_ref, bias_ref, next_ref, cut_ref = refs
+    else:
+        part_ref, gain_ref, bias_ref, next_ref, cut_ref = refs
+        state_ref = None
+    state = state_total(part_ref, state_ref)
+    next_ref[...] = state
+    average = jnp.mean(state, axis=-1, keepdims=True)
+    centred = state - average
+    variance = jnp.mean(centred * centred, axis=-1, keepdims=True)
+    gain = gain_ref[0, 0][None, :]
+    bias = bias_ref[0, 0][None, :]
+    normed = (centred * lax.rsqrt(variance + 1e-05) * gain + bias).astype(jnp.bfloat16)
+    width = cut_ref.shape[2]
+    for place in range(cut_ref.shape[0]):
+        start = (place // tp_count) * width
+        cut_ref[place] = normed[:, start : start + width]
+
+
+def norm_rows(parts, state, ln_gain, ln_bias, layer_index, devices, tp_count):
+    count, rows, width = parts.shape
+    cut = width // (devices // tp_count)
+    gains = [ln_gain[:, None, :], ln_bias[:, None, :]]
+    operands = [parts] + ([] if state is None else [state]) + gains
+    in_specs = [same_block(parts.shape)] + ([] if state is None else [same_block(state.shape)])
+    in_specs += [layer_block(layer_index, (1, width))] * 2
+    return pl.pallas_call(
+        functools.partial(norm_kernel, state is not None, tp_count),
+        grid=(1,),
+        out_shape=(
+            jax.ShapeDtypeStruct((rows, width), jnp.float32),
+            jax.ShapeDtypeStruct((devices, rows, cut), jnp.bfloat16),
+        ),
+        in_specs=in_specs,
+        out_specs=(same_block((rows, width)), same_block((devices, rows, cut))),
+        compiler_params=compiler_params(),
+        name="norm_rows",
+    )(*operands)
+
+
+def last_kernel(part_ref, state_ref, out_ref):
+    state = state_total(part_ref, state_ref).astype(jnp.bfloat16)
+    for place in range(out_ref.shape[0]):
+        out_ref[place] = state
+
+
+def last_rows(parts, state):
+    return pl.pallas_call(
+        last_kernel,
+        out_shape=jax.ShapeDtypeStruct(parts.shape, jnp.bfloat16),
+        in_specs=[whole(), whole()],
+        out_specs=whole(),
+        compiler_params=compiler_params(),
+        name="last_rows",
+    )(parts, state)
+
+
+def project_kernel(parity_ref, hidden_ref, qkv_ref, fc1_ref, out_ref):
+    parity = parity_ref[0]
+    chips = out_ref.shape[0]
+    rows, depth = hidden_ref.shape
+    unit = fc1_ref.shape[2] // (2 * chips)
+    share = rows // (2 * chips)
+    hidden = hidden_ref[...]
+    picked = []
+    for chip in range(chips):
+        place = 2 * chip + parity
+        columns = pl.ds(pl.multiple_of(place * unit, unit), unit)
+        out_ref[chip, :rows] = jnp.dot(
+            hidden, fc1_ref[0, :, columns], preferred_element_type=jnp.float32
+        ).astype(jnp.bfloat16)
+        picked.append(hidden_ref[pl.ds(pl.multiple_of(place * share, share), share), :])
+    heads = jnp.dot(
+        jnp.concatenate(picked, axis=0), qkv_ref[...], preferred_element_type=jnp.float32
+    ).astype(jnp.bfloat16)
+    for chip in range(chips):
+        for piece in range(heads.shape[1] // unit):
+            start = rows + piece * share
+            out_ref[chip, start : start + share] = heads[
+                chip * share : (chip + 1) * share, piece * unit : (piece + 1) * unit
+            ]
+
+
+def project(parity, hidden, weights_qkv, w_fc1, layer_index, chips):
+    rows, depth = hidden.shape
+    unit = w_fc1.shape[2] // (2 * chips)
+    share = rows // (2 * chips)
+    height = rows + share * (weights_qkv.shape[1] // unit)
+    return pl.pallas_call(
+        project_kernel,
+        grid=(1,),
+        out_shape=jax.ShapeDtypeStruct((chips, height, unit), jnp.bfloat16),
+        in_specs=[
+            whole(pltpu.SMEM),
+            same_block(hidden.shape),
+            same_block(weights_qkv.shape),
+            layer_block(layer_index, w_fc1.shape[1:]),
+        ],
+        out_specs=same_block((chips, height, unit)),
+        compiler_params=compiler_params(),
+        name="project",
+    )(parity, hidden, weights_qkv, w_fc1)
+
+
+def activate_kernel(part_ref, bias_ref, keep_ref, down_ref, up_ref, gelu_ref, query_ref, key_ref, value_ref):
+    total = part_ref[0].astype(jnp.float32)
+    for chip in range(1, part_ref.shape[0]):
+        total = total + part_ref[chip].astype(jnp.float32)
+    rows, unit = gelu_ref.shape
+    share, width = query_ref.shape
+    gelu_ref[...] = jax.nn.gelu(total[:rows] + bias_ref[...], approximate=True).astype(jnp.bfloat16)
+    pieces = width // unit
+
+    def one(index):
+        start = rows + index * pieces * share
+        return jnp.concatenate(
+            [total[start + i * share : start + (i + 1) * share] for i in range(pieces)], axis=1
+        )
+
+    def turned(values):
+        return (
+            values * keep_ref[...]
+            + pltpu.roll(values, width - ROT // 2, 1) * down_ref[...]
+            + pltpu.roll(values, ROT // 2, 1) * up_ref[...]
+        )
+
+    query_ref[...] = turned(one(0)).astype(jnp.bfloat16)
+    key_ref[...] = turned(one(1)).astype(jnp.bfloat16)
+    value_ref[...] = one(2).astype(jnp.bfloat16)
+
+
+def activate(parts, bias, tables, rows):
+    chips, height, unit = parts.shape
+    share, width = tables[0].shape
+    small = jax.ShapeDtypeStruct((share, width), jnp.bfloat16)
+    return pl.pallas_call(
+        activate_kernel,
+        out_shape=(jax.ShapeDtypeStruct((rows, unit), jnp.bfloat16), small, small, small),
+        in_specs=[whole()] * 5,
+        out_specs=(whole(),) * 4,
+        compiler_params=compiler_params(),
+        name="activate",
+    )(parts, bias, *tables)
+
+
+def rotary_tables(positions, width):
+    half = ROT // 2
+    feature = lax.broadcasted_iota(jnp.int32, (1, width), 1) % HEAD_DIM
+    frequency = jnp.exp((feature % half).astype(jnp.float32) * (-2.0 * math.log(10000.0) / ROT))
+    angles = positions.astype(jnp.float32)[:, None] * frequency
+    cosine, sine = jnp.cos(angles), jnp.sin(angles)
+    return (
+        jnp.where(feature < ROT, cosine, 1.0),
+        jnp.where(feature < half, -sine, 0.0),
+        jnp.where((feature >= half) & (feature < ROT), sine, 0.0),
+    )
+
+
+def attend_kernel(
+    layer_index, new_tokens,
+    place_ref, rank_ref, map_ref, prefix_ref, tail_ref, query_ref, new_key_ref, new_value_ref,
+    key_hbm, value_hbm, out_ref, key_ref, value_ref, top_ref, sum_ref, mix_ref, semaphores,
+):
+    blocks = map_ref.shape[0]
+    groups, tall, lanes = mix_ref.shape
+    requests = rank_ref.shape[0]
+    per_group = requests // groups
+    share = per_group * new_tokens
+    pairs = tall // (2 * share)
+    chunks = semaphores.shape[1]
+    chunk = key_ref.shape[0] // chunks
+    scale = 1.0 / math.sqrt(HEAD_DIM)
+
+    def copies(index):
+        span = pl.ds(index * chunk, chunk)
+        return (
+            pltpu.make_async_copy(key_hbm.at[layer_index, span], key_ref.at[span], semaphores.at[0, index]),
+            pltpu.make_async_copy(value_hbm.at[layer_index, span], value_ref.at[span], semaphores.at[1, index]),
+        )
+
+    for index in range(chunks):
+        for copy in copies(index):
+            copy.start()
+    lane = lax.broadcasted_iota(jnp.int32, (share, lanes), 1)
+    wide_lane = lax.broadcasted_iota(jnp.int32, (tall, BLOCK), 1)
+    wide_row = lax.broadcasted_iota(jnp.int32, (tall, BLOCK), 0) % share
+    top_ref[...] = jnp.full(top_ref.shape, very_negative, jnp.float32)
+    sum_ref[...] = jnp.zeros(sum_ref.shape, jnp.float32)
+    mix_ref[...] = jnp.zeros(mix_ref.shape, jnp.float32)
+
+    def visit(group, keys, values, mask):
+        rows = pl.ds(pl.multiple_of(group * share, share), share)
+        scores = []
+        for pair in range(pairs):
+            both = query_ref[rows, pair * lanes : (pair + 1) * lanes]
+            none = jnp.zeros_like(both)
+            split = jnp.concatenate(
+                [jnp.where(lane < HEAD_DIM, both, none), jnp.where(lane < HEAD_DIM, none, both)], axis=0
+            )
+            scores.append(
+                lax.dot_general(
+                    split, keys[:, pair * lanes : (pair + 1) * lanes], (((1,), (1,)), ((), ())),
+                    preferred_element_type=jnp.float32,
+                )
+            )
+        score = jnp.where(mask, jnp.concatenate(scores, axis=0) * scale, very_negative)
+        top = jnp.max(score, axis=1, keepdims=True)
+        weight = jnp.where(mask, jnp.exp(score - top), 0.0)
+        total = jnp.sum(weight, axis=1, keepdims=True)
+        rounded = weight.astype(jnp.bfloat16)
+        mixed = jnp.concatenate(
+            [
+                jnp.dot(
+                    rounded[pair * 2 * share : (pair + 1) * 2 * share],
+                    values[:, pair * lanes : (pair + 1) * lanes],
+                    preferred_element_type=jnp.float32,
+                )
+                for pair in range(pairs)
+            ],
+            axis=0,
+        )
+        old_top = top_ref[group]
+        joint = jnp.maximum(old_top, top)
+        shrink, scale_new = jnp.exp(old_top - joint), jnp.exp(top - joint)
+        top_ref[group] = joint
+        sum_ref[group] = sum_ref[group] * shrink + total * scale_new
+        mix_ref[group] = mix_ref[group] * shrink + mixed * scale_new
+
+    for block in range(blocks):
+        if (block * BLOCK) % chunk == 0:
+            for copy in copies(block * BLOCK // chunk):
+                copy.wait()
+        segment, depth = map_ref[block, 0], map_ref[block, 1]
+        is_tail = segment >= groups
+        request = jnp.clip(segment - groups, 0, requests - 1)
+        prompt = jnp.clip(segment, 0, groups - 1)
+        seat = rank_ref[request]
+        group = jnp.where(is_tail, seat // per_group, prompt)
+        length = jnp.where(is_tail, tail_ref[request], prefix_ref[prompt])
+        live = jnp.where(segment < 0, 0, length - depth * BLOCK)
+        first = jnp.where(is_tail, (seat % per_group) * new_tokens, 0)
+        end = jnp.where(is_tail, first + new_tokens, share)
+        mask = (wide_lane < live) & (wide_row >= first) & (wide_row < end)
+        span = slice(block * BLOCK, (block + 1) * BLOCK)
+        visit(group, key_ref[span, :], value_ref[span, :], mask)
+
+    fill = jnp.zeros((BLOCK - share, new_key_ref.shape[1]), jnp.bfloat16)
+    mask = (wide_lane // new_tokens == wide_row // new_tokens) & (wide_lane <= wide_row)
+    visit(
+        place_ref[0],
+        jnp.concatenate([new_key_ref[...], fill], axis=0),
+        jnp.concatenate([new_value_ref[...], fill], axis=0),
+        mask,
+    )
+
+    for group in range(groups):
+        total = sum_ref[group]
+        empty = total <= 0.0
+        mean = mix_ref[group] / jnp.where(empty, 1.0, total)
+        level = jnp.where(empty, very_negative, top_ref[group] + jnp.log(jnp.where(empty, 1.0, total)))
+        high = level.astype(jnp.bfloat16).astype(jnp.float32)
+        middle = (level - high).astype(jnp.bfloat16).astype(jnp.float32)
+        low = level - high - middle
+        for head in range(2 * pairs):
+            rows = slice(head * share, (head + 1) * share)
+            own = mean[rows]
+            if head % 2:
+                own = pltpu.roll(own, lanes - HEAD_DIM, 1)
+            packed = jnp.where(lane < HEAD_DIM, own, 0.0)
+            packed = jnp.where(lane == HEAD_DIM, high[rows], packed)
+            packed = jnp.where(lane == HEAD_DIM + 1, middle[rows], packed)
+            packed = jnp.where(lane == HEAD_DIM + 2, low[rows], packed)
+            out_ref[head, group * share : (group + 1) * share] = packed.astype(jnp.bfloat16)
+
+
+def attend(place, rank, block_map, prefix_len, tail_len, query, new_key, new_value, k_cache, v_cache, layer_index, new_tokens):
+    rows, width = query.shape
+    groups = prefix_len.shape[0]
+    slots = k_cache.shape[1]
+    heads = width // HEAD_DIM
+    tall = heads * (rows // groups)
+    lanes = 2 * HEAD_DIM
+    chunks = 4
+    return pl.pallas_call(
+        functools.partial(attend_kernel, layer_index, new_tokens),
+        out_shape=jax.ShapeDtypeStruct((heads, rows, lanes), jnp.bfloat16),
+        in_specs=[whole(pltpu.SMEM)] * 5 + [whole()] * 3 + [whole(pl.ANY)] * 2,
+        out_specs=whole(),
+        scratch_shapes=[
+            pltpu.VMEM((slots, width), jnp.bfloat16),
+            pltpu.VMEM((slots, width), jnp.bfloat16),
+            pltpu.VMEM((groups, tall, 1), jnp.float32),
+            pltpu.VMEM((groups, tall, 1), jnp.float32),
+            pltpu.VMEM((groups, tall, lanes), jnp.float32),
+            pltpu.SemaphoreType.DMA((2, chunks)),
+        ],
+        compiler_params=compiler_params(),
+        name="attend",
+    )(place, rank, block_map, prefix_len, tail_len, query, new_key, new_value, k_cache, v_cache)
+
+
+def update_kernel(share, parity_ref, part_ref, gelu_ref, out_weight_ref, fc2_ref, out_ref):
+    parity = parity_ref[0]
+    pieces = out_ref.shape[0] // share
+    attended, hidden = [], []
+    for piece in range(pieces):
+        rows = pl.ds(pl.multiple_of((2 * piece + parity) * share, share), share)
+        parts = [part_ref[source, rows, :].astype(jnp.float32) for source in range(part_ref.shape[0])]
+        levels = [
+            part[:, HEAD_DIM : HEAD_DIM + 1] + part[:, HEAD_DIM + 1 : HEAD_DIM + 2] + part[:, HEAD_DIM + 2 : HEAD_DIM + 3]
+            for part in parts
+        ]
+        top = functools.reduce(jnp.maximum, levels)
+        scales = [jnp.exp(level - top) for level in levels]
+        total = functools.reduce(jnp.add, scales)
+        mixed = functools.reduce(jnp.add, [part * scale for part, scale in zip(parts, scales)])
+        attended.append((mixed / total)[:, :HEAD_DIM].astype(jnp.bfloat16))
+        hidden.append(gelu_ref[rows, :])
+    out_ref[...] = (
+        jnp.dot(jnp.concatenate(attended, axis=0), out_weight_ref[0], preferred_element_type=jnp.float32)
+        + jnp.dot(jnp.concatenate(hidden, axis=0), fc2_ref[0], preferred_element_type=jnp.float32)
+    ).astype(jnp.bfloat16)
+
+
+def update(parity, parts, gelu, w_out, w_fc2, layer_index, share):
+    rows = gelu.shape[0] // 2
+    width = w_out.shape[2]
+    return pl.pallas_call(
+        functools.partial(update_kernel, share),
+        grid=(1,),
+        out_shape=jax.ShapeDtypeStruct((rows, width), jnp.bfloat16),
+        in_specs=[
+            whole(pltpu.SMEM),
+            same_block(parts.shape),
+            same_block(gelu.shape),
+            layer_block(layer_index, w_out.shape[1:]),
+            layer_block(layer_index, w_fc2.shape[1:]),
+        ],
+        out_specs=same_block((rows, width)),
+        compiler_params=compiler_params(),
+        name="update",
+    )(parity, parts, gelu, w_out, w_fc2)
+
+
+def per_device(
+    token_ids, embedding, group_of, prefix_len, tail_len, block_map, k_cache, v_cache,
+    ln_gain, ln_bias, w_qkv, w_fc1, b_fc1, w_out, w_fc2,
+):
+    seq_count, tp_count = lax.axis_size("seq"), lax.axis_size("tp")
+    seq_index, tp_index = lax.axis_index("seq"), lax.axis_index("tp")
+    devices = seq_count * tp_count
+    chips = seq_count // 2
+    core = seq_index % 2
+    own = jnp.reshape(core, (1,)).astype(jnp.int32)
+    other = 1 - own
+    requests, new_tokens = token_ids.shape
+    rows = requests * new_tokens
+    share = rows // seq_count
+    mine = rows // devices
+    width = embedding.shape[1]
+    width_local = k_cache.shape[2]
+    unit = w_fc2.shape[1]
+    same_core = [[s * tp_count + p for s in range(c, seq_count, 2) for p in range(tp_count)] for c in range(2)]
+    same_core_seq = [list(range(c, seq_count, 2)) for c in range(2)]
+
+    def to_owners(half):
+        parts = half.reshape(devices // 2, mine, width)
+        return lax.all_to_all(parts, ("seq", "tp"), 0, 0, axis_index_groups=same_core)
+
+    rank, ids, positions = order_requests(token_ids, group_of, prefix_len, tail_len)
+    vocab_rows = embedding.shape[0]
+    local_ids = (ids - (seq_index * tp_count + tp_index) * vocab_rows).reshape(chips, 2, share)
+
+    def pick(parity):
+        chosen = lax.dynamic_index_in_dim(local_ids, parity, 1, keepdims=False).reshape(-1)
+        hot = (chosen[:, None] == jnp.arange(vocab_rows, dtype=jnp.int32)[None, :]).astype(jnp.bfloat16)
+        return jnp.dot(hot, embedding, preferred_element_type=jnp.float32).astype(jnp.bfloat16)
+
+    arriving = swap_cores(pick(1 - core), seq_count)
+    parts = to_owners(pick(core) + arriving)
+    tables = rotary_tables(lax.dynamic_slice_in_dim(positions, seq_index * share, share, 0), width_local)
+    place = jnp.reshape(seq_index, (1,)).astype(jnp.int32)
+    state = None
+    for layer_index in range(LAYERS):
+        weights_qkv = w_qkv[layer_index].reshape(w_qkv.shape[1], -1)
+        bias = lax.dynamic_slice_in_dim(b_fc1[layer_index], seq_index * unit, unit, 0)[None, :]
+        state, cut = norm_rows(parts, state, ln_gain, ln_bias, layer_index, devices, tp_count)
+        hidden = lax.all_to_all(cut, ("seq", "tp"), 0, 0).reshape(rows, -1)
+        arriving = swap_cores(project(other, hidden, weights_qkv, w_fc1, layer_index, chips), seq_count)
+        kept = project(own, hidden, weights_qkv, w_fc1, layer_index, chips)
+        joined = lax.all_to_all(kept + arriving, "seq", 0, 0, axis_index_groups=same_core_seq)
+        gelu, query, new_key, new_value = activate(joined, bias, tables, rows)
+        queries = lax.all_gather(query, "seq").reshape(rows, width_local)
+        parts = attend(
+            place, rank, block_map, prefix_len, tail_len, queries, new_key, new_value,
+            k_cache, v_cache, layer_index, new_tokens,
+        )
+        parts = lax.all_to_all(parts, "seq", 0, 0)
+        arriving = swap_cores(update(other, parts, gelu, w_out, w_fc2, layer_index, share), seq_count)
+        parts = to_owners(update(own, parts, gelu, w_out, w_fc2, layer_index, share) + arriving)
+    last = lax.all_to_all(last_rows(parts, state), ("seq", "tp"), 0, 0, axis_index_groups=same_core)
+    last = last.reshape(rows // 2, width)
+    arriving = swap_cores(last, seq_count)
+    wanted = (rank[:, None] * new_tokens + jnp.arange(new_tokens, dtype=jnp.int32)[None, :]).reshape(-1)
+    index = jnp.arange(rows // 2, dtype=jnp.int32)
+
+    def placed(half, parity):
+        held = (2 * (index // share) + parity) * share + index % share
+        hot = (wanted[:, None] == held[None, :]).astype(jnp.bfloat16)
+        return jnp.dot(hot, half, preferred_element_type=jnp.float32)
+
+    return (placed(last, core) + placed(arriving, 1 - core)).reshape(requests, new_tokens, width)
+
+
 def solution(mesh):
     in_specs = (
         P(),
@@ -249,6 +736,8 @@
         P(None, ("tp", "seq"), None),
     )
     out_specs = P()
+    seq_count, tp_count = mesh.shape["seq"], mesh.shape["tp"]
+    fits = seq_count == HEADS // tp_count and seq_count == 8
     return jax.shard_map(
-        per_device, mesh=mesh, in_specs=in_specs, out_specs=out_specs, check_vma=False
+        per_device if fits else per_device_any, mesh=mesh, in_specs=in_specs, out_specs=out_specs, check_vma=False
     )

time: 1080 us -> 249 us (0.23)
  waiting for transfers between devices: 637 us -> 74.1 us
  matrix products: 143 us -> 9.78 us
  local copies, waits for them, and re-layouts: 131 us -> 21.6 us
  other arithmetic: 69.8 us -> 3.62 us
  Pallas kernels: 0 us -> 30.3 us
  starting transfers between devices: 0.43 us -> 25.2 us
  between operations: 15.3 us -> 0.46 us
  blocking collectives: 70.9 us -> 82.3 us
    psum x7 -> x0, waiting for transfers between devices: 637 us -> none  [the longest x3 387 us: full_total(): return lax.psum(values, ('seq', 'tp'))]
    dot_general x112 -> x4, matrix products: 143 us -> 9.78 us  [the longest x2 8.84 us: pick(): jnp.dot(hot, embedding, preferred_element_type=jnp.float32)]
    all_to_all x0 -> x6, waiting for transfers between devices: none -> 65.9 us  [the longest x2 24.3 us: per_device(): lax.all_to_all(kept + arriving, 'seq', 0, 0, axis_index_groups=same_core_...]
    all_to_all x0 -> x4, blocking collectives: none -> 63.4 us  [the longest x2 38.8 us: to_owners(): lax.all_to_all(parts, ('seq', 'tp'), 0, 0, axis_index_groups=same_core)]
    pmax x2 -> x0, blocking collectives: 46.8 us -> none  [per_device(): cache_max = lax.pmax(part_max, 'seq')]
    pallas_call x0 -> x16, Pallas kernels: none -> 30.3 us  [the longest x2 19.2 us: attend(): pl.pallas_call(functools.partial(attend_kernel, layer_index, new_tokens),...]
    all_to_all x0 -> x6, starting transfers between devices: none -> 24.4 us  [the longest x1 8.36 us: to_owners(): lax.all_to_all(parts, ('seq', 'tp'), 0, 0, axis_index_groups=same_core)]
    psum x2 -> x0, blocking collectives: 24 us -> none  [per_device(): lax.psum((part_sum * factor).astype(jnp.bfloat16), 'seq')]
  transfers between devices with their start and end apart: 7 -> 12, of which waited for: 7 -> 12; matrix products, arithmetic and copies ran while one was open for 6% -> 4% of each run, Pallas kernels for 0% -> 1%
where the time goes in v1:
time: 249 us; the launch traced here: 247 us
  blocking collectives  82.3 us (33%)
  waiting for transfers between devices  74.1 us (30%)
  Pallas kernels  30.3 us (12%)
  starting transfers between devices  25.2 us (10%)
  local copies, waits for them, and re-layouts  21.6 us (9%)
  matrix products  9.78 us (4%)
  other arithmetic  3.62 us (1%)
    all_to_all x2, blocking collectives, to_owners(): lax.all_to_all(parts, ('seq', 'tp'), 0, 0, axis_index_groups=same_core)  38.8 us
    all_to_all x2, blocking collectives, per_device(): parts = lax.all_to_all(parts, 'seq', 0, 0)  24.6 us
    all_to_all x2, waiting for transfers between devices, per_device(): lax.all_to_all(kept + arriving, 'seq', 0, 0, axis_index_groups=same_core_...  24.3 us
    pallas_call x2, Pallas kernels, attend(): pl.pallas_call(functools.partial(attend_kernel, layer_index, new_tokens),...  19.2 us
    all_gather x2, blocking collectives, per_device(): queries = lax.all_gather(query, 'seq').reshape(rows, width_local)  18.9 us
    all_to_all x1, waiting for transfers between devices, to_owners(): lax.all_to_all(parts, ('seq', 'tp'), 0, 0, axis_index_groups=same_core)  16.4 us
    all_to_all x1, waiting for transfers between devices, per_device(): lax.all_to_all(last_rows(parts, state), ('seq', 'tp'), 0, 0, axis_index_g...  15.7 us
    unnamed x56, local copies, waits for them, and re-layouts  14.4 us
  transfers between devices with their start and end apart: 12, of which 12 were waited for; matrix products, arithmetic and copies ran while one was open for 4% of the time, Pallas kernels for 1%

profile of v1, /device:TPU:0, one launch (start us, length us, event | category | flops | bytes accessed | tf_op | source)
XLA Modules:
  0.0 247.3 jit_solution(4495914049563270964)
XLA Ops:
  1.4 2.9 %order_requests.1 = (s32[64]{0:T(128)}, s32[256]{0:T(256)}, s32[256]{0:T(256)}) custom-call(s32[64,4]{1,0:T(8,128)} %copy.21.token_ref, s32[64]{0:T(128)} %group_ref.1, s32[8]{0:T(128)} %prefix_ref.5, s32[64]{0:T(128)} %tail_ref.5), custom_call_target="tpu_custom_call" | custom-call | tf_op jit(solution)/shard_map/order_requests/pallas_call | solution.py:282
  5.1 4.0 %convolution_convert_fusion = bf16[128,2048]{1,0:T(8,128)(2,1)S(1)} fusion(bf16[1600,2048]{1,0:T(8,128)(2,1)} %param.16, s32[128]{0:T(128)S(1)} %eq.69), kind=kOutput, calls=%fused_computation.1 | convolution fusion | flops 839327744 | bytes 7078400 | tf_op jit(solution)/shard_map/dot_general | solution.py:682
  9.8 1.4 collective-permute-done
  11.2 4.8 %fusion.1 = bf16[16,8,2048]{2,1,0:T(8,128)(2,1)} fusion(bf16[128,2048]{1,0:T(8,128)(2,1)S(1)} %collective-permute-done, bf16[1600,2048]{1,0:T(8,128)(2,1)} %param.16, s32[128]{0:T(128)S(1)} %eq.65), kind=kOutput, calls=%fused_computation.4 | convolution fusion | flops 839589888 | bytes 7602688 | tf_op jit(solution)/shard_map/dot_general | solution.py:682
  16.0 8.4 %all-to-all-start = ((bf16[16,8,2048]{2,1,0:T(8,128)(2,1)}), bf16[16,8,2048]{2,1,0:T(8,128)(2,1)S(1)}, u32[]{:S(2)}, u32[]{:S(2)}) async-start(bf16[16,8,2048]{2,1,0:T(8,128)(2,1)} %fusion.1), calls=%async_computation | async-start | bytes 1048576 | tf_op jit(solution)/shard_map/all_to_all | solution.py:673
  24.5 16.4 %all-to-all-done.refs_0_ = bf16[16,8,2048]{2,1,0:T(8,128)(2,1)S(1)} async-done(((bf16[16,8,2048]{2,1,0:T(8,128)(2,1)}), bf16[16,8,2048]{2,1,0:T(8,128)(2,1)S(1)}, u32[]{:S(2)}, u32[]{:S(2)}) %all-to-all-start) | async-done | bytes 524320 | tf_op jit(solution)/shard_map/all_to_all | solution.py:673
  41.8 2.6 %all-to-all-start.1 = ((bf16[32,8,256]{2,1,0:T(8,128)(2,1)}), bf16[32,8,256]{2,1,0:T(8,128)(2,1)S(1)}, u32[]{:S(2)}, u32[]{:S(2)}) async-start(bf16[32,8,256]{2,1,0:T(8,128)(2,1)} %get-tuple-element.22), calls=%async_computation.1 | async-start | bytes 262144 | tf_op jit(solution)/shard_map/all_to_all | solution.py:693
  46.6 1.4 copy.23.qkv_ref
  48.1 4.7 %all-to-all-done.1 = bf16[32,8,256]{2,1,0:T(8,128)(2,1)S(1)} async-done(((bf16[32,8,256]{2,1,0:T(8,128)(2,1)}), bf16[32,8,256]{2,1,0:T(8,128)(2,1)S(1)}, u32[]{:S(2)}, u32[]{:S(2)}) %all-to-all-start.1) | async-done | bytes 131104 | tf_op jit(solution)/shard_map/all_to_all | solution.py:693
  56.9 3.6 %all-to-all-start.2 = ((bf16[4,448,256]{2,1,0:T(8,128)(2,1)}), bf16[4,448,256]{2,1,0:T(8,128)(2,1)S(1)}, u32[]{:S(2)}, u32[]{:S(2)}) async-start(bf16[4,448,256]{2,1,0:T(8,128)(2,1)} %add.167), calls=%async_computation.2 | async-start | bytes 1835008 | tf_op jit(solution)/shard_map/all_to_all | solution.py:696
  61.2 12.2 %all-to-all-done.2.part_ref = bf16[4,448,256]{2,1,0:T(8,128)(2,1)S(1)} async-done(((bf16[4,448,256]{2,1,0:T(8,128)(2,1)}), bf16[4,448,256]{2,1,0:T(8,128)(2,1)S(1)}, u32[]{:S(2)}, u32[]{:S(2)}) %all-to-all-start.2) | async-done | bytes 917536 | tf_op jit(solution)/shard_map/all_to_all | solution.py:696
  73.7 9.4 %all-gather.query_ref = bf16[256,512]{1,0:T(8,128)(2,1)S(1)} all-gather(bf16[32,512]{1,0:T(8,128)(2,1)S(1)} %get-tuple-element.24), channel_id=2, replica_groups=mesh['seq'=8,'tp'=4] {'seq'}, dimensions={0}, use_global_device_ids=true | all-gather | bytes 294912 | tf_op jit(solution)/shard_map/all_gather | solution.py:698
  83.2 2.2 copy-done.3
  85.3 2.2 copy-done.5
  87.5 9.6 %attend.2 = bf16[8,256,128]{2,1,0:T(8,128)(2,1)S(1)} custom-call(s32[1]{0:T(128)} %bitcast.1.place_ref, s32[64]{0:T(128)S(1)} %copy-done.18, s32[16,2]{1,0:T(8,128)S(1)} %copy.29.map_ref, s32[8]{0:T(128)S(1)} %copy-done.16, s32[64]{0:T(128)S(1)} %copy-done.17, bf16[256,512]{1,0:T(8,128)(2,1)S(1)} %all-gather.query_ref, ...), custom_call_target="tpu_custom_call" | custom-call | tf_op jit(solution)/shard_map/attend/pallas_call | solution.py:589
  97.2 12.3 %all_to_all.50.part_ref = bf16[8,256,128]{2,1,0:T(8,128)(2,1)S(1)} all-to-all(bf16[8,256,128]{2,1,0:T(8,128)(2,1)S(1)} %attend.2), channel_id=1, replica_groups=mesh['seq'=8,'tp'=4] {'seq'}, dimensions={0} | all-to-all | bytes 1048576 | tf_op jit(solution)/shard_map/all_to_all | solution.py:703
  112.3 19.4 %all_to_all.51.refs_0_ = bf16[16,8,2048]{2,1,0:T(8,128)(2,1)S(1)} all-to-all(bf16[16,8,2048]{2,1,0:T(8,128)(2,1)S(1)} %add_bitcast_fusion.1), channel_id=1, replica_groups={{0,1,2,3,8,9,10,11,16,17,18,19,24,25,26,27},{4,5,6,7,12,13,14,15,20,21,..., dimensions={0} | all-to-all | bytes 1048576 | tf_op jit(solution)/shard_map/all_to_all | solution.py:673
  133.2 2.6 %all-to-all-start.5 = ((bf16[32,8,256]{2,1,0:T(8,128)(2,1)}), bf16[32,8,256]{2,1,0:T(8,128)(2,1)S(1)}, u32[]{:S(2)}, u32[]{:S(2)}) async-start(bf16[32,8,256]{2,1,0:T(8,128)(2,1)} %get-tuple-element.29), calls=%async_computation.5 | async-start | bytes 262144 | tf_op jit(solution)/shard_map/all_to_all | solution.py:693
  135.8 2.3 copy.31
  139.5 4.7 %all-to-all-done.5 = bf16[32,8,256]{2,1,0:T(8,128)(2,1)S(1)} async-done(((bf16[32,8,256]{2,1,0:T(8,128)(2,1)}), bf16[32,8,256]{2,1,0:T(8,128)(2,1)S(1)}, u32[]{:S(2)}, u32[]{:S(2)}) %all-to-all-start.5) | async-done | bytes 131104 | tf_op jit(solution)/shard_map/all_to_all | solution.py:693
  145.2 2.0 collective-permute-done.3
  148.4 3.6 %all-to-all-start.6 = ((bf16[4,448,256]{2,1,0:T(8,128)(2,1)}), bf16[4,448,256]{2,1,0:T(8,128)(2,1)S(1)}, u32[]{:S(2)}, u32[]{:S(2)}) async-start(bf16[4,448,256]{2,1,0:T(8,128)(2,1)} %add.173), calls=%async_computation.6 | async-start | bytes 1835008 | tf_op jit(solution)/shard_map/all_to_all | solution.py:696
  152.7 12.1 %all-to-all-done.6.part_ref = bf16[4,448,256]{2,1,0:T(8,128)(2,1)S(1)} async-done(((bf16[4,448,256]{2,1,0:T(8,128)(2,1)}), bf16[4,448,256]{2,1,0:T(8,128)(2,1)S(1)}, u32[]{:S(2)}, u32[]{:S(2)}) %all-to-all-start.6) | async-done | bytes 917536 | tf_op jit(solution)/shard_map/all_to_all | solution.py:696
  165.1 9.5 %all-gather.1.query_ref = bf16[256,512]{1,0:T(8,128)(2,1)S(1)} all-gather(bf16[32,512]{1,0:T(8,128)(2,1)S(1)} %get-tuple-element.30), channel_id=3, replica_groups=mesh['seq'=8,'tp'=4] {'seq'}, dimensions={0}, use_global_device_ids=true | all-gather | bytes 294912 | tf_op jit(solution)/shard_map/all_gather | solution.py:698
  174.6 2.2 copy-done.4
  176.8 2.2 copy-done.6
  179.0 9.6 %attend.3 = bf16[8,256,128]{2,1,0:T(8,128)(2,1)S(1)} custom-call(s32[1]{0:T(128)} %bitcast.1.place_ref, s32[64]{0:T(128)S(1)} %copy-done.19, s32[16,2]{1,0:T(8,128)S(1)} %copy.29.map_ref, s32[8]{0:T(128)S(1)} %copy-done.16, s32[64]{0:T(128)S(1)} %copy-done.17, bf16[256,512]{1,0:T(8,128)(2,1)S(1)} %all-gather.1.query_ref, ...), custom_call_target="tpu_custom_call" | custom-call | tf_op jit(solution)/shard_map/attend/pallas_call | solution.py:589
  188.6 12.3 %all_to_all.52.part_ref = bf16[8,256,128]{2,1,0:T(8,128)(2,1)S(1)} all-to-all(bf16[8,256,128]{2,1,0:T(8,128)(2,1)S(1)} %attend.3), channel_id=1, replica_groups=mesh['seq'=8,'tp'=4] {'seq'}, dimensions={0} | all-to-all | bytes 1048576 | tf_op jit(solution)/shard_map/all_to_all | solution.py:703
  203.7 19.4 %all_to_all.53.part_ref = bf16[16,8,2048]{2,1,0:T(8,128)(2,1)S(1)} all-to-all(bf16[16,8,2048]{2,1,0:T(8,128)(2,1)S(1)} %add_bitcast_fusion), channel_id=1, replica_groups={{0,1,2,3,8,9,10,11,16,17,18,19,24,25,26,27},{4,5,6,7,12,13,14,15,20,21,..., dimensions={0} | all-to-all | bytes 1048576 | tf_op jit(solution)/shard_map/all_to_all | solution.py:673
  224.0 3.6 %all-to-all-start.9 = ((bf16[16,8,2048]{2,1,0:T(8,128)(2,1)}), bf16[16,8,2048]{2,1,0:T(8,128)(2,1)S(1)}, u32[]{:S(2)}, u32[]{:S(2)}) async-start(bf16[16,8,2048]{2,1,0:T(8,128)(2,1)} %last_rows.1), calls=%async_computation.9 | async-start | bytes 1048576 | tf_op jit(solution)/shard_map/all_to_all | solution.py:706
  227.6 15.7 %all-to-all-done.9 = bf16[16,8,2048]{2,1,0:T(8,128)(2,1)S(1)} async-done(((bf16[16,8,2048]{2,1,0:T(8,128)(2,1)}), bf16[16,8,2048]{2,1,0:T(8,128)(2,1)S(1)}, u32[]{:S(2)}, u32[]{:S(2)}) %all-to-all-start.9) | async-done | bytes 524320 | tf_op jit(solution)/shard_map/all_to_all | solution.py:706
  245.7 1.6 reshape.150
  (102 shorter events, 25.9 us)
Async XLA Ops:
  9.1 2.1 collective-permute-start
  9.7 14.7 %copy-start.21 = (f32[2,2048]{1,0:T(2,128)S(1)}, f32[2,2048]{1,0:T(2,128)}, u32[]{:S(2)}) copy-start(f32[2,2048]{1,0:T(2,128)} %param.23) | copy-start | bytes 49156
  9.8 14.7 %copy-start.22 = (f32[2,2048]{1,0:T(2,128)S(1)}, f32[2,2048]{1,0:T(2,128)}, u32[]{:S(2)}) copy-start(f32[2,2048]{1,0:T(2,128)} %param.24) | copy-start | bytes 49156
  16.0 28.4 %copy-start.20 = (bf16[2,256,3,512]{3,1,2,0:T(8,128)(2,1)S(1)}, bf16[2,256,3,512]{3,1,2,0:T(8,128)(2,1)}, u32[]{:S(2)}) copy-start(bf16[2,256,3,512]{3,1,2,0:T(8,128)(2,1)} %param.25) | copy-start | bytes 4718596
  16.0 24.9 %all-to-all-start = ((bf16[16,8,2048]{2,1,0:T(8,128)(2,1)}), bf16[16,8,2048]{2,1,0:T(8,128)(2,1)S(1)}, u32[]{:S(2)}, u32[]{:S(2)}) async-start(bf16[16,8,2048]{2,1,0:T(8,128)(2,1)} %fusion.1), calls=%async_computation | async-start | bytes 1048576 | tf_op jit(solution)/shard_map/all_to_all | solution.py:673
  41.8 11.0 %all-to-all-start.1 = ((bf16[32,8,256]{2,1,0:T(8,128)(2,1)}), bf16[32,8,256]{2,1,0:T(8,128)(2,1)S(1)}, u32[]{:S(2)}, u32[]{:S(2)}) async-start(bf16[32,8,256]{2,1,0:T(8,128)(2,1)} %get-tuple-element.22), calls=%async_computation.1 | async-start | bytes 262144 | tf_op jit(solution)/shard_map/all_to_all | solution.py:693
  45.5 7.3 %copy-start = (bf16[2,256,2048]{2,1,0:T(8,128)(2,1)S(1)}, bf16[2,256,2048]{2,1,0:T(8,128)(2,1)}, u32[]{:S(2)}) copy-start(bf16[2,256,2048]{2,1,0:T(8,128)(2,1)} %fc1_ref.7) | copy-start | bytes 6291460
  53.2 2.5 %collective-permute-start.1 = (bf16[4,448,256]{2,1,0:T(8,128)(2,1)S(1)}, bf16[4,448,256]{2,1,0:T(8,128)(2,1)S(1)}, u32[]{:S(2)}, u32[]{:S(2)}) collective-permute-start(bf16[4,448,256]{2,1,0:T(8,128)(2,1)S(1)} %project.5), channel_id=1, source_target_pairs={{0,4},{4,0},{8,12},{12,8},{16,20},{20,16},{24,28},{28,24},{1,5},{5... | collective-permute-start | bytes 2752520 | tf_op jit(solution)/shard_map/ppermute | solution.py:237
  54.3 6.3 %copy-start.24 = (s32[16,2]{0,1:T(2,128)S(1)}, s32[16,2]{0,1:T(2,128)}, u32[]{:S(2)}) copy-start(s32[16,2]{0,1:T(2,128)} %param.20) | copy-start | bytes 388
  54.4 6.3 %copy-start.25 = (s32[256]{0:T(256)S(1)}, s32[256]{0:T(256)}, u32[]{:S(2)}) copy-start(s32[256]{0:T(256)} %get-tuple-element.23) | copy-start | bytes 3076
  56.9 26.2 %copy-start.16 = (s32[8]{0:T(128)S(1)}, s32[8]{0:T(128)}, u32[]{:S(2)}) copy-start(s32[8]{0:T(128)} %prefix_ref.5) | copy-start | bytes 100
  56.9 26.2 %copy-start.17 = (s32[64]{0:T(128)S(1)}, s32[64]{0:T(128)}, u32[]{:S(2)}) copy-start(s32[64]{0:T(128)} %tail_ref.5) | copy-start | bytes 772
  56.9 26.2 %copy-start.18 = (s32[64]{0:T(128)S(1)}, s32[64]{0:T(128)}, u32[]{:S(2)}) copy-start(s32[64]{0:T(128)} %get-tuple-element.20.rank_ref) | copy-start | bytes 772
  56.9 16.4 %all-to-all-start.2 = ((bf16[4,448,256]{2,1,0:T(8,128)(2,1)}), bf16[4,448,256]{2,1,0:T(8,128)(2,1)S(1)}, u32[]{:S(2)}, u32[]{:S(2)}) async-start(bf16[4,448,256]{2,1,0:T(8,128)(2,1)} %add.167), calls=%async_computation.2 | async-start | bytes 1835008 | tf_op jit(solution)/shard_map/all_to_all | solution.py:696
  61.1 36.0 %copy-start.8 = (f32[32,512]{1,0:T(8,128)}, f32[32,512]{1,0:T(8,128)S(1)}, u32[]{:S(2)}) copy-start(f32[32,512]{1,0:T(8,128)S(1)} %get-tuple-element.41.up_ref) | copy-start | bytes 196612
  61.1 36.0 %copy-start.10 = (f32[32,512]{1,0:T(8,128)}, f32[32,512]{1,0:T(8,128)S(1)}, u32[]{:S(2)}) copy-start(f32[32,512]{1,0:T(8,128)S(1)} %get-tuple-element.42.down_ref) | copy-start | bytes 196612
  61.1 36.0 %copy-start.12 = (f32[32,512]{1,0:T(8,128)}, f32[32,512]{1,0:T(8,128)S(1)}, u32[]{:S(2)}) copy-start(f32[32,512]{1,0:T(8,128)S(1)} %get-tuple-element.43.keep_ref) | copy-start | bytes 196612
  87.5 21.9 %copy-start.1 = (bf16[2,256,2048]{2,1,0:T(8,128)(2,1)S(1)}, bf16[2,256,2048]{2,1,0:T(8,128)(2,1)}, u32[]{:S(2)}) copy-start(bf16[2,256,2048]{2,1,0:T(8,128)(2,1)} %fc2_ref.7) | copy-start | bytes 6291460
  87.5 21.9 %copy-start.7 = (bf16[2,64,2048]{2,1,0:T(8,128)(2,1)S(1)}, bf16[2,64,2048]{2,1,0:T(8,128)(2,1)}, u32[]{:S(2)}) copy-start(bf16[2,64,2048]{2,1,0:T(8,128)(2,1)} %out_weight_ref.7) | copy-start | bytes 1572868
  110.3 2.0 collective-permute-start.2
  133.2 11.0 %all-to-all-start.5 = ((bf16[32,8,256]{2,1,0:T(8,128)(2,1)}), bf16[32,8,256]{2,1,0:T(8,128)(2,1)S(1)}, u32[]{:S(2)}, u32[]{:S(2)}) async-start(bf16[32,8,256]{2,1,0:T(8,128)(2,1)} %get-tuple-element.29), calls=%async_computation.5 | async-start | bytes 262144 | tf_op jit(solution)/shard_map/all_to_all | solution.py:693
  144.7 2.5 %collective-permute-start.3 = (bf16[4,448,256]{2,1,0:T(8,128)(2,1)S(1)}, bf16[4,448,256]{2,1,0:T(8,128)(2,1)S(1)}, u32[]{:S(2)}, u32[]{:S(2)}) collective-permute-start(bf16[4,448,256]{2,1,0:T(8,128)(2,1)S(1)} %project.7), channel_id=1, source_target_pairs={{0,4},{4,0},{8,12},{12,8},{16,20},{20,16},{24,28},{28,24},{1,5},{5... | collective-permute-start | bytes 2752520 | tf_op jit(solution)/shard_map/ppermute | solution.py:237
  145.2 19.6 %copy-start.9 = (f32[32,512]{1,0:T(8,128)S(1)}, f32[32,512]{1,0:T(8,128)}, u32[]{:S(2)}) copy-start(f32[32,512]{1,0:T(8,128)} %copy-done.8) | copy-start | bytes 196612
  145.2 19.6 %copy-start.11 = (f32[32,512]{1,0:T(8,128)S(1)}, f32[32,512]{1,0:T(8,128)}, u32[]{:S(2)}) copy-start(f32[32,512]{1,0:T(8,128)} %copy-done.10) | copy-start | bytes 196612
  145.2 19.6 %copy-start.13 = (f32[32,512]{1,0:T(8,128)S(1)}, f32[32,512]{1,0:T(8,128)}, u32[]{:S(2)}) copy-start(f32[32,512]{1,0:T(8,128)} %copy-done.12) | copy-start | bytes 196612
  148.4 26.3 %copy-start.19 = (s32[64]{0:T(128)S(1)}, s32[64]{0:T(128)}, u32[]{:S(2)}) copy-start(s32[64]{0:T(128)} %get-tuple-element.20.rank_ref) | copy-start | bytes 772
  148.4 16.4 %all-to-all-start.6 = ((bf16[4,448,256]{2,1,0:T(8,128)(2,1)}), bf16[4,448,256]{2,1,0:T(8,128)(2,1)S(1)}, u32[]{:S(2)}, u32[]{:S(2)}) async-start(bf16[4,448,256]{2,1,0:T(8,128)(2,1)} %add.173), calls=%async_computation.6 | async-start | bytes 1835008 | tf_op jit(solution)/shard_map/all_to_all | solution.py:696
  179.0 21.9 %copy-start.2 = (bf16[2,256,2048]{2,1,0:T(8,128)(2,1)S(1)}, bf16[2,256,2048]{2,1,0:T(8,128)(2,1)}, u32[]{:S(2)}) copy-start(bf16[2,256,2048]{2,1,0:T(8,128)(2,1)} %fc2_ref.7) | copy-start | bytes 6291460
  201.7 2.0 collective-permute-start.4
  202.6 20.5 %copy-start.15 = (f32[8,2048]{1,0:T(8,128)S(1)}, f32[8,2048]{1,0:T(8,128)}, u32[]{:S(2)}) copy-start(f32[8,2048]{1,0:T(8,128)} %copy-done.14) | copy-start | bytes 196612
  224.0 19.3 %all-to-all-start.9 = ((bf16[16,8,2048]{2,1,0:T(8,128)(2,1)}), bf16[16,8,2048]{2,1,0:T(8,128)(2,1)S(1)}, u32[]{:S(2)}, u32[]{:S(2)}) async-start(bf16[16,8,2048]{2,1,0:T(8,128)(2,1)} %last_rows.1), calls=%async_computation.9 | async-start | bytes 1048576 | tf_op jit(solution)/shard_map/all_to_all | solution.py:706
  243.3 1.9 collective-permute-start.5
  (6 other events, 14.7 us)

commit v2 on v0

--- a/solution.py
+++ b/solution.py
@@ -1,8 +1,11 @@
+import functools
 import math
 
 import jax
 import jax.numpy as jnp
 from jax import lax
+from jax.experimental import pallas as pl
+from jax.experimental.pallas import tpu as pltpu
 from jax.sharding import PartitionSpec as P
 
 HEADS = 32
@@ -11,6 +14,7 @@
 LAYERS = 2
 BLOCK = 128
 SPAN = 512
+CHIPS = 4
 
 
 very_negative = -1e30
@@ -60,7 +64,7 @@
     return lax.psum(values, ("seq", "tp"))
 
 
-def per_device(
+def per_device_any(
     token_ids,
     embedding,
     group_of,
@@ -230,6 +234,685 @@
     return stacked
 
 
+def swap_cores(values, seq_count):
+    return lax.ppermute(values, "seq", [(i, i ^ 1) for i in range(seq_count)])
+
+
+def compiler_params(megabytes=32):
+    return pltpu.CompilerParams(vmem_limit_bytes=megabytes * 2**20)
+
+
+def whole(memory_space=pltpu.VMEM):
+    return pl.BlockSpec(memory_space=memory_space)
+
+
+def layer_block(layer_index, shape):
+    return pl.BlockSpec((1,) + shape, lambda step: (layer_index,) + (0,) * len(shape))
+
+
+def same_block(shape):
+    return pl.BlockSpec(shape, lambda step: (0,) * len(shape))
+
+
+def order_kernel(new_tokens, group_ref, prefix_ref, tail_ref, map_ref, rank_ref, position_ref, visit_ref, count_ref):
+    requests = group_ref.shape[0]
+    groups = prefix_ref.shape[0]
+    per_group = requests // groups
+    blocks = map_ref.shape[1]
+    for group in range(groups):
+        count_ref[group] = 0
+
+    def place(request, unused):
+        group = group_ref[request]
+        seat = count_ref[group]
+        count_ref[group] = seat + 1
+        rank = group * per_group + seat
+        rank_ref[request] = rank
+        start = prefix_ref[group] + tail_ref[request]
+        for token in range(new_tokens):
+            position_ref[rank * new_tokens + token] = start + token
+        return unused
+
+    lax.fori_loop(0, requests, place, 0)
+
+    def look(block, unused):
+        segment, depth = map_ref[0, block], map_ref[1, block]
+        is_tail = segment >= groups
+        request = jnp.clip(segment - groups, 0, requests - 1)
+        prompt = jnp.clip(segment, 0, groups - 1)
+        seat = rank_ref[request]
+        first = jnp.where(is_tail, (seat % per_group) * new_tokens, 0)
+        length = jnp.where(is_tail, tail_ref[request], prefix_ref[prompt])
+        visit_ref[block] = jnp.where(is_tail, seat // per_group, prompt)
+        visit_ref[blocks + block] = jnp.where(segment < 0, 0, length - depth * BLOCK)
+        visit_ref[2 * blocks + block] = first
+        visit_ref[3 * blocks + block] = jnp.where(is_tail, first + new_tokens, per_group * new_tokens)
+        return unused
+
+    lax.fori_loop(0, blocks, look, 0)
+
+
+def order_requests(group_of, prefix_len, tail_len, block_map, new_tokens):
+    requests = group_of.shape[0]
+    smem = whole(pltpu.SMEM)
+    return pl.pallas_call(
+        functools.partial(order_kernel, new_tokens),
+        out_shape=(
+            jax.ShapeDtypeStruct((requests,), jnp.int32),
+            jax.ShapeDtypeStruct((requests * new_tokens,), jnp.int32),
+            jax.ShapeDtypeStruct((4 * block_map.shape[0],), jnp.int32),
+        ),
+        in_specs=[smem] * 4,
+        out_specs=(smem, smem, smem),
+        scratch_shapes=[pltpu.SMEM((prefix_len.shape[0],), jnp.int32)],
+        name="order_requests",
+    )(group_of, prefix_len, tail_len, block_map.T)
+
+
+def embed_kernel(place_ref, token_ref, group_ref, table_hbm, near_ref, far_ref, table_ref, hot_ref, semaphores):
+    core = place_ref[0] % 2
+    first = place_ref[1] * table_ref.shape[0]
+    new_tokens, requests = token_ref.shape
+    rows = 2 * near_ref.shape[0]
+    cuts = semaphores.shape[0]
+    width = table_ref.shape[1] // cuts
+    columns = [slice(cut * width, (cut + 1) * width) for cut in range(cuts)]
+    copies = [
+        pltpu.make_async_copy(table_hbm.at[:, column], table_ref.at[:, column], semaphores.at[cut])
+        for cut, column in enumerate(columns)
+    ]
+    for copy in copies:
+        copy.start()
+    across = lax.broadcasted_iota(jnp.int32, (requests, requests), 1)
+    down = lax.broadcasted_iota(jnp.int32, (requests, requests), 0)
+    group_row = group_ref[0:1, :]
+    group_column = jnp.sum(jnp.where(across == down, group_row, 0), axis=1, keepdims=True)
+    ahead = (group_column < group_row) | ((group_column == group_row) & (down < across))
+    rank_row = jnp.sum(jnp.where(ahead, 1, 0), axis=0, keepdims=True)
+    line = lax.broadcasted_iota(jnp.int32, (rows, requests), 0)
+    half, share = rows // 2, rows // CHIPS // 2
+    parity = jnp.where(line < half, core, 1 - core)
+    line = line % half
+    line = ((line // share) * 2 + parity) * share + line % share
+    ids = jnp.zeros((rows, 1), jnp.int32)
+    for token in range(new_tokens):
+        token_row = token_ref[token : token + 1, :]
+        match = (rank_row == line // new_tokens) & (line % new_tokens == token)
+        ids = ids + jnp.sum(jnp.where(match, token_row, 0), axis=1, keepdims=True)
+    entry = lax.broadcasted_iota(jnp.int32, hot_ref.shape, 1)
+    hot_ref[...] = jnp.where(entry == ids - first, 1.0, 0.0).astype(jnp.bfloat16)
+    for copy, column in zip(copies, columns):
+        copy.wait()
+        chosen = jnp.dot(hot_ref[...], table_ref[:, column], preferred_element_type=jnp.float32)
+        chosen = chosen.astype(jnp.bfloat16)
+        near_ref[:, column] = chosen[:half]
+        far_ref[:, column] = chosen[half:]
+
+
+def embed(place, token_ids, group_of, embedding):
+    rows = token_ids.shape[0] * token_ids.shape[1]
+    half = jax.ShapeDtypeStruct((rows // 2, embedding.shape[1]), jnp.bfloat16)
+    return pl.pallas_call(
+        embed_kernel,
+        out_shape=(half, half),
+        in_specs=[whole(pltpu.SMEM), whole(), whole(), whole(pltpu.HBM)],
+        out_specs=(whole(), whole()),
+        scratch_shapes=[
+            pltpu.VMEM(embedding.shape, jnp.bfloat16),
+            pltpu.VMEM((rows, embedding.shape[0]), jnp.bfloat16),
+            pltpu.SemaphoreType.DMA((4,)),
+        ],
+        compiler_params=compiler_params(56),
+        name="embed",
+    )(place, token_ids.T, group_of[None, :], embedding)
+
+
+def state_total(part_ref, state_ref):
+    total = part_ref[0].astype(jnp.float32)
+    for source in range(1, part_ref.shape[0]):
+        total = total + part_ref[source].astype(jnp.float32)
+    if state_ref is not None:
+        total = total + state_ref[...]
+    return total
+
+
+def norm_kernel(has_state, layer_index, tp_count, *refs):
+    if has_state:
+        part_ref, state_ref, gain_ref, bias_ref, next_ref, cut_ref = refs
+    else:
+        part_ref, gain_ref, bias_ref, next_ref, cut_ref = refs
+        state_ref = None
+    state = state_total(part_ref, state_ref)
+    next_ref[...] = state
+    average = jnp.mean(state, axis=-1, keepdims=True)
+    centred = state - average
+    variance = jnp.mean(centred * centred, axis=-1, keepdims=True)
+    gain = gain_ref[layer_index : layer_index + 1, :]
+    bias = bias_ref[layer_index : layer_index + 1, :]
+    normed = (centred * lax.rsqrt(variance + 1e-05) * gain + bias).astype(jnp.bfloat16)
+    width = cut_ref.shape[2]
+    for place in range(cut_ref.shape[0]):
+        start = (place // tp_count) * width
+        cut_ref[place] = normed[:, start : start + width]
+
+
+def norm_rows(parts, state, ln_gain, ln_bias, layer_index, devices, tp_count):
+    count, rows, width = parts.shape
+    cut = width // (devices // tp_count)
+    operands = [parts] + ([] if state is None else [state]) + [ln_gain, ln_bias]
+    return pl.pallas_call(
+        functools.partial(norm_kernel, state is not None, layer_index, tp_count),
+        out_shape=(
+            jax.ShapeDtypeStruct((rows, width), jnp.float32),
+            jax.ShapeDtypeStruct((devices, rows, cut), jnp.bfloat16),
+        ),
+        in_specs=[whole()] * len(operands),
+        out_specs=(whole(), whole()),
+        compiler_params=compiler_params(16),
+        name="norm_rows",
+    )(*operands)
+
+
+def gather_kernel(tp_count, place_ref, part_ref, state_ref, out_ref):
+    total = part_ref[0].astype(jnp.float32)
+    for chip in range(1, part_ref.shape[0]):
+        total = total + part_ref[chip].astype(jnp.float32)
+    mine = state_ref.shape[0]
+    owner = place_ref[1] % tp_count
+    for place in range(tp_count):
+        rows = slice(place * mine, (place + 1) * mine)
+        total_rows = total[rows] + jnp.where(owner == place, 1.0, 0.0) * state_ref[...]
+        out_ref[rows] = total_rows
+
+
+def gather_rows(place, parts, state, tp_count):
+    return pl.pallas_call(
+        functools.partial(gather_kernel, tp_count),
+        out_shape=jax.ShapeDtypeStruct(parts.shape[1:], jnp.float32),
+        in_specs=[whole(pltpu.SMEM), whole(), whole()],
+        out_specs=whole(),
+        compiler_params=compiler_params(16),
+        name="gather_rows",
+    )(place, parts, state)
+
+
+def last_kernel(a_ref, b_ref, c_ref, d_ref, out_ref):
+    near = a_ref[...].astype(jnp.float32) + b_ref[...].astype(jnp.float32)
+    far = c_ref[...].astype(jnp.float32) + d_ref[...].astype(jnp.float32)
+    total = (near + far).astype(jnp.bfloat16)
+    for place in range(out_ref.shape[0]):
+        out_ref[place] = total
+
+
+def last_rows(parts):
+    return pl.pallas_call(
+        last_kernel,
+        out_shape=jax.ShapeDtypeStruct((CHIPS,) + parts[0].shape, jnp.bfloat16),
+        in_specs=[whole()] * 4,
+        out_specs=whole(),
+        compiler_params=compiler_params(16),
+        name="last_rows",
+    )(*parts)
+
+
+def project_kernel(joins, place_ref, hidden_ref, qkv_ref, fc1_ref, *refs):
+    if joins:
+        arrived_ref, head_ref, *unit_refs = refs
+    else:
+        out_ref = refs[0]
+    seq_index = place_ref[0]
+    parity = seq_index % 2 if joins else 1 - seq_index % 2
+    here = seq_index // 2
+    rows, depth = hidden_ref.shape
+    width = qkv_ref.shape[1] // 3
+    unit = fc1_ref.shape[2] // CHIPS // 2
+    share = rows // CHIPS // 2
+    half = rows // 2
+    pieces = width // unit
+    hidden = hidden_ref[...]
+    tall = 2 * pieces * share
+
+    def joined(values, start):
+        if joins:
+            values = values + arrived_ref[start : start + values.shape[0]].astype(jnp.float32)
+        return values.astype(jnp.bfloat16)
+
+    picked = jnp.concatenate(
+        [
+            hidden_ref[pl.ds(pl.multiple_of((2 * chip + parity) * share, share), share), :]
+            for chip in range(CHIPS)
+        ],
+        axis=0,
+    )
+    heads = jnp.dot(picked, qkv_ref[...], preferred_element_type=jnp.float32)
+    for piece in range(pieces):
+        start = piece * half
+        query = joined(heads[:, piece * unit : (piece + 1) * unit], start)
+        if joins:
+            for chip in range(CHIPS):
+                head_ref[chip, tall + start : tall + start + half] = query
+        else:
+            out_ref[start : start + half] = query
+    base = pieces * half
+    for chip in range(CHIPS):
+        for piece in range(2 * pieces):
+            column = width + piece * unit
+            start = base + (chip * 2 * pieces + piece) * share
+            value = joined(heads[chip * share : (chip + 1) * share, column : column + unit], start)
+            if joins:
+                head_ref[chip, piece * share : (piece + 1) * share] = value
+            else:
+                out_ref[start : start + share] = value
+    base = base + CHIPS * tall
+    for distance in range(CHIPS):
+        target = 2 * (here ^ distance) + parity
+        columns = pl.ds(pl.multiple_of(target * unit, unit), unit)
+        start = base + distance * rows
+        pre = joined(jnp.dot(hidden, fc1_ref[0, :, columns], preferred_element_type=jnp.float32), start)
+        if joins:
+            unit_refs[distance][...] = pre
+        else:
+            out_ref[start : start + rows] = pre
+
+
+def project(place, hidden, weights_qkv, w_fc1, layer_index, arrived=None):
+    rows = hidden.shape[0]
+    unit = w_fc1.shape[2] // CHIPS // 2
+    pieces = weights_qkv.shape[1] // 3 // unit
+    tall = 2 * pieces * (rows // CHIPS // 2)
+    common = pieces * (rows // 2)
+
+    def result(*shape):
+        return jax.ShapeDtypeStruct(shape, jnp.bfloat16)
+
+    if arrived is None:
+        extra = []
+        out_shape = result(common + CHIPS * (tall + rows), unit)
+    else:
+        extra = [arrived]
+        out_shape = (result(CHIPS, tall + common, unit),) + (result(rows, unit),) * CHIPS
+    return pl.pallas_call(
+        functools.partial(project_kernel, arrived is not None),
+        grid=(1,),
+        out_shape=out_shape,
+        in_specs=[
+            whole(pltpu.SMEM),
+            same_block(hidden.shape),
+            same_block(weights_qkv.shape),
+            layer_block(layer_index, w_fc1.shape[1:]),
+        ]
+        + [same_block(values.shape) for values in extra],
+        out_specs=jax.tree.map(lambda leaf: same_block(leaf.shape), out_shape),
+        compiler_params=compiler_params(),
+        name="project",
+    )(place, hidden, weights_qkv, w_fc1, *extra)
+
+
+def activate_kernel(place_ref, part_ref, table_ref, query_ref, key_ref, value_ref):
+    total = part_ref[0].astype(jnp.float32)
+    for chip in range(1, part_ref.shape[0]):
+        total = total + part_ref[chip].astype(jnp.float32)
+    share, width = key_ref.shape
+    half = query_ref.shape[0]
+    unit = part_ref.shape[2]
+    lanes = table_ref.shape[2]
+    pieces = width // unit
+    own = pl.ds(pl.multiple_of((place_ref[0] // 2) * share, share), share)
+
+    def put(target_ref, start, height, span, scale):
+        for piece in range(pieces):
+            for column in range(0, unit, lanes):
+                first = start + piece * height
+                values = total[first : first + height, column : column + lanes]
+                if span is not None:
+                    values = (
+                        values * table_ref[0, span]
+                        + pltpu.roll(values, lanes - ROT // 2, 1) * table_ref[1, span]
+                        + pltpu.roll(values, ROT // 2, 1) * table_ref[2, span]
+                    )
+                values = values.astype(jnp.bfloat16)
+                if scale is not None:
+                    values = (values.astype(jnp.float32) * scale).astype(jnp.bfloat16)
+                column_out = piece * unit + column
+                target_ref[:, column_out : column_out + lanes] = values
+
+    put(key_ref, 0, share, own, None)
+    put(value_ref, pieces * share, share, None, None)
+    put(query_ref, 2 * pieces * share, half, slice(None), 1.0 / math.sqrt(HEAD_DIM))
+
+
+def activate(place, parts, tables, width):
+    half = tables.shape[1]
+    small = jax.ShapeDtypeStruct((half // CHIPS, width), jnp.bfloat16)
+    return pl.pallas_call(
+        activate_kernel,
+        out_shape=(jax.ShapeDtypeStruct((half, width), jnp.bfloat16), small, small),
+        in_specs=[whole(pltpu.SMEM), whole(), whole()],
+        out_specs=(whole(),) * 3,
+        compiler_params=compiler_params(16),
+        name="activate",
+    )(place, parts, tables)
+
+
+def rotary_tables(positions, width):
+    half = ROT // 2
+    feature = lax.broadcasted_iota(jnp.int32, (1, width), 1) % HEAD_DIM
+    frequency = jnp.exp((feature % half).astype(jnp.float32) * (-2.0 * math.log(10000.0) / ROT))
+    angles = positions.astype(jnp.float32)[:, None] * frequency
+    cosine, sine = jnp.cos(angles), jnp.sin(angles)
+    return jnp.stack(
+        [
+            jnp.where(feature < ROT, cosine, 1.0),
+            jnp.where(feature < half, -sine, 0.0),
+            jnp.where((feature >= half) & (feature < ROT), sine, 0.0),
+        ]
+    )
+
+
+def attend_kernel(
+    layer_index, new_tokens,
+    place_ref, visit_ref, query_ref, far_query_ref, new_key_ref, new_value_ref,
+    key_hbm, value_hbm, out_ref,
+    key_ref, value_ref, both_ref, score_ref, top_ref, sum_ref, mix_ref, semaphores,
+):
+    blocks = visit_ref.shape[0] // 4
+    groups, tall, lanes = mix_ref.shape
+    share = new_key_ref.shape[0]
+    heads = tall // share
+    chunks = semaphores.shape[1]
+    chunk = key_ref.shape[0] // chunks
+
+    def copy(kind, index):
+        span = pl.ds(index * chunk, chunk)
+        source, target = ((key_hbm, key_ref), (value_hbm, value_ref))[kind]
+        return pltpu.make_async_copy(
+            source.at[layer_index, span], target.at[span], semaphores.at[kind, index]
+        )
+
+    for kind in range(2):
+        for index in range(chunks):
+            copy(kind, index).start()
+    core = place_ref[0] % 2
+    for chip in range(groups // 2):
+        span = slice(chip * share, (chip + 1) * share)
+        both_ref[2 * chip + core] = query_ref[span]
+        both_ref[2 * chip + 1 - core] = far_query_ref[span]
+    lane = lax.broadcasted_iota(jnp.int32, (share, lanes), 1)
+    row = lax.broadcasted_iota(jnp.int32, (share, lanes), 0)
+    top_ref[...] = jnp.full(top_ref.shape, very_negative, jnp.float32)
+    sum_ref[...] = jnp.zeros(sum_ref.shape, jnp.float32)
+    mix_ref[...] = jnp.zeros(mix_ref.shape, jnp.float32)
+
+    def score(index, group, keys, mask):
+        scores = []
+        for pair in range(heads // 2):
+            both = both_ref[group, :, pair * lanes : (pair + 1) * lanes]
+            none = jnp.zeros_like(both)
+            split = jnp.concatenate(
+                [jnp.where(lane < HEAD_DIM, both, none), jnp.where(lane < HEAD_DIM, none, both)], axis=0
+            )
+            scores.append(
+                lax.dot_general(
+                    split, keys[:, pair * lanes : (pair + 1) * lanes], (((1,), (1,)), ((), ())),
+                    preferred_element_type=jnp.float32,
+                )
+            )
+        scores = jnp.concatenate(scores, axis=0).reshape(heads, share, BLOCK)
+        scores = jnp.where(mask[None], scores, very_negative).reshape(tall, BLOCK)
+        score_ref[index] = scores
+        top_ref[group] = jnp.maximum(top_ref[group], scores)
+
+    def mix(index, group, values):
+        weight = jnp.exp(score_ref[index] - top_ref[group])
+        sum_ref[group] += weight
+        rounded = weight.astype(jnp.bfloat16)
+        mix_ref[group] += jnp.concatenate(
+            [
+                jnp.dot(
+                    rounded[pair * 2 * share : (pair + 1) * 2 * share],
+                    values[:, pair * lanes : (pair + 1) * lanes],
+                    preferred_element_type=jnp.float32,
+                )
+                for pair in range(heads // 2)
+            ],
+            axis=0,
+        )
+
+    own = place_ref[0]
+    fill = jnp.zeros((BLOCK - share, new_key_ref.shape[1]), jnp.bfloat16)
+    score(
+        blocks, own, jnp.concatenate([new_key_ref[...], fill], axis=0),
+        (lane // new_tokens == row // new_tokens) & (lane <= row),
+    )
+    owners = []
+    for block in range(blocks):
+        if (block * BLOCK) % chunk == 0:
+            copy(0, block * BLOCK // chunk).wait()
+        group, live, first, end = (visit_ref[field * blocks + block] for field in range(4))
+        owners.append(group)
+        score(
+            block, group, key_ref[block * BLOCK : (block + 1) * BLOCK, :],
+            (lane < live) & (row >= first) & (row < end),
+        )
+    for group in range(groups):
+        top = jnp.max(top_ref[group], axis=1, keepdims=True)
+        top_ref[group] = jnp.broadcast_to(top, (tall, lanes))
+    mix(blocks, own, jnp.concatenate([new_value_ref[...], fill], axis=0))
+    for block in range(blocks):
+        if (block * BLOCK) % chunk == 0:
+            copy(1, block * BLOCK // chunk).wait()
+        mix(block, owners[block], value_ref[block * BLOCK : (block + 1) * BLOCK, :])
+
+    level = jnp.zeros((tall, lanes), jnp.float32)
+    column = lax.broadcasted_iota(jnp.int32, (tall, lanes), 1)
+
+    def mean(group):
+        total = jnp.sum(sum_ref[group], axis=1, keepdims=True)
+        total = jnp.where(total <= 0.0, 1.0, total)
+        own_level = jnp.where(column == group, top_ref[group] + jnp.log(total), 0.0)
+        return mix_ref[group] / total, own_level
+
+    for group in range(groups // 2):
+        left, left_level = mean(group)
+        right, right_level = mean(group + groups // 2)
+        level = level + left_level + right_level
+        for head in range(heads):
+            rows = slice(head * share, (head + 1) * share)
+            first, second = left[rows], right[rows]
+            if head % 2:
+                first = pltpu.roll(first, HEAD_DIM, 1)
+            else:
+                second = pltpu.roll(second, HEAD_DIM, 1)
+            packed = jnp.where(lane < HEAD_DIM, first, second)
+            out_ref[head, group * share : (group + 1) * share] = packed.astype(jnp.bfloat16)
+    level = level.T[:groups]
+    high = level.astype(jnp.bfloat16).astype(jnp.float32)
+    middle = (level - high).astype(jnp.bfloat16).astype(jnp.float32)
+    low = level - high - middle
+    rest = jnp.concatenate([high, middle, low, jnp.zeros_like(low)], axis=0).astype(jnp.bfloat16)
+    start = (groups // 2) * share
+    for head in range(heads):
+        column = head * share // lanes * lanes
+        out_ref[head, start:] = rest[:, column : column + lanes]
+
+
+def attend(place, visits, query, far_query, new_key, new_value, k_cache, v_cache, layer_index, new_tokens, groups):
+    width = query.shape[1]
+    rows = 2 * query.shape[0]
+    slots = k_cache.shape[1]
+    heads = width // HEAD_DIM
+    share = rows // groups
+    tall = heads * share
+    lanes = 2 * HEAD_DIM
+    chunks = 4
+    state = pltpu.VMEM((groups, tall, lanes), jnp.float32)
+    return pl.pallas_call(
+        functools.partial(attend_kernel, layer_index, new_tokens),
+        out_shape=jax.ShapeDtypeStruct((heads, rows // 2 + 4 * groups, lanes), jnp.bfloat16),
+        in_specs=[whole(pltpu.SMEM)] * 2 + [whole()] * 4 + [whole(pltpu.HBM)] * 2,
+        out_specs=whole(),
+        scratch_shapes=[
+            pltpu.VMEM((slots, width), jnp.bfloat16),
+            pltpu.VMEM((slots, width), jnp.bfloat16),
+            pltpu.VMEM((groups, share, width), jnp.bfloat16),
+            pltpu.VMEM((visits.shape[0] // 4 + 1, tall, BLOCK), jnp.float32),
+            state,
+            state,
+            state,
+            pltpu.SemaphoreType.DMA((2, chunks)),
+        ],
+        compiler_params=compiler_params(24),
+        name="attend",
+    )(place, visits, query, far_query, new_key, new_value, k_cache, v_cache)
+
+
+def update_kernel(
+    layer_index, other, place_ref, part_ref, bias_ref, out_weight_ref, fc2_ref, *refs
+):
+    *unit_refs, out_ref, scale_ref = refs
+    seq_index = place_ref[0]
+    parity = 1 - seq_index % 2 if other else seq_index % 2
+    sources, tall, lanes = part_ref.shape
+    unit = unit_refs[0].shape[1]
+    share = unit_refs[0].shape[0] // sources
+    groups = (tall - (sources // 2) * share) // 4
+    levels = []
+    for source in range(sources):
+        parts = part_ref[source, (sources // 2) * share :, :].astype(jnp.float32)
+        levels.append(parts[:groups] + parts[groups : 2 * groups] + parts[2 * groups : 3 * groups])
+    top = functools.reduce(jnp.maximum, levels)
+    scales = [jnp.exp(level - top) for level in levels]
+    total = functools.reduce(jnp.add, scales)
+    scales = [scale / total for scale in scales]
+    blank = jnp.zeros((lanes - groups * sources, lanes), jnp.float32)
+    scale_ref[...] = jnp.concatenate(scales + [blank], axis=0).T
+    place = seq_index % (lanes // share)
+    scale = scale_ref[pl.ds(pl.multiple_of(place * share, share), share), :]
+    scale = jnp.where(parity == 0, scale, pltpu.roll(scale, lanes - 1, 1))
+    lane = lax.broadcasted_iota(jnp.int32, (share, lanes), 1)
+    first, second = [], []
+    for pair in range(CHIPS // 2):
+        rows = pl.ds(pl.multiple_of((2 * pair + parity) * share, share), share)
+        mixed = jnp.zeros((share, lanes), jnp.float32)
+        for source in range(sources):
+            column = source * groups + 2 * pair
+            left = scale[:, column : column + 1]
+            right = scale[:, column + groups // 2 : column + groups // 2 + 1]
+            mixed = mixed + part_ref[source, rows, :].astype(jnp.float32) * jnp.where(
+                lane < HEAD_DIM, left, right
+            )
+        first.append(mixed[:, :HEAD_DIM])
+        second.append(pltpu.roll(mixed, HEAD_DIM, 1)[:, :HEAD_DIM])
+    attended = jnp.concatenate(first + second, axis=0).astype(jnp.bfloat16)
+    bias = bias_ref[
+        layer_index : layer_index + 1, pl.ds(pl.multiple_of(seq_index * unit, unit), unit)
+    ]
+    hidden = []
+    for piece in range(CHIPS):
+        rows = pl.ds(pl.multiple_of((2 * piece + parity) * share, share), share)
+        pre = functools.reduce(jnp.add, [ref[rows, :].astype(jnp.float32) for ref in unit_refs])
+        hidden.append(jax.nn.gelu(pre + bias, approximate=True).astype(jnp.bfloat16))
+    out_ref[...] = (
+        jnp.dot(attended, out_weight_ref[0], preferred_element_type=jnp.float32)
+        + jnp.dot(jnp.concatenate(hidden, axis=0), fc2_ref[0], preferred_element_type=jnp.float32)
+    ).astype(jnp.bfloat16)
+
+
+def update(place, parts, units, b_fc1, w_out, w_fc2, layer_index, other):
+    rows = units[0].shape[0] // 2
+    width = w_out.shape[2]
+    lanes = parts.shape[2]
+    return pl.pallas_call(
+        functools.partial(update_kernel, layer_index, other),
+        grid=(1,),
+        out_shape=jax.ShapeDtypeStruct((rows, width), jnp.bfloat16),
+        in_specs=[
+            whole(pltpu.SMEM),
+            same_block(parts.shape),
+            same_block(b_fc1.shape),
+            layer_block(layer_index, w_out.shape[1:]),
+            layer_block(layer_index, w_fc2.shape[1:]),
+        ]
+        + [same_block(units[0].shape)] * len(units),
+        out_specs=same_block((rows, width)),
+        scratch_shapes=[pltpu.VMEM((lanes, lanes), jnp.float32)],
+        compiler_params=compiler_params(),
+        name="update",
+    )(place, parts, b_fc1, w_out, w_fc2, *units)
+
+
+def per_device(
+    token_ids, embedding, group_of, prefix_len, tail_len, block_map, k_cache, v_cache,
+    ln_gain, ln_bias, w_qkv, w_fc1, b_fc1, w_out, w_fc2,
+):
+    seq_count, tp_count = lax.axis_size("seq"), lax.axis_size("tp")
+    seq_index, tp_index = lax.axis_index("seq"), lax.axis_index("tp")
+    devices = seq_count * tp_count
+    core = seq_index % 2
+    place = jnp.stack([seq_index, seq_index * tp_count + tp_index]).astype(jnp.int32)
+    requests, new_tokens = token_ids.shape
+    rows = requests * new_tokens
+    groups = prefix_len.shape[0]
+    share = rows // seq_count
+    mine = rows // devices
+    width = embedding.shape[1]
+    width_local = k_cache.shape[2]
+    same_core = [[s * tp_count + p for s in range(c, seq_count, 2) for p in range(tp_count)] for c in range(2)]
+    same_core_seq = [list(range(c, seq_count, 2)) for c in range(2)]
+
+    def to_owners(half):
+        parts = half.reshape(devices // 2, mine, width)
+        return lax.all_to_all(parts, ("seq", "tp"), 0, 0, axis_index_groups=same_core)
+
+    def to_chips(parts):
+        return lax.all_to_all(parts, "seq", 0, 0, axis_index_groups=same_core_seq)
+
+    near, far = embed(place, token_ids, group_of, embedding)
+    parts = to_owners(near + swap_cores(far, seq_count))
+    rank, positions, visits = order_requests(group_of, prefix_len, tail_len, block_map, new_tokens)
+    own_positions = lax.dynamic_index_in_dim(positions.reshape(CHIPS, 2, share), core, 1, keepdims=False)
+    tables = rotary_tables(own_positions.reshape(-1), 2 * HEAD_DIM)
+    parts, tables, visits = lax.optimization_barrier((parts, tables, visits))
+    state = None
+    for layer_index in range(LAYERS):
+        weights_qkv = w_qkv[layer_index].reshape(w_qkv.shape[1], -1)
+        state, cut = norm_rows(parts, state, ln_gain, ln_bias, layer_index, devices, tp_count)
+        hidden = lax.all_to_all(cut, ("seq", "tp"), 0, 0).reshape(rows, -1)
+        arriving = swap_cores(project(place, hidden, weights_qkv, w_fc1, layer_index), seq_count)
+        heads, *units = project(place, hidden, weights_qkv, w_fc1, layer_index, arriving)
+        query, new_key, new_value = activate(place, to_chips(heads), tables, width_local)
+        query, *units = lax.optimization_barrier((query, *units))
+        units = units[:1] + [
+            lax.ppermute(units[k], "seq", [(i, i ^ (2 * k)) for i in range(seq_count)])
+            for k in range(1, CHIPS)
+        ]
+        parts = attend(
+            place, visits, query, swap_cores(query, seq_count), new_key, new_value,
+            k_cache, v_cache, layer_index, new_tokens, groups,
+        )
+        parts = lax.all_to_all(parts, "seq", 0, 0)
+        arriving = swap_cores(update(place, parts, units, b_fc1, w_out, w_fc2, layer_index, True), seq_count)
+        half = update(place, parts, units, b_fc1, w_out, w_fc2, layer_index, False) + arriving
+        if layer_index < LAYERS - 1:
+            parts = to_owners(half)
+    last = gather_rows(place, to_chips(half.reshape(CHIPS, share, width)), state, tp_count)
+    last = last.astype(jnp.bfloat16)
+    last = [last] + [
+        lax.ppermute(last, "tp", [(i, i ^ k) for i in range(tp_count)]) for k in range(1, tp_count)
+    ]
+    last = to_chips(last_rows(last)).reshape(rows // 2, width)
+    arriving = swap_cores(last, seq_count)
+    wanted = (rank[:, None] * new_tokens + jnp.arange(new_tokens, dtype=jnp.int32)[None, :]).reshape(-1)
+    index = jnp.arange(rows // 2, dtype=jnp.int32)
+
+    def placed(half, parity):
+        held = (2 * (index // share) + parity) * share + index % share
+        hot = (wanted[:, None] == held[None, :]).astype(jnp.bfloat16)
+        return jnp.dot(hot, half, preferred_element_type=jnp.float32)
+
+    return (placed(last, core) + placed(arriving, 1 - core)).reshape(requests, new_tokens, width)
+
+
 def solution(mesh):
     in_specs = (
         P(),
@@ -249,6 +932,8 @@
         P(None, ("tp", "seq"), None),
     )
     out_specs = P()
+    seq_count, tp_count = mesh.shape["seq"], mesh.shape["tp"]
+    fits = tp_count == 4 and seq_count == HEADS // tp_count and seq_count == 2 * CHIPS
     return jax.shard_map(
-        per_device, mesh=mesh, in_specs=in_specs, out_specs=out_specs, check_vma=False
+        per_device if fits else per_device_any, mesh=mesh, in_specs=in_specs, out_specs=out_specs, check_vma=False
     )

time: 1080 us -> 216 us (0.20)
  waiting for transfers between devices: 637 us -> 61.3 us
  matrix products: 143 us -> 0.94 us
  local copies, waits for them, and re-layouts: 131 us -> 12.9 us
  other arithmetic: 69.8 us -> 3.13 us
  Pallas kernels: 0 us -> 33.5 us
  starting transfers between devices: 0.43 us -> 32.9 us
  between operations: 15.3 us -> 0.62 us
    psum x7 -> x0, waiting for transfers between devices: 637 us -> none  [the longest x3 387 us: full_total(): return lax.psum(values, ('seq', 'tp'))]
    dot_general x112 -> x2, matrix products: 143 us -> 0.94 us  [placed(): return jnp.dot(hot, half, preferred_element_type=jnp.float32)]
    all_to_all x0 -> x5, blocking collectives: none -> 69.3 us  [the longest x4 49.8 us: to_chips(): return lax.all_to_all(parts, 'seq', 0, 0, axis_index_groups=same_core_seq)]
    pmax x2 -> x0, blocking collectives: 46.8 us -> none  [per_device(): cache_max = lax.pmax(part_max, 'seq')]
    ppermute x0 -> x17, waiting for transfers between devices: none -> 38.3 us  [the longest x6 18.4 us: per_device(): lax.ppermute(units[k], 'seq', [(i, i ^ 2 * k) for i in range(seq_count)])]
    pallas_call x0 -> x18, Pallas kernels: none -> 33.5 us  [the longest x2 11.9 us: attend(): pl.pallas_call(functools.partial(attend_kernel, layer_index, new_tokens),...]
    psum x2 -> x0, blocking collectives: 24 us -> none  [per_device(): lax.psum((part_sum * factor).astype(jnp.bfloat16), 'seq')]
    unnamed x184 -> x68, local copies, waits for them, and re-layouts: 30 us -> 6.49 us
  transfers between devices with their start and end apart: 7 -> 22, of which waited for: 7 -> 16; matrix products, arithmetic and copies ran while one was open for 6% -> 4% of each run, Pallas kernels for 0% -> 2%
where the time goes in v2:
time: 216 us; the launch traced here: 215 us
  blocking collectives  69.3 us (32%)
  waiting for transfers between devices  61.3 us (28%)
  Pallas kernels  33.5 us (16%)
  starting transfers between devices  32.9 us (15%)
  local copies, waits for them, and re-layouts  12.9 us (6%)
  other arithmetic  3.13 us (1%)
    all_to_all x4, blocking collectives, to_chips(): return lax.all_to_all(parts, 'seq', 0, 0, axis_index_groups=same_core_seq)  49.8 us
    all_to_all x1, blocking collectives, to_owners(): lax.all_to_all(parts, ('seq', 'tp'), 0, 0, axis_index_groups=same_core)  19.5 us
    ppermute x6, waiting for transfers between devices, per_device(): lax.ppermute(units[k], 'seq', [(i, i ^ 2 * k) for i in range(seq_count)])  18.4 us
    all_to_all x1, waiting for transfers between devices, to_owners(): lax.all_to_all(parts, ('seq', 'tp'), 0, 0, axis_index_groups=same_core)  12.7 us
    ppermute x8, waiting for transfers between devices, swap_cores(): return lax.ppermute(values, 'seq', [(i, i ^ 1) for i in range(seq_count)])  12 us
    pallas_call x2, Pallas kernels, attend(): pl.pallas_call(functools.partial(attend_kernel, layer_index, new_tokens),...  11.9 us
    all_to_all x2, waiting for transfers between devices, per_device(): hidden = lax.all_to_all(cut, ('seq', 'tp'), 0, 0).reshape(rows, -1)  10.4 us
    all_to_all x1, starting transfers between devices, to_owners(): lax.all_to_all(parts, ('seq', 'tp'), 0, 0, axis_index_groups=same_core)  8.23 us
  transfers between devices with their start and end apart: 22, of which 16 were waited for; matrix products, arithmetic and copies ran while one was open for 4% of the time, Pallas kernels for 2%

profile of v2, /device:TPU:0, one launch (start us, length us, event | category | flops | bytes accessed | tf_op | source)
XLA Modules:
  0.0 214.7 jit_solution(9933274981923508889)
XLA Ops:
  0.6 5.7 %embed.1 = (bf16[128,2048]{1,0:T(8,128)(2,1)}, bf16[128,2048]{1,0:T(8,128)(2,1)}) custom-call(s32[2]{0:T(128)} %pad_add_fusion.place_ref, s32[4,64]{1,0:T(4,128)} %bitcast.26, s32[1,64]{1,0:T(1,128)} %bitcast.27, bf16[1600,2048]{1,0:T(8,128)(2,1)} %table_hbm.1), custom_call_target="tpu_custom_call" | custom-call | tf_op jit(solution)/shard_map/embed/pallas_call | solution.py:355
  6.8 1.7 collective-permute-done
  8.5 1.9 add_bitcast_fusion.1
  10.4 8.2 %all-to-all-start = ((bf16[16,8,2048]{2,1,0:T(8,128)(2,1)}), bf16[16,8,2048]{2,1,0:T(8,128)(2,1)S(1)}, u32[]{:S(2)}, u32[]{:S(2)}) async-start(bf16[16,8,2048]{2,1,0:T(8,128)(2,1)} %add_bitcast_fusion.1), calls=%async_computation | async-start | bytes 1048576 | tf_op jit(solution)/shard_map/all_to_all | solution.py:865
  18.7 2.5 %order_requests.1 = (s32[64]{0:T(128)}, s32[256]{0:T(256)}, s32[64]{0:T(128)}) custom-call(s32[64]{0:T(128)} %group_ref.1, s32[8]{0:T(128)} %prefix_ref.1, s32[64]{0:T(128)} %tail_ref.1, s32[2,16]{1,0:T(2,128)} %bitcast.28), custom_call_target="tpu_custom_call" | custom-call | tf_op jit(solution)/shard_map/order_requests/pallas_call | solution.py:298
  22.5 12.7 %all-to-all-done.refs_0_ = bf16[16,8,2048]{2,1,0:T(8,128)(2,1)S(1)} async-done(((bf16[16,8,2048]{2,1,0:T(8,128)(2,1)}), bf16[16,8,2048]{2,1,0:T(8,128)(2,1)S(1)}, u32[]{:S(2)}, u32[]{:S(2)}) %all-to-all-start) | async-done | bytes 524320 | tf_op jit(solution)/shard_map/all_to_all | solution.py:865
  36.8 2.6 %all-to-all-start.1 = ((bf16[32,8,256]{2,1,0:T(8,128)(2,1)}), bf16[32,8,256]{2,1,0:T(8,128)(2,1)S(1)}, u32[]{:S(2)}, u32[]{:S(2)}) async-start(bf16[32,8,256]{2,1,0:T(8,128)(2,1)} %get-tuple-element.50), calls=%async_computation.1 | async-start | bytes 262144 | tf_op jit(solution)/shard_map/all_to_all | solution.py:880
  43.0 4.7 %all-to-all-done.1 = bf16[32,8,256]{2,1,0:T(8,128)(2,1)S(1)} async-done(((bf16[32,8,256]{2,1,0:T(8,128)(2,1)}), bf16[32,8,256]{2,1,0:T(8,128)(2,1)S(1)}, u32[]{:S(2)}, u32[]{:S(2)}) %all-to-all-start.1) | async-done | bytes 131104 | tf_op jit(solution)/shard_map/all_to_all | solution.py:880
  48.8 2.5 %collective-permute-done.1.refs_0_ = bf16[1792,256]{1,0:T(8,128)(2,1)S(1)} collective-permute-done((bf16[1792,256]{1,0:T(8,128)(2,1)S(1)}, bf16[1792,256]{1,0:T(8,128)(2,1)S(1)}, u32[]{:S(2)}, u32[]{:S(2)}) %collective-permute-start.1) | collective-permute-done | bytes 917536 | tf_op jit(solution)/shard_map/ppermute | solution.py:238
  52.8 14.3 %all_to_all.50.part_ref = bf16[4,384,256]{2,1,0:T(8,128)(2,1)S(1)} all-to-all(bf16[4,384,256]{2,1,0:T(8,128)(2,1)S(1)} %get-tuple-element.51), channel_id=1, replica_groups={{0,8,16,24},{4,12,20,28},{1,9,17,25},{5,13,21,29},{2,10,18,26},{6,14,22..., dimensions={0} | all-to-all | bytes 1572864 | tf_op jit(solution)/shard_map/all_to_all | solution.py:868
  69.4 5.9 %attend.2 = bf16[8,160,128]{2,1,0:T(8,128)(2,1)} custom-call(s32[2]{0:T(128)S(1)} %copy-done.13, s32[64]{0:T(128)S(1)} %copy-done.22, bf16[128,512]{1,0:T(8,128)(2,1)S(1)} %get-tuple-element.58.query_ref, bf16[128,512]{1,0:T(8,128)(2,1)S(1)} %collective-permute-done.2.far_query_ref, bf16[32,512]{1,0:T(8,128)(2,1)S(1)} %get-tuple-element.59.new_key_ref, ...), custom_call_target="tpu_custom_call" | custom-call | tf_op jit(solution)/shard_map/attend/pallas_call | solution.py:749
  75.4 3.4 %all-to-all-start.3 = ((bf16[8,160,128]{2,1,0:T(8,128)(2,1)}), bf16[8,160,128]{2,1,0:T(8,128)(2,1)S(1)}, u32[]{:S(2)}, u32[]{:S(2)}) async-start(bf16[8,160,128]{2,1,0:T(8,128)(2,1)} %attend.2), calls=%async_computation.3 | async-start | bytes 655360 | tf_op jit(solution)/shard_map/all_to_all | solution.py:893
  78.8 1.9 collective-permute-start.3
  80.8 1.5 collective-permute-start.4
  82.4 6.4 %collective-permute-done.3.refs_1_ = bf16[256,256]{1,0:T(8,128)(2,1)S(1)} collective-permute-done((bf16[256,256]{1,0:T(8,128)(2,1)}, bf16[256,256]{1,0:T(8,128)(2,1)S(1)}, u32[]{:S(2)}, u32[]{:S(2)}) %collective-permute-start.3) | collective-permute-done | bytes 131104 | tf_op jit(solution)/shard_map/ppermute | solution.py:886
  88.8 3.3 %collective-permute-done.5.refs_3_ = bf16[256,256]{1,0:T(8,128)(2,1)S(1)} collective-permute-done((bf16[256,256]{1,0:T(8,128)(2,1)}, bf16[256,256]{1,0:T(8,128)(2,1)S(1)}, u32[]{:S(2)}, u32[]{:S(2)}) %collective-permute-start.5) | collective-permute-done | bytes 131104 | tf_op jit(solution)/shard_map/ppermute | solution.py:886
  92.0 1.6 copy-done.1
  97.0 19.5 %all_to_all.51.refs_0_ = bf16[16,8,2048]{2,1,0:T(8,128)(2,1)S(1)} all-to-all(bf16[16,8,2048]{2,1,0:T(8,128)(2,1)S(1)} %add_bitcast_fusion), channel_id=1, replica_groups={{0,1,2,3,8,9,10,11,16,17,18,19,24,25,26,27},{4,5,6,7,12,13,14,15,20,21,..., dimensions={0} | all-to-all | bytes 1048576 | tf_op jit(solution)/shard_map/all_to_all | solution.py:865
  118.1 2.8 %all-to-all-start.5 = ((bf16[32,8,256]{2,1,0:T(8,128)(2,1)}), bf16[32,8,256]{2,1,0:T(8,128)(2,1)S(1)}, u32[]{:S(2)}, u32[]{:S(2)}) async-start(bf16[32,8,256]{2,1,0:T(8,128)(2,1)} %get-tuple-element.66), calls=%async_computation.5 | async-start | bytes 262144 | tf_op jit(solution)/shard_map/all_to_all | solution.py:880
  123.4 5.7 %all-to-all-done.5 = bf16[32,8,256]{2,1,0:T(8,128)(2,1)S(1)} async-done(((bf16[32,8,256]{2,1,0:T(8,128)(2,1)}), bf16[32,8,256]{2,1,0:T(8,128)(2,1)S(1)}, u32[]{:S(2)}, u32[]{:S(2)}) %all-to-all-start.5) | async-done | bytes 131104 | tf_op jit(solution)/shard_map/all_to_all | solution.py:880
  130.7 2.5 %collective-permute-done.7.refs_0_ = bf16[1792,256]{1,0:T(8,128)(2,1)S(1)} collective-permute-done((bf16[1792,256]{1,0:T(8,128)(2,1)S(1)}, bf16[1792,256]{1,0:T(8,128)(2,1)S(1)}, u32[]{:S(2)}, u32[]{:S(2)}) %collective-permute-start.7) | collective-permute-done | bytes 917536 | tf_op jit(solution)/shard_map/ppermute | solution.py:238
  134.2 14.4 %all_to_all.52.part_ref = bf16[4,384,256]{2,1,0:T(8,128)(2,1)S(1)} all-to-all(bf16[4,384,256]{2,1,0:T(8,128)(2,1)S(1)} %get-tuple-element.67), channel_id=1, replica_groups={{0,8,16,24},{4,12,20,28},{1,9,17,25},{5,13,21,29},{2,10,18,26},{6,14,22..., dimensions={0} | all-to-all | bytes 1572864 | tf_op jit(solution)/shard_map/all_to_all | solution.py:868
  150.9 5.9 %attend.3 = bf16[8,160,128]{2,1,0:T(8,128)(2,1)} custom-call(s32[2]{0:T(128)S(1)} %copy-done.14, s32[64]{0:T(128)S(1)} %copy-done.23, bf16[128,512]{1,0:T(8,128)(2,1)S(1)} %get-tuple-element.73.query_ref, bf16[128,512]{1,0:T(8,128)(2,1)S(1)} %collective-permute-done.8.far_query_ref, bf16[32,512]{1,0:T(8,128)(2,1)S(1)} %get-tuple-element.74.new_key_ref, ...), custom_call_target="tpu_custom_call" | custom-call | tf_op jit(solution)/shard_map/attend/pallas_call | solution.py:749
  156.9 3.4 %all-to-all-start.7 = ((bf16[8,160,128]{2,1,0:T(8,128)(2,1)}), bf16[8,160,128]{2,1,0:T(8,128)(2,1)S(1)}, u32[]{:S(2)}, u32[]{:S(2)}) async-start(bf16[8,160,128]{2,1,0:T(8,128)(2,1)} %attend.3), calls=%async_computation.7 | async-start | bytes 655360 | tf_op jit(solution)/shard_map/all_to_all | solution.py:893
  160.3 1.9 collective-permute-start.10
  163.9 8.7 %collective-permute-done.10.refs_2_ = bf16[256,256]{1,0:T(8,128)(2,1)S(1)} collective-permute-done((bf16[256,256]{1,0:T(8,128)(2,1)}, bf16[256,256]{1,0:T(8,128)(2,1)S(1)}, u32[]{:S(2)}, u32[]{:S(2)}) %collective-permute-start.10) | collective-permute-done | bytes 131104 | tf_op jit(solution)/shard_map/ppermute | solution.py:886
  176.1 11.5 %all_to_all.53.part_ref = bf16[4,32,2048]{2,1,0:T(8,128)(2,1)S(1)} all-to-all(bf16[4,32,2048]{2,1,0:T(8,128)(2,1)S(1)} %bitcast.23), channel_id=1, replica_groups={{0,8,16,24},{4,12,20,28},{1,9,17,25},{5,13,21,29},{2,10,18,26},{6,14,22..., dimensions={0} | all-to-all | bytes 1048576 | tf_op jit(solution)/shard_map/all_to_all | solution.py:868
  190.1 2.7 %collective-permute-start.15 = (bf16[32,2048]{1,0:T(8,128)(2,1)S(1)}, bf16[32,2048]{1,0:T(8,128)(2,1)S(1)}, u32[]{:S(2)}, u32[]{:S(2)}) collective-permute-start(bf16[32,2048]{1,0:T(8,128)(2,1)S(1)} %convert_element_type.26.a_ref), channel_id=1, source_target_pairs={{0,3},{1,2},{2,1},{3,0},{4,7},{5,6},{6,5},{7,4},{8,11},{9,10},{10,... | collective-permute-start | bytes 393224 | tf_op jit(solution)/shard_map/ppermute | solution.py:901
  194.2 6.4 %collective-permute-done.14.c_ref = bf16[32,2048]{1,0:T(8,128)(2,1)S(1)} collective-permute-done((bf16[32,2048]{1,0:T(8,128)(2,1)S(1)}, bf16[32,2048]{1,0:T(8,128)(2,1)S(1)}, u32[]{:S(2)}, u32[]{:S(2)}) %collective-permute-start.14) | collective-permute-done | bytes 131104 | tf_op jit(solution)/shard_map/ppermute | solution.py:901
  200.7 9.5 %all_to_all.54 = bf16[4,32,2048]{2,1,0:T(8,128)(2,1)S(1)} all-to-all(bf16[4,32,2048]{2,1,0:T(8,128)(2,1)S(1)} %last_rows.1), channel_id=1, replica_groups={{0,8,16,24},{4,12,20,28},{1,9,17,25},{5,13,21,29},{2,10,18,26},{6,14,22..., dimensions={0} | all-to-all | bytes 1048576 | tf_op jit(solution)/shard_map/all_to_all | solution.py:868
  210.4 1.7 collective-permute-done.16
  213.1 1.6 reshape.337
  (127 shorter events, 35.0 us)
Async XLA Ops:
  6.2 28.9 %copy-start.20 = (f32[2,2048]{1,0:T(2,128)S(1)}, f32[2,2048]{1,0:T(2,128)}, u32[]{:S(2)}) copy-start(f32[2,2048]{1,0:T(2,128)} %refs_2_.3) | copy-start | bytes 49156
  6.3 28.9 %copy-start.21 = (f32[2,2048]{1,0:T(2,128)S(1)}, f32[2,2048]{1,0:T(2,128)}, u32[]{:S(2)}) copy-start(f32[2,2048]{1,0:T(2,128)} %refs_3_.1) | copy-start | bytes 49156
  6.3 33.1 %copy-start.31 = (bf16[2,256,3,512]{3,1,2,0:T(8,128)(2,1)S(1)}, bf16[2,256,3,512]{3,1,2,0:T(8,128)(2,1)}, u32[]{:S(2)}) copy-start(bf16[2,256,3,512]{3,1,2,0:T(8,128)(2,1)} %param.25) | copy-start | bytes 4718596
  6.3 2.3 %collective-permute-start = (bf16[128,2048]{1,0:T(8,128)(2,1)}, bf16[128,2048]{1,0:T(8,128)(2,1)S(1)}, u32[]{:S(2)}, u32[]{:S(2)}) collective-permute-start(bf16[128,2048]{1,0:T(8,128)(2,1)} %get-tuple-element.45), channel_id=1, source_target_pairs={{0,4},{4,0},{8,12},{12,8},{16,20},{20,16},{24,28},{28,24},{1,5},{5... | collective-permute-start | bytes 1572872 | tf_op jit(solution)/shard_map/ppermute | solution.py:238
  10.4 24.7 %all-to-all-start = ((bf16[16,8,2048]{2,1,0:T(8,128)(2,1)}), bf16[16,8,2048]{2,1,0:T(8,128)(2,1)S(1)}, u32[]{:S(2)}, u32[]{:S(2)}) async-start(bf16[16,8,2048]{2,1,0:T(8,128)(2,1)} %add_bitcast_fusion.1), calls=%async_computation | async-start | bytes 1048576 | tf_op jit(solution)/shard_map/all_to_all | solution.py:865
  22.5 44.7 %copy-start.8 = (f32[3,128,128]{2,1,0:T(8,128)}, f32[3,128,128]{2,1,0:T(8,128)S(1)}, u32[]{:S(2)}) copy-start(f32[3,128,128]{2,1,0:T(8,128)S(1)} %pad_maximum_fusion.table_ref) | copy-start | bytes 589828
  36.8 11.0 %all-to-all-start.1 = ((bf16[32,8,256]{2,1,0:T(8,128)(2,1)}), bf16[32,8,256]{2,1,0:T(8,128)(2,1)S(1)}, u32[]{:S(2)}, u32[]{:S(2)}) async-start(bf16[32,8,256]{2,1,0:T(8,128)(2,1)} %get-tuple-element.50), calls=%async_computation.1 | async-start | bytes 262144 | tf_op jit(solution)/shard_map/all_to_all | solution.py:880
  48.7 2.5 %collective-permute-start.1 = (bf16[1792,256]{1,0:T(8,128)(2,1)S(1)}, bf16[1792,256]{1,0:T(8,128)(2,1)S(1)}, u32[]{:S(2)}, u32[]{:S(2)}) collective-permute-start(bf16[1792,256]{1,0:T(8,128)(2,1)S(1)} %project.4), channel_id=1, source_target_pairs={{0,4},{4,0},{8,12},{12,8},{16,20},{20,16},{24,28},{28,24},{1,5},{5... | collective-permute-start | bytes 2752520 | tf_op jit(solution)/shard_map/ppermute | solution.py:238
  68.0 1.4 collective-permute-start.2
  69.4 22.6 %copy-start.7 = (bf16[2,64,2048]{2,1,0:T(8,128)(2,1)S(1)}, bf16[2,64,2048]{2,1,0:T(8,128)(2,1)}, u32[]{:S(2)}) copy-start(bf16[2,64,2048]{2,1,0:T(8,128)(2,1)} %out_weight_ref.7) | copy-start | bytes 1572868
  69.4 22.6 %copy-start.12 = (f32[2,2048]{1,0:T(2,128)S(1)}, f32[2,2048]{1,0:T(2,128)}, u32[]{:S(2)}) copy-start(f32[2,2048]{1,0:T(2,128)} %bias_ref.7) | copy-start | bytes 49156
  75.4 16.6 %all-to-all-start.3 = ((bf16[8,160,128]{2,1,0:T(8,128)(2,1)}), bf16[8,160,128]{2,1,0:T(8,128)(2,1)S(1)}, u32[]{:S(2)}, u32[]{:S(2)}) async-start(bf16[8,160,128]{2,1,0:T(8,128)(2,1)} %attend.2), calls=%async_computation.3 | async-start | bytes 655360 | tf_op jit(solution)/shard_map/all_to_all | solution.py:893
  78.8 9.9 %collective-permute-start.3 = (bf16[256,256]{1,0:T(8,128)(2,1)}, bf16[256,256]{1,0:T(8,128)(2,1)S(1)}, u32[]{:S(2)}, u32[]{:S(2)}) collective-permute-start(bf16[256,256]{1,0:T(8,128)(2,1)} %copy-done.29), channel_id=1, source_target_pairs={{0,8},{4,12},{8,0},{12,4},{16,24},{20,28},{24,16},{28,20},{1,9},{5... | collective-permute-start | bytes 393224 | tf_op jit(solution)/shard_map/ppermute | solution.py:886
  80.8 8.0 %collective-permute-start.4 = (bf16[256,256]{1,0:T(8,128)(2,1)}, bf16[256,256]{1,0:T(8,128)(2,1)S(1)}, u32[]{:S(2)}, u32[]{:S(2)}) collective-permute-start(bf16[256,256]{1,0:T(8,128)(2,1)} %copy-done.27), channel_id=1, source_target_pairs={{0,16},{4,20},{8,24},{12,28},{16,0},{20,4},{24,8},{28,12},{1,17},{... | collective-permute-start | bytes 393224 | tf_op jit(solution)/shard_map/ppermute | solution.py:886
  82.2 9.8 %collective-permute-start.5 = (bf16[256,256]{1,0:T(8,128)(2,1)}, bf16[256,256]{1,0:T(8,128)(2,1)S(1)}, u32[]{:S(2)}, u32[]{:S(2)}) collective-permute-start(bf16[256,256]{1,0:T(8,128)(2,1)} %copy-done.25), channel_id=1, source_target_pairs={{0,24},{4,28},{8,16},{12,20},{16,8},{20,12},{24,0},{28,4},{1,25},{... | collective-permute-start | bytes 393224 | tf_op jit(solution)/shard_map/ppermute | solution.py:886
  95.0 2.0 collective-permute-start.6
  96.5 24.4 %copy-start.30 = (bf16[1,256,3,512]{3,1,2,0:T(8,128)(2,1)S(1)}, bf16[1,256,3,512]{3,1,2,0:T(8,128)(2,1)}, u32[]{:S(2)}) copy-start(bf16[1,256,3,512]{3,1,2,0:T(8,128)(2,1)} %get-tuple-element.81) | copy-start | bytes 2359300
  118.1 11.0 %all-to-all-start.5 = ((bf16[32,8,256]{2,1,0:T(8,128)(2,1)}), bf16[32,8,256]{2,1,0:T(8,128)(2,1)S(1)}, u32[]{:S(2)}, u32[]{:S(2)}) async-start(bf16[32,8,256]{2,1,0:T(8,128)(2,1)} %get-tuple-element.66), calls=%async_computation.5 | async-start | bytes 262144 | tf_op jit(solution)/shard_map/all_to_all | solution.py:880
  130.6 2.5 %collective-permute-start.7 = (bf16[1792,256]{1,0:T(8,128)(2,1)S(1)}, bf16[1792,256]{1,0:T(8,128)(2,1)S(1)}, u32[]{:S(2)}, u32[]{:S(2)}) collective-permute-start(bf16[1792,256]{1,0:T(8,128)(2,1)S(1)} %project.6), channel_id=1, source_target_pairs={{0,4},{4,0},{8,12},{12,8},{16,20},{20,16},{24,28},{28,24},{1,5},{5... | collective-permute-start | bytes 2752520 | tf_op jit(solution)/shard_map/ppermute | solution.py:238
  149.4 1.4 collective-permute-start.8
  150.9 21.7 %copy-start.2 = (bf16[2,256,2048]{2,1,0:T(8,128)(2,1)S(1)}, bf16[2,256,2048]{2,1,0:T(8,128)(2,1)}, u32[]{:S(2)}) copy-start(bf16[2,256,2048]{2,1,0:T(8,128)(2,1)} %fc2_ref.7) | copy-start | bytes 6291460
  150.9 21.7 %copy-start.11 = (bf16[256,256]{1,0:T(8,128)(2,1)S(1)}, bf16[256,256]{1,0:T(8,128)(2,1)}, u32[]{:S(2)}) copy-start(bf16[256,256]{1,0:T(8,128)(2,1)} %copy-done.10) | copy-start | bytes 393220
  156.9 15.7 %all-to-all-start.7 = ((bf16[8,160,128]{2,1,0:T(8,128)(2,1)}), bf16[8,160,128]{2,1,0:T(8,128)(2,1)S(1)}, u32[]{:S(2)}, u32[]{:S(2)}) async-start(bf16[8,160,128]{2,1,0:T(8,128)(2,1)} %attend.3), calls=%async_computation.7 | async-start | bytes 655360 | tf_op jit(solution)/shard_map/all_to_all | solution.py:893
  160.3 12.3 %collective-permute-start.10 = (bf16[256,256]{1,0:T(8,128)(2,1)}, bf16[256,256]{1,0:T(8,128)(2,1)S(1)}, u32[]{:S(2)}, u32[]{:S(2)}) collective-permute-start(bf16[256,256]{1,0:T(8,128)(2,1)} %copy-done.28), channel_id=1, source_target_pairs={{0,16},{4,20},{8,24},{12,28},{16,0},{20,4},{24,8},{28,12},{1,17},{... | collective-permute-start | bytes 393224 | tf_op jit(solution)/shard_map/ppermute | solution.py:886
  162.3 10.3 %collective-permute-start.11 = (bf16[256,256]{1,0:T(8,128)(2,1)}, bf16[256,256]{1,0:T(8,128)(2,1)S(1)}, u32[]{:S(2)}, u32[]{:S(2)}) collective-permute-start(bf16[256,256]{1,0:T(8,128)(2,1)} %copy-done.26), channel_id=1, source_target_pairs={{0,24},{4,28},{8,16},{12,20},{16,8},{20,12},{24,0},{28,4},{1,25},{... | collective-permute-start | bytes 393224 | tf_op jit(solution)/shard_map/ppermute | solution.py:886
  163.7 8.9 %collective-permute-start.9 = (bf16[256,256]{1,0:T(8,128)(2,1)}, bf16[256,256]{1,0:T(8,128)(2,1)S(1)}, u32[]{:S(2)}, u32[]{:S(2)}) collective-permute-start(bf16[256,256]{1,0:T(8,128)(2,1)} %copy-done.24), channel_id=1, source_target_pairs={{0,8},{4,12},{8,0},{12,4},{16,24},{20,28},{24,16},{28,20},{1,9},{5... | collective-permute-start | bytes 393224 | tf_op jit(solution)/shard_map/ppermute | solution.py:886
  174.0 2.0 collective-permute-start.12
  176.1 34.1 %copy-start.32 = (s32[64]{0:T(128)S(1)}, s32[64]{0:T(128)}, u32[]{:S(2)}) copy-start(s32[64]{0:T(128)} %get-tuple-element.43) | copy-start | bytes 772
  188.3 5.9 %collective-permute-start.13 = (bf16[32,2048]{1,0:T(8,128)(2,1)S(1)}, bf16[32,2048]{1,0:T(8,128)(2,1)S(1)}, u32[]{:S(2)}, u32[]{:S(2)}) collective-permute-start(bf16[32,2048]{1,0:T(8,128)(2,1)S(1)} %convert_element_type.26.a_ref), channel_id=1, source_target_pairs={{0,1},{1,0},{2,3},{3,2},{4,5},{5,4},{6,7},{7,6},{8,9},{9,8},{10,11... | collective-permute-start | bytes 393224 | tf_op jit(solution)/shard_map/ppermute | solution.py:901
  188.6 12.0 %collective-permute-start.14 = (bf16[32,2048]{1,0:T(8,128)(2,1)S(1)}, bf16[32,2048]{1,0:T(8,128)(2,1)S(1)}, u32[]{:S(2)}, u32[]{:S(2)}) collective-permute-start(bf16[32,2048]{1,0:T(8,128)(2,1)S(1)} %convert_element_type.26.a_ref), channel_id=1, source_target_pairs={{0,2},{1,3},{2,0},{3,1},{4,6},{5,7},{6,4},{7,5},{8,10},{9,11},{10,... | collective-permute-start | bytes 393224 | tf_op jit(solution)/shard_map/ppermute | solution.py:901
  190.1 10.5 %collective-permute-start.15 = (bf16[32,2048]{1,0:T(8,128)(2,1)S(1)}, bf16[32,2048]{1,0:T(8,128)(2,1)S(1)}, u32[]{:S(2)}, u32[]{:S(2)}) collective-permute-start(bf16[32,2048]{1,0:T(8,128)(2,1)S(1)} %convert_element_type.26.a_ref), channel_id=1, source_target_pairs={{0,3},{1,2},{2,1},{3,0},{4,7},{5,6},{6,5},{7,4},{8,11},{9,10},{10,... | collective-permute-start | bytes 393224 | tf_op jit(solution)/shard_map/ppermute | solution.py:901
  210.2 1.9 collective-permute-start.16
  (23 other events, 304.6 us)

commit v3 on v2

--- a/solution.py
+++ b/solution.py
@@ -15,6 +15,7 @@
 BLOCK = 128
 SPAN = 512
 CHIPS = 4
+LANES = 128
 
 
 very_negative = -1e30
@@ -238,6 +239,10 @@
     return lax.ppermute(values, "seq", [(i, i ^ 1) for i in range(seq_count)])
 
 
+def in_hbm(values):
+    return pltpu.with_memory_space_constraint(values, pltpu.HBM)
+
+
 def compiler_params(megabytes=32):
     return pltpu.CompilerParams(vmem_limit_bytes=megabytes * 2**20)
 
@@ -309,62 +314,192 @@
     )(group_of, prefix_len, tail_len, block_map.T)
 
 
-def embed_kernel(place_ref, token_ref, group_ref, table_hbm, near_ref, far_ref, table_ref, hot_ref, semaphores):
-    core = place_ref[0] % 2
-    first = place_ref[1] * table_ref.shape[0]
-    new_tokens, requests = token_ref.shape
-    rows = 2 * near_ref.shape[0]
-    cuts = semaphores.shape[0]
-    width = table_ref.shape[1] // cuts
-    columns = [slice(cut * width, (cut + 1) * width) for cut in range(cuts)]
-    copies = [
-        pltpu.make_async_copy(table_hbm.at[:, column], table_ref.at[:, column], semaphores.at[cut])
-        for cut, column in enumerate(columns)
-    ]
-    for copy in copies:
-        copy.start()
+def thirds(values):
+    high = values.astype(jnp.bfloat16).astype(jnp.float32)
+    middle = (values - high).astype(jnp.bfloat16).astype(jnp.float32)
+    return high, middle, values - high - middle
+
+
+def row_block(rows):
+    width = rows[0].shape[1]
+    line = lax.broadcasted_iota(jnp.int32, (8, width), 0)
+    block = jnp.zeros((8, width), jnp.float32)
+    for index, row in enumerate(rows):
+        block = jnp.where(line == index, row, block)
+    return block
+
+
+def column_to_row(column):
+    return jnp.broadcast_to(column, (column.shape[0], LANES)).T[0:1]
+
+
+def row_to_column(row):
+    return jnp.broadcast_to(row, (LANES, row.shape[1])).T
+
+
+def ranks(group_ref):
+    requests = group_ref.shape[1]
     across = lax.broadcasted_iota(jnp.int32, (requests, requests), 1)
     down = lax.broadcasted_iota(jnp.int32, (requests, requests), 0)
     group_row = group_ref[0:1, :]
     group_column = jnp.sum(jnp.where(across == down, group_row, 0), axis=1, keepdims=True)
     ahead = (group_column < group_row) | ((group_column == group_row) & (down < across))
-    rank_row = jnp.sum(jnp.where(ahead, 1, 0), axis=0, keepdims=True)
+    return jnp.sum(jnp.where(ahead, 1, 0), axis=0, keepdims=True)
+
+
+def row_sums(lines):
+    block = row_block([part for line in lines for part in thirds(line)])
+    return jnp.concatenate([block, jnp.zeros_like(block)], axis=0).astype(jnp.bfloat16)
+
+
+def from_row_sums(block):
+    block = block.astype(jnp.float32)
+    line = lax.broadcasted_iota(jnp.int32, block.shape, 0)
+    return [
+        jnp.sum(jnp.where((line >= start) & (line < start + 3), block, 0.0), axis=0, keepdims=True)
+        for start in (0, 3)
+    ]
+
+
+def embed_kernel(
+    place_ref, token_ref, group_ref, table_hbm, near_ref, far_ref, own_ref,
+    table_ref, hot_ref, row_ref, semaphores,
+):
+    core = place_ref[0] % 2
+    first = place_ref[1] * table_ref.shape[1]
+    new_tokens, requests = token_ref.shape
+    rows, unit = near_ref.shape[1:]
+    copies = []
+    for chip in range(CHIPS):
+        copies.append(
+            pltpu.make_async_copy(
+                table_hbm.at[:, pl.ds(chip * 2 * unit, 2 * unit)], table_ref.at[chip], semaphores.at[chip]
+            )
+        )
+        copies[-1].start()
+    rank_row = ranks(group_ref)
     line = lax.broadcasted_iota(jnp.int32, (rows, requests), 0)
-    half, share = rows // 2, rows // CHIPS // 2
-    parity = jnp.where(line < half, core, 1 - core)
-    line = line % half
-    line = ((line // share) * 2 + parity) * share + line % share
-    ids = jnp.zeros((rows, 1), jnp.int32)
+    ids = jnp.zeros((rows, requests), jnp.int32)
     for token in range(new_tokens):
-        token_row = token_ref[token : token + 1, :]
         match = (rank_row == line // new_tokens) & (line % new_tokens == token)
-        ids = ids + jnp.sum(jnp.where(match, token_row, 0), axis=1, keepdims=True)
+        ids = jnp.where(match, token_ref[token : token + 1, :], ids)
+    ids = jnp.sum(ids, axis=1, keepdims=True) - first
     entry = lax.broadcasted_iota(jnp.int32, hot_ref.shape, 1)
-    hot_ref[...] = jnp.where(entry == ids - first, 1.0, 0.0).astype(jnp.bfloat16)
-    for copy, column in zip(copies, columns):
+    hot_ref[...] = jnp.where(entry == ids, 1.0, 0.0).astype(jnp.bfloat16)
+    total = jnp.zeros((rows, LANES), jnp.float32)
+    for chip, copy in enumerate(copies):
         copy.wait()
-        chosen = jnp.dot(hot_ref[...], table_ref[:, column], preferred_element_type=jnp.float32)
+        chosen = jnp.dot(hot_ref[...], table_ref[chip], preferred_element_type=jnp.float32)
+        for start in range(0, 2 * unit, LANES):
+            total = total + chosen[:, start : start + LANES]
         chosen = chosen.astype(jnp.bfloat16)
-        near_ref[:, column] = chosen[:half]
-        far_ref[:, column] = chosen[half:]
-
-
-def embed(place, token_ids, group_of, embedding):
+        row_ref[:, chip * 2 * unit : (chip + 1) * 2 * unit] = chosen
+        left, right = chosen[:, :unit], chosen[:, unit:]
+        near_ref[chip] = jnp.where(core == 0, left, right)
+        far_ref[chip * rows : (chip + 1) * rows] = jnp.where(core == 0, right, left)
+    features = row_ref.shape[1]
+    mean = jnp.sum(total, axis=1, keepdims=True) * (1.0 / features)
+    squares = jnp.zeros((rows, LANES), jnp.float32)
+    for start in range(0, features, LANES):
+        centred = row_ref[:, start : start + LANES].astype(jnp.float32) - mean
+        squares = squares + centred * centred
+    variance = jnp.sum(squares, axis=1, keepdims=True) * (1.0 / features)
+    held = (ids >= 0) & (ids < hot_ref.shape[1])
+    scale = jnp.where(held, lax.rsqrt(variance + 1e-05), 0.0)
+    mean, scale = column_to_row(mean), column_to_row(scale)
+    own_ref[...] = row_block([mean, scale])
+    far_ref[CHIPS * rows :] = row_sums([mean, scale])
+
+
+def embed(place, token_ids, group_of, embedding, unit):
     rows = token_ids.shape[0] * token_ids.shape[1]
-    half = jax.ShapeDtypeStruct((rows // 2, embedding.shape[1]), jnp.bfloat16)
     return pl.pallas_call(
         embed_kernel,
-        out_shape=(half, half),
+        out_shape=(
+            jax.ShapeDtypeStruct((CHIPS, rows, unit), jnp.bfloat16),
+            pltpu.HBM((CHIPS * rows + 16, unit), jnp.bfloat16),
+            jax.ShapeDtypeStruct((8, rows), jnp.float32),
+        ),
         in_specs=[whole(pltpu.SMEM), whole(), whole(), whole(pltpu.HBM)],
+        out_specs=(whole(),) * 3,
+        scratch_shapes=[
+            pltpu.VMEM((CHIPS, embedding.shape[0], 2 * unit), jnp.bfloat16),
+            pltpu.VMEM((rows, embedding.shape[0]), jnp.bfloat16),
+            pltpu.VMEM((rows, embedding.shape[1]), jnp.bfloat16),
+            pltpu.SemaphoreType.DMA((CHIPS,)),
+        ],
+        compiler_params=compiler_params(24),
+        name="embed",
+    )(in_hbm(place), in_hbm(token_ids.T), in_hbm(group_of[None, :]), in_hbm(embedding))
+
+
+def join_kernel(near_ref, far_ref, own_ref, out_ref):
+    rows = near_ref.shape[1]
+    for chip in range(CHIPS):
+        far = far_ref[chip * rows : (chip + 1) * rows].astype(jnp.float32)
+        out_ref[chip, :rows] = (near_ref[chip].astype(jnp.float32) + far).astype(jnp.bfloat16)
+    mean, scale = from_row_sums(far_ref[CHIPS * rows :])
+    lines = row_sums([mean + own_ref[0:1, :], scale + own_ref[1:2, :]])
+    for chip in range(CHIPS):
+        out_ref[chip, rows:] = lines
+
+
+def join(near, far, own):
+    chips, rows, unit = near.shape
+    return pl.pallas_call(
+        join_kernel,
+        out_shape=pltpu.HBM((chips, rows + 16, unit), jnp.bfloat16),
+        in_specs=[whole()] * 3,
+        out_specs=whole(),
+        compiler_params=compiler_params(16),
+        name="join",
+    )(near, far, own)
+
+
+def gather_kernel(part_ref, out_ref):
+    rows = part_ref.shape[1] - 16
+    total = part_ref[0].astype(jnp.float32)
+    for chip in range(1, CHIPS):
+        total = total + part_ref[chip].astype(jnp.float32)
+    out_ref[:rows] = total[:rows].astype(jnp.bfloat16)
+    out_ref[rows:] = row_sums(from_row_sums(total[rows:]))
+
+
+def gather(parts):
+    return pl.pallas_call(
+        gather_kernel,
+        out_shape=jax.ShapeDtypeStruct(parts.shape[1:], jnp.bfloat16),
+        in_specs=[whole()],
+        out_specs=whole(),
+        compiler_params=compiler_params(16),
+        name="gather",
+    )(parts)
+
+
+def first_kernel(place_ref, a_ref, b_ref, c_ref, d_ref, gain_ref, bias_ref, start_ref, hidden_ref):
+    rows, unit = hidden_ref.shape
+    parts = [ref[...].astype(jnp.float32) for ref in (a_ref, b_ref, c_ref, d_ref)]
+    total = (parts[0] + parts[1]) + (parts[2] + parts[3])
+    mean, scale = (row_to_column(line) for line in from_row_sums(total[rows:]))
+    columns = pl.ds(pl.multiple_of(place_ref[0] * unit, unit), unit)
+    gain, bias = gain_ref[0:1, columns], bias_ref[0:1, columns]
+    for start in range(0, unit, LANES):
+        span = slice(start, start + LANES)
+        state = total[:rows, span]
+        start_ref[:, span] = state.astype(jnp.bfloat16)
+        hidden_ref[:, span] = ((state - mean) * scale * gain[:, span] + bias[:, span]).astype(jnp.bfloat16)
+
+
+def first_hidden(place, parts, ln_gain, ln_bias):
+    one = jax.ShapeDtypeStruct((parts[0].shape[0] - 16, parts[0].shape[1]), jnp.bfloat16)
+    return pl.pallas_call(
+        first_kernel,
+        out_shape=(one, one),
+        in_specs=[whole(pltpu.SMEM)] + [whole()] * 6,
         out_specs=(whole(), whole()),
-        scratch_shapes=[
-            pltpu.VMEM(embedding.shape, jnp.bfloat16),
-            pltpu.VMEM((rows, embedding.shape[0]), jnp.bfloat16),
-            pltpu.SemaphoreType.DMA((4,)),
-        ],
-        compiler_params=compiler_params(56),
-        name="embed",
-    )(place, token_ids.T, group_of[None, :], embedding)
+        compiler_params=compiler_params(16),
+        name="first_hidden",
+    )(in_hbm(place), *parts, ln_gain, ln_bias)
 
 
 def state_total(part_ref, state_ref):
@@ -413,7 +548,7 @@
     )(*operands)
 
 
-def gather_kernel(tp_count, place_ref, part_ref, state_ref, out_ref):
+def last_parts_kernel(tp_count, place_ref, part_ref, state_ref, out_ref):
     total = part_ref[0].astype(jnp.float32)
     for chip in range(1, part_ref.shape[0]):
         total = total + part_ref[chip].astype(jnp.float32)
@@ -425,15 +560,15 @@
         out_ref[rows] = total_rows
 
 
-def gather_rows(place, parts, state, tp_count):
-    return pl.pallas_call(
-        functools.partial(gather_kernel, tp_count),
+def last_parts(place, parts, state, tp_count):
+    return pl.pallas_call(
+        functools.partial(last_parts_kernel, tp_count),
         out_shape=jax.ShapeDtypeStruct(parts.shape[1:], jnp.float32),
         in_specs=[whole(pltpu.SMEM), whole(), whole()],
         out_specs=whole(),
         compiler_params=compiler_params(16),
-        name="gather_rows",
-    )(place, parts, state)
+        name="last_parts",
+    )(in_hbm(place), parts, state)
 
 
 def last_kernel(a_ref, b_ref, c_ref, d_ref, out_ref):
@@ -455,21 +590,19 @@
     )(*parts)
 
 
-def project_kernel(joins, place_ref, hidden_ref, qkv_ref, fc1_ref, *refs):
-    if joins:
-        arrived_ref, head_ref, *unit_refs = refs
-    else:
-        out_ref = refs[0]
-    seq_index = place_ref[0]
-    parity = seq_index % 2 if joins else 1 - seq_index % 2
-    here = seq_index // 2
-    rows, depth = hidden_ref.shape
+def core_parity(place_ref, other):
+    return 1 - place_ref[0] % 2 if other else place_ref[0] % 2
+
+
+def heads_kernel(joins, place_ref, hidden_ref, qkv_ref, *refs):
+    arrived_ref, out_ref = refs if joins else (None, refs[0])
+    parity = core_parity(place_ref, not joins)
+    rows = hidden_ref.shape[0]
     width = qkv_ref.shape[1] // 3
-    unit = fc1_ref.shape[2] // CHIPS // 2
+    unit = out_ref.shape[-1]
     share = rows // CHIPS // 2
     half = rows // 2
     pieces = width // unit
-    hidden = hidden_ref[...]
     tall = 2 * pieces * share
 
     def joined(values, start):
@@ -490,7 +623,7 @@
         query = joined(heads[:, piece * unit : (piece + 1) * unit], start)
         if joins:
             for chip in range(CHIPS):
-                head_ref[chip, tall + start : tall + start + half] = query
+                out_ref[chip, tall + start : tall + start + half] = query
         else:
             out_ref[start : start + half] = query
     base = pieces * half
@@ -500,52 +633,63 @@
             start = base + (chip * 2 * pieces + piece) * share
             value = joined(heads[chip * share : (chip + 1) * share, column : column + unit], start)
             if joins:
-                head_ref[chip, piece * share : (piece + 1) * share] = value
+                out_ref[chip, piece * share : (piece + 1) * share] = value
             else:
                 out_ref[start : start + share] = value
-    base = base + CHIPS * tall
+
+
+def project_heads(place, hidden, weights_qkv, unit, arrived=None):
+    rows = hidden.shape[0]
+    pieces = weights_qkv.shape[1] // 3 // unit
+    tall = 2 * pieces * (rows // CHIPS // 2)
+    common = pieces * (rows // 2)
+    extra = [] if arrived is None else [arrived]
+    shape = (common + CHIPS * tall, unit) if arrived is None else (CHIPS, tall + common, unit)
+    return pl.pallas_call(
+        functools.partial(heads_kernel, arrived is not None),
+        out_shape=jax.ShapeDtypeStruct(shape, jnp.bfloat16),
+        in_specs=[whole(pltpu.SMEM)] + [whole()] * (2 + len(extra)),
+        out_specs=whole(),
+        compiler_params=compiler_params(24),
+        name="project_heads",
+    )(in_hbm(place), hidden, weights_qkv, *extra)
+
+
+def units_kernel(joins, place_ref, hidden_ref, fc1_ref, *refs):
+    arrived_ref, out_refs = (refs[0], refs[1:]) if joins else (None, refs)
+    parity = core_parity(place_ref, not joins)
+    here = place_ref[0] // 2
+    unit = fc1_ref.shape[2] // CHIPS // 2
+    hidden = hidden_ref[...]
     for distance in range(CHIPS):
         target = 2 * (here ^ distance) + parity
         columns = pl.ds(pl.multiple_of(target * unit, unit), unit)
-        start = base + distance * rows
-        pre = joined(jnp.dot(hidden, fc1_ref[0, :, columns], preferred_element_type=jnp.float32), start)
+        pre = jnp.dot(hidden, fc1_ref[0, :, columns], preferred_element_type=jnp.float32)
         if joins:
-            unit_refs[distance][...] = pre
+            pre = pre + arrived_ref[distance].astype(jnp.float32)
+            out_refs[distance][...] = pre.astype(jnp.bfloat16)
         else:
-            out_ref[start : start + rows] = pre
-
-
-def project(place, hidden, weights_qkv, w_fc1, layer_index, arrived=None):
+            out_refs[0][distance] = pre.astype(jnp.bfloat16)
+
+
+def project_units(place, hidden, w_fc1, layer_index, arrived=None):
     rows = hidden.shape[0]
     unit = w_fc1.shape[2] // CHIPS // 2
-    pieces = weights_qkv.shape[1] // 3 // unit
-    tall = 2 * pieces * (rows // CHIPS // 2)
-    common = pieces * (rows // 2)
-
-    def result(*shape):
-        return jax.ShapeDtypeStruct(shape, jnp.bfloat16)
-
+    extra = [] if arrived is None else [arrived]
     if arrived is None:
-        extra = []
-        out_shape = result(common + CHIPS * (tall + rows), unit)
+        out_shape = jax.ShapeDtypeStruct((CHIPS, rows, unit), jnp.bfloat16)
     else:
-        extra = [arrived]
-        out_shape = (result(CHIPS, tall + common, unit),) + (result(rows, unit),) * CHIPS
-    return pl.pallas_call(
-        functools.partial(project_kernel, arrived is not None),
+        out_shape = (jax.ShapeDtypeStruct((rows, unit), jnp.bfloat16),) * CHIPS
+    return pl.pallas_call(
+        functools.partial(units_kernel, arrived is not None),
         grid=(1,),
         out_shape=out_shape,
-        in_specs=[
-            whole(pltpu.SMEM),
-            same_block(hidden.shape),
-            same_block(weights_qkv.shape),
-            layer_block(layer_index, w_fc1.shape[1:]),
-        ]
+        in_specs=[whole(pltpu.SMEM), same_block(hidden.shape), layer_block(layer_index, w_fc1.shape[1:])]
         + [same_block(values.shape) for values in extra],
         out_specs=jax.tree.map(lambda leaf: same_block(leaf.shape), out_shape),
-        compiler_params=compiler_params(),
-        name="project",
-    )(place, hidden, weights_qkv, w_fc1, *extra)
+        compiler_params=compiler_params(24),
+        name="project_units",
+    )(in_hbm(place), hidden, w_fc1, *extra)
 
 
 def activate_kernel(place_ref, part_ref, table_ref, query_ref, key_ref, value_ref):
@@ -591,7 +735,7 @@
         out_specs=(whole(),) * 3,
         compiler_params=compiler_params(16),
         name="activate",
-    )(place, parts, tables)
+    )(in_hbm(place), parts, tables)
 
 
 def rotary_tables(positions, width):
@@ -763,13 +907,15 @@
         ],
         compiler_params=compiler_params(24),
         name="attend",
-    )(place, visits, query, far_query, new_key, new_value, k_cache, v_cache)
+    )(in_hbm(place), in_hbm(visits), query, far_query, new_key, new_value, in_hbm(k_cache), in_hbm(v_cache))
 
 
 def update_kernel(
-    layer_index, other, place_ref, part_ref, bias_ref, out_weight_ref, fc2_ref, *refs
+    layer_index, other, tp_count, has_start, place_ref, part_ref, bias_ref, out_weight_ref, fc2_ref, *refs
 ):
     *unit_refs, out_ref, scale_ref = refs
+    if has_start:
+        *unit_refs, start_ref = unit_refs
     seq_index = place_ref[0]
     parity = 1 - seq_index % 2 if other else seq_index % 2
     sources, tall, lanes = part_ref.shape
@@ -807,25 +953,36 @@
     bias = bias_ref[
         layer_index : layer_index + 1, pl.ds(pl.multiple_of(seq_index * unit, unit), unit)
     ]
-    hidden = []
+    hidden, started = [], []
     for piece in range(CHIPS):
         rows = pl.ds(pl.multiple_of((2 * piece + parity) * share, share), share)
         pre = functools.reduce(jnp.add, [ref[rows, :].astype(jnp.float32) for ref in unit_refs])
         hidden.append(jax.nn.gelu(pre + bias, approximate=True).astype(jnp.bfloat16))
-    out_ref[...] = (
-        jnp.dot(attended, out_weight_ref[0], preferred_element_type=jnp.float32)
-        + jnp.dot(jnp.concatenate(hidden, axis=0), fc2_ref[0], preferred_element_type=jnp.float32)
-    ).astype(jnp.bfloat16)
-
-
-def update(place, parts, units, b_fc1, w_out, w_fc2, layer_index, other):
+        if has_start:
+            started.append(start_ref[rows, :].astype(jnp.float32))
+    change = jnp.dot(attended, out_weight_ref[0], preferred_element_type=jnp.float32) + jnp.dot(
+        jnp.concatenate(hidden, axis=0), fc2_ref[0], preferred_element_type=jnp.float32
+    )
+    if not has_start:
+        out_ref[...] = change.astype(out_ref.dtype)
+        return
+    started = jnp.concatenate(started, axis=0)
+    for column in range(0, change.shape[1], unit):
+        here = (seq_index * unit == column) & (place_ref[1] % tp_count == 0)
+        out_ref[:, column : column + unit] = (
+            change[:, column : column + unit] + jnp.where(here, started, 0.0)
+        ).astype(out_ref.dtype)
+
+
+def update(place, parts, units, start, b_fc1, w_out, w_fc2, layer_index, other, tp_count):
     rows = units[0].shape[0] // 2
     width = w_out.shape[2]
     lanes = parts.shape[2]
-    return pl.pallas_call(
-        functools.partial(update_kernel, layer_index, other),
+    extra = list(units) + ([] if start is None else [start])
+    return pl.pallas_call(
+        functools.partial(update_kernel, layer_index, other, tp_count, start is not None),
         grid=(1,),
-        out_shape=jax.ShapeDtypeStruct((rows, width), jnp.bfloat16),
+        out_shape=jax.ShapeDtypeStruct((rows, width), jnp.bfloat16 if other else jnp.float32),
         in_specs=[
             whole(pltpu.SMEM),
             same_block(parts.shape),
@@ -833,12 +990,12 @@
             layer_block(layer_index, w_out.shape[1:]),
             layer_block(layer_index, w_fc2.shape[1:]),
         ]
-        + [same_block(units[0].shape)] * len(units),
+        + [same_block(units[0].shape)] * len(extra),
         out_specs=same_block((rows, width)),
         scratch_shapes=[pltpu.VMEM((lanes, lanes), jnp.float32)],
         compiler_params=compiler_params(),
         name="update",
-    )(place, parts, b_fc1, w_out, w_fc2, *units)
+    )(in_hbm(place), parts, b_fc1, w_out, w_fc2, *extra)
 
 
 def per_device(
@@ -857,6 +1014,7 @@
     mine = rows // devices
     width = embedding.shape[1]
     width_local = k_cache.shape[2]
+    unit = w_fc2.shape[1]
     same_core = [[s * tp_count + p for s in range(c, seq_count, 2) for p in range(tp_count)] for c in range(2)]
     same_core_seq = [list(range(c, seq_count, 2)) for c in range(2)]
 
@@ -867,20 +1025,31 @@
     def to_chips(parts):
         return lax.all_to_all(parts, "seq", 0, 0, axis_index_groups=same_core_seq)
 
-    near, far = embed(place, token_ids, group_of, embedding)
-    parts = to_owners(near + swap_cores(far, seq_count))
+    def from_tp(part):
+        return [part] + [
+            lax.ppermute(part, "tp", [(i, i ^ k) for i in range(tp_count)]) for k in range(1, tp_count)
+        ]
+
+    near, far, own = embed(place, token_ids, group_of, embedding, unit)
+    parts = join(near, swap_cores(far, seq_count), own)
+    gathered = gather(to_chips(parts))
+    gathered, group_of = lax.optimization_barrier((gathered, group_of))
     rank, positions, visits = order_requests(group_of, prefix_len, tail_len, block_map, new_tokens)
     own_positions = lax.dynamic_index_in_dim(positions.reshape(CHIPS, 2, share), core, 1, keepdims=False)
     tables = rotary_tables(own_positions.reshape(-1), 2 * HEAD_DIM)
-    parts, tables, visits = lax.optimization_barrier((parts, tables, visits))
+    weights_qkv = w_qkv[0].reshape(w_qkv.shape[1], -1)
+    start, hidden = first_hidden(place, from_tp(gathered), ln_gain, ln_bias)
     state = None
     for layer_index in range(LAYERS):
-        weights_qkv = w_qkv[layer_index].reshape(w_qkv.shape[1], -1)
-        state, cut = norm_rows(parts, state, ln_gain, ln_bias, layer_index, devices, tp_count)
-        hidden = lax.all_to_all(cut, ("seq", "tp"), 0, 0).reshape(rows, -1)
-        arriving = swap_cores(project(place, hidden, weights_qkv, w_fc1, layer_index), seq_count)
-        heads, *units = project(place, hidden, weights_qkv, w_fc1, layer_index, arriving)
-        query, new_key, new_value = activate(place, to_chips(heads), tables, width_local)
+        if layer_index:
+            weights_qkv = w_qkv[layer_index].reshape(w_qkv.shape[1], -1)
+            state, cut = norm_rows(parts, state, ln_gain, ln_bias, layer_index, devices, tp_count)
+            hidden = lax.all_to_all(cut, ("seq", "tp"), 0, 0).reshape(rows, -1)
+        arriving = swap_cores(project_heads(place, hidden, weights_qkv, unit), seq_count)
+        heads = to_chips(project_heads(place, hidden, weights_qkv, unit, arriving))
+        arriving = swap_cores(project_units(place, hidden, w_fc1, layer_index), seq_count)
+        units = project_units(place, hidden, w_fc1, layer_index, arriving)
+        query, new_key, new_value = activate(place, heads, tables, width_local)
         query, *units = lax.optimization_barrier((query, *units))
         units = units[:1] + [
             lax.ppermute(units[k], "seq", [(i, i ^ (2 * k)) for i in range(seq_count)])
@@ -890,16 +1059,18 @@
             place, visits, query, swap_cores(query, seq_count), new_key, new_value,
             k_cache, v_cache, layer_index, new_tokens, groups,
         )
+        parts, *units = lax.optimization_barrier((parts, *units))
         parts = lax.all_to_all(parts, "seq", 0, 0)
-        arriving = swap_cores(update(place, parts, units, b_fc1, w_out, w_fc2, layer_index, True), seq_count)
-        half = update(place, parts, units, b_fc1, w_out, w_fc2, layer_index, False) + arriving
+        arriving, half = (
+            update(place, parts, units, start, b_fc1, w_out, w_fc2, layer_index, other, tp_count)
+            for other in (True, False)
+        )
+        half = (half + swap_cores(arriving, seq_count).astype(jnp.float32)).astype(jnp.bfloat16)
+        start = None
         if layer_index < LAYERS - 1:
             parts = to_owners(half)
-    last = gather_rows(place, to_chips(half.reshape(CHIPS, share, width)), state, tp_count)
-    last = last.astype(jnp.bfloat16)
-    last = [last] + [
-        lax.ppermute(last, "tp", [(i, i ^ k) for i in range(tp_count)]) for k in range(1, tp_count)
-    ]
+    last = last_parts(place, to_chips(half.reshape(CHIPS, share, width)), state, tp_count)
+    last = from_tp(last.astype(jnp.bfloat16))
     last = to_chips(last_rows(last)).reshape(rows // 2, width)
     arriving = swap_cores(last, seq_count)
     wanted = (rank[:, None] * new_tokens + jnp.arange(new_tokens, dtype=jnp.int32)[None, :]).reshape(-1)

time: 216 us -> 204 us (0.944)
  waiting for transfers between devices: 61.3 us -> 44.6 us
  Pallas kernels: 33.5 us -> 41.6 us
  local copies, waits for them, and re-layouts: 12.9 us -> 17.3 us
  blocking collectives: 69.3 us -> 66.6 us
  starting transfers between devices: 32.9 us -> 30.5 us
    all_to_all x4 -> x2, blocking collectives: 49.8 us -> 26 us  [to_chips(): return lax.all_to_all(parts, 'seq', 0, 0, axis_index_groups=same_core_seq)]
    all_to_all x0 -> x2, blocking collectives: none -> 20.4 us  [per_device(): parts = lax.all_to_all(parts, 'seq', 0, 0)]
    ppermute x6, waiting for transfers between devices: 18.4 us -> 0.84 us  [per_device(): lax.ppermute(units[k], 'seq', [(i, i ^ 2 * k) for i in range(seq_count)])]
    ppermute x3 -> x6, waiting for transfers between devices: 7.86 us -> 17 us  [from_tp(): lax.ppermute(part, 'tp', [(i, i ^ k) for i in range(tp_count)])]
    pallas_call x10 -> x17, Pallas kernels: 15.6 us -> 23.4 us  [the longest x1 5.94 us: embed(): pl.pallas_call(embed_kernel, out_shape=(jax.ShapeDtypeStruct((CHIPS, rows...]
    all_to_all x2 -> x1, waiting for transfers between devices: 10.4 us -> 4.49 us  [per_device(): hidden = lax.all_to_all(cut, ('seq', 'tp'), 0, 0).reshape(rows, -1)]
    unnamed x68 -> x48, local copies, waits for them, and re-layouts: 6.49 us -> 12.1 us
    all_to_all x3, starting transfers between devices: 15.1 us -> 10.5 us  [to_chips(): return lax.all_to_all(parts, 'seq', 0, 0, axis_index_groups=same_core_seq)]
  transfers between devices with their start and end apart: 22 -> 26, of which waited for: 16 -> 17; matrix products, arithmetic and copies ran while one was open for 4% -> 3% of each run, Pallas kernels for 2% -> 11%
where the time goes in v3:
time: 204 us; the launch traced here: 203 us
  blocking collectives  66.6 us (33%)
  waiting for transfers between devices  44.6 us (22%)
  Pallas kernels  41.6 us (20%)
  starting transfers between devices  30.5 us (15%)
  local copies, waits for them, and re-layouts  17.3 us (8%)
    all_to_all x2, blocking collectives, to_chips(): return lax.all_to_all(parts, 'seq', 0, 0, axis_index_groups=same_core_seq)  26 us
    all_to_all x2, blocking collectives, per_device(): parts = lax.all_to_all(parts, 'seq', 0, 0)  20.4 us
    all_to_all x1, blocking collectives, to_owners(): lax.all_to_all(parts, ('seq', 'tp'), 0, 0, axis_index_groups=same_core)  20.1 us
    ppermute x6, waiting for transfers between devices, from_tp(): lax.ppermute(part, 'tp', [(i, i ^ k) for i in range(tp_count)])  17 us
    all_to_all x3, waiting for transfers between devices, to_chips(): return lax.all_to_all(parts, 'seq', 0, 0, axis_index_groups=same_core_seq)  12.8 us
    pallas_call x2, Pallas kernels, attend(): pl.pallas_call(functools.partial(attend_kernel, layer_index, new_tokens),...  12.1 us
    unnamed x48, local copies, waits for them, and re-layouts  12.1 us
    all_to_all x3, starting transfers between devices, to_chips(): return lax.all_to_all(parts, 'seq', 0, 0, axis_index_groups=same_core_seq)  10.5 us
  transfers between devices with their start and end apart: 26, of which 17 were waited for; matrix products, arithmetic and copies ran while one was open for 3% of the time, Pallas kernels for 11%

profile of v3, /device:TPU:0, one launch (start us, length us, event | category | flops | bytes accessed | tf_op | source)
XLA Modules:
  0.0 203.4 jit_solution(770913351785843171)
XLA Ops:
  0.6 5.9 %embed.1 = (bf16[4,256,256]{2,1,0:T(8,128)(2,1)S(1)}, bf16[1040,256]{1,0:T(8,128)(2,1)}, f32[8,256]{1,0:T(8,128)S(1)}) custom-call(s32[2]{0:T(128)} %pad_add_fusion.place_ref, s32[4,64]{1,0:T(4,128)} %bitcast.23, s32[1,64]{1,0:T(1,128)} %bitcast.24, bf16[1600,2048]{1,0:T(8,128)(2,1)} %table_hbm.1), custom_call_target="tpu_custom_call" | custom-call | tf_op jit(solution)/shard_map/embed/pallas_call | solution.py:416
  7.1 1.8 collective-permute-done.far_ref
  9.8 14.5 %all_to_all.45.part_ref = bf16[4,272,256]{2,1,0:T(8,128)(2,1)S(1)} all-to-all(bf16[4,272,256]{2,1,0:T(8,128)(2,1)} %join.1), channel_id=1, replica_groups={{0,8,16,24},{4,12,20,28},{1,9,17,25},{5,13,21,29},{2,10,18,26},{6,14,22..., dimensions={0} | all-to-all | bytes 1114112 | tf_op jit(solution)/shard_map/all_to_all | solution.py:1026
  24.4 3.7 %collective-permute-start.3 = (bf16[272,256]{1,0:T(8,128)(2,1)S(1)}, bf16[272,256]{1,0:T(8,128)(2,1)S(1)}, u32[]{:S(2)}, u32[]{:S(2)}) collective-permute-start(bf16[272,256]{1,0:T(8,128)(2,1)S(1)} %gather.1.a_ref), channel_id=1, source_target_pairs={{0,3},{1,2},{2,1},{3,0},{4,7},{5,6},{6,5},{7,4},{8,11},{9,10},{10,... | collective-permute-start | bytes 417800 | tf_op jit(solution)/shard_map/ppermute | solution.py:1030
  30.4 2.4 %collective-permute-done.3.d_ref = bf16[272,256]{1,0:T(8,128)(2,1)S(1)} collective-permute-done((bf16[272,256]{1,0:T(8,128)(2,1)S(1)}, bf16[272,256]{1,0:T(8,128)(2,1)S(1)}, u32[]{:S(2)}, u32[]{:S(2)}) %collective-permute-start.3) | collective-permute-done | bytes 139296 | tf_op jit(solution)/shard_map/ppermute | solution.py:1030
  32.8 6.0 %collective-permute-done.2.c_ref = bf16[272,256]{1,0:T(8,128)(2,1)S(1)} collective-permute-done((bf16[272,256]{1,0:T(8,128)(2,1)S(1)}, bf16[272,256]{1,0:T(8,128)(2,1)S(1)}, u32[]{:S(2)}, u32[]{:S(2)}) %collective-permute-start.2) | collective-permute-done | bytes 139296 | tf_op jit(solution)/shard_map/ppermute | solution.py:1030
  40.7 1.7 collective-permute-done.4.refs_0_
  44.3 3.5 %all-to-all-start.1 = ((bf16[4,384,256]{2,1,0:T(8,128)(2,1)}), bf16[4,384,256]{2,1,0:T(8,128)(2,1)S(1)}, u32[]{:S(2)}, u32[]{:S(2)}) async-start(bf16[4,384,256]{2,1,0:T(8,128)(2,1)} %copy-done.4), calls=%async_computation.1 | async-start | bytes 1572864 | tf_op jit(solution)/shard_map/all_to_all | solution.py:1026
  47.8 1.8 project_units.4
  49.8 2.5 %order_requests.1 = (s32[64]{0:T(128)}, s32[256]{0:T(256)}, s32[64]{0:T(128)}) custom-call(s32[64]{0:T(128)} %group_ref, s32[8]{0:T(128)} %prefix_ref.1, s32[64]{0:T(128)} %tail_ref.1, s32[2,16]{1,0:T(2,128)} %bitcast.25), custom_call_target="tpu_custom_call" | custom-call | tf_op jit(solution)/shard_map/order_requests/pallas_call | solution.py:303
  56.9 2.3 %all-to-all-done.1.part_ref = bf16[4,384,256]{2,1,0:T(8,128)(2,1)S(1)} async-done(((bf16[4,384,256]{2,1,0:T(8,128)(2,1)}), bf16[4,384,256]{2,1,0:T(8,128)(2,1)S(1)}, u32[]{:S(2)}, u32[]{:S(2)}) %all-to-all-start.1) | async-done | bytes 786464 | tf_op jit(solution)/shard_map/all_to_all | solution.py:1026
  63.7 6.1 %attend.2 = bf16[8,160,128]{2,1,0:T(8,128)(2,1)S(1)} custom-call(s32[2]{0:T(128)} %pad_add_fusion.place_ref, s32[64]{0:T(128)} %get-tuple-element.56.visit_ref, bf16[128,512]{1,0:T(8,128)(2,1)S(1)} %get-tuple-element.65.query_ref, bf16[128,512]{1,0:T(8,128)(2,1)S(1)} %collective-permute-done.6.far_query_ref, ...), custom_call_target="tpu_custom_call" | custom-call | tf_op jit(solution)/shard_map/attend/pallas_call | solution.py:893
  70.2 10.2 %all_to_all.46.part_ref = bf16[8,160,128]{2,1,0:T(8,128)(2,1)S(1)} all-to-all(bf16[8,160,128]{2,1,0:T(8,128)(2,1)S(1)} %attend.2), channel_id=1, replica_groups=mesh['seq'=8,'tp'=4] {'seq'}, dimensions={0} | all-to-all | bytes 655360 | tf_op jit(solution)/shard_map/all_to_all | solution.py:1063
  84.0 20.1 %all_to_all.47.refs_0_ = bf16[16,8,2048]{2,1,0:T(8,128)(2,1)S(1)} all-to-all(bf16[16,8,2048]{2,1,0:T(8,128)(2,1)S(1)} %fusion), channel_id=1, replica_groups={{0,1,2,3,8,9,10,11,16,17,18,19,24,25,26,27},{4,5,6,7,12,13,14,15,20,21,..., dimensions={0} | all-to-all | bytes 1048576 | tf_op jit(solution)/shard_map/all_to_all | solution.py:1023
  105.7 2.8 %all-to-all-start.4 = ((bf16[32,8,256]{2,1,0:T(8,128)(2,1)}), bf16[32,8,256]{2,1,0:T(8,128)(2,1)S(1)}, u32[]{:S(2)}, u32[]{:S(2)}) async-start(bf16[32,8,256]{2,1,0:T(8,128)(2,1)} %get-tuple-element.78), calls=%async_computation.4 | async-start | bytes 262144 | tf_op jit(solution)/shard_map/all_to_all | solution.py:1047
  108.5 2.3 %copy.25 = bf16[1,256,3,512]{1,3,2,0:T(8,128)(2,1)} copy(bf16[1,256,3,512]{3,1,2,0:T(8,128)(2,1)} %get-tuple-element.97) | data formatting | bytes 1572864
  112.2 4.5 %all-to-all-done.4 = bf16[32,8,256]{2,1,0:T(8,128)(2,1)S(1)} async-done(((bf16[32,8,256]{2,1,0:T(8,128)(2,1)}), bf16[32,8,256]{2,1,0:T(8,128)(2,1)S(1)}, u32[]{:S(2)}, u32[]{:S(2)}) %all-to-all-start.4) | async-done | bytes 131104 | tf_op jit(solution)/shard_map/all_to_all | solution.py:1047
  117.7 1.7 collective-permute-done.11.refs_0_
  121.2 3.5 %all-to-all-start.5 = ((bf16[4,384,256]{2,1,0:T(8,128)(2,1)}), bf16[4,384,256]{2,1,0:T(8,128)(2,1)S(1)}, u32[]{:S(2)}, u32[]{:S(2)}) async-start(bf16[4,384,256]{2,1,0:T(8,128)(2,1)} %copy-done.5), calls=%async_computation.5 | async-start | bytes 1572864 | tf_op jit(solution)/shard_map/all_to_all | solution.py:1026
  124.7 1.6 copy-done.2
  127.5 1.8 collective-permute-done.12.refs_0_
  132.9 3.2 %all-to-all-done.5.part_ref = bf16[4,384,256]{2,1,0:T(8,128)(2,1)S(1)} async-done(((bf16[4,384,256]{2,1,0:T(8,128)(2,1)}), bf16[4,384,256]{2,1,0:T(8,128)(2,1)S(1)}, u32[]{:S(2)}, u32[]{:S(2)}) %all-to-all-start.5) | async-done | bytes 786464 | tf_op jit(solution)/shard_map/all_to_all | solution.py:1026
  141.6 6.1 %attend.3 = bf16[8,160,128]{2,1,0:T(8,128)(2,1)S(1)} custom-call(s32[2]{0:T(128)} %pad_add_fusion.place_ref, s32[64]{0:T(128)} %get-tuple-element.56.visit_ref, bf16[128,512]{1,0:T(8,128)(2,1)S(1)} %get-tuple-element.84.query_ref, bf16[128,512]{1,0:T(8,128)(2,1)S(1)} %collective-permute-done.13.far_query_ref, ...), custom_call_target="tpu_custom_call" | custom-call | tf_op jit(solution)/shard_map/attend/pallas_call | solution.py:893
  148.1 10.2 %all_to_all.48.part_ref = bf16[8,160,128]{2,1,0:T(8,128)(2,1)S(1)} all-to-all(bf16[8,160,128]{2,1,0:T(8,128)(2,1)S(1)} %attend.3), channel_id=1, replica_groups=mesh['seq'=8,'tp'=4] {'seq'}, dimensions={0} | all-to-all | bytes 655360 | tf_op jit(solution)/shard_map/all_to_all | solution.py:1063
  161.9 11.5 %all_to_all.49.part_ref = bf16[4,32,2048]{2,1,0:T(8,128)(2,1)S(1)} all-to-all(bf16[4,32,2048]{2,1,0:T(8,128)(2,1)S(1)} %bitcast.20), channel_id=1, replica_groups={{0,8,16,24},{4,12,20,28},{1,9,17,25},{5,13,21,29},{2,10,18,26},{6,14,22..., dimensions={0} | all-to-all | bytes 1048576 | tf_op jit(solution)/shard_map/all_to_all | solution.py:1026
  175.9 2.8 %collective-permute-start.18 = (bf16[32,2048]{1,0:T(8,128)(2,1)S(1)}, bf16[32,2048]{1,0:T(8,128)(2,1)S(1)}, u32[]{:S(2)}, u32[]{:S(2)}) collective-permute-start(bf16[32,2048]{1,0:T(8,128)(2,1)S(1)} %convert_element_type.42.a_ref), channel_id=1, source_target_pairs={{0,1},{1,0},{2,3},{3,2},{4,5},{5,4},{6,7},{7,6},{8,9},{9,8},{10,11... | collective-permute-start | bytes 393224 | tf_op jit(solution)/shard_map/ppermute | solution.py:1030
  178.6 3.8 %collective-permute-done.20.d_ref = bf16[32,2048]{1,0:T(8,128)(2,1)S(1)} collective-permute-done((bf16[32,2048]{1,0:T(8,128)(2,1)S(1)}, bf16[32,2048]{1,0:T(8,128)(2,1)S(1)}, u32[]{:S(2)}, u32[]{:S(2)}) %collective-permute-start.20) | collective-permute-done | bytes 131104 | tf_op jit(solution)/shard_map/ppermute | solution.py:1030
  182.5 4.8 %collective-permute-done.19.c_ref = bf16[32,2048]{1,0:T(8,128)(2,1)S(1)} collective-permute-done((bf16[32,2048]{1,0:T(8,128)(2,1)S(1)}, bf16[32,2048]{1,0:T(8,128)(2,1)S(1)}, u32[]{:S(2)}, u32[]{:S(2)}) %collective-permute-start.19) | collective-permute-done | bytes 131104 | tf_op jit(solution)/shard_map/ppermute | solution.py:1030
  188.1 3.5 %all-to-all-start.8 = ((bf16[4,32,2048]{2,1,0:T(8,128)(2,1)}), bf16[4,32,2048]{2,1,0:T(8,128)(2,1)S(1)}, u32[]{:S(2)}, u32[]{:S(2)}) async-start(bf16[4,32,2048]{2,1,0:T(8,128)(2,1)} %last_rows.1), calls=%async_computation.8 | async-start | bytes 1048576 | tf_op jit(solution)/shard_map/all_to_all | solution.py:1026
  191.6 7.3 %all-to-all-done.8 = bf16[4,32,2048]{2,1,0:T(8,128)(2,1)S(1)} async-done(((bf16[4,32,2048]{2,1,0:T(8,128)(2,1)}), bf16[4,32,2048]{2,1,0:T(8,128)(2,1)S(1)}, u32[]{:S(2)}, u32[]{:S(2)}) %all-to-all-start.8) | async-done | bytes 524320 | tf_op jit(solution)/shard_map/all_to_all | solution.py:1026
  199.1 1.7 collective-permute-done.21
  201.7 1.6 reshape.329
  (120 shorter events, 45.8 us)
Async XLA Ops:
  6.5 22.3 %copy-start.21 = (bf16[2,256,3,512]{3,1,2,0:T(8,128)(2,1)S(1)}, bf16[2,256,3,512]{3,1,2,0:T(8,128)(2,1)}, u32[]{:S(2)}) copy-start(bf16[2,256,3,512]{3,1,2,0:T(8,128)(2,1)} %param.25) | copy-start | bytes 4718596
  6.5 2.3 %collective-permute-start = (bf16[1040,256]{1,0:T(8,128)(2,1)}, bf16[1040,256]{1,0:T(8,128)(2,1)S(1)}, u32[]{:S(2)}, u32[]{:S(2)}) collective-permute-start(bf16[1040,256]{1,0:T(8,128)(2,1)} %get-tuple-element.52), channel_id=1, source_target_pairs={{0,4},{4,0},{8,12},{12,8},{16,20},{20,16},{24,28},{28,24},{1,5},{5... | collective-permute-start | bytes 1597448 | tf_op jit(solution)/shard_map/ppermute | solution.py:239
  24.4 8.5 %collective-permute-start.3 = (bf16[272,256]{1,0:T(8,128)(2,1)S(1)}, bf16[272,256]{1,0:T(8,128)(2,1)S(1)}, u32[]{:S(2)}, u32[]{:S(2)}) collective-permute-start(bf16[272,256]{1,0:T(8,128)(2,1)S(1)} %gather.1.a_ref), channel_id=1, source_target_pairs={{0,3},{1,2},{2,1},{3,0},{4,7},{5,6},{6,5},{7,4},{8,11},{9,10},{10,... | collective-permute-start | bytes 417800 | tf_op jit(solution)/shard_map/ppermute | solution.py:1030
  28.0 10.8 %collective-permute-start.2 = (bf16[272,256]{1,0:T(8,128)(2,1)S(1)}, bf16[272,256]{1,0:T(8,128)(2,1)S(1)}, u32[]{:S(2)}, u32[]{:S(2)}) collective-permute-start(bf16[272,256]{1,0:T(8,128)(2,1)S(1)} %gather.1.a_ref), channel_id=1, source_target_pairs={{0,2},{1,3},{2,0},{3,1},{4,6},{5,7},{6,4},{7,5},{8,10},{9,11},{10,... | collective-permute-start | bytes 417800 | tf_op jit(solution)/shard_map/ppermute | solution.py:1030
  28.0 10.8 %collective-permute-start.1 = (bf16[272,256]{1,0:T(8,128)(2,1)S(1)}, bf16[272,256]{1,0:T(8,128)(2,1)S(1)}, u32[]{:S(2)}, u32[]{:S(2)}) collective-permute-start(bf16[272,256]{1,0:T(8,128)(2,1)S(1)} %gather.1.a_ref), channel_id=1, source_target_pairs={{0,1},{1,0},{2,3},{3,2},{4,5},{5,4},{6,7},{7,6},{8,9},{9,8},{10,11... | collective-permute-start | bytes 417800 | tf_op jit(solution)/shard_map/ppermute | solution.py:1030
  40.6 1.8 collective-permute-start.4
  44.3 14.9 %all-to-all-start.1 = ((bf16[4,384,256]{2,1,0:T(8,128)(2,1)}), bf16[4,384,256]{2,1,0:T(8,128)(2,1)S(1)}, u32[]{:S(2)}, u32[]{:S(2)}) async-start(bf16[4,384,256]{2,1,0:T(8,128)(2,1)} %copy-done.4), calls=%async_computation.1 | async-start | bytes 1572864 | tf_op jit(solution)/shard_map/all_to_all | solution.py:1026
  49.6 3.9 %collective-permute-start.5 = (bf16[4,256,256]{2,1,0:T(8,128)(2,1)}, bf16[4,256,256]{2,1,0:T(8,128)(2,1)}, u32[]{:S(2)}, u32[]{:S(2)}) collective-permute-start(bf16[4,256,256]{2,1,0:T(8,128)(2,1)} %project_units.4), channel_id=1, source_target_pairs={{0,4},{4,0},{8,12},{12,8},{16,20},{20,16},{24,28},{28,24},{1,5},{5... | collective-permute-start | bytes 1572872 | tf_op jit(solution)/shard_map/ppermute | solution.py:239
  60.1 3.6 %collective-permute-start.6 = (bf16[128,512]{1,0:T(8,128)(2,1)S(1)}, bf16[128,512]{1,0:T(8,128)(2,1)S(1)}, u32[]{:S(2)}, u32[]{:S(2)}) collective-permute-start(bf16[128,512]{1,0:T(8,128)(2,1)S(1)} %get-tuple-element.65.query_ref), channel_id=1, source_target_pairs={{0,4},{4,0},{8,12},{12,8},{16,20},{20,16},{24,28},{28,24},{1,5},{5... | collective-permute-start | bytes 393224 | tf_op jit(solution)/shard_map/ppermute | solution.py:239
  60.1 9.7 %collective-permute-start.7 = (bf16[256,256]{1,0:T(8,128)(2,1)}, bf16[256,256]{1,0:T(8,128)(2,1)S(1)}, u32[]{:S(2)}, u32[]{:S(2)}) collective-permute-start(bf16[256,256]{1,0:T(8,128)(2,1)} %copy-done.20), channel_id=1, source_target_pairs={{0,8},{4,12},{8,0},{12,4},{16,24},{20,28},{24,16},{28,20},{1,9},{5... | collective-permute-start | bytes 393224 | tf_op jit(solution)/shard_map/ppermute | solution.py:1055
  61.6 8.6 %collective-permute-start.8 = (bf16[256,256]{1,0:T(8,128)(2,1)}, bf16[256,256]{1,0:T(8,128)(2,1)S(1)}, u32[]{:S(2)}, u32[]{:S(2)}) collective-permute-start(bf16[256,256]{1,0:T(8,128)(2,1)} %copy-done.18), channel_id=1, source_target_pairs={{0,16},{4,20},{8,24},{12,28},{16,0},{20,4},{24,8},{28,12},{1,17},{... | collective-permute-start | bytes 393224 | tf_op jit(solution)/shard_map/ppermute | solution.py:1055
  62.2 8.0 %collective-permute-start.9 = (bf16[256,256]{1,0:T(8,128)(2,1)}, bf16[256,256]{1,0:T(8,128)(2,1)S(1)}, u32[]{:S(2)}, u32[]{:S(2)}) collective-permute-start(bf16[256,256]{1,0:T(8,128)(2,1)} %copy-done.16), channel_id=1, source_target_pairs={{0,24},{4,28},{8,16},{12,20},{16,8},{20,12},{24,0},{28,4},{1,25},{... | collective-permute-start | bytes 393224 | tf_op jit(solution)/shard_map/ppermute | solution.py:1055
  63.7 16.7 %copy-start = (bf16[2,256,2048]{2,1,0:T(8,128)(2,1)S(1)}, bf16[2,256,2048]{2,1,0:T(8,128)(2,1)}, u32[]{:S(2)}) copy-start(bf16[2,256,2048]{2,1,0:T(8,128)(2,1)} %fc2_ref.7) | copy-start | bytes 6291460
  63.7 16.7 %copy-start.3 = (bf16[2,64,2048]{2,1,0:T(8,128)(2,1)S(1)}, bf16[2,64,2048]{2,1,0:T(8,128)(2,1)}, u32[]{:S(2)}) copy-start(bf16[2,64,2048]{2,1,0:T(8,128)(2,1)} %out_weight_ref.7) | copy-start | bytes 1572868
  63.7 16.7 %copy-start.10 = (f32[2,2048]{1,0:T(2,128)S(1)}, f32[2,2048]{1,0:T(2,128)}, u32[]{:S(2)}) copy-start(f32[2,2048]{1,0:T(2,128)} %bias_ref.9) | copy-start | bytes 49156
  81.9 2.0 collective-permute-start.10
  105.7 11.0 %all-to-all-start.4 = ((bf16[32,8,256]{2,1,0:T(8,128)(2,1)}), bf16[32,8,256]{2,1,0:T(8,128)(2,1)S(1)}, u32[]{:S(2)}, u32[]{:S(2)}) async-start(bf16[32,8,256]{2,1,0:T(8,128)(2,1)} %get-tuple-element.78), calls=%async_computation.4 | async-start | bytes 262144 | tf_op jit(solution)/shard_map/all_to_all | solution.py:1047
  117.6 1.8 collective-permute-start.11
  121.2 14.9 %all-to-all-start.5 = ((bf16[4,384,256]{2,1,0:T(8,128)(2,1)}), bf16[4,384,256]{2,1,0:T(8,128)(2,1)S(1)}, u32[]{:S(2)}, u32[]{:S(2)}) async-start(bf16[4,384,256]{2,1,0:T(8,128)(2,1)} %copy-done.5), calls=%async_computation.5 | async-start | bytes 1572864 | tf_op jit(solution)/shard_map/all_to_all | solution.py:1026
  127.3 2.0 collective-permute-start.12
  137.9 3.6 %collective-permute-start.13 = (bf16[128,512]{1,0:T(8,128)(2,1)S(1)}, bf16[128,512]{1,0:T(8,128)(2,1)S(1)}, u32[]{:S(2)}, u32[]{:S(2)}) collective-permute-start(bf16[128,512]{1,0:T(8,128)(2,1)S(1)} %get-tuple-element.84.query_ref), channel_id=1, source_target_pairs={{0,4},{4,0},{8,12},{12,8},{16,20},{20,16},{24,28},{28,24},{1,5},{5... | collective-permute-start | bytes 393224 | tf_op jit(solution)/shard_map/ppermute | solution.py:239
  138.0 9.6 %collective-permute-start.14 = (bf16[256,256]{1,0:T(8,128)(2,1)}, bf16[256,256]{1,0:T(8,128)(2,1)S(1)}, u32[]{:S(2)}, u32[]{:S(2)}) collective-permute-start(bf16[256,256]{1,0:T(8,128)(2,1)} %copy-done.19), channel_id=1, source_target_pairs={{0,8},{4,12},{8,0},{12,4},{16,24},{20,28},{24,16},{28,20},{1,9},{5... | collective-permute-start | bytes 393224 | tf_op jit(solution)/shard_map/ppermute | solution.py:1055
  139.5 8.6 %collective-permute-start.15 = (bf16[256,256]{1,0:T(8,128)(2,1)}, bf16[256,256]{1,0:T(8,128)(2,1)S(1)}, u32[]{:S(2)}, u32[]{:S(2)}) collective-permute-start(bf16[256,256]{1,0:T(8,128)(2,1)} %copy-done.17), channel_id=1, source_target_pairs={{0,16},{4,20},{8,24},{12,28},{16,0},{20,4},{24,8},{28,12},{1,17},{... | collective-permute-start | bytes 393224 | tf_op jit(solution)/shard_map/ppermute | solution.py:1055
  140.1 8.0 %collective-permute-start.16 = (bf16[256,256]{1,0:T(8,128)(2,1)}, bf16[256,256]{1,0:T(8,128)(2,1)S(1)}, u32[]{:S(2)}, u32[]{:S(2)}) collective-permute-start(bf16[256,256]{1,0:T(8,128)(2,1)} %copy-done.15), channel_id=1, source_target_pairs={{0,24},{4,28},{8,16},{12,20},{16,8},{20,12},{24,0},{28,4},{1,25},{... | collective-permute-start | bytes 393224 | tf_op jit(solution)/shard_map/ppermute | solution.py:1055
  141.6 16.7 %copy-start.9 = (bf16[256,256]{1,0:T(8,128)(2,1)S(1)}, bf16[256,256]{1,0:T(8,128)(2,1)}, u32[]{:S(2)}) copy-start(bf16[256,256]{1,0:T(8,128)(2,1)} %copy-done.8) | copy-start | bytes 393220
  159.8 2.0 collective-permute-start.17
  161.9 37.0 %copy-start.22 = (s32[64]{0:T(128)S(1)}, s32[64]{0:T(128)}, u32[]{:S(2)}) copy-start(s32[64]{0:T(128)} %get-tuple-element.55) | copy-start | bytes 772
  174.2 8.3 %collective-permute-start.20 = (bf16[32,2048]{1,0:T(8,128)(2,1)S(1)}, bf16[32,2048]{1,0:T(8,128)(2,1)S(1)}, u32[]{:S(2)}, u32[]{:S(2)}) collective-permute-start(bf16[32,2048]{1,0:T(8,128)(2,1)S(1)} %convert_element_type.42.a_ref), channel_id=1, source_target_pairs={{0,3},{1,2},{2,1},{3,0},{4,7},{5,6},{6,5},{7,4},{8,11},{9,10},{10,... | collective-permute-start | bytes 393224 | tf_op jit(solution)/shard_map/ppermute | solution.py:1030
  175.4 11.8 %collective-permute-start.19 = (bf16[32,2048]{1,0:T(8,128)(2,1)S(1)}, bf16[32,2048]{1,0:T(8,128)(2,1)S(1)}, u32[]{:S(2)}, u32[]{:S(2)}) collective-permute-start(bf16[32,2048]{1,0:T(8,128)(2,1)S(1)} %convert_element_type.42.a_ref), channel_id=1, source_target_pairs={{0,2},{1,3},{2,0},{3,1},{4,6},{5,7},{6,4},{7,5},{8,10},{9,11},{10,... | collective-permute-start | bytes 393224 | tf_op jit(solution)/shard_map/ppermute | solution.py:1030
  175.9 11.4 %collective-permute-start.18 = (bf16[32,2048]{1,0:T(8,128)(2,1)S(1)}, bf16[32,2048]{1,0:T(8,128)(2,1)S(1)}, u32[]{:S(2)}, u32[]{:S(2)}) collective-permute-start(bf16[32,2048]{1,0:T(8,128)(2,1)S(1)} %convert_element_type.42.a_ref), channel_id=1, source_target_pairs={{0,1},{1,0},{2,3},{3,2},{4,5},{5,4},{6,7},{7,6},{8,9},{9,8},{10,11... | collective-permute-start | bytes 393224 | tf_op jit(solution)/shard_map/ppermute | solution.py:1030
  188.1 10.8 %all-to-all-start.8 = ((bf16[4,32,2048]{2,1,0:T(8,128)(2,1)}), bf16[4,32,2048]{2,1,0:T(8,128)(2,1)S(1)}, u32[]{:S(2)}, u32[]{:S(2)}) async-start(bf16[4,32,2048]{2,1,0:T(8,128)(2,1)} %last_rows.1), calls=%async_computation.8 | async-start | bytes 1048576 | tf_op jit(solution)/shard_map/all_to_all | solution.py:1026
  198.9 1.9 collective-permute-start.21
  (17 other events, 63.0 us)

commit v4 on v3

--- a/solution.py
+++ b/solution.py
@@ -362,11 +362,11 @@
 
 
 def embed_kernel(
-    place_ref, token_ref, group_ref, table_hbm, near_ref, far_ref, own_ref,
+    token_ref, group_ref, table_hbm, near_ref, far_ref, own_ref,
     table_ref, hot_ref, row_ref, semaphores,
 ):
-    core = place_ref[0] % 2
-    first = place_ref[1] * table_ref.shape[1]
+    core = lax.axis_index("seq") % 2
+    first = (lax.axis_index("seq") * lax.axis_size("tp") + lax.axis_index("tp")) * table_ref.shape[1]
     new_tokens, requests = token_ref.shape
     rows, unit = near_ref.shape[1:]
     copies = []
@@ -411,7 +411,7 @@
     far_ref[CHIPS * rows :] = row_sums([mean, scale])
 
 
-def embed(place, token_ids, group_of, embedding, unit):
+def embed(token_ids, group_of, embedding, unit):
     rows = token_ids.shape[0] * token_ids.shape[1]
     return pl.pallas_call(
         embed_kernel,
@@ -420,7 +420,7 @@
             pltpu.HBM((CHIPS * rows + 16, unit), jnp.bfloat16),
             jax.ShapeDtypeStruct((8, rows), jnp.float32),
         ),
-        in_specs=[whole(pltpu.SMEM), whole(), whole(), whole(pltpu.HBM)],
+        in_specs=[whole(), whole(), whole(pltpu.HBM)],
         out_specs=(whole(),) * 3,
         scratch_shapes=[
             pltpu.VMEM((CHIPS, embedding.shape[0], 2 * unit), jnp.bfloat16),
@@ -430,37 +430,55 @@
         ],
         compiler_params=compiler_params(24),
         name="embed",
-    )(in_hbm(place), in_hbm(token_ids.T), in_hbm(group_of[None, :]), in_hbm(embedding))
-
-
-def join_kernel(near_ref, far_ref, own_ref, out_ref):
+    )(in_hbm(token_ids.T), in_hbm(group_of[None, :]), in_hbm(embedding))
+
+
+def join_kernel(near_ref, far_ref, own_ref, out_ref, *refs):
+    *out_hbms, leave_ref, semaphores = refs
+    here = lax.axis_index("seq") // 2
     rows = near_ref.shape[1]
-    for chip in range(CHIPS):
-        far = far_ref[chip * rows : (chip + 1) * rows].astype(jnp.float32)
-        out_ref[chip, :rows] = (near_ref[chip].astype(jnp.float32) + far).astype(jnp.bfloat16)
     mean, scale = from_row_sums(far_ref[CHIPS * rows :])
     lines = row_sums([mean + own_ref[0:1, :], scale + own_ref[1:2, :]])
-    for chip in range(CHIPS):
-        out_ref[chip, rows:] = lines
+    leaving = []
+    for distance in reversed(range(CHIPS)):
+        chip = here ^ distance
+        far = far_ref[pl.ds(pl.multiple_of(chip * rows, rows), rows), :].astype(jnp.float32)
+        joined = (near_ref[chip].astype(jnp.float32) + far).astype(jnp.bfloat16)
+        if distance:
+            leave_ref[distance - 1, :rows] = joined
+            leave_ref[distance - 1, rows:] = lines
+            leaving.append(
+                pltpu.make_async_copy(
+                    leave_ref.at[distance - 1], out_hbms[distance - 1], semaphores.at[distance - 1]
+                )
+            )
+            leaving[-1].start()
+        else:
+            out_ref[:rows] = joined
+            out_ref[rows:] = lines
+    for copy in leaving:
+        copy.wait()
 
 
 def join(near, far, own):
     chips, rows, unit = near.shape
+    one = (rows + 16, unit)
     return pl.pallas_call(
         join_kernel,
-        out_shape=pltpu.HBM((chips, rows + 16, unit), jnp.bfloat16),
+        out_shape=(jax.ShapeDtypeStruct(one, jnp.bfloat16),) + (pltpu.HBM(one, jnp.bfloat16),) * (chips - 1),
         in_specs=[whole()] * 3,
-        out_specs=whole(),
+        out_specs=(whole(),) + (whole(pltpu.HBM),) * (chips - 1),
+        scratch_shapes=[pltpu.VMEM((chips - 1,) + one, jnp.bfloat16), pltpu.SemaphoreType.DMA((chips - 1,))],
         compiler_params=compiler_params(16),
         name="join",
     )(near, far, own)
 
 
-def gather_kernel(part_ref, out_ref):
-    rows = part_ref.shape[1] - 16
-    total = part_ref[0].astype(jnp.float32)
-    for chip in range(1, CHIPS):
-        total = total + part_ref[chip].astype(jnp.float32)
+def gather_kernel(a_ref, b_ref, c_ref, d_ref, out_ref):
+    rows = out_ref.shape[0] - 16
+    near = a_ref[...].astype(jnp.float32) + b_ref[...].astype(jnp.float32)
+    far = c_ref[...].astype(jnp.float32) + d_ref[...].astype(jnp.float32)
+    total = near + far
     out_ref[:rows] = total[:rows].astype(jnp.bfloat16)
     out_ref[rows:] = row_sums(from_row_sums(total[rows:]))
 
@@ -468,20 +486,20 @@
 def gather(parts):
     return pl.pallas_call(
         gather_kernel,
-        out_shape=jax.ShapeDtypeStruct(parts.shape[1:], jnp.bfloat16),
-        in_specs=[whole()],
+        out_shape=jax.ShapeDtypeStruct(parts[0].shape, jnp.bfloat16),
+        in_specs=[whole()] * 4,
         out_specs=whole(),
         compiler_params=compiler_params(16),
         name="gather",
-    )(parts)
-
-
-def first_kernel(place_ref, a_ref, b_ref, c_ref, d_ref, gain_ref, bias_ref, start_ref, hidden_ref):
+    )(*parts)
+
+
+def first_kernel(a_ref, b_ref, c_ref, d_ref, gain_ref, bias_ref, start_ref, hidden_ref):
     rows, unit = hidden_ref.shape
     parts = [ref[...].astype(jnp.float32) for ref in (a_ref, b_ref, c_ref, d_ref)]
     total = (parts[0] + parts[1]) + (parts[2] + parts[3])
     mean, scale = (row_to_column(line) for line in from_row_sums(total[rows:]))
-    columns = pl.ds(pl.multiple_of(place_ref[0] * unit, unit), unit)
+    columns = pl.ds(pl.multiple_of(lax.axis_index("seq") * unit, unit), unit)
     gain, bias = gain_ref[0:1, columns], bias_ref[0:1, columns]
     for start in range(0, unit, LANES):
         span = slice(start, start + LANES)
@@ -490,34 +508,25 @@
         hidden_ref[:, span] = ((state - mean) * scale * gain[:, span] + bias[:, span]).astype(jnp.bfloat16)
 
 
-def first_hidden(place, parts, ln_gain, ln_bias):
+def first_hidden(parts, ln_gain, ln_bias):
     one = jax.ShapeDtypeStruct((parts[0].shape[0] - 16, parts[0].shape[1]), jnp.bfloat16)
     return pl.pallas_call(
         first_kernel,
         out_shape=(one, one),
-        in_specs=[whole(pltpu.SMEM)] + [whole()] * 6,
+        in_specs=[whole()] * 6,
         out_specs=(whole(), whole()),
         compiler_params=compiler_params(16),
         name="first_hidden",
-    )(in_hbm(place), *parts, ln_gain, ln_bias)
-
-
-def state_total(part_ref, state_ref):
-    total = part_ref[0].astype(jnp.float32)
+    )(*parts, ln_gain, ln_bias)
+
+
+def norm_kernel(layer_index, tp_count, *refs):
+    part_ref, *state_refs, gain_ref, bias_ref, next_ref, cut_ref = refs
+    state = part_ref[0].astype(jnp.float32)
     for source in range(1, part_ref.shape[0]):
-        total = total + part_ref[source].astype(jnp.float32)
-    if state_ref is not None:
-        total = total + state_ref[...]
-    return total
-
-
-def norm_kernel(has_state, layer_index, tp_count, *refs):
-    if has_state:
-        part_ref, state_ref, gain_ref, bias_ref, next_ref, cut_ref = refs
-    else:
-        part_ref, gain_ref, bias_ref, next_ref, cut_ref = refs
-        state_ref = None
-    state = state_total(part_ref, state_ref)
+        state = state + part_ref[source].astype(jnp.float32)
+    for ref in state_refs:
+        state = state + ref[...]
     next_ref[...] = state
     average = jnp.mean(state, axis=-1, keepdims=True)
     centred = state - average
@@ -536,7 +545,7 @@
     cut = width // (devices // tp_count)
     operands = [parts] + ([] if state is None else [state]) + [ln_gain, ln_bias]
     return pl.pallas_call(
-        functools.partial(norm_kernel, state is not None, layer_index, tp_count),
+        functools.partial(norm_kernel, layer_index, tp_count),
         out_shape=(
             jax.ShapeDtypeStruct((rows, width), jnp.float32),
             jax.ShapeDtypeStruct((devices, rows, cut), jnp.bfloat16),
@@ -548,41 +557,39 @@
     )(*operands)
 
 
-def last_parts_kernel(tp_count, place_ref, part_ref, state_ref, out_ref):
+def last_parts_kernel(tp_count, part_ref, state_ref, out_ref):
     total = part_ref[0].astype(jnp.float32)
     for chip in range(1, part_ref.shape[0]):
         total = total + part_ref[chip].astype(jnp.float32)
     mine = state_ref.shape[0]
-    owner = place_ref[1] % tp_count
+    owner = lax.axis_index("tp")
     for place in range(tp_count):
         rows = slice(place * mine, (place + 1) * mine)
         total_rows = total[rows] + jnp.where(owner == place, 1.0, 0.0) * state_ref[...]
         out_ref[rows] = total_rows
 
 
-def last_parts(place, parts, state, tp_count):
+def last_parts(parts, state, tp_count):
     return pl.pallas_call(
         functools.partial(last_parts_kernel, tp_count),
         out_shape=jax.ShapeDtypeStruct(parts.shape[1:], jnp.float32),
-        in_specs=[whole(pltpu.SMEM), whole(), whole()],
+        in_specs=[whole(), whole()],
         out_specs=whole(),
         compiler_params=compiler_params(16),
         name="last_parts",
-    )(in_hbm(place), parts, state)
+    )(parts, state)
 
 
 def last_kernel(a_ref, b_ref, c_ref, d_ref, out_ref):
     near = a_ref[...].astype(jnp.float32) + b_ref[...].astype(jnp.float32)
     far = c_ref[...].astype(jnp.float32) + d_ref[...].astype(jnp.float32)
-    total = (near + far).astype(jnp.bfloat16)
-    for place in range(out_ref.shape[0]):
-        out_ref[place] = total
+    out_ref[...] = (near + far).astype(jnp.bfloat16)
 
 
 def last_rows(parts):
     return pl.pallas_call(
         last_kernel,
-        out_shape=jax.ShapeDtypeStruct((CHIPS,) + parts[0].shape, jnp.bfloat16),
+        out_shape=jax.ShapeDtypeStruct(parts[0].shape, jnp.bfloat16),
         in_specs=[whole()] * 4,
         out_specs=whole(),
         compiler_params=compiler_params(16),
@@ -590,16 +597,77 @@
     )(*parts)
 
 
-def core_parity(place_ref, other):
-    return 1 - place_ref[0] % 2 if other else place_ref[0] % 2
-
-
-def heads_kernel(joins, place_ref, hidden_ref, qkv_ref, *refs):
-    arrived_ref, out_ref = refs if joins else (None, refs[0])
-    parity = core_parity(place_ref, not joins)
-    rows = hidden_ref.shape[0]
+def back_kernel(new_tokens, group_ref, near_ref, far_ref):
+    rows, half = near_ref.shape
+    requests = group_ref.shape[1]
+    rank_row = ranks(group_ref)
+    line = lax.broadcasted_iota(jnp.int32, (rows, requests), 0)
+    column = lax.broadcasted_iota(jnp.int32, (rows, requests), 1)
+    wanted = jnp.sum(jnp.where(column == line // new_tokens, rank_row, 0), axis=1, keepdims=True)
+    line = lax.broadcasted_iota(jnp.int32, near_ref.shape, 0)
+    entry = lax.broadcasted_iota(jnp.int32, near_ref.shape, 1)
+    share = half // CHIPS
+    here = lax.axis_index("seq") // 2
+    for ref, other in ((near_ref, False), (far_ref, True)):
+        held = (((entry // share) ^ here) * 2 + core_parity(other)) * share + entry % share
+        back = held == wanted * new_tokens + line % new_tokens
+        ref[...] = jnp.where(back, 1.0, 0.0).astype(jnp.bfloat16)
+
+
+def back_rows(group_of, new_tokens):
+    rows = group_of.shape[0] * new_tokens
+    one = jax.ShapeDtypeStruct((rows, rows // 2), jnp.bfloat16)
+    return pl.pallas_call(
+        functools.partial(back_kernel, new_tokens),
+        out_shape=(one, one),
+        in_specs=[whole()],
+        out_specs=(whole(), whole()),
+        compiler_params=compiler_params(16),
+        name="back_rows",
+    )(group_of[None, :])
+
+
+def restore_kernel(near_back_ref, far_back_ref, *refs):
+    *row_refs, out_ref = refs
+    requests, new_tokens, width = out_ref.shape
+    step = 2 * LANES
+    for start in range(0, width, step):
+        span = slice(start, start + step)
+        near, far = (
+            jnp.concatenate([ref[:, span] for ref in half], axis=0)
+            for half in (row_refs[:CHIPS], row_refs[CHIPS:])
+        )
+        rows = jnp.dot(near_back_ref[...], near, preferred_element_type=jnp.float32) + jnp.dot(
+            far_back_ref[...], far, preferred_element_type=jnp.float32
+        )
+        out_ref[:, :, span] = rows.reshape(requests, new_tokens, step)
+
+
+def restore(backs, near, far, new_tokens):
+    rows = backs[0].shape[0]
+    return pl.pallas_call(
+        restore_kernel,
+        out_shape=jax.ShapeDtypeStruct((rows // new_tokens, new_tokens, near[0].shape[1]), jnp.float32),
+        in_specs=[whole()] * (2 + 2 * CHIPS),
+        out_specs=whole(),
+        compiler_params=compiler_params(24),
+        name="restore",
+    )(*backs, *near, *far)
+
+
+def core_parity(other):
+    return 1 - lax.axis_index("seq") % 2 if other else lax.axis_index("seq") % 2
+
+
+def heads_kernel(joins, hidden_ref, qkv_ref, *refs):
+    if joins:
+        arrived_ref, near_ref, *out_hbms, out_ref, semaphores = refs
+    else:
+        out_ref = refs[0]
+    parity = core_parity(not joins)
+    here = lax.axis_index("seq") // 2
+    rows, unit = hidden_ref.shape
     width = qkv_ref.shape[1] // 3
-    unit = out_ref.shape[-1]
     share = rows // CHIPS // 2
     half = rows // 2
     pieces = width // unit
@@ -610,55 +678,80 @@
             values = values + arrived_ref[start : start + values.shape[0]].astype(jnp.float32)
         return values.astype(jnp.bfloat16)
 
-    picked = jnp.concatenate(
-        [
-            hidden_ref[pl.ds(pl.multiple_of((2 * chip + parity) * share, share), share), :]
-            for chip in range(CHIPS)
-        ],
-        axis=0,
-    )
-    heads = jnp.dot(picked, qkv_ref[...], preferred_element_type=jnp.float32)
+    def picked(chips):
+        return jnp.concatenate(
+            [
+                hidden_ref[pl.ds(pl.multiple_of((2 * chip + parity) * share, share), share), :]
+                for chip in chips
+            ],
+            axis=0,
+        )
+
+    queries = jnp.dot(picked(range(CHIPS)), qkv_ref[:, :width], preferred_element_type=jnp.float32)
     for piece in range(pieces):
         start = piece * half
-        query = joined(heads[:, piece * unit : (piece + 1) * unit], start)
+        query = joined(queries[:, piece * unit : (piece + 1) * unit], start)
         if joins:
-            for chip in range(CHIPS):
-                out_ref[chip, tall + start : tall + start + half] = query
+            for distance in range(CHIPS):
+                out_ref[distance, tall + start : tall + start + half] = query
         else:
             out_ref[start : start + half] = query
+    others = jnp.dot(
+        picked([here ^ distance for distance in range(CHIPS)]), qkv_ref[:, width:], preferred_element_type=jnp.float32
+    )
     base = pieces * half
-    for chip in range(CHIPS):
+    leaving = []
+    for distance in reversed(range(CHIPS)):
         for piece in range(2 * pieces):
-            column = width + piece * unit
-            start = base + (chip * 2 * pieces + piece) * share
-            value = joined(heads[chip * share : (chip + 1) * share, column : column + unit], start)
+            start = base + (distance * 2 * pieces + piece) * share
+            value = joined(
+                others[distance * share : (distance + 1) * share, piece * unit : (piece + 1) * unit], start
+            )
             if joins:
-                out_ref[chip, piece * share : (piece + 1) * share] = value
+                out_ref[distance, piece * share : (piece + 1) * share] = value
             else:
                 out_ref[start : start + share] = value
-
-
-def project_heads(place, hidden, weights_qkv, unit, arrived=None):
+        if joins and distance:
+            copy = pltpu.make_async_copy(
+                out_ref.at[distance], out_hbms[distance - 1], semaphores.at[distance - 1]
+            )
+            copy.start()
+            leaving.append(copy)
+    if joins:
+        near_ref[...] = out_ref[0]
+    for copy in leaving:
+        copy.wait()
+
+
+def project_heads(hidden, weights_qkv, unit, arrived=None):
     rows = hidden.shape[0]
     pieces = weights_qkv.shape[1] // 3 // unit
     tall = 2 * pieces * (rows // CHIPS // 2)
     common = pieces * (rows // 2)
     extra = [] if arrived is None else [arrived]
-    shape = (common + CHIPS * tall, unit) if arrived is None else (CHIPS, tall + common, unit)
+    out_shape = jax.ShapeDtypeStruct((common + CHIPS * tall, unit), jnp.bfloat16)
+    out_specs = whole()
+    scratch = []
+    if arrived is not None:
+        one = (tall + common, unit)
+        out_shape = (jax.ShapeDtypeStruct(one, jnp.bfloat16),) + (pltpu.HBM(one, jnp.bfloat16),) * (CHIPS - 1)
+        out_specs = (whole(),) + (whole(pltpu.HBM),) * (CHIPS - 1)
+        scratch = [pltpu.VMEM((CHIPS,) + one, jnp.bfloat16), pltpu.SemaphoreType.DMA((CHIPS - 1,))]
     return pl.pallas_call(
         functools.partial(heads_kernel, arrived is not None),
-        out_shape=jax.ShapeDtypeStruct(shape, jnp.bfloat16),
-        in_specs=[whole(pltpu.SMEM)] + [whole()] * (2 + len(extra)),
-        out_specs=whole(),
+        out_shape=out_shape,
+        in_specs=[whole()] * (2 + len(extra)),
+        out_specs=out_specs,
+        scratch_shapes=scratch,
         compiler_params=compiler_params(24),
         name="project_heads",
-    )(in_hbm(place), hidden, weights_qkv, *extra)
-
-
-def units_kernel(joins, place_ref, hidden_ref, fc1_ref, *refs):
+    )(hidden, weights_qkv, *extra)
+
+
+def units_kernel(joins, hidden_ref, fc1_ref, *refs):
     arrived_ref, out_refs = (refs[0], refs[1:]) if joins else (None, refs)
-    parity = core_parity(place_ref, not joins)
-    here = place_ref[0] // 2
+    parity = core_parity(not joins)
+    here = lax.axis_index("seq") // 2
     unit = fc1_ref.shape[2] // CHIPS // 2
     hidden = hidden_ref[...]
     for distance in range(CHIPS):
@@ -672,7 +765,7 @@
             out_refs[0][distance] = pre.astype(jnp.bfloat16)
 
 
-def project_units(place, hidden, w_fc1, layer_index, arrived=None):
+def project_units(hidden, w_fc1, layer_index, arrived=None):
     rows = hidden.shape[0]
     unit = w_fc1.shape[2] // CHIPS // 2
     extra = [] if arrived is None else [arrived]
@@ -684,24 +777,24 @@
         functools.partial(units_kernel, arrived is not None),
         grid=(1,),
         out_shape=out_shape,
-        in_specs=[whole(pltpu.SMEM), same_block(hidden.shape), layer_block(layer_index, w_fc1.shape[1:])]
+        in_specs=[same_block(hidden.shape), layer_block(layer_index, w_fc1.shape[1:])]
         + [same_block(values.shape) for values in extra],
         out_specs=jax.tree.map(lambda leaf: same_block(leaf.shape), out_shape),
         compiler_params=compiler_params(24),
         name="project_units",
-    )(in_hbm(place), hidden, w_fc1, *extra)
-
-
-def activate_kernel(place_ref, part_ref, table_ref, query_ref, key_ref, value_ref):
-    total = part_ref[0].astype(jnp.float32)
-    for chip in range(1, part_ref.shape[0]):
-        total = total + part_ref[chip].astype(jnp.float32)
+    )(hidden, w_fc1, *extra)
+
+
+def activate_kernel(a_ref, b_ref, c_ref, d_ref, table_ref, query_ref, key_ref, value_ref):
+    near = a_ref[...].astype(jnp.float32) + b_ref[...].astype(jnp.float32)
+    far = c_ref[...].astype(jnp.float32) + d_ref[...].astype(jnp.float32)
+    total = near + far
     share, width = key_ref.shape
     half = query_ref.shape[0]
-    unit = part_ref.shape[2]
+    unit = a_ref.shape[1]
     lanes = table_ref.shape[2]
     pieces = width // unit
-    own = pl.ds(pl.multiple_of((place_ref[0] // 2) * share, share), share)
+    own = pl.ds(pl.multiple_of((lax.axis_index("seq") // 2) * share, share), share)
 
     def put(target_ref, start, height, span, scale):
         for piece in range(pieces):
@@ -725,17 +818,17 @@
     put(query_ref, 2 * pieces * share, half, slice(None), 1.0 / math.sqrt(HEAD_DIM))
 
 
-def activate(place, parts, tables, width):
+def activate(parts, tables, width):
     half = tables.shape[1]
     small = jax.ShapeDtypeStruct((half // CHIPS, width), jnp.bfloat16)
     return pl.pallas_call(
         activate_kernel,
         out_shape=(jax.ShapeDtypeStruct((half, width), jnp.bfloat16), small, small),
-        in_specs=[whole(pltpu.SMEM), whole(), whole()],
+        in_specs=[whole()] * 5,
         out_specs=(whole(),) * 3,
         compiler_params=compiler_params(16),
         name="activate",
-    )(in_hbm(place), parts, tables)
+    )(*parts, tables)
 
 
 def rotary_tables(positions, width):
@@ -755,9 +848,9 @@
 
 def attend_kernel(
     layer_index, new_tokens,
-    place_ref, visit_ref, query_ref, far_query_ref, new_key_ref, new_value_ref,
+    visit_hbm, query_ref, far_query_ref, new_key_ref, new_value_ref,
     key_hbm, value_hbm, out_ref,
-    key_ref, value_ref, both_ref, score_ref, top_ref, sum_ref, mix_ref, semaphores,
+    key_ref, value_ref, visit_ref, both_ref, score_ref, top_ref, sum_ref, mix_ref, semaphores, visit_semaphore,
 ):
     blocks = visit_ref.shape[0] // 4
     groups, tall, lanes = mix_ref.shape
@@ -773,10 +866,12 @@
             source.at[layer_index, span], target.at[span], semaphores.at[kind, index]
         )
 
+    looking = pltpu.make_async_copy(visit_hbm, visit_ref, visit_semaphore)
+    looking.start()
     for kind in range(2):
         for index in range(chunks):
             copy(kind, index).start()
-    core = place_ref[0] % 2
+    core = lax.axis_index("seq") % 2
     for chip in range(groups // 2):
         span = slice(chip * share, (chip + 1) * share)
         both_ref[2 * chip + core] = query_ref[span]
@@ -822,12 +917,13 @@
             axis=0,
         )
 
-    own = place_ref[0]
+    own = lax.axis_index("seq")
     fill = jnp.zeros((BLOCK - share, new_key_ref.shape[1]), jnp.bfloat16)
     score(
         blocks, own, jnp.concatenate([new_key_ref[...], fill], axis=0),
         (lane // new_tokens == row // new_tokens) & (lane <= row),
     )
+    looking.wait()
     owners = []
     for block in range(blocks):
         if (block * BLOCK) % chunk == 0:
@@ -880,7 +976,7 @@
         out_ref[head, start:] = rest[:, column : column + lanes]
 
 
-def attend(place, visits, query, far_query, new_key, new_value, k_cache, v_cache, layer_index, new_tokens, groups):
+def attend(visits, query, far_query, new_key, new_value, k_cache, v_cache, layer_index, new_tokens, groups):
     width = query.shape[1]
     rows = 2 * query.shape[0]
     slots = k_cache.shape[1]
@@ -888,35 +984,37 @@
     share = rows // groups
     tall = heads * share
     lanes = 2 * HEAD_DIM
-    chunks = 4
+    chunks = 2
     state = pltpu.VMEM((groups, tall, lanes), jnp.float32)
     return pl.pallas_call(
         functools.partial(attend_kernel, layer_index, new_tokens),
         out_shape=jax.ShapeDtypeStruct((heads, rows // 2 + 4 * groups, lanes), jnp.bfloat16),
-        in_specs=[whole(pltpu.SMEM)] * 2 + [whole()] * 4 + [whole(pltpu.HBM)] * 2,
+        in_specs=[whole(pltpu.HBM)] + [whole()] * 4 + [whole(pltpu.HBM)] * 2,
         out_specs=whole(),
         scratch_shapes=[
             pltpu.VMEM((slots, width), jnp.bfloat16),
             pltpu.VMEM((slots, width), jnp.bfloat16),
+            pltpu.SMEM(visits.shape, jnp.int32),
             pltpu.VMEM((groups, share, width), jnp.bfloat16),
             pltpu.VMEM((visits.shape[0] // 4 + 1, tall, BLOCK), jnp.float32),
             state,
             state,
             state,
             pltpu.SemaphoreType.DMA((2, chunks)),
+            pltpu.SemaphoreType.DMA,
         ],
         compiler_params=compiler_params(24),
         name="attend",
-    )(in_hbm(place), in_hbm(visits), query, far_query, new_key, new_value, in_hbm(k_cache), in_hbm(v_cache))
+    )(in_hbm(visits), query, far_query, new_key, new_value, in_hbm(k_cache), in_hbm(v_cache))
 
 
 def update_kernel(
-    layer_index, other, tp_count, has_start, place_ref, part_ref, bias_ref, out_weight_ref, fc2_ref, *refs
+    layer_index, other, tp_count, has_start, part_ref, bias_ref, out_weight_ref, fc2_ref, *refs
 ):
     *unit_refs, out_ref, scale_ref = refs
     if has_start:
         *unit_refs, start_ref = unit_refs
-    seq_index = place_ref[0]
+    seq_index = lax.axis_index("seq")
     parity = 1 - seq_index % 2 if other else seq_index % 2
     sources, tall, lanes = part_ref.shape
     unit = unit_refs[0].shape[1]
@@ -968,13 +1066,13 @@
         return
     started = jnp.concatenate(started, axis=0)
     for column in range(0, change.shape[1], unit):
-        here = (seq_index * unit == column) & (place_ref[1] % tp_count == 0)
+        here = (seq_index * unit == column) & (lax.axis_index("tp") == 0)
         out_ref[:, column : column + unit] = (
             change[:, column : column + unit] + jnp.where(here, started, 0.0)
         ).astype(out_ref.dtype)
 
 
-def update(place, parts, units, start, b_fc1, w_out, w_fc2, layer_index, other, tp_count):
+def update(parts, units, start, b_fc1, w_out, w_fc2, layer_index, other, tp_count):
     rows = units[0].shape[0] // 2
     width = w_out.shape[2]
     lanes = parts.shape[2]
@@ -984,7 +1082,6 @@
         grid=(1,),
         out_shape=jax.ShapeDtypeStruct((rows, width), jnp.bfloat16 if other else jnp.float32),
         in_specs=[
-            whole(pltpu.SMEM),
             same_block(parts.shape),
             same_block(b_fc1.shape),
             layer_block(layer_index, w_out.shape[1:]),
@@ -995,7 +1092,7 @@
         scratch_shapes=[pltpu.VMEM((lanes, lanes), jnp.float32)],
         compiler_params=compiler_params(),
         name="update",
-    )(in_hbm(place), parts, b_fc1, w_out, w_fc2, *extra)
+    )(parts, b_fc1, w_out, w_fc2, *extra)
 
 
 def per_device(
@@ -1006,82 +1103,77 @@
     seq_index, tp_index = lax.axis_index("seq"), lax.axis_index("tp")
     devices = seq_count * tp_count
     core = seq_index % 2
-    place = jnp.stack([seq_index, seq_index * tp_count + tp_index]).astype(jnp.int32)
     requests, new_tokens = token_ids.shape
     rows = requests * new_tokens
     groups = prefix_len.shape[0]
     share = rows // seq_count
     mine = rows // devices
-    width = embedding.shape[1]
+    features = embedding.shape[1]
     width_local = k_cache.shape[2]
     unit = w_fc2.shape[1]
     same_core = [[s * tp_count + p for s in range(c, seq_count, 2) for p in range(tp_count)] for c in range(2)]
     same_core_seq = [list(range(c, seq_count, 2)) for c in range(2)]
 
     def to_owners(half):
-        parts = half.reshape(devices // 2, mine, width)
+        parts = half.reshape(devices // 2, mine, features)
         return lax.all_to_all(parts, ("seq", "tp"), 0, 0, axis_index_groups=same_core)
 
     def to_chips(parts):
         return lax.all_to_all(parts, "seq", 0, 0, axis_index_groups=same_core_seq)
 
+    def to_distances(parts):
+        return [parts[0]] + [
+            lax.ppermute(parts[k], "seq", [(i, i ^ (2 * k)) for i in range(seq_count)])
+            for k in range(1, CHIPS)
+        ]
+
+    def over_tp(part, distance):
+        return lax.ppermute(part, "tp", [(i, i ^ distance) for i in range(tp_count)])
+
     def from_tp(part):
-        return [part] + [
-            lax.ppermute(part, "tp", [(i, i ^ k) for i in range(tp_count)]) for k in range(1, tp_count)
-        ]
-
-    near, far, own = embed(place, token_ids, group_of, embedding, unit)
+        return [part] + [over_tp(part, k) for k in range(1, tp_count)]
+
+    near, far, own = embed(token_ids, group_of, embedding, unit)
     parts = join(near, swap_cores(far, seq_count), own)
-    gathered = gather(to_chips(parts))
+    gathered = gather(to_distances(parts))
     gathered, group_of = lax.optimization_barrier((gathered, group_of))
     rank, positions, visits = order_requests(group_of, prefix_len, tail_len, block_map, new_tokens)
     own_positions = lax.dynamic_index_in_dim(positions.reshape(CHIPS, 2, share), core, 1, keepdims=False)
+    backs = back_rows(group_of, new_tokens)
     tables = rotary_tables(own_positions.reshape(-1), 2 * HEAD_DIM)
     weights_qkv = w_qkv[0].reshape(w_qkv.shape[1], -1)
-    start, hidden = first_hidden(place, from_tp(gathered), ln_gain, ln_bias)
+    parts, backs, tables, visits = lax.optimization_barrier((from_tp(gathered), backs, tables, visits))
+    start, hidden = first_hidden(parts, ln_gain, ln_bias)
     state = None
     for layer_index in range(LAYERS):
         if layer_index:
             weights_qkv = w_qkv[layer_index].reshape(w_qkv.shape[1], -1)
             state, cut = norm_rows(parts, state, ln_gain, ln_bias, layer_index, devices, tp_count)
             hidden = lax.all_to_all(cut, ("seq", "tp"), 0, 0).reshape(rows, -1)
-        arriving = swap_cores(project_heads(place, hidden, weights_qkv, unit), seq_count)
-        heads = to_chips(project_heads(place, hidden, weights_qkv, unit, arriving))
-        arriving = swap_cores(project_units(place, hidden, w_fc1, layer_index), seq_count)
-        units = project_units(place, hidden, w_fc1, layer_index, arriving)
-        query, new_key, new_value = activate(place, heads, tables, width_local)
-        query, *units = lax.optimization_barrier((query, *units))
-        units = units[:1] + [
-            lax.ppermute(units[k], "seq", [(i, i ^ (2 * k)) for i in range(seq_count)])
-            for k in range(1, CHIPS)
-        ]
+        arriving = swap_cores(project_heads(hidden, weights_qkv, unit), seq_count)
+        heads = to_distances(project_heads(hidden, weights_qkv, unit, arriving))
+        arriving = swap_cores(project_units(hidden, w_fc1, layer_index), seq_count)
+        units = project_units(hidden, w_fc1, layer_index, arriving)
+        query, new_key, new_value = activate(heads, tables, width_local)
+        units = to_distances(units)
         parts = attend(
-            place, visits, query, swap_cores(query, seq_count), new_key, new_value,
+            visits, query, swap_cores(query, seq_count), new_key, new_value,
             k_cache, v_cache, layer_index, new_tokens, groups,
         )
         parts, *units = lax.optimization_barrier((parts, *units))
         parts = lax.all_to_all(parts, "seq", 0, 0)
         arriving, half = (
-            update(place, parts, units, start, b_fc1, w_out, w_fc2, layer_index, other, tp_count)
+            update(parts, units, start, b_fc1, w_out, w_fc2, layer_index, other, tp_count)
             for other in (True, False)
         )
         half = (half + swap_cores(arriving, seq_count).astype(jnp.float32)).astype(jnp.bfloat16)
         start = None
         if layer_index < LAYERS - 1:
             parts = to_owners(half)
-    last = last_parts(place, to_chips(half.reshape(CHIPS, share, width)), state, tp_count)
+    last = last_parts(to_chips(half.reshape(CHIPS, share, features)), state, tp_count)
     last = from_tp(last.astype(jnp.bfloat16))
-    last = to_chips(last_rows(last)).reshape(rows // 2, width)
-    arriving = swap_cores(last, seq_count)
-    wanted = (rank[:, None] * new_tokens + jnp.arange(new_tokens, dtype=jnp.int32)[None, :]).reshape(-1)
-    index = jnp.arange(rows // 2, dtype=jnp.int32)
-
-    def placed(half, parity):
-        held = (2 * (index // share) + parity) * share + index % share
-        hot = (wanted[:, None] == held[None, :]).astype(jnp.bfloat16)
-        return jnp.dot(hot, half, preferred_element_type=jnp.float32)
-
-    return (placed(last, core) + placed(arriving, 1 - core)).reshape(requests, new_tokens, width)
+    last = to_distances([last_rows(last)] * CHIPS)
+    return restore(backs, last, [swap_cores(part, seq_count) for part in last], new_tokens)
 
 
 def solution(mesh):

time: 204 us -> 183 us (0.90)
  blocking collectives: 66.6 us -> 52.4 us
  Pallas kernels: 41.6 us -> 30.8 us
  waiting for transfers between devices: 44.6 us -> 52.6 us
  local copies, waits for them, and re-layouts: 17.3 us -> 9.45 us
  starting transfers between devices: 30.5 us -> 35.9 us
    ppermute x12 -> x24, waiting for transfers between devices: 17.9 us -> 41.1 us  [the longest x18 27.2 us: to_distances(): lax.ppermute(parts[k], 'seq', [(i, i ^ 2 * k) for i in range(seq_count)])]
    ppermute x12 -> x24, starting transfers between devices: 16 us -> 31.1 us  [the longest x18 22.2 us: to_distances(): lax.ppermute(parts[k], 'seq', [(i, i ^ 2 * k) for i in range(seq_count)])]
    all_to_all x2 -> x1, blocking collectives: 26 us -> 11.5 us  [to_chips(): return lax.all_to_all(parts, 'seq', 0, 0, axis_index_groups=same_core_seq)]
    all_to_all x3 -> x0, waiting for transfers between devices: 12.8 us -> none  [to_chips(): return lax.all_to_all(parts, 'seq', 0, 0, axis_index_groups=same_core_seq)]
    all_to_all x3 -> x0, starting transfers between devices: 10.5 us -> none  [to_chips(): return lax.all_to_all(parts, 'seq', 0, 0, axis_index_groups=same_core_seq)]
    unnamed x48 -> x42, local copies, waits for them, and re-layouts: 12.1 us -> 4.61 us
    pallas_call x4, Pallas kernels: 5.19 us -> 1.29 us  [project_units(): pl.pallas_call(functools.partial(units_kernel, arrived is not None), grid...]
    ppermute x10 -> x13, waiting for transfers between devices: 9.46 us -> 5.8 us  [swap_cores(): return lax.ppermute(values, 'seq', [(i, i ^ 1) for i in range(seq_count)])]
  transfers between devices with their start and end apart: 26 -> 38, of which waited for: 17 -> 21; matrix products, arithmetic and copies ran while one was open for 3% -> 4% of each run, Pallas kernels for 11% -> 10%
where the time goes in v4:
time: 183 us; the launch traced here: 182 us
  waiting for transfers between devices  52.6 us (29%)
  blocking collectives  52.4 us (29%)
  starting transfers between devices  35.9 us (20%)
  Pallas kernels  30.8 us (17%)
  local copies, waits for them, and re-layouts  9.45 us (5%)
    ppermute x18, waiting for transfers between devices, to_distances(): lax.ppermute(parts[k], 'seq', [(i, i ^ 2 * k) for i in range(seq_count)])  27.2 us
    ppermute x18, starting transfers between devices, to_distances(): lax.ppermute(parts[k], 'seq', [(i, i ^ 2 * k) for i in range(seq_count)])  22.2 us
    all_to_all x1, blocking collectives, to_owners(): lax.all_to_all(parts, ('seq', 'tp'), 0, 0, axis_index_groups=same_core)  20.7 us
    all_to_all x2, blocking collectives, per_device(): parts = lax.all_to_all(parts, 'seq', 0, 0)  20.2 us
    ppermute x6, waiting for transfers between devices, over_tp(): lax.ppermute(part, 'tp', [(i, i ^ distance) for i in range(tp_count)])  13.9 us
    all_to_all x1, blocking collectives, to_chips(): return lax.all_to_all(parts, 'seq', 0, 0, axis_index_groups=same_core_seq)  11.5 us
    pallas_call x2, Pallas kernels, attend(): pl.pallas_call(functools.partial(attend_kernel, layer_index, new_tokens),...  9.92 us
    ppermute x6, starting transfers between devices, over_tp(): lax.ppermute(part, 'tp', [(i, i ^ distance) for i in range(tp_count)])  8.9 us
  transfers between devices with their start and end apart: 38, of which 21 were waited for; matrix products, arithmetic and copies ran while one was open for 4% of the time, Pallas kernels for 10%

profile of v4, /device:TPU:0, one launch (start us, length us, event | category | flops | bytes accessed | tf_op | source)
XLA Modules:
  0.0 182.3 jit_solution(4721310986580709057)
XLA Ops:
  0.0 6.1 %embed.1 = (bf16[4,256,256]{2,1,0:T(8,128)(2,1)S(1)}, bf16[1040,256]{1,0:T(8,128)(2,1)}, f32[8,256]{1,0:T(8,128)S(1)}) custom-call(s32[4,64]{1,0:T(4,128)} %bitcast.19, s32[1,64]{1,0:T(1,128)} %bitcast.14, bf16[1600,2048]{1,0:T(8,128)(2,1)} %table_hbm.1), custom_call_target="tpu_custom_call" | custom-call | tf_op jit(solution)/shard_map/embed/pallas_call | solution.py:416
  9.2 2.9 %collective-permute-start.1 = (bf16[272,256]{1,0:T(8,128)(2,1)}, bf16[272,256]{1,0:T(8,128)(2,1)S(1)}, u32[]{:S(2)}, u32[]{:S(2)}) collective-permute-start(bf16[272,256]{1,0:T(8,128)(2,1)} %get-tuple-element.66), channel_id=1, source_target_pairs={{0,8},{4,12},{8,0},{12,4},{16,24},{20,28},{24,16},{28,20},{1,9},{5... | collective-permute-start | bytes 417800 | tf_op jit(solution)/shard_map/ppermute | solution.py:1126
  12.1 1.5 collective-permute-start.2
  14.9 1.6 copy.20.qkv_ref
  16.6 4.2 %collective-permute-done.2.c_ref = bf16[272,256]{1,0:T(8,128)(2,1)S(1)} collective-permute-done((bf16[272,256]{1,0:T(8,128)(2,1)}, bf16[272,256]{1,0:T(8,128)(2,1)S(1)}, u32[]{:S(2)}, u32[]{:S(2)}) %collective-permute-start.2) | collective-permute-done | bytes 139296 | tf_op jit(solution)/shard_map/ppermute | solution.py:1126
  22.4 1.6 collective-permute-start.4
  24.1 2.6 %collective-permute-start.5 = (bf16[272,256]{1,0:T(8,128)(2,1)S(1)}, bf16[272,256]{1,0:T(8,128)(2,1)S(1)}, u32[]{:S(2)}, u32[]{:S(2)}) collective-permute-start(bf16[272,256]{1,0:T(8,128)(2,1)S(1)} %gather.1.a_ref), channel_id=1, source_target_pairs={{0,2},{1,3},{2,0},{3,1},{4,6},{5,7},{6,4},{7,5},{8,10},{9,11},{10,... | collective-permute-start | bytes 417800 | tf_op jit(solution)/shard_map/ppermute | solution.py:1131
  26.9 2.5 %order_requests.1 = (s32[64]{0:T(128)}, s32[256]{0:T(256)}, s32[64]{0:T(128)}) custom-call(s32[64]{0:T(128)} %group_ref, s32[8]{0:T(128)} %prefix_ref.1, s32[64]{0:T(128)} %tail_ref.1, s32[2,16]{1,0:T(2,128)} %bitcast.20), custom_call_target="tpu_custom_call" | custom-call | tf_op jit(solution)/shard_map/order_requests/pallas_call | solution.py:303
  30.9 5.9 %collective-permute-done.5.c_ref = bf16[272,256]{1,0:T(8,128)(2,1)S(1)} collective-permute-done((bf16[272,256]{1,0:T(8,128)(2,1)S(1)}, bf16[272,256]{1,0:T(8,128)(2,1)S(1)}, u32[]{:S(2)}, u32[]{:S(2)}) %collective-permute-start.5) | collective-permute-done | bytes 139296 | tf_op jit(solution)/shard_map/ppermute | solution.py:1131
  40.2 1.6 collective-permute-start.8
  43.8 4.5 %collective-permute-done.8.b_ref = bf16[384,256]{1,0:T(8,128)(2,1)S(1)} collective-permute-done((bf16[384,256]{1,0:T(8,128)(2,1)}, bf16[384,256]{1,0:T(8,128)(2,1)S(1)}, u32[]{:S(2)}, u32[]{:S(2)}) %collective-permute-start.8) | collective-permute-done | bytes 196640 | tf_op jit(solution)/shard_map/ppermute | solution.py:1126
  48.3 4.6 %collective-permute-done.9.c_ref = bf16[384,256]{1,0:T(8,128)(2,1)S(1)} collective-permute-done((bf16[384,256]{1,0:T(8,128)(2,1)}, bf16[384,256]{1,0:T(8,128)(2,1)S(1)}, u32[]{:S(2)}, u32[]{:S(2)}) %collective-permute-start.9) | collective-permute-done | bytes 196640 | tf_op jit(solution)/shard_map/ppermute | solution.py:1126
  54.2 1.5 collective-permute-start.14
  55.6 1.5 collective-permute-start.15
  57.2 5.0 %attend.2 = bf16[8,160,128]{2,1,0:T(8,128)(2,1)S(1)} custom-call(s32[64]{0:T(128)} %get-tuple-element.77.visit_hbm, bf16[128,512]{1,0:T(8,128)(2,1)S(1)} %get-tuple-element.88.query_ref, bf16[128,512]{1,0:T(8,128)(2,1)S(1)} %collective-permute-done.11.far_query_ref, bf16[32,512]{1,0:T(8,128)(2,1)S(1)} %get-tuple-element.89.new_key_ref, ...), custom_call_target="tpu_custom_call" | custom-call | tf_op jit(solution)/shard_map/attend/pallas_call | solution.py:989
  62.6 10.2 %all_to_all.25.part_ref = bf16[8,160,128]{2,1,0:T(8,128)(2,1)S(1)} all-to-all(bf16[8,160,128]{2,1,0:T(8,128)(2,1)S(1)} %attend.2), channel_id=1, replica_groups=mesh['seq'=8,'tp'=4] {'seq'}, dimensions={0} | all-to-all | bytes 655360 | tf_op jit(solution)/shard_map/all_to_all | solution.py:1164
  75.7 20.7 %all_to_all.26.refs_0_ = bf16[16,8,2048]{2,1,0:T(8,128)(2,1)S(1)} all-to-all(bf16[16,8,2048]{2,1,0:T(8,128)(2,1)S(1)} %fusion), channel_id=1, replica_groups={{0,1,2,3,8,9,10,11,16,17,18,19,24,25,26,27},{4,5,6,7,12,13,14,15,20,21,..., dimensions={0} | all-to-all | bytes 1048576 | tf_op jit(solution)/shard_map/all_to_all | solution.py:1119
  98.0 2.7 %all-to-all-start.2 = ((bf16[32,8,256]{2,1,0:T(8,128)(2,1)}), bf16[32,8,256]{2,1,0:T(8,128)(2,1)S(1)}, u32[]{:S(2)}, u32[]{:S(2)}) async-start(bf16[32,8,256]{2,1,0:T(8,128)(2,1)} %get-tuple-element.101), calls=%async_computation.2 | async-start | bytes 262144 | tf_op jit(solution)/shard_map/all_to_all | solution.py:1152
  103.3 5.7 %all-to-all-done.2 = bf16[32,8,256]{2,1,0:T(8,128)(2,1)S(1)} async-done(((bf16[32,8,256]{2,1,0:T(8,128)(2,1)}), bf16[32,8,256]{2,1,0:T(8,128)(2,1)S(1)}, u32[]{:S(2)}, u32[]{:S(2)}) %all-to-all-start.2) | async-done | bytes 131104 | tf_op jit(solution)/shard_map/all_to_all | solution.py:1152
  113.5 2.2 %collective-permute-start.20 = (bf16[384,256]{1,0:T(8,128)(2,1)}, bf16[384,256]{1,0:T(8,128)(2,1)S(1)}, u32[]{:S(2)}, u32[]{:S(2)}) collective-permute-start(bf16[384,256]{1,0:T(8,128)(2,1)} %get-tuple-element.105), channel_id=1, source_target_pairs={{0,24},{4,28},{8,16},{12,20},{16,8},{20,12},{24,0},{28,4},{1,25},{... | collective-permute-start | bytes 589832 | tf_op jit(solution)/shard_map/ppermute | solution.py:1126
  116.0 4.1 %collective-permute-done.18.b_ref = bf16[384,256]{1,0:T(8,128)(2,1)S(1)} collective-permute-done((bf16[384,256]{1,0:T(8,128)(2,1)}, bf16[384,256]{1,0:T(8,128)(2,1)S(1)}, u32[]{:S(2)}, u32[]{:S(2)}) %collective-permute-start.18) | collective-permute-done | bytes 196640 | tf_op jit(solution)/shard_map/ppermute | solution.py:1126
  120.2 3.9 %collective-permute-done.19.c_ref = bf16[384,256]{1,0:T(8,128)(2,1)S(1)} collective-permute-done((bf16[384,256]{1,0:T(8,128)(2,1)}, bf16[384,256]{1,0:T(8,128)(2,1)S(1)}, u32[]{:S(2)}, u32[]{:S(2)}) %collective-permute-start.19) | collective-permute-done | bytes 196640 | tf_op jit(solution)/shard_map/ppermute | solution.py:1126
  128.0 4.9 %attend.3 = bf16[8,160,128]{2,1,0:T(8,128)(2,1)S(1)} custom-call(s32[64]{0:T(128)} %get-tuple-element.77.visit_hbm, bf16[128,512]{1,0:T(8,128)(2,1)S(1)} %get-tuple-element.106.query_ref, bf16[128,512]{1,0:T(8,128)(2,1)S(1)} %collective-permute-done.21.far_query_ref, bf16[32,512]{1,0:T(8,128)(2,1)S(1)} %get-tuple-element.107.new_key_ref, ...), custom_call_target="tpu_custom_call" | custom-call | tf_op jit(solution)/shard_map/attend/pallas_call | solution.py:989
  134.1 10.0 %all_to_all.27.part_ref = bf16[8,160,128]{2,1,0:T(8,128)(2,1)S(1)} all-to-all(bf16[8,160,128]{2,1,0:T(8,128)(2,1)S(1)} %attend.3), channel_id=1, replica_groups=mesh['seq'=8,'tp'=4] {'seq'}, dimensions={0} | all-to-all | bytes 655360 | tf_op jit(solution)/shard_map/all_to_all | solution.py:1164
  147.0 11.5 %all_to_all.28.part_ref = bf16[4,32,2048]{2,1,0:T(8,128)(2,1)S(1)} all-to-all(bf16[4,32,2048]{2,1,0:T(8,128)(2,1)S(1)} %bitcast.18), channel_id=1, replica_groups={{0,8,16,24},{4,12,20,28},{1,9,17,25},{5,13,21,29},{2,10,18,26},{6,14,22..., dimensions={0} | all-to-all | bytes 1048576 | tf_op jit(solution)/shard_map/all_to_all | solution.py:1122
  158.9 1.5 collective-permute-start.28
  160.4 2.7 %collective-permute-start.29 = (bf16[32,2048]{1,0:T(8,128)(2,1)S(1)}, bf16[32,2048]{1,0:T(8,128)(2,1)S(1)}, u32[]{:S(2)}, u32[]{:S(2)}) collective-permute-start(bf16[32,2048]{1,0:T(8,128)(2,1)S(1)} %convert_element_type.40.a_ref), channel_id=1, source_target_pairs={{0,3},{1,2},{2,1},{3,0},{4,7},{5,6},{6,5},{7,4},{8,11},{9,10},{10,... | collective-permute-start | bytes 393224 | tf_op jit(solution)/shard_map/ppermute | solution.py:1131
  163.1 1.7 collective-permute-done.27.b_ref
  164.8 6.3 %collective-permute-done.28.c_ref = bf16[32,2048]{1,0:T(8,128)(2,1)S(1)} collective-permute-done((bf16[32,2048]{1,0:T(8,128)(2,1)S(1)}, bf16[32,2048]{1,0:T(8,128)(2,1)S(1)}, u32[]{:S(2)}, u32[]{:S(2)}) %collective-permute-start.28) | collective-permute-done | bytes 131104 | tf_op jit(solution)/shard_map/ppermute | solution.py:1131
  173.0 1.7 collective-permute-start.32
  174.7 1.5 collective-permute-done.30.refs_1_
  180.2 2.0 %restore.1 = f32[64,4,2048]{2,1,0:T(4,128)} custom-call(bf16[256,128]{1,0:T(8,128)(2,1)S(1)} %copy-done.10, bf16[256,128]{1,0:T(8,128)(2,1)S(1)} %copy-done.12, bf16[32,2048]{1,0:T(8,128)(2,1)S(1)} %last_rows.1.refs_0_, bf16[32,2048]{1,0:T(8,128)(2,1)S(1)} %collective-permute-done.30.refs_1_, bf16[32,2048]{1,0:T(8,128)(2,1)S(1)} %collective-permute-done.31.refs_2_, ...), custom_call_target="tpu_custom_call" | custom-call | tf_op jit(solution)/shard_map/restore/pallas_call | solution.py:648
  (130 shorter events, 40.8 us)
Async XLA Ops:
  6.1 2.3 %collective-permute-start = (bf16[1040,256]{1,0:T(8,128)(2,1)}, bf16[1040,256]{1,0:T(8,128)(2,1)S(1)}, u32[]{:S(2)}, u32[]{:S(2)}) collective-permute-start(bf16[1040,256]{1,0:T(8,128)(2,1)} %get-tuple-element.63), channel_id=1, source_target_pairs={{0,4},{4,0},{8,12},{12,8},{16,20},{20,16},{24,28},{28,24},{1,5},{5... | collective-permute-start | bytes 1597448 | tf_op jit(solution)/shard_map/ppermute | solution.py:239
  9.2 7.4 %collective-permute-start.1 = (bf16[272,256]{1,0:T(8,128)(2,1)}, bf16[272,256]{1,0:T(8,128)(2,1)S(1)}, u32[]{:S(2)}, u32[]{:S(2)}) collective-permute-start(bf16[272,256]{1,0:T(8,128)(2,1)} %get-tuple-element.66), channel_id=1, source_target_pairs={{0,8},{4,12},{8,0},{12,4},{16,24},{20,28},{24,16},{28,20},{1,9},{5... | collective-permute-start | bytes 417800 | tf_op jit(solution)/shard_map/ppermute | solution.py:1126
  12.1 8.6 %collective-permute-start.2 = (bf16[272,256]{1,0:T(8,128)(2,1)}, bf16[272,256]{1,0:T(8,128)(2,1)S(1)}, u32[]{:S(2)}, u32[]{:S(2)}) collective-permute-start(bf16[272,256]{1,0:T(8,128)(2,1)} %get-tuple-element.67), channel_id=1, source_target_pairs={{0,16},{4,20},{8,24},{12,28},{16,0},{20,4},{24,8},{28,12},{1,17},{... | collective-permute-start | bytes 417800 | tf_op jit(solution)/shard_map/ppermute | solution.py:1126
  13.7 7.1 %collective-permute-start.3 = (bf16[272,256]{1,0:T(8,128)(2,1)}, bf16[272,256]{1,0:T(8,128)(2,1)S(1)}, u32[]{:S(2)}, u32[]{:S(2)}) collective-permute-start(bf16[272,256]{1,0:T(8,128)(2,1)} %get-tuple-element.68), channel_id=1, source_target_pairs={{0,24},{4,28},{8,16},{12,20},{16,8},{20,12},{24,0},{28,4},{1,25},{... | collective-permute-start | bytes 417800 | tf_op jit(solution)/shard_map/ppermute | solution.py:1126
  22.4 8.5 %collective-permute-start.4 = (bf16[272,256]{1,0:T(8,128)(2,1)S(1)}, bf16[272,256]{1,0:T(8,128)(2,1)S(1)}, u32[]{:S(2)}, u32[]{:S(2)}) collective-permute-start(bf16[272,256]{1,0:T(8,128)(2,1)S(1)} %gather.1.a_ref), channel_id=1, source_target_pairs={{0,1},{1,0},{2,3},{3,2},{4,5},{5,4},{6,7},{7,6},{8,9},{9,8},{10,11... | collective-permute-start | bytes 417800 | tf_op jit(solution)/shard_map/ppermute | solution.py:1131
  24.1 12.7 %collective-permute-start.5 = (bf16[272,256]{1,0:T(8,128)(2,1)S(1)}, bf16[272,256]{1,0:T(8,128)(2,1)S(1)}, u32[]{:S(2)}, u32[]{:S(2)}) collective-permute-start(bf16[272,256]{1,0:T(8,128)(2,1)S(1)} %gather.1.a_ref), channel_id=1, source_target_pairs={{0,2},{1,3},{2,0},{3,1},{4,6},{5,7},{6,4},{7,5},{8,10},{9,11},{10,... | collective-permute-start | bytes 417800 | tf_op jit(solution)/shard_map/ppermute | solution.py:1131
  26.7 10.2 %collective-permute-start.6 = (bf16[272,256]{1,0:T(8,128)(2,1)S(1)}, bf16[272,256]{1,0:T(8,128)(2,1)S(1)}, u32[]{:S(2)}, u32[]{:S(2)}) collective-permute-start(bf16[272,256]{1,0:T(8,128)(2,1)S(1)} %gather.1.a_ref), channel_id=1, source_target_pairs={{0,3},{1,2},{2,1},{3,0},{4,7},{5,6},{6,5},{7,4},{8,11},{9,10},{10,... | collective-permute-start | bytes 417800 | tf_op jit(solution)/shard_map/ppermute | solution.py:1131
  37.7 15.5 %collective-permute-start.12 = (bf16[4,256,256]{2,1,0:T(8,128)(2,1)S(1)}, bf16[4,256,256]{2,1,0:T(8,128)(2,1)S(1)}, u32[]{:S(2)}, u32[]{:S(2)}) collective-permute-start(bf16[4,256,256]{2,1,0:T(8,128)(2,1)S(1)} %project_units.4), channel_id=1, source_target_pairs={{0,4},{4,0},{8,12},{12,8},{16,20},{20,16},{24,28},{28,24},{1,5},{5... | collective-permute-start | bytes 1572872 | tf_op jit(solution)/shard_map/ppermute | solution.py:239
  40.2 8.0 %collective-permute-start.8 = (bf16[384,256]{1,0:T(8,128)(2,1)}, bf16[384,256]{1,0:T(8,128)(2,1)S(1)}, u32[]{:S(2)}, u32[]{:S(2)}) collective-permute-start(bf16[384,256]{1,0:T(8,128)(2,1)} %get-tuple-element.84), channel_id=1, source_target_pairs={{0,8},{4,12},{8,0},{12,4},{16,24},{20,28},{24,16},{28,20},{1,9},{5... | collective-permute-start | bytes 589832 | tf_op jit(solution)/shard_map/ppermute | solution.py:1126
  41.8 11.1 %collective-permute-start.9 = (bf16[384,256]{1,0:T(8,128)(2,1)}, bf16[384,256]{1,0:T(8,128)(2,1)S(1)}, u32[]{:S(2)}, u32[]{:S(2)}) collective-permute-start(bf16[384,256]{1,0:T(8,128)(2,1)} %get-tuple-element.85), channel_id=1, source_target_pairs={{0,16},{4,20},{8,24},{12,28},{16,0},{20,4},{24,8},{28,12},{1,17},{... | collective-permute-start | bytes 589832 | tf_op jit(solution)/shard_map/ppermute | solution.py:1126
  42.4 10.5 %collective-permute-start.10 = (bf16[384,256]{1,0:T(8,128)(2,1)}, bf16[384,256]{1,0:T(8,128)(2,1)S(1)}, u32[]{:S(2)}, u32[]{:S(2)}) collective-permute-start(bf16[384,256]{1,0:T(8,128)(2,1)} %get-tuple-element.86), channel_id=1, source_target_pairs={{0,24},{4,28},{8,16},{12,20},{16,8},{20,12},{24,0},{28,4},{1,25},{... | collective-permute-start | bytes 589832 | tf_op jit(solution)/shard_map/ppermute | solution.py:1126
  53.2 4.0 %collective-permute-start.11 = (bf16[128,512]{1,0:T(8,128)(2,1)S(1)}, bf16[128,512]{1,0:T(8,128)(2,1)S(1)}, u32[]{:S(2)}, u32[]{:S(2)}) collective-permute-start(bf16[128,512]{1,0:T(8,128)(2,1)S(1)} %get-tuple-element.88.query_ref), channel_id=1, source_target_pairs={{0,4},{4,0},{8,12},{12,8},{16,20},{20,16},{24,28},{28,24},{1,5},{5... | collective-permute-start | bytes 393224 | tf_op jit(solution)/shard_map/ppermute | solution.py:239
  53.6 8.6 %collective-permute-start.13 = (bf16[256,256]{1,0:T(8,128)(2,1)S(1)}, bf16[256,256]{1,0:T(8,128)(2,1)S(1)}, u32[]{:S(2)}, u32[]{:S(2)}) collective-permute-start(bf16[256,256]{1,0:T(8,128)(2,1)S(1)} %get-tuple-element.92), channel_id=1, source_target_pairs={{0,8},{4,12},{8,0},{12,4},{16,24},{20,28},{24,16},{28,20},{1,9},{5... | collective-permute-start | bytes 393224 | tf_op jit(solution)/shard_map/ppermute | solution.py:1126
  54.2 8.4 %collective-permute-start.14 = (bf16[256,256]{1,0:T(8,128)(2,1)S(1)}, bf16[256,256]{1,0:T(8,128)(2,1)S(1)}, u32[]{:S(2)}, u32[]{:S(2)}) collective-permute-start(bf16[256,256]{1,0:T(8,128)(2,1)S(1)} %get-tuple-element.93), channel_id=1, source_target_pairs={{0,16},{4,20},{8,24},{12,28},{16,0},{20,4},{24,8},{28,12},{1,17},{... | collective-permute-start | bytes 393224 | tf_op jit(solution)/shard_map/ppermute | solution.py:1126
  55.6 6.9 %collective-permute-start.15 = (bf16[256,256]{1,0:T(8,128)(2,1)S(1)}, bf16[256,256]{1,0:T(8,128)(2,1)S(1)}, u32[]{:S(2)}, u32[]{:S(2)}) collective-permute-start(bf16[256,256]{1,0:T(8,128)(2,1)S(1)} %get-tuple-element.94), channel_id=1, source_target_pairs={{0,24},{4,28},{8,16},{12,20},{16,8},{20,12},{24,0},{28,4},{1,25},{... | collective-permute-start | bytes 393224 | tf_op jit(solution)/shard_map/ppermute | solution.py:1126
  98.0 11.0 %all-to-all-start.2 = ((bf16[32,8,256]{2,1,0:T(8,128)(2,1)}), bf16[32,8,256]{2,1,0:T(8,128)(2,1)S(1)}, u32[]{:S(2)}, u32[]{:S(2)}) async-start(bf16[32,8,256]{2,1,0:T(8,128)(2,1)} %get-tuple-element.101), calls=%async_computation.2 | async-start | bytes 262144 | tf_op jit(solution)/shard_map/all_to_all | solution.py:1152
  109.7 6.0 %collective-permute-start.22 = (bf16[4,256,256]{2,1,0:T(8,128)(2,1)S(1)}, bf16[4,256,256]{2,1,0:T(8,128)(2,1)S(1)}, u32[]{:S(2)}, u32[]{:S(2)}) collective-permute-start(bf16[4,256,256]{2,1,0:T(8,128)(2,1)S(1)} %project_units.6), channel_id=1, source_target_pairs={{0,4},{4,0},{8,12},{12,8},{16,20},{20,16},{24,28},{28,24},{1,5},{5... | collective-permute-start | bytes 1572872 | tf_op jit(solution)/shard_map/ppermute | solution.py:239
  112.1 8.0 %collective-permute-start.18 = (bf16[384,256]{1,0:T(8,128)(2,1)}, bf16[384,256]{1,0:T(8,128)(2,1)S(1)}, u32[]{:S(2)}, u32[]{:S(2)}) collective-permute-start(bf16[384,256]{1,0:T(8,128)(2,1)} %get-tuple-element.103), channel_id=1, source_target_pairs={{0,8},{4,12},{8,0},{12,4},{16,24},{20,28},{24,16},{28,20},{1,9},{5... | collective-permute-start | bytes 589832 | tf_op jit(solution)/shard_map/ppermute | solution.py:1126
  113.0 11.1 %collective-permute-start.19 = (bf16[384,256]{1,0:T(8,128)(2,1)}, bf16[384,256]{1,0:T(8,128)(2,1)S(1)}, u32[]{:S(2)}, u32[]{:S(2)}) collective-permute-start(bf16[384,256]{1,0:T(8,128)(2,1)} %get-tuple-element.104), channel_id=1, source_target_pairs={{0,16},{4,20},{8,24},{12,28},{16,0},{20,4},{24,8},{28,12},{1,17},{... | collective-permute-start | bytes 589832 | tf_op jit(solution)/shard_map/ppermute | solution.py:1126
  113.5 10.6 %collective-permute-start.20 = (bf16[384,256]{1,0:T(8,128)(2,1)}, bf16[384,256]{1,0:T(8,128)(2,1)S(1)}, u32[]{:S(2)}, u32[]{:S(2)}) collective-permute-start(bf16[384,256]{1,0:T(8,128)(2,1)} %get-tuple-element.105), channel_id=1, source_target_pairs={{0,24},{4,28},{8,16},{12,20},{16,8},{20,12},{24,0},{28,4},{1,25},{... | collective-permute-start | bytes 589832 | tf_op jit(solution)/shard_map/ppermute | solution.py:1126
  124.3 3.6 %collective-permute-start.21 = (bf16[128,512]{1,0:T(8,128)(2,1)S(1)}, bf16[128,512]{1,0:T(8,128)(2,1)S(1)}, u32[]{:S(2)}, u32[]{:S(2)}) collective-permute-start(bf16[128,512]{1,0:T(8,128)(2,1)S(1)} %get-tuple-element.106.query_ref), channel_id=1, source_target_pairs={{0,4},{4,0},{8,12},{12,8},{16,20},{20,16},{24,28},{28,24},{1,5},{5... | collective-permute-start | bytes 393224 | tf_op jit(solution)/shard_map/ppermute | solution.py:239
  124.4 8.5 %collective-permute-start.23 = (bf16[256,256]{1,0:T(8,128)(2,1)S(1)}, bf16[256,256]{1,0:T(8,128)(2,1)S(1)}, u32[]{:S(2)}, u32[]{:S(2)}) collective-permute-start(bf16[256,256]{1,0:T(8,128)(2,1)S(1)} %get-tuple-element.110), channel_id=1, source_target_pairs={{0,8},{4,12},{8,0},{12,4},{16,24},{20,28},{24,16},{28,20},{1,9},{5... | collective-permute-start | bytes 393224 | tf_op jit(solution)/shard_map/ppermute | solution.py:1126
  125.7 8.4 %collective-permute-start.24 = (bf16[256,256]{1,0:T(8,128)(2,1)S(1)}, bf16[256,256]{1,0:T(8,128)(2,1)S(1)}, u32[]{:S(2)}, u32[]{:S(2)}) collective-permute-start(bf16[256,256]{1,0:T(8,128)(2,1)S(1)} %get-tuple-element.111), channel_id=1, source_target_pairs={{0,16},{4,20},{8,24},{12,28},{16,0},{20,4},{24,8},{28,12},{1,17},{... | collective-permute-start | bytes 393224 | tf_op jit(solution)/shard_map/ppermute | solution.py:1126
  126.5 7.6 %collective-permute-start.25 = (bf16[256,256]{1,0:T(8,128)(2,1)S(1)}, bf16[256,256]{1,0:T(8,128)(2,1)S(1)}, u32[]{:S(2)}, u32[]{:S(2)}) collective-permute-start(bf16[256,256]{1,0:T(8,128)(2,1)S(1)} %get-tuple-element.112), channel_id=1, source_target_pairs={{0,24},{4,28},{8,16},{12,20},{16,8},{20,12},{24,0},{28,4},{1,25},{... | collective-permute-start | bytes 393224 | tf_op jit(solution)/shard_map/ppermute | solution.py:1126
  158.6 6.2 %collective-permute-start.27 = (bf16[32,2048]{1,0:T(8,128)(2,1)S(1)}, bf16[32,2048]{1,0:T(8,128)(2,1)S(1)}, u32[]{:S(2)}, u32[]{:S(2)}) collective-permute-start(bf16[32,2048]{1,0:T(8,128)(2,1)S(1)} %convert_element_type.40.a_ref), channel_id=1, source_target_pairs={{0,1},{1,0},{2,3},{3,2},{4,5},{5,4},{6,7},{7,6},{8,9},{9,8},{10,11... | collective-permute-start | bytes 393224 | tf_op jit(solution)/shard_map/ppermute | solution.py:1131
  158.9 12.2 %collective-permute-start.28 = (bf16[32,2048]{1,0:T(8,128)(2,1)S(1)}, bf16[32,2048]{1,0:T(8,128)(2,1)S(1)}, u32[]{:S(2)}, u32[]{:S(2)}) collective-permute-start(bf16[32,2048]{1,0:T(8,128)(2,1)S(1)} %convert_element_type.40.a_ref), channel_id=1, source_target_pairs={{0,2},{1,3},{2,0},{3,1},{4,6},{5,7},{6,4},{7,5},{8,10},{9,11},{10,... | collective-permute-start | bytes 393224 | tf_op jit(solution)/shard_map/ppermute | solution.py:1131
  160.4 10.7 %collective-permute-start.29 = (bf16[32,2048]{1,0:T(8,128)(2,1)S(1)}, bf16[32,2048]{1,0:T(8,128)(2,1)S(1)}, u32[]{:S(2)}, u32[]{:S(2)}) collective-permute-start(bf16[32,2048]{1,0:T(8,128)(2,1)S(1)} %convert_element_type.40.a_ref), channel_id=1, source_target_pairs={{0,3},{1,2},{2,1},{3,0},{4,7},{5,6},{6,5},{7,4},{8,11},{9,10},{10,... | collective-permute-start | bytes 393224 | tf_op jit(solution)/shard_map/ppermute | solution.py:1131
  171.2 5.0 %collective-permute-start.30 = (bf16[32,2048]{1,0:T(8,128)(2,1)S(1)}, bf16[32,2048]{1,0:T(8,128)(2,1)S(1)}, u32[]{:S(2)}, u32[]{:S(2)}) collective-permute-start(bf16[32,2048]{1,0:T(8,128)(2,1)S(1)} %last_rows.1.refs_0_), channel_id=1, source_target_pairs={{0,8},{4,12},{8,0},{12,4},{16,24},{20,28},{24,16},{28,20},{1,9},{5... | collective-permute-start | bytes 393224 | tf_op jit(solution)/shard_map/ppermute | solution.py:1126
  172.5 5.0 %collective-permute-start.31 = (bf16[32,2048]{1,0:T(8,128)(2,1)S(1)}, bf16[32,2048]{1,0:T(8,128)(2,1)S(1)}, u32[]{:S(2)}, u32[]{:S(2)}) collective-permute-start(bf16[32,2048]{1,0:T(8,128)(2,1)S(1)} %last_rows.1.refs_0_), channel_id=1, source_target_pairs={{0,16},{4,20},{8,24},{12,28},{16,0},{20,4},{24,8},{28,12},{1,17},{... | collective-permute-start | bytes 393224 | tf_op jit(solution)/shard_map/ppermute | solution.py:1126
  173.0 5.9 %collective-permute-start.32 = (bf16[32,2048]{1,0:T(8,128)(2,1)S(1)}, bf16[32,2048]{1,0:T(8,128)(2,1)S(1)}, u32[]{:S(2)}, u32[]{:S(2)}) collective-permute-start(bf16[32,2048]{1,0:T(8,128)(2,1)S(1)} %last_rows.1.refs_0_), channel_id=1, source_target_pairs={{0,24},{4,28},{8,16},{12,20},{16,8},{20,12},{24,0},{28,4},{1,25},{... | collective-permute-start | bytes 393224 | tf_op jit(solution)/shard_map/ppermute | solution.py:1126
  174.7 4.2 %collective-permute-start.33 = (bf16[32,2048]{1,0:T(8,128)(2,1)S(1)}, bf16[32,2048]{1,0:T(8,128)(2,1)S(1)}, u32[]{:S(2)}, u32[]{:S(2)}) collective-permute-start(bf16[32,2048]{1,0:T(8,128)(2,1)S(1)} %last_rows.1.refs_0_), channel_id=1, source_target_pairs={{0,4},{4,0},{8,12},{12,8},{16,20},{20,16},{24,28},{28,24},{1,5},{5... | collective-permute-start | bytes 393224 | tf_op jit(solution)/shard_map/ppermute | solution.py:239
  176.2 2.7 %collective-permute-start.34 = (bf16[32,2048]{1,0:T(8,128)(2,1)S(1)}, bf16[32,2048]{1,0:T(8,128)(2,1)S(1)}, u32[]{:S(2)}, u32[]{:S(2)}) collective-permute-start(bf16[32,2048]{1,0:T(8,128)(2,1)S(1)} %collective-permute-done.30.refs_1_), channel_id=1, source_target_pairs={{0,4},{4,0},{8,12},{12,8},{16,20},{20,16},{24,28},{28,24},{1,5},{5... | collective-permute-start | bytes 393224 | tf_op jit(solution)/shard_map/ppermute | solution.py:239
  (26 other events, 328.6 us)

commit v5 on v4

--- a/solution.py
+++ b/solution.py
@@ -474,30 +474,37 @@
     )(near, far, own)
 
 
-def gather_kernel(a_ref, b_ref, c_ref, d_ref, out_ref):
+def gather_kernel(a_ref, b_ref, c_ref, d_ref, out_hbm, out_ref, semaphore):
     rows = out_ref.shape[0] - 16
     near = a_ref[...].astype(jnp.float32) + b_ref[...].astype(jnp.float32)
     far = c_ref[...].astype(jnp.float32) + d_ref[...].astype(jnp.float32)
     total = near + far
     out_ref[:rows] = total[:rows].astype(jnp.bfloat16)
     out_ref[rows:] = row_sums(from_row_sums(total[rows:]))
+    copy = pltpu.make_async_copy(out_ref, out_hbm, semaphore)
+    copy.start()
+    copy.wait()
 
 
 def gather(parts):
     return pl.pallas_call(
         gather_kernel,
-        out_shape=jax.ShapeDtypeStruct(parts[0].shape, jnp.bfloat16),
+        out_shape=pltpu.HBM(parts[0].shape, jnp.bfloat16),
         in_specs=[whole()] * 4,
-        out_specs=whole(),
+        out_specs=whole(pltpu.HBM),
+        scratch_shapes=[pltpu.VMEM(parts[0].shape, jnp.bfloat16), pltpu.SemaphoreType.DMA],
         compiler_params=compiler_params(16),
         name="gather",
     )(*parts)
 
 
-def first_kernel(a_ref, b_ref, c_ref, d_ref, gain_ref, bias_ref, start_ref, hidden_ref):
+def first_kernel(a_hbm, b_ref, c_ref, d_ref, gain_ref, bias_ref, start_ref, hidden_ref, a_ref, semaphore):
     rows, unit = hidden_ref.shape
-    parts = [ref[...].astype(jnp.float32) for ref in (a_ref, b_ref, c_ref, d_ref)]
-    total = (parts[0] + parts[1]) + (parts[2] + parts[3])
+    copy = pltpu.make_async_copy(a_hbm, a_ref, semaphore)
+    copy.start()
+    far = c_ref[...].astype(jnp.float32) + d_ref[...].astype(jnp.float32)
+    copy.wait()
+    total = (a_ref[...].astype(jnp.float32) + b_ref[...].astype(jnp.float32)) + far
     mean, scale = (row_to_column(line) for line in from_row_sums(total[rows:]))
     columns = pl.ds(pl.multiple_of(lax.axis_index("seq") * unit, unit), unit)
     gain, bias = gain_ref[0:1, columns], bias_ref[0:1, columns]
@@ -513,20 +520,17 @@
     return pl.pallas_call(
         first_kernel,
         out_shape=(one, one),
-        in_specs=[whole()] * 6,
+        in_specs=[whole(pltpu.HBM)] + [whole()] * 5,
         out_specs=(whole(), whole()),
+        scratch_shapes=[pltpu.VMEM(parts[0].shape, jnp.bfloat16), pltpu.SemaphoreType.DMA],
         compiler_params=compiler_params(16),
         name="first_hidden",
-    )(*parts, ln_gain, ln_bias)
+    )(in_hbm(parts[0]), *parts[1:], ln_gain, ln_bias)
 
 
 def norm_kernel(layer_index, tp_count, *refs):
-    part_ref, *state_refs, gain_ref, bias_ref, next_ref, cut_ref = refs
-    state = part_ref[0].astype(jnp.float32)
-    for source in range(1, part_ref.shape[0]):
-        state = state + part_ref[source].astype(jnp.float32)
-    for ref in state_refs:
-        state = state + ref[...]
+    *part_refs, gain_ref, bias_ref, next_ref, cut_ref = refs
+    state = functools.reduce(jnp.add, [ref[...].astype(jnp.float32) for ref in part_refs])
     next_ref[...] = state
     average = jnp.mean(state, axis=-1, keepdims=True)
     centred = state - average
@@ -541,9 +545,9 @@
 
 
 def norm_rows(parts, state, ln_gain, ln_bias, layer_index, devices, tp_count):
-    count, rows, width = parts.shape
+    rows, width = parts[0].shape
     cut = width // (devices // tp_count)
-    operands = [parts] + ([] if state is None else [state]) + [ln_gain, ln_bias]
+    operands = list(parts) + ([] if state is None else [state]) + [ln_gain, ln_bias]
     return pl.pallas_call(
         functools.partial(norm_kernel, layer_index, tp_count),
         out_shape=(
@@ -557,10 +561,34 @@
     )(*operands)
 
 
-def last_parts_kernel(tp_count, part_ref, state_ref, out_ref):
-    total = part_ref[0].astype(jnp.float32)
-    for chip in range(1, part_ref.shape[0]):
-        total = total + part_ref[chip].astype(jnp.float32)
+def share_kernel(a_ref, b_ref, c_ref, d_ref, *out_refs):
+    total = functools.reduce(jnp.add, [ref[...].astype(jnp.float32) for ref in (a_ref, b_ref, c_ref, d_ref)])
+    mine = out_refs[0].shape[0]
+    for owner in range(len(out_refs)):
+        for distance, ref in enumerate(out_refs):
+            @pl.when(lax.axis_index("tp") == owner ^ distance)
+            def put(ref=ref, owner=owner):
+                ref[...] = total[owner * mine : (owner + 1) * mine].astype(ref.dtype)
+
+
+def share_rows(parts, tp_count):
+    rows, width = parts[0].shape
+    one = (rows // tp_count, width)
+    return pl.pallas_call(
+        share_kernel,
+        out_shape=(jax.ShapeDtypeStruct(one, jnp.float32),)
+        + (jax.ShapeDtypeStruct(one, jnp.bfloat16),) * (tp_count - 1),
+        in_specs=[whole()] * 4,
+        out_specs=(whole(),) * tp_count,
+        compiler_params=compiler_params(16),
+        name="share_rows",
+    )(*parts)
+
+
+def last_parts_kernel(tp_count, a_ref, b_ref, c_ref, d_ref, state_ref, out_ref):
+    near = a_ref[...].astype(jnp.float32) + b_ref[...].astype(jnp.float32)
+    far = c_ref[...].astype(jnp.float32) + d_ref[...].astype(jnp.float32)
+    total = near + far
     mine = state_ref.shape[0]
     owner = lax.axis_index("tp")
     for place in range(tp_count):
@@ -572,12 +600,46 @@
 def last_parts(parts, state, tp_count):
     return pl.pallas_call(
         functools.partial(last_parts_kernel, tp_count),
-        out_shape=jax.ShapeDtypeStruct(parts.shape[1:], jnp.float32),
-        in_specs=[whole(), whole()],
+        out_shape=jax.ShapeDtypeStruct(parts[0].shape, jnp.float32),
+        in_specs=[whole()] * 5,
         out_specs=whole(),
         compiler_params=compiler_params(16),
         name="last_parts",
-    )(parts, state)
+    )(*parts, state)
+
+
+def split_kernel(half_ref, arrived_ref, out_ref, *refs):
+    *out_hbms, leave_ref, semaphores = refs
+    share = out_ref.shape[0]
+    leaving = []
+    for distance in reversed(range(CHIPS)):
+        rows = slice(distance * share, (distance + 1) * share)
+        joined = half_ref[rows] + arrived_ref[rows].astype(jnp.float32)
+        if distance:
+            leave_ref[distance - 1] = joined.astype(jnp.bfloat16)
+            leaving.append(
+                pltpu.make_async_copy(
+                    leave_ref.at[distance - 1], out_hbms[distance - 1], semaphores.at[distance - 1]
+                )
+            )
+            leaving[-1].start()
+        else:
+            out_ref[...] = joined
+    for copy in leaving:
+        copy.wait()
+
+
+def split(half, arrived):
+    one = (half.shape[0] // CHIPS, half.shape[1])
+    return pl.pallas_call(
+        split_kernel,
+        out_shape=(jax.ShapeDtypeStruct(one, jnp.float32),) + (pltpu.HBM(one, jnp.bfloat16),) * (CHIPS - 1),
+        in_specs=[whole()] * 2,
+        out_specs=(whole(),) + (whole(pltpu.HBM),) * (CHIPS - 1),
+        scratch_shapes=[pltpu.VMEM((CHIPS - 1,) + one, jnp.bfloat16), pltpu.SemaphoreType.DMA((CHIPS - 1,))],
+        compiler_params=compiler_params(16),
+        name="split",
+    )(half, arrived)
 
 
 def last_kernel(a_ref, b_ref, c_ref, d_ref, out_ref):
@@ -628,10 +690,11 @@
 
 
 def restore_kernel(near_back_ref, far_back_ref, *refs):
-    *row_refs, out_ref = refs
+    *row_refs, out_hbm, out_ref, semaphores = refs
     requests, new_tokens, width = out_ref.shape
-    step = 2 * LANES
-    for start in range(0, width, step):
+    step = width // semaphores.shape[0]
+    leaving = []
+    for index, start in enumerate(range(0, width, step)):
         span = slice(start, start + step)
         near, far = (
             jnp.concatenate([ref[:, span] for ref in half], axis=0)
@@ -641,15 +704,24 @@
             far_back_ref[...], far, preferred_element_type=jnp.float32
         )
         out_ref[:, :, span] = rows.reshape(requests, new_tokens, step)
+        span = pl.ds(start, step)
+        leaving.append(
+            pltpu.make_async_copy(out_ref.at[:, :, span], out_hbm.at[:, :, span], semaphores.at[index])
+        )
+        leaving[-1].start()
+    for copy in leaving:
+        copy.wait()
 
 
 def restore(backs, near, far, new_tokens):
     rows = backs[0].shape[0]
+    shape = (rows // new_tokens, new_tokens, near[0].shape[1])
     return pl.pallas_call(
         restore_kernel,
-        out_shape=jax.ShapeDtypeStruct((rows // new_tokens, new_tokens, near[0].shape[1]), jnp.float32),
+        out_shape=pltpu.HBM(shape, jnp.float32),
         in_specs=[whole()] * (2 + 2 * CHIPS),
-        out_specs=whole(),
+        out_specs=whole(pltpu.HBM),
+        scratch_shapes=[pltpu.VMEM(shape, jnp.float32), pltpu.SemaphoreType.DMA((4,))],
         compiler_params=compiler_params(24),
         name="restore",
     )(*backs, *near, *far)
@@ -1033,27 +1105,32 @@
     place = seq_index % (lanes // share)
     scale = scale_ref[pl.ds(pl.multiple_of(place * share, share), share), :]
     scale = jnp.where(parity == 0, scale, pltpu.roll(scale, lanes - 1, 1))
+    here = lax.axis_index("seq") // 2
+    next_scale = pltpu.roll(scale, lanes - 2, 1)
     lane = lax.broadcasted_iota(jnp.int32, (share, lanes), 1)
     first, second = [], []
     for pair in range(CHIPS // 2):
-        rows = pl.ds(pl.multiple_of((2 * pair + parity) * share, share), share)
+        pack = (here % 2) ^ pair
+        rows = pl.ds(pl.multiple_of((2 * pack + parity) * share, share), share)
+        pair_scale = jnp.where(pack == 0, scale, next_scale)
         mixed = jnp.zeros((share, lanes), jnp.float32)
         for source in range(sources):
-            column = source * groups + 2 * pair
-            left = scale[:, column : column + 1]
-            right = scale[:, column + groups // 2 : column + groups // 2 + 1]
+            column = source * groups
+            left = pair_scale[:, column : column + 1]
+            right = pair_scale[:, column + groups // 2 : column + groups // 2 + 1]
             mixed = mixed + part_ref[source, rows, :].astype(jnp.float32) * jnp.where(
                 lane < HEAD_DIM, left, right
             )
-        first.append(mixed[:, :HEAD_DIM])
-        second.append(pltpu.roll(mixed, HEAD_DIM, 1)[:, :HEAD_DIM])
+        turned = pltpu.roll(mixed, HEAD_DIM, 1)
+        first.append(jnp.where(here < 2, mixed, turned)[:, :HEAD_DIM])
+        second.append(jnp.where(here < 2, turned, mixed)[:, :HEAD_DIM])
     attended = jnp.concatenate(first + second, axis=0).astype(jnp.bfloat16)
     bias = bias_ref[
         layer_index : layer_index + 1, pl.ds(pl.multiple_of(seq_index * unit, unit), unit)
     ]
     hidden, started = [], []
     for piece in range(CHIPS):
-        rows = pl.ds(pl.multiple_of((2 * piece + parity) * share, share), share)
+        rows = pl.ds(pl.multiple_of((2 * (piece ^ here) + parity) * share, share), share)
         pre = functools.reduce(jnp.add, [ref[rows, :].astype(jnp.float32) for ref in unit_refs])
         hidden.append(jax.nn.gelu(pre + bias, approximate=True).astype(jnp.bfloat16))
         if has_start:
@@ -1107,19 +1184,9 @@
     rows = requests * new_tokens
     groups = prefix_len.shape[0]
     share = rows // seq_count
-    mine = rows // devices
     features = embedding.shape[1]
     width_local = k_cache.shape[2]
     unit = w_fc2.shape[1]
-    same_core = [[s * tp_count + p for s in range(c, seq_count, 2) for p in range(tp_count)] for c in range(2)]
-    same_core_seq = [list(range(c, seq_count, 2)) for c in range(2)]
-
-    def to_owners(half):
-        parts = half.reshape(devices // 2, mine, features)
-        return lax.all_to_all(parts, ("seq", "tp"), 0, 0, axis_index_groups=same_core)
-
-    def to_chips(parts):
-        return lax.all_to_all(parts, "seq", 0, 0, axis_index_groups=same_core_seq)
 
     def to_distances(parts):
         return [parts[0]] + [
@@ -1142,7 +1209,9 @@
     backs = back_rows(group_of, new_tokens)
     tables = rotary_tables(own_positions.reshape(-1), 2 * HEAD_DIM)
     weights_qkv = w_qkv[0].reshape(w_qkv.shape[1], -1)
-    parts, backs, tables, visits = lax.optimization_barrier((from_tp(gathered), backs, tables, visits))
+    parts, backs, tables, visits = lax.optimization_barrier(
+        (from_tp(gathered), backs, tables, visits)
+    )
     start, hidden = first_hidden(parts, ln_gain, ln_bias)
     state = None
     for layer_index in range(LAYERS):
@@ -1166,11 +1235,12 @@
             update(parts, units, start, b_fc1, w_out, w_fc2, layer_index, other, tp_count)
             for other in (True, False)
         )
-        half = (half + swap_cores(arriving, seq_count).astype(jnp.float32)).astype(jnp.bfloat16)
+        parts = to_distances(split(half, swap_cores(arriving, seq_count)))
         start = None
         if layer_index < LAYERS - 1:
-            parts = to_owners(half)
-    last = last_parts(to_chips(half.reshape(CHIPS, share, features)), state, tp_count)
+            parts = share_rows(parts, tp_count)
+            parts = [parts[0]] + [over_tp(parts[k], k) for k in range(1, tp_count)]
+    last = last_parts(parts, state, tp_count)
     last = from_tp(last.astype(jnp.bfloat16))
     last = to_distances([last_rows(last)] * CHIPS)
     return restore(backs, last, [swap_cores(part, seq_count) for part in last], new_tokens)

time: 183 us -> 179 us (0.978)
  blocking collectives: 52.4 us -> 20.2 us
  waiting for transfers between devices: 52.6 us -> 66.5 us
  starting transfers between devices: 35.9 us -> 47.8 us
  Pallas kernels: 30.8 us -> 34 us
    all_to_all x2 -> x0, blocking collectives: 32.2 us -> none  [the longest x1 20.7 us: to_owners(): lax.all_to_all(parts, ('seq', 'tp'), 0, 0, axis_index_groups=same_core)]
    ppermute x18 -> x24, waiting for transfers between devices: 27.2 us -> 37.8 us  [to_distances(): lax.ppermute(parts[k], 'seq', [(i, i ^ 2 * k) for i in range(seq_count)])]
    ppermute x18 -> x24, starting transfers between devices: 22.2 us -> 29.3 us  [to_distances(): lax.ppermute(parts[k], 'seq', [(i, i ^ 2 * k) for i in range(seq_count)])]
    ppermute x6 -> x9, waiting for transfers between devices: 13.9 us -> 18.5 us  [over_tp(): lax.ppermute(part, 'tp', [(i, i ^ distance) for i in range(tp_count)])]
    ppermute x6 -> x9, starting transfers between devices: 8.9 us -> 13.5 us  [over_tp(): lax.ppermute(part, 'tp', [(i, i ^ distance) for i in range(tp_count)])]
    pallas_call x3 -> x6, Pallas kernels: 2.26 us -> 5.21 us  [the longest x1 1.63 us: restore(): pl.pallas_call(restore_kernel, out_shape=pltpu.HBM(shape, jnp.float32), i...]
    unnamed x42 -> x36, local copies, waits for them, and re-layouts: 4.61 us -> 4.24 us
  transfers between devices with their start and end apart: 38 -> 47, of which waited for: 21 -> 27; matrix products, arithmetic and copies ran while one was open for 4% -> 5% of each run, Pallas kernels for 10% -> 10%
where the time goes in v5:
time: 179 us
  waiting for transfers between devices  66.5 us (37%)
  starting transfers between devices  47.8 us (27%)
  Pallas kernels  34 us (19%)
  blocking collectives  20.2 us (11%)
  local copies, waits for them, and re-layouts  9.08 us (5%)
    ppermute x24, waiting for transfers between devices, to_distances(): lax.ppermute(parts[k], 'seq', [(i, i ^ 2 * k) for i in range(seq_count)])  37.8 us
    ppermute x24, starting transfers between devices, to_distances(): lax.ppermute(parts[k], 'seq', [(i, i ^ 2 * k) for i in range(seq_count)])  29.3 us
    all_to_all x2, blocking collectives, per_device(): parts = lax.all_to_all(parts, 'seq', 0, 0)  20.2 us
    ppermute x9, waiting for transfers between devices, over_tp(): lax.ppermute(part, 'tp', [(i, i ^ distance) for i in range(tp_count)])  18.5 us
    ppermute x9, starting transfers between devices, over_tp(): lax.ppermute(part, 'tp', [(i, i ^ distance) for i in range(tp_count)])  13.5 us
    pallas_call x2, Pallas kernels, attend(): pl.pallas_call(functools.partial(attend_kernel, layer_index, new_tokens),...  9.92 us
    pallas_call x1, Pallas kernels, embed(): pl.pallas_call(embed_kernel, out_shape=(jax.ShapeDtypeStruct((CHIPS, rows...  6.08 us
    ppermute x13, waiting for transfers between devices, swap_cores(): return lax.ppermute(values, 'seq', [(i, i ^ 1) for i in range(seq_count)])  5.66 us
  transfers between devices with their start and end apart: 47, of which 27 were waited for; matrix products, arithmetic and copies ran while one was open for 5% of the time, Pallas kernels for 10%

profile of v5, /device:TPU:0, one launch (start us, length us, event | category | flops | bytes accessed | tf_op | source)
XLA Modules:
  0.0 178.7 jit_solution(5637222934604999075)
XLA Ops:
  0.0 6.1 %embed.1 = (bf16[4,256,256]{2,1,0:T(8,128)(2,1)S(1)}, bf16[1040,256]{1,0:T(8,128)(2,1)}, f32[8,256]{1,0:T(8,128)S(1)}) custom-call(s32[4,64]{1,0:T(4,128)} %bitcast.15, s32[1,64]{1,0:T(1,128)} %bitcast.11, bf16[1600,2048]{1,0:T(8,128)(2,1)} %table_hbm.1), custom_call_target="tpu_custom_call" | custom-call | tf_op jit(solution)/shard_map/embed/pallas_call | solution.py:416
  9.2 2.9 %collective-permute-start.1 = (bf16[272,256]{1,0:T(8,128)(2,1)}, bf16[272,256]{1,0:T(8,128)(2,1)S(1)}, u32[]{:S(2)}, u32[]{:S(2)}) collective-permute-start(bf16[272,256]{1,0:T(8,128)(2,1)} %get-tuple-element.78), channel_id=1, source_target_pairs={{0,8},{4,12},{8,0},{12,4},{16,24},{20,28},{24,16},{28,20},{1,9},{5... | collective-permute-start | bytes 417800 | tf_op jit(solution)/shard_map/ppermute | solution.py:1193
  16.6 4.2 %collective-permute-done.2.c_ref = bf16[272,256]{1,0:T(8,128)(2,1)S(1)} collective-permute-done((bf16[272,256]{1,0:T(8,128)(2,1)}, bf16[272,256]{1,0:T(8,128)(2,1)S(1)}, u32[]{:S(2)}, u32[]{:S(2)}) %collective-permute-start.2) | collective-permute-done | bytes 139296 | tf_op jit(solution)/shard_map/ppermute | solution.py:1193
  21.6 1.6 collective-permute-start.4
  23.2 2.6 %collective-permute-start.5 = (bf16[272,256]{1,0:T(8,128)(2,1)}, bf16[272,256]{1,0:T(8,128)(2,1)S(1)}, u32[]{:S(2)}, u32[]{:S(2)}) collective-permute-start(bf16[272,256]{1,0:T(8,128)(2,1)} %gather.1.a_hbm), channel_id=1, source_target_pairs={{0,2},{1,3},{2,0},{3,1},{4,6},{5,7},{6,4},{7,5},{8,10},{9,11},{10,... | collective-permute-start | bytes 417800 | tf_op jit(solution)/shard_map/ppermute | solution.py:1198
  26.0 2.5 %order_requests.1 = (s32[64]{0:T(128)}, s32[256]{0:T(256)}, s32[64]{0:T(128)}) custom-call(s32[64]{0:T(128)} %group_ref, s32[8]{0:T(128)} %prefix_ref.1, s32[64]{0:T(128)} %tail_ref.1, s32[2,16]{1,0:T(2,128)} %bitcast.16), custom_call_target="tpu_custom_call" | custom-call | tf_op jit(solution)/shard_map/order_requests/pallas_call | solution.py:303
  30.1 6.1 %collective-permute-done.5.c_ref = bf16[272,256]{1,0:T(8,128)(2,1)S(1)} collective-permute-done((bf16[272,256]{1,0:T(8,128)(2,1)}, bf16[272,256]{1,0:T(8,128)(2,1)S(1)}, u32[]{:S(2)}, u32[]{:S(2)}) %collective-permute-start.5) | collective-permute-done | bytes 139296 | tf_op jit(solution)/shard_map/ppermute | solution.py:1198
  44.0 4.5 %collective-permute-done.8.b_ref = bf16[384,256]{1,0:T(8,128)(2,1)S(1)} collective-permute-done((bf16[384,256]{1,0:T(8,128)(2,1)}, bf16[384,256]{1,0:T(8,128)(2,1)S(1)}, u32[]{:S(2)}, u32[]{:S(2)}) %collective-permute-start.8) | collective-permute-done | bytes 196640 | tf_op jit(solution)/shard_map/ppermute | solution.py:1193
  48.5 4.6 %collective-permute-done.9.c_ref = bf16[384,256]{1,0:T(8,128)(2,1)S(1)} collective-permute-done((bf16[384,256]{1,0:T(8,128)(2,1)}, bf16[384,256]{1,0:T(8,128)(2,1)S(1)}, u32[]{:S(2)}, u32[]{:S(2)}) %collective-permute-start.9) | collective-permute-done | bytes 196640 | tf_op jit(solution)/shard_map/ppermute | solution.py:1193
  57.4 5.0 %attend.2 = bf16[8,160,128]{2,1,0:T(8,128)(2,1)S(1)} custom-call(s32[64]{0:T(128)} %get-tuple-element.89.visit_hbm, bf16[128,512]{1,0:T(8,128)(2,1)S(1)} %get-tuple-element.100.query_ref, bf16[128,512]{1,0:T(8,128)(2,1)S(1)} %collective-permute-done.11.far_query_ref, bf16[32,512]{1,0:T(8,128)(2,1)S(1)} %get-tuple-element.101.new_key_ref, ...), custom_call_target="tpu_custom_call" | custom-call | tf_op jit(solution)/shard_map/attend/pallas_call | solution.py:1061
  62.8 10.2 %all_to_all.15.part_ref = bf16[8,160,128]{2,1,0:T(8,128)(2,1)S(1)} all-to-all(bf16[8,160,128]{2,1,0:T(8,128)(2,1)S(1)} %attend.2), channel_id=1, replica_groups=mesh['seq'=8,'tp'=4] {'seq'}, dimensions={0} | all-to-all | bytes 655360 | tf_op jit(solution)/shard_map/all_to_all | solution.py:1233
  77.9 2.4 %collective-permute-start.19 = (bf16[32,2048]{1,0:T(8,128)(2,1)}, bf16[32,2048]{1,0:T(8,128)(2,1)S(1)}, u32[]{:S(2)}, u32[]{:S(2)}) collective-permute-start(bf16[32,2048]{1,0:T(8,128)(2,1)} %get-tuple-element.116), channel_id=1, source_target_pairs={{0,24},{4,28},{8,16},{12,20},{16,8},{20,12},{24,0},{28,4},{1,25},{... | collective-permute-start | bytes 393224 | tf_op jit(solution)/shard_map/ppermute | solution.py:1193
  80.3 3.1 %collective-permute-done.17.b_ref = bf16[32,2048]{1,0:T(8,128)(2,1)S(1)} collective-permute-done((bf16[32,2048]{1,0:T(8,128)(2,1)}, bf16[32,2048]{1,0:T(8,128)(2,1)S(1)}, u32[]{:S(2)}, u32[]{:S(2)}) %collective-permute-start.17) | collective-permute-done | bytes 131104 | tf_op jit(solution)/shard_map/ppermute | solution.py:1193
  83.4 2.3 %collective-permute-done.18.c_ref = bf16[32,2048]{1,0:T(8,128)(2,1)S(1)} collective-permute-done((bf16[32,2048]{1,0:T(8,128)(2,1)}, bf16[32,2048]{1,0:T(8,128)(2,1)S(1)}, u32[]{:S(2)}, u32[]{:S(2)}) %collective-permute-start.18) | collective-permute-done | bytes 131104 | tf_op jit(solution)/shard_map/ppermute | solution.py:1193
  85.8 2.1 %collective-permute-start.20 = (bf16[8,2048]{1,0:T(8,128)(2,1)S(1)}, bf16[8,2048]{1,0:T(8,128)(2,1)S(1)}, u32[]{:S(2)}, u32[]{:S(2)}) collective-permute-start(bf16[8,2048]{1,0:T(8,128)(2,1)S(1)} %get-tuple-element.118), channel_id=1, source_target_pairs={{0,1},{1,0},{2,3},{3,2},{4,5},{5,4},{6,7},{7,6},{8,9},{9,8},{10,11... | collective-permute-start | bytes 98312 | tf_op jit(solution)/shard_map/ppermute | solution.py:1198
  90.4 2.9 %collective-permute-done.21.refs_2_ = bf16[8,2048]{1,0:T(8,128)(2,1)S(1)} collective-permute-done((bf16[8,2048]{1,0:T(8,128)(2,1)S(1)}, bf16[8,2048]{1,0:T(8,128)(2,1)S(1)}, u32[]{:S(2)}, u32[]{:S(2)}) %collective-permute-start.21) | collective-permute-done | bytes 32800 | tf_op jit(solution)/shard_map/ppermute | solution.py:1198
  96.2 2.8 %all-to-all-start.1 = ((bf16[32,8,256]{2,1,0:T(8,128)(2,1)}), bf16[32,8,256]{2,1,0:T(8,128)(2,1)S(1)}, u32[]{:S(2)}, u32[]{:S(2)}) async-start(bf16[32,8,256]{2,1,0:T(8,128)(2,1)} %get-tuple-element.121), calls=%async_computation.1 | async-start | bytes 262144 | tf_op jit(solution)/shard_map/all_to_all | solution.py:1221
  99.0 2.3 %copy.25 = bf16[1,256,3,512]{1,3,2,0:T(8,128)(2,1)} copy(bf16[1,256,3,512]{3,1,2,0:T(8,128)(2,1)} %get-tuple-element.143) | data formatting | bytes 1572864
  102.8 4.5 %all-to-all-done.1 = bf16[32,8,256]{2,1,0:T(8,128)(2,1)S(1)} async-done(((bf16[32,8,256]{2,1,0:T(8,128)(2,1)}), bf16[32,8,256]{2,1,0:T(8,128)(2,1)S(1)}, u32[]{:S(2)}, u32[]{:S(2)}) %all-to-all-start.1) | async-done | bytes 131104 | tf_op jit(solution)/shard_map/all_to_all | solution.py:1221
  111.8 2.2 %collective-permute-start.26 = (bf16[384,256]{1,0:T(8,128)(2,1)}, bf16[384,256]{1,0:T(8,128)(2,1)S(1)}, u32[]{:S(2)}, u32[]{:S(2)}) collective-permute-start(bf16[384,256]{1,0:T(8,128)(2,1)} %get-tuple-element.125), channel_id=1, source_target_pairs={{0,24},{4,28},{8,16},{12,20},{16,8},{20,12},{24,0},{28,4},{1,25},{... | collective-permute-start | bytes 589832 | tf_op jit(solution)/shard_map/ppermute | solution.py:1193
  114.3 4.1 %collective-permute-done.24.b_ref = bf16[384,256]{1,0:T(8,128)(2,1)S(1)} collective-permute-done((bf16[384,256]{1,0:T(8,128)(2,1)}, bf16[384,256]{1,0:T(8,128)(2,1)S(1)}, u32[]{:S(2)}, u32[]{:S(2)}) %collective-permute-start.24) | collective-permute-done | bytes 196640 | tf_op jit(solution)/shard_map/ppermute | solution.py:1193
  118.5 3.9 %collective-permute-done.25.c_ref = bf16[384,256]{1,0:T(8,128)(2,1)S(1)} collective-permute-done((bf16[384,256]{1,0:T(8,128)(2,1)}, bf16[384,256]{1,0:T(8,128)(2,1)S(1)}, u32[]{:S(2)}, u32[]{:S(2)}) %collective-permute-start.25) | collective-permute-done | bytes 196640 | tf_op jit(solution)/shard_map/ppermute | solution.py:1193
  126.3 4.9 %attend.3 = bf16[8,160,128]{2,1,0:T(8,128)(2,1)S(1)} custom-call(s32[64]{0:T(128)} %get-tuple-element.89.visit_hbm, bf16[128,512]{1,0:T(8,128)(2,1)S(1)} %get-tuple-element.126.query_ref, bf16[128,512]{1,0:T(8,128)(2,1)S(1)} %collective-permute-done.27.far_query_ref, bf16[32,512]{1,0:T(8,128)(2,1)S(1)} %get-tuple-element.127.new_key_ref, ...), custom_call_target="tpu_custom_call" | custom-call | tf_op jit(solution)/shard_map/attend/pallas_call | solution.py:1061
  132.4 10.0 %all_to_all.16.part_ref = bf16[8,160,128]{2,1,0:T(8,128)(2,1)S(1)} all-to-all(bf16[8,160,128]{2,1,0:T(8,128)(2,1)S(1)} %attend.3), channel_id=1, replica_groups=mesh['seq'=8,'tp'=4] {'seq'}, dimensions={0} | all-to-all | bytes 655360 | tf_op jit(solution)/shard_map/all_to_all | solution.py:1233
  147.3 2.4 %collective-permute-start.35 = (bf16[32,2048]{1,0:T(8,128)(2,1)}, bf16[32,2048]{1,0:T(8,128)(2,1)S(1)}, u32[]{:S(2)}, u32[]{:S(2)}) collective-permute-start(bf16[32,2048]{1,0:T(8,128)(2,1)} %get-tuple-element.141), channel_id=1, source_target_pairs={{0,24},{4,28},{8,16},{12,20},{16,8},{20,12},{24,0},{28,4},{1,25},{... | collective-permute-start | bytes 393224 | tf_op jit(solution)/shard_map/ppermute | solution.py:1193
  149.7 3.1 %collective-permute-done.33.b_ref = bf16[32,2048]{1,0:T(8,128)(2,1)S(1)} collective-permute-done((bf16[32,2048]{1,0:T(8,128)(2,1)}, bf16[32,2048]{1,0:T(8,128)(2,1)S(1)}, u32[]{:S(2)}, u32[]{:S(2)}) %collective-permute-start.33) | collective-permute-done | bytes 131104 | tf_op jit(solution)/shard_map/ppermute | solution.py:1193
  152.7 2.3 %collective-permute-done.34.c_ref = bf16[32,2048]{1,0:T(8,128)(2,1)S(1)} collective-permute-done((bf16[32,2048]{1,0:T(8,128)(2,1)}, bf16[32,2048]{1,0:T(8,128)(2,1)S(1)}, u32[]{:S(2)}, u32[]{:S(2)}) %collective-permute-start.34) | collective-permute-done | bytes 131104 | tf_op jit(solution)/shard_map/ppermute | solution.py:1193
  157.0 2.6 %collective-permute-start.38 = (bf16[32,2048]{1,0:T(8,128)(2,1)S(1)}, bf16[32,2048]{1,0:T(8,128)(2,1)S(1)}, u32[]{:S(2)}, u32[]{:S(2)}) collective-permute-start(bf16[32,2048]{1,0:T(8,128)(2,1)S(1)} %convert_element_type.24.a_ref), channel_id=1, source_target_pairs={{0,3},{1,2},{2,1},{3,0},{4,7},{5,6},{6,5},{7,4},{8,11},{9,10},{10,... | collective-permute-start | bytes 393224 | tf_op jit(solution)/shard_map/ppermute | solution.py:1198
  159.6 1.8 collective-permute-done.36.b_ref
  161.3 6.4 %collective-permute-done.37.c_ref = bf16[32,2048]{1,0:T(8,128)(2,1)S(1)} collective-permute-done((bf16[32,2048]{1,0:T(8,128)(2,1)S(1)}, bf16[32,2048]{1,0:T(8,128)(2,1)S(1)}, u32[]{:S(2)}, u32[]{:S(2)}) %collective-permute-start.37) | collective-permute-done | bytes 131104 | tf_op jit(solution)/shard_map/ppermute | solution.py:1198
  169.7 1.7 collective-permute-start.41
  173.3 2.2 %collective-permute-done.41.refs_3_ = bf16[32,2048]{1,0:T(8,128)(2,1)S(1)} collective-permute-done((bf16[32,2048]{1,0:T(8,128)(2,1)S(1)}, bf16[32,2048]{1,0:T(8,128)(2,1)S(1)}, u32[]{:S(2)}, u32[]{:S(2)}) %collective-permute-start.41) | collective-permute-done | bytes 131104 | tf_op jit(solution)/shard_map/ppermute | solution.py:1193
  (141 shorter events, 57.8 us)
Async XLA Ops:
  9.2 7.4 %collective-permute-start.1 = (bf16[272,256]{1,0:T(8,128)(2,1)}, bf16[272,256]{1,0:T(8,128)(2,1)S(1)}, u32[]{:S(2)}, u32[]{:S(2)}) collective-permute-start(bf16[272,256]{1,0:T(8,128)(2,1)} %get-tuple-element.78), channel_id=1, source_target_pairs={{0,8},{4,12},{8,0},{12,4},{16,24},{20,28},{24,16},{28,20},{1,9},{5... | collective-permute-start | bytes 417800 | tf_op jit(solution)/shard_map/ppermute | solution.py:1193
  12.2 8.6 %collective-permute-start.2 = (bf16[272,256]{1,0:T(8,128)(2,1)}, bf16[272,256]{1,0:T(8,128)(2,1)S(1)}, u32[]{:S(2)}, u32[]{:S(2)}) collective-permute-start(bf16[272,256]{1,0:T(8,128)(2,1)} %get-tuple-element.79), channel_id=1, source_target_pairs={{0,16},{4,20},{8,24},{12,28},{16,0},{20,4},{24,8},{28,12},{1,17},{... | collective-permute-start | bytes 417800 | tf_op jit(solution)/shard_map/ppermute | solution.py:1193
  13.7 7.1 %collective-permute-start.3 = (bf16[272,256]{1,0:T(8,128)(2,1)}, bf16[272,256]{1,0:T(8,128)(2,1)S(1)}, u32[]{:S(2)}, u32[]{:S(2)}) collective-permute-start(bf16[272,256]{1,0:T(8,128)(2,1)} %get-tuple-element.80), channel_id=1, source_target_pairs={{0,24},{4,28},{8,16},{12,20},{16,8},{20,12},{24,0},{28,4},{1,25},{... | collective-permute-start | bytes 417800 | tf_op jit(solution)/shard_map/ppermute | solution.py:1193
  21.6 8.5 %collective-permute-start.4 = (bf16[272,256]{1,0:T(8,128)(2,1)}, bf16[272,256]{1,0:T(8,128)(2,1)S(1)}, u32[]{:S(2)}, u32[]{:S(2)}) collective-permute-start(bf16[272,256]{1,0:T(8,128)(2,1)} %gather.1.a_hbm), channel_id=1, source_target_pairs={{0,1},{1,0},{2,3},{3,2},{4,5},{5,4},{6,7},{7,6},{8,9},{9,8},{10,11... | collective-permute-start | bytes 417800 | tf_op jit(solution)/shard_map/ppermute | solution.py:1198
  23.2 13.0 %collective-permute-start.5 = (bf16[272,256]{1,0:T(8,128)(2,1)}, bf16[272,256]{1,0:T(8,128)(2,1)S(1)}, u32[]{:S(2)}, u32[]{:S(2)}) collective-permute-start(bf16[272,256]{1,0:T(8,128)(2,1)} %gather.1.a_hbm), channel_id=1, source_target_pairs={{0,2},{1,3},{2,0},{3,1},{4,6},{5,7},{6,4},{7,5},{8,10},{9,11},{10,... | collective-permute-start | bytes 417800 | tf_op jit(solution)/shard_map/ppermute | solution.py:1198
  25.8 10.4 %collective-permute-start.6 = (bf16[272,256]{1,0:T(8,128)(2,1)}, bf16[272,256]{1,0:T(8,128)(2,1)S(1)}, u32[]{:S(2)}, u32[]{:S(2)}) collective-permute-start(bf16[272,256]{1,0:T(8,128)(2,1)} %gather.1.a_hbm), channel_id=1, source_target_pairs={{0,3},{1,2},{2,1},{3,0},{4,7},{5,6},{6,5},{7,4},{8,11},{9,10},{10,... | collective-permute-start | bytes 417800 | tf_op jit(solution)/shard_map/ppermute | solution.py:1198
  38.0 15.5 %collective-permute-start.12 = (bf16[4,256,256]{2,1,0:T(8,128)(2,1)S(1)}, bf16[4,256,256]{2,1,0:T(8,128)(2,1)S(1)}, u32[]{:S(2)}, u32[]{:S(2)}) collective-permute-start(bf16[4,256,256]{2,1,0:T(8,128)(2,1)S(1)} %project_units.4), channel_id=1, source_target_pairs={{0,4},{4,0},{8,12},{12,8},{16,20},{20,16},{24,28},{28,24},{1,5},{5... | collective-permute-start | bytes 1572872 | tf_op jit(solution)/shard_map/ppermute | solution.py:239
  40.5 8.0 %collective-permute-start.8 = (bf16[384,256]{1,0:T(8,128)(2,1)}, bf16[384,256]{1,0:T(8,128)(2,1)S(1)}, u32[]{:S(2)}, u32[]{:S(2)}) collective-permute-start(bf16[384,256]{1,0:T(8,128)(2,1)} %get-tuple-element.96), channel_id=1, source_target_pairs={{0,8},{4,12},{8,0},{12,4},{16,24},{20,28},{24,16},{28,20},{1,9},{5... | collective-permute-start | bytes 589832 | tf_op jit(solution)/shard_map/ppermute | solution.py:1193
  42.1 11.1 %collective-permute-start.9 = (bf16[384,256]{1,0:T(8,128)(2,1)}, bf16[384,256]{1,0:T(8,128)(2,1)S(1)}, u32[]{:S(2)}, u32[]{:S(2)}) collective-permute-start(bf16[384,256]{1,0:T(8,128)(2,1)} %get-tuple-element.97), channel_id=1, source_target_pairs={{0,16},{4,20},{8,24},{12,28},{16,0},{20,4},{24,8},{28,12},{1,17},{... | collective-permute-start | bytes 589832 | tf_op jit(solution)/shard_map/ppermute | solution.py:1193
  42.6 10.5 %collective-permute-start.10 = (bf16[384,256]{1,0:T(8,128)(2,1)}, bf16[384,256]{1,0:T(8,128)(2,1)S(1)}, u32[]{:S(2)}, u32[]{:S(2)}) collective-permute-start(bf16[384,256]{1,0:T(8,128)(2,1)} %get-tuple-element.98), channel_id=1, source_target_pairs={{0,24},{4,28},{8,16},{12,20},{16,8},{20,12},{24,0},{28,4},{1,25},{... | collective-permute-start | bytes 589832 | tf_op jit(solution)/shard_map/ppermute | solution.py:1193
  53.8 8.6 %collective-permute-start.13 = (bf16[256,256]{1,0:T(8,128)(2,1)S(1)}, bf16[256,256]{1,0:T(8,128)(2,1)S(1)}, u32[]{:S(2)}, u32[]{:S(2)}) collective-permute-start(bf16[256,256]{1,0:T(8,128)(2,1)S(1)} %get-tuple-element.104), channel_id=1, source_target_pairs={{0,8},{4,12},{8,0},{12,4},{16,24},{20,28},{24,16},{28,20},{1,9},{5... | collective-permute-start | bytes 393224 | tf_op jit(solution)/shard_map/ppermute | solution.py:1193
  54.4 8.4 %collective-permute-start.14 = (bf16[256,256]{1,0:T(8,128)(2,1)S(1)}, bf16[256,256]{1,0:T(8,128)(2,1)S(1)}, u32[]{:S(2)}, u32[]{:S(2)}) collective-permute-start(bf16[256,256]{1,0:T(8,128)(2,1)S(1)} %get-tuple-element.105), channel_id=1, source_target_pairs={{0,16},{4,20},{8,24},{12,28},{16,0},{20,4},{24,8},{28,12},{1,17},{... | collective-permute-start | bytes 393224 | tf_op jit(solution)/shard_map/ppermute | solution.py:1193
  55.9 6.9 %collective-permute-start.15 = (bf16[256,256]{1,0:T(8,128)(2,1)S(1)}, bf16[256,256]{1,0:T(8,128)(2,1)S(1)}, u32[]{:S(2)}, u32[]{:S(2)}) collective-permute-start(bf16[256,256]{1,0:T(8,128)(2,1)S(1)} %get-tuple-element.106), channel_id=1, source_target_pairs={{0,24},{4,28},{8,16},{12,20},{16,8},{20,12},{24,0},{28,4},{1,25},{... | collective-permute-start | bytes 393224 | tf_op jit(solution)/shard_map/ppermute | solution.py:1193
  76.8 6.6 %collective-permute-start.17 = (bf16[32,2048]{1,0:T(8,128)(2,1)}, bf16[32,2048]{1,0:T(8,128)(2,1)S(1)}, u32[]{:S(2)}, u32[]{:S(2)}) collective-permute-start(bf16[32,2048]{1,0:T(8,128)(2,1)} %get-tuple-element.114), channel_id=1, source_target_pairs={{0,8},{4,12},{8,0},{12,4},{16,24},{20,28},{24,16},{28,20},{1,9},{5... | collective-permute-start | bytes 393224 | tf_op jit(solution)/shard_map/ppermute | solution.py:1193
  77.4 8.3 %collective-permute-start.18 = (bf16[32,2048]{1,0:T(8,128)(2,1)}, bf16[32,2048]{1,0:T(8,128)(2,1)S(1)}, u32[]{:S(2)}, u32[]{:S(2)}) collective-permute-start(bf16[32,2048]{1,0:T(8,128)(2,1)} %get-tuple-element.115), channel_id=1, source_target_pairs={{0,16},{4,20},{8,24},{12,28},{16,0},{20,4},{24,8},{28,12},{1,17},{... | collective-permute-start | bytes 393224 | tf_op jit(solution)/shard_map/ppermute | solution.py:1193
  77.9 7.7 %collective-permute-start.19 = (bf16[32,2048]{1,0:T(8,128)(2,1)}, bf16[32,2048]{1,0:T(8,128)(2,1)S(1)}, u32[]{:S(2)}, u32[]{:S(2)}) collective-permute-start(bf16[32,2048]{1,0:T(8,128)(2,1)} %get-tuple-element.116), channel_id=1, source_target_pairs={{0,24},{4,28},{8,16},{12,20},{16,8},{20,12},{24,0},{28,4},{1,25},{... | collective-permute-start | bytes 393224 | tf_op jit(solution)/shard_map/ppermute | solution.py:1193
  89.0 5.7 %collective-permute-start.22 = (bf16[8,2048]{1,0:T(8,128)(2,1)S(1)}, bf16[8,2048]{1,0:T(8,128)(2,1)S(1)}, u32[]{:S(2)}, u32[]{:S(2)}) collective-permute-start(bf16[8,2048]{1,0:T(8,128)(2,1)S(1)} %get-tuple-element.120), channel_id=1, source_target_pairs={{0,3},{1,2},{2,1},{3,0},{4,7},{5,6},{6,5},{7,4},{8,11},{9,10},{10,... | collective-permute-start | bytes 98312 | tf_op jit(solution)/shard_map/ppermute | solution.py:1198
  96.2 11.1 %all-to-all-start.1 = ((bf16[32,8,256]{2,1,0:T(8,128)(2,1)}), bf16[32,8,256]{2,1,0:T(8,128)(2,1)S(1)}, u32[]{:S(2)}, u32[]{:S(2)}) async-start(bf16[32,8,256]{2,1,0:T(8,128)(2,1)} %get-tuple-element.121), calls=%async_computation.1 | async-start | bytes 262144 | tf_op jit(solution)/shard_map/all_to_all | solution.py:1221
  108.0 6.0 %collective-permute-start.28 = (bf16[4,256,256]{2,1,0:T(8,128)(2,1)S(1)}, bf16[4,256,256]{2,1,0:T(8,128)(2,1)S(1)}, u32[]{:S(2)}, u32[]{:S(2)}) collective-permute-start(bf16[4,256,256]{2,1,0:T(8,128)(2,1)S(1)} %project_units.6), channel_id=1, source_target_pairs={{0,4},{4,0},{8,12},{12,8},{16,20},{20,16},{24,28},{28,24},{1,5},{5... | collective-permute-start | bytes 1572872 | tf_op jit(solution)/shard_map/ppermute | solution.py:239
  110.4 8.0 %collective-permute-start.24 = (bf16[384,256]{1,0:T(8,128)(2,1)}, bf16[384,256]{1,0:T(8,128)(2,1)S(1)}, u32[]{:S(2)}, u32[]{:S(2)}) collective-permute-start(bf16[384,256]{1,0:T(8,128)(2,1)} %get-tuple-element.123), channel_id=1, source_target_pairs={{0,8},{4,12},{8,0},{12,4},{16,24},{20,28},{24,16},{28,20},{1,9},{5... | collective-permute-start | bytes 589832 | tf_op jit(solution)/shard_map/ppermute | solution.py:1193
  111.3 11.1 %collective-permute-start.25 = (bf16[384,256]{1,0:T(8,128)(2,1)}, bf16[384,256]{1,0:T(8,128)(2,1)S(1)}, u32[]{:S(2)}, u32[]{:S(2)}) collective-permute-start(bf16[384,256]{1,0:T(8,128)(2,1)} %get-tuple-element.124), channel_id=1, source_target_pairs={{0,16},{4,20},{8,24},{12,28},{16,0},{20,4},{24,8},{28,12},{1,17},{... | collective-permute-start | bytes 589832 | tf_op jit(solution)/shard_map/ppermute | solution.py:1193
  111.8 10.6 %collective-permute-start.26 = (bf16[384,256]{1,0:T(8,128)(2,1)}, bf16[384,256]{1,0:T(8,128)(2,1)S(1)}, u32[]{:S(2)}, u32[]{:S(2)}) collective-permute-start(bf16[384,256]{1,0:T(8,128)(2,1)} %get-tuple-element.125), channel_id=1, source_target_pairs={{0,24},{4,28},{8,16},{12,20},{16,8},{20,12},{24,0},{28,4},{1,25},{... | collective-permute-start | bytes 589832 | tf_op jit(solution)/shard_map/ppermute | solution.py:1193
  122.7 8.5 %collective-permute-start.29 = (bf16[256,256]{1,0:T(8,128)(2,1)S(1)}, bf16[256,256]{1,0:T(8,128)(2,1)S(1)}, u32[]{:S(2)}, u32[]{:S(2)}) collective-permute-start(bf16[256,256]{1,0:T(8,128)(2,1)S(1)} %get-tuple-element.130), channel_id=1, source_target_pairs={{0,8},{4,12},{8,0},{12,4},{16,24},{20,28},{24,16},{28,20},{1,9},{5... | collective-permute-start | bytes 393224 | tf_op jit(solution)/shard_map/ppermute | solution.py:1193
  124.0 8.4 %collective-permute-start.30 = (bf16[256,256]{1,0:T(8,128)(2,1)S(1)}, bf16[256,256]{1,0:T(8,128)(2,1)S(1)}, u32[]{:S(2)}, u32[]{:S(2)}) collective-permute-start(bf16[256,256]{1,0:T(8,128)(2,1)S(1)} %get-tuple-element.131), channel_id=1, source_target_pairs={{0,16},{4,20},{8,24},{12,28},{16,0},{20,4},{24,8},{28,12},{1,17},{... | collective-permute-start | bytes 393224 | tf_op jit(solution)/shard_map/ppermute | solution.py:1193
  124.8 7.6 %collective-permute-start.31 = (bf16[256,256]{1,0:T(8,128)(2,1)S(1)}, bf16[256,256]{1,0:T(8,128)(2,1)S(1)}, u32[]{:S(2)}, u32[]{:S(2)}) collective-permute-start(bf16[256,256]{1,0:T(8,128)(2,1)S(1)} %get-tuple-element.132), channel_id=1, source_target_pairs={{0,24},{4,28},{8,16},{12,20},{16,8},{20,12},{24,0},{28,4},{1,25},{... | collective-permute-start | bytes 393224 | tf_op jit(solution)/shard_map/ppermute | solution.py:1193
  146.1 6.6 %collective-permute-start.33 = (bf16[32,2048]{1,0:T(8,128)(2,1)}, bf16[32,2048]{1,0:T(8,128)(2,1)S(1)}, u32[]{:S(2)}, u32[]{:S(2)}) collective-permute-start(bf16[32,2048]{1,0:T(8,128)(2,1)} %get-tuple-element.139), channel_id=1, source_target_pairs={{0,8},{4,12},{8,0},{12,4},{16,24},{20,28},{24,16},{28,20},{1,9},{5... | collective-permute-start | bytes 393224 | tf_op jit(solution)/shard_map/ppermute | solution.py:1193
  146.7 8.3 %collective-permute-start.34 = (bf16[32,2048]{1,0:T(8,128)(2,1)}, bf16[32,2048]{1,0:T(8,128)(2,1)S(1)}, u32[]{:S(2)}, u32[]{:S(2)}) collective-permute-start(bf16[32,2048]{1,0:T(8,128)(2,1)} %get-tuple-element.140), channel_id=1, source_target_pairs={{0,16},{4,20},{8,24},{12,28},{16,0},{20,4},{24,8},{28,12},{1,17},{... | collective-permute-start | bytes 393224 | tf_op jit(solution)/shard_map/ppermute | solution.py:1193
  147.3 7.7 %collective-permute-start.35 = (bf16[32,2048]{1,0:T(8,128)(2,1)}, bf16[32,2048]{1,0:T(8,128)(2,1)S(1)}, u32[]{:S(2)}, u32[]{:S(2)}) collective-permute-start(bf16[32,2048]{1,0:T(8,128)(2,1)} %get-tuple-element.141), channel_id=1, source_target_pairs={{0,24},{4,28},{8,16},{12,20},{16,8},{20,12},{24,0},{28,4},{1,25},{... | collective-permute-start | bytes 393224 | tf_op jit(solution)/shard_map/ppermute | solution.py:1193
  155.1 6.2 %collective-permute-start.36 = (bf16[32,2048]{1,0:T(8,128)(2,1)S(1)}, bf16[32,2048]{1,0:T(8,128)(2,1)S(1)}, u32[]{:S(2)}, u32[]{:S(2)}) collective-permute-start(bf16[32,2048]{1,0:T(8,128)(2,1)S(1)} %convert_element_type.24.a_ref), channel_id=1, source_target_pairs={{0,1},{1,0},{2,3},{3,2},{4,5},{5,4},{6,7},{7,6},{8,9},{9,8},{10,11... | collective-permute-start | bytes 393224 | tf_op jit(solution)/shard_map/ppermute | solution.py:1198
  155.3 12.4 %collective-permute-start.37 = (bf16[32,2048]{1,0:T(8,128)(2,1)S(1)}, bf16[32,2048]{1,0:T(8,128)(2,1)S(1)}, u32[]{:S(2)}, u32[]{:S(2)}) collective-permute-start(bf16[32,2048]{1,0:T(8,128)(2,1)S(1)} %convert_element_type.24.a_ref), channel_id=1, source_target_pairs={{0,2},{1,3},{2,0},{3,1},{4,6},{5,7},{6,4},{7,5},{8,10},{9,11},{10,... | collective-permute-start | bytes 393224 | tf_op jit(solution)/shard_map/ppermute | solution.py:1198
  157.0 10.7 %collective-permute-start.38 = (bf16[32,2048]{1,0:T(8,128)(2,1)S(1)}, bf16[32,2048]{1,0:T(8,128)(2,1)S(1)}, u32[]{:S(2)}, u32[]{:S(2)}) collective-permute-start(bf16[32,2048]{1,0:T(8,128)(2,1)S(1)} %convert_element_type.24.a_ref), channel_id=1, source_target_pairs={{0,3},{1,2},{2,1},{3,0},{4,7},{5,6},{6,5},{7,4},{8,11},{9,10},{10,... | collective-permute-start | bytes 393224 | tf_op jit(solution)/shard_map/ppermute | solution.py:1198
  169.7 5.9 %collective-permute-start.41 = (bf16[32,2048]{1,0:T(8,128)(2,1)S(1)}, bf16[32,2048]{1,0:T(8,128)(2,1)S(1)}, u32[]{:S(2)}, u32[]{:S(2)}) collective-permute-start(bf16[32,2048]{1,0:T(8,128)(2,1)S(1)} %last_rows.1.refs_0_), channel_id=1, source_target_pairs={{0,24},{4,28},{8,16},{12,20},{16,8},{20,12},{24,0},{28,4},{1,25},{... | collective-permute-start | bytes 393224 | tf_op jit(solution)/shard_map/ppermute | solution.py:1193
  (32 other events, 335.4 us)

commit v6 on v5

--- a/solution.py
+++ b/solution.py
@@ -594,13 +594,13 @@
     for place in range(tp_count):
         rows = slice(place * mine, (place + 1) * mine)
         total_rows = total[rows] + jnp.where(owner == place, 1.0, 0.0) * state_ref[...]
-        out_ref[rows] = total_rows
+        out_ref[rows] = total_rows.astype(jnp.bfloat16)
 
 
 def last_parts(parts, state, tp_count):
     return pl.pallas_call(
         functools.partial(last_parts_kernel, tp_count),
-        out_shape=jax.ShapeDtypeStruct(parts[0].shape, jnp.float32),
+        out_shape=jax.ShapeDtypeStruct(parts[0].shape, jnp.bfloat16),
         in_specs=[whole()] * 5,
         out_specs=whole(),
         compiler_params=compiler_params(16),
@@ -1223,6 +1223,7 @@
         heads = to_distances(project_heads(hidden, weights_qkv, unit, arriving))
         arriving = swap_cores(project_units(hidden, w_fc1, layer_index), seq_count)
         units = project_units(hidden, w_fc1, layer_index, arriving)
+        heads, units = lax.optimization_barrier((heads, units))
         query, new_key, new_value = activate(heads, tables, width_local)
         units = to_distances(units)
         parts = attend(
@@ -1241,7 +1242,7 @@
             parts = share_rows(parts, tp_count)
             parts = [parts[0]] + [over_tp(parts[k], k) for k in range(1, tp_count)]
     last = last_parts(parts, state, tp_count)
-    last = from_tp(last.astype(jnp.bfloat16))
+    last = from_tp(last)
     last = to_distances([last_rows(last)] * CHIPS)
     return restore(backs, last, [swap_cores(part, seq_count) for part in last], new_tokens)
 

time: 179 us -> 179 us (level)
  no operation moved by 1% of the time
where the time goes in v6:
time: 179 us; the launch traced here: 178 us
  waiting for transfers between devices  66.2 us (37%)
  starting transfers between devices  47.8 us (27%)
  Pallas kernels  34 us (19%)
  blocking collectives  20.2 us (11%)
  local copies, waits for them, and re-layouts  9.08 us (5%)
    ppermute x24, waiting for transfers between devices, to_distances(): lax.ppermute(parts[k], 'seq', [(i, i ^ 2 * k) for i in range(seq_count)])  37.5 us
    ppermute x24, starting transfers between devices, to_distances(): lax.ppermute(parts[k], 'seq', [(i, i ^ 2 * k) for i in range(seq_count)])  29.3 us
    all_to_all x2, blocking collectives, per_device(): parts = lax.all_to_all(parts, 'seq', 0, 0)  20.2 us
    ppermute x9, waiting for transfers between devices, over_tp(): lax.ppermute(part, 'tp', [(i, i ^ distance) for i in range(tp_count)])  18.5 us
    ppermute x9, starting transfers between devices, over_tp(): lax.ppermute(part, 'tp', [(i, i ^ distance) for i in range(tp_count)])  13.5 us
    pallas_call x2, Pallas kernels, attend(): pl.pallas_call(functools.partial(attend_kernel, layer_index, new_tokens),...  9.92 us
    pallas_call x1, Pallas kernels, embed(): pl.pallas_call(embed_kernel, out_shape=(jax.ShapeDtypeStruct((CHIPS, rows...  6.08 us
    ppermute x13, waiting for transfers between devices, swap_cores(): return lax.ppermute(values, 'seq', [(i, i ^ 1) for i in range(seq_count)])  5.67 us
  transfers between devices with their start and end apart: 47, of which 27 were waited for; matrix products, arithmetic and copies ran while one was open for 5% of the time, Pallas kernels for 10%

profile of v6, /device:TPU:0, one launch (start us, length us, event | category | flops | bytes accessed | tf_op | source)
XLA Modules:
  0.0 178.3 jit_solution(12616863107633738362)
XLA Ops:
  0.0 6.1 %embed.1 = (bf16[4,256,256]{2,1,0:T(8,128)(2,1)S(1)}, bf16[1040,256]{1,0:T(8,128)(2,1)}, f32[8,256]{1,0:T(8,128)S(1)}) custom-call(s32[4,64]{1,0:T(4,128)} %bitcast.15, s32[1,64]{1,0:T(1,128)} %bitcast.11, bf16[1600,2048]{1,0:T(8,128)(2,1)} %table_hbm.1), custom_call_target="tpu_custom_call" | custom-call | tf_op jit(solution)/shard_map/embed/pallas_call | solution.py:416
  9.2 2.9 %collective-permute-start.1 = (bf16[272,256]{1,0:T(8,128)(2,1)}, bf16[272,256]{1,0:T(8,128)(2,1)S(1)}, u32[]{:S(2)}, u32[]{:S(2)}) collective-permute-start(bf16[272,256]{1,0:T(8,128)(2,1)} %get-tuple-element.94), channel_id=1, source_target_pairs={{0,8},{4,12},{8,0},{12,4},{16,24},{20,28},{24,16},{28,20},{1,9},{5... | collective-permute-start | bytes 417800 | tf_op jit(solution)/shard_map/ppermute | solution.py:1193
  16.6 4.2 %collective-permute-done.2.c_ref = bf16[272,256]{1,0:T(8,128)(2,1)S(1)} collective-permute-done((bf16[272,256]{1,0:T(8,128)(2,1)}, bf16[272,256]{1,0:T(8,128)(2,1)S(1)}, u32[]{:S(2)}, u32[]{:S(2)}) %collective-permute-start.2) | collective-permute-done | bytes 139296 | tf_op jit(solution)/shard_map/ppermute | solution.py:1193
  21.6 1.6 collective-permute-start.4
  23.2 2.6 %collective-permute-start.5 = (bf16[272,256]{1,0:T(8,128)(2,1)}, bf16[272,256]{1,0:T(8,128)(2,1)S(1)}, u32[]{:S(2)}, u32[]{:S(2)}) collective-permute-start(bf16[272,256]{1,0:T(8,128)(2,1)} %gather.1.a_hbm), channel_id=1, source_target_pairs={{0,2},{1,3},{2,0},{3,1},{4,6},{5,7},{6,4},{7,5},{8,10},{9,11},{10,... | collective-permute-start | bytes 417800 | tf_op jit(solution)/shard_map/ppermute | solution.py:1198
  26.0 2.5 %order_requests.1 = (s32[64]{0:T(128)}, s32[256]{0:T(256)}, s32[64]{0:T(128)}) custom-call(s32[64]{0:T(128)} %group_ref, s32[8]{0:T(128)} %prefix_ref.1, s32[64]{0:T(128)} %tail_ref.1, s32[2,16]{1,0:T(2,128)} %bitcast.16), custom_call_target="tpu_custom_call" | custom-call | tf_op jit(solution)/shard_map/order_requests/pallas_call | solution.py:303
  30.1 6.1 %collective-permute-done.5.c_ref = bf16[272,256]{1,0:T(8,128)(2,1)S(1)} collective-permute-done((bf16[272,256]{1,0:T(8,128)(2,1)}, bf16[272,256]{1,0:T(8,128)(2,1)S(1)}, u32[]{:S(2)}, u32[]{:S(2)}) %collective-permute-start.5) | collective-permute-done | bytes 139296 | tf_op jit(solution)/shard_map/ppermute | solution.py:1198
  44.4 4.1 %collective-permute-done.8.b_ref = bf16[384,256]{1,0:T(8,128)(2,1)S(1)} collective-permute-done((bf16[384,256]{1,0:T(8,128)(2,1)}, bf16[384,256]{1,0:T(8,128)(2,1)S(1)}, u32[]{:S(2)}, u32[]{:S(2)}) %collective-permute-start.8) | collective-permute-done | bytes 196640 | tf_op jit(solution)/shard_map/ppermute | solution.py:1193
  48.5 4.6 %collective-permute-done.9.c_ref = bf16[384,256]{1,0:T(8,128)(2,1)S(1)} collective-permute-done((bf16[384,256]{1,0:T(8,128)(2,1)}, bf16[384,256]{1,0:T(8,128)(2,1)S(1)}, u32[]{:S(2)}, u32[]{:S(2)}) %collective-permute-start.9) | collective-permute-done | bytes 196640 | tf_op jit(solution)/shard_map/ppermute | solution.py:1193
  57.1 5.0 %attend.2 = bf16[8,160,128]{2,1,0:T(8,128)(2,1)S(1)} custom-call(s32[64]{0:T(128)} %get-tuple-element.105.visit_hbm, bf16[128,512]{1,0:T(8,128)(2,1)S(1)} %get-tuple-element.124.query_ref, bf16[128,512]{1,0:T(8,128)(2,1)S(1)} %collective-permute-done.12.far_query_ref, bf16[32,512]{1,0:T(8,128)(2,1)S(1)} %get-tuple-element.125.new_key_ref, ...), custom_call_target="tpu_custom_call" | custom-call | tf_op jit(solution)/shard_map/attend/pallas_call | solution.py:1061
  62.5 10.2 %all_to_all.15.part_ref = bf16[8,160,128]{2,1,0:T(8,128)(2,1)S(1)} all-to-all(bf16[8,160,128]{2,1,0:T(8,128)(2,1)S(1)} %attend.2), channel_id=1, replica_groups=mesh['seq'=8,'tp'=4] {'seq'}, dimensions={0} | all-to-all | bytes 655360 | tf_op jit(solution)/shard_map/all_to_all | solution.py:1234
  77.6 2.4 %collective-permute-start.19 = (bf16[32,2048]{1,0:T(8,128)(2,1)}, bf16[32,2048]{1,0:T(8,128)(2,1)S(1)}, u32[]{:S(2)}, u32[]{:S(2)}) collective-permute-start(bf16[32,2048]{1,0:T(8,128)(2,1)} %get-tuple-element.140), channel_id=1, source_target_pairs={{0,24},{4,28},{8,16},{12,20},{16,8},{20,12},{24,0},{28,4},{1,25},{... | collective-permute-start | bytes 393224 | tf_op jit(solution)/shard_map/ppermute | solution.py:1193
  79.9 3.1 %collective-permute-done.17.b_ref = bf16[32,2048]{1,0:T(8,128)(2,1)S(1)} collective-permute-done((bf16[32,2048]{1,0:T(8,128)(2,1)}, bf16[32,2048]{1,0:T(8,128)(2,1)S(1)}, u32[]{:S(2)}, u32[]{:S(2)}) %collective-permute-start.17) | collective-permute-done | bytes 131104 | tf_op jit(solution)/shard_map/ppermute | solution.py:1193
  83.0 2.3 %collective-permute-done.18.c_ref = bf16[32,2048]{1,0:T(8,128)(2,1)S(1)} collective-permute-done((bf16[32,2048]{1,0:T(8,128)(2,1)}, bf16[32,2048]{1,0:T(8,128)(2,1)S(1)}, u32[]{:S(2)}, u32[]{:S(2)}) %collective-permute-start.18) | collective-permute-done | bytes 131104 | tf_op jit(solution)/shard_map/ppermute | solution.py:1193
  85.4 2.1 %collective-permute-start.20 = (bf16[8,2048]{1,0:T(8,128)(2,1)S(1)}, bf16[8,2048]{1,0:T(8,128)(2,1)S(1)}, u32[]{:S(2)}, u32[]{:S(2)}) collective-permute-start(bf16[8,2048]{1,0:T(8,128)(2,1)S(1)} %get-tuple-element.142), channel_id=1, source_target_pairs={{0,1},{1,0},{2,3},{3,2},{4,5},{5,4},{6,7},{7,6},{8,9},{9,8},{10,11... | collective-permute-start | bytes 98312 | tf_op jit(solution)/shard_map/ppermute | solution.py:1198
  90.0 2.9 %collective-permute-done.21.refs_2_ = bf16[8,2048]{1,0:T(8,128)(2,1)S(1)} collective-permute-done((bf16[8,2048]{1,0:T(8,128)(2,1)S(1)}, bf16[8,2048]{1,0:T(8,128)(2,1)S(1)}, u32[]{:S(2)}, u32[]{:S(2)}) %collective-permute-start.21) | collective-permute-done | bytes 32800 | tf_op jit(solution)/shard_map/ppermute | solution.py:1198
  95.8 2.8 %all-to-all-start.1 = ((bf16[32,8,256]{2,1,0:T(8,128)(2,1)}), bf16[32,8,256]{2,1,0:T(8,128)(2,1)S(1)}, u32[]{:S(2)}, u32[]{:S(2)}) async-start(bf16[32,8,256]{2,1,0:T(8,128)(2,1)} %get-tuple-element.145), calls=%async_computation.1 | async-start | bytes 262144 | tf_op jit(solution)/shard_map/all_to_all | solution.py:1221
  98.7 2.3 %copy.25 = bf16[1,256,3,512]{1,3,2,0:T(8,128)(2,1)} copy(bf16[1,256,3,512]{3,1,2,0:T(8,128)(2,1)} %get-tuple-element.175) | data formatting | bytes 1572864
  102.4 4.5 %all-to-all-done.1 = bf16[32,8,256]{2,1,0:T(8,128)(2,1)S(1)} async-done(((bf16[32,8,256]{2,1,0:T(8,128)(2,1)}), bf16[32,8,256]{2,1,0:T(8,128)(2,1)S(1)}, u32[]{:S(2)}, u32[]{:S(2)}) %all-to-all-start.1) | async-done | bytes 131104 | tf_op jit(solution)/shard_map/all_to_all | solution.py:1221
  111.4 2.2 %collective-permute-start.26 = (bf16[384,256]{1,0:T(8,128)(2,1)}, bf16[384,256]{1,0:T(8,128)(2,1)S(1)}, u32[]{:S(2)}, u32[]{:S(2)}) collective-permute-start(bf16[384,256]{1,0:T(8,128)(2,1)} %get-tuple-element.149), channel_id=1, source_target_pairs={{0,24},{4,28},{8,16},{12,20},{16,8},{20,12},{24,0},{28,4},{1,25},{... | collective-permute-start | bytes 589832 | tf_op jit(solution)/shard_map/ppermute | solution.py:1193
  113.9 4.1 %collective-permute-done.24.b_ref = bf16[384,256]{1,0:T(8,128)(2,1)S(1)} collective-permute-done((bf16[384,256]{1,0:T(8,128)(2,1)}, bf16[384,256]{1,0:T(8,128)(2,1)S(1)}, u32[]{:S(2)}, u32[]{:S(2)}) %collective-permute-start.24) | collective-permute-done | bytes 196640 | tf_op jit(solution)/shard_map/ppermute | solution.py:1193
  118.1 3.9 %collective-permute-done.25.c_ref = bf16[384,256]{1,0:T(8,128)(2,1)S(1)} collective-permute-done((bf16[384,256]{1,0:T(8,128)(2,1)}, bf16[384,256]{1,0:T(8,128)(2,1)S(1)}, u32[]{:S(2)}, u32[]{:S(2)}) %collective-permute-start.25) | collective-permute-done | bytes 196640 | tf_op jit(solution)/shard_map/ppermute | solution.py:1193
  125.9 4.9 %attend.3 = bf16[8,160,128]{2,1,0:T(8,128)(2,1)S(1)} custom-call(s32[64]{0:T(128)} %get-tuple-element.105.visit_hbm, bf16[128,512]{1,0:T(8,128)(2,1)S(1)} %get-tuple-element.158.query_ref, bf16[128,512]{1,0:T(8,128)(2,1)S(1)} %collective-permute-done.28.far_query_ref, bf16[32,512]{1,0:T(8,128)(2,1)S(1)} %get-tuple-element.159.new_key_ref, ...), custom_call_target="tpu_custom_call" | custom-call | tf_op jit(solution)/shard_map/attend/pallas_call | solution.py:1061
  132.0 10.0 %all_to_all.16.part_ref = bf16[8,160,128]{2,1,0:T(8,128)(2,1)S(1)} all-to-all(bf16[8,160,128]{2,1,0:T(8,128)(2,1)S(1)} %attend.3), channel_id=1, replica_groups=mesh['seq'=8,'tp'=4] {'seq'}, dimensions={0} | all-to-all | bytes 655360 | tf_op jit(solution)/shard_map/all_to_all | solution.py:1234
  146.9 2.4 %collective-permute-start.35 = (bf16[32,2048]{1,0:T(8,128)(2,1)}, bf16[32,2048]{1,0:T(8,128)(2,1)S(1)}, u32[]{:S(2)}, u32[]{:S(2)}) collective-permute-start(bf16[32,2048]{1,0:T(8,128)(2,1)} %get-tuple-element.173), channel_id=1, source_target_pairs={{0,24},{4,28},{8,16},{12,20},{16,8},{20,12},{24,0},{28,4},{1,25},{... | collective-permute-start | bytes 393224 | tf_op jit(solution)/shard_map/ppermute | solution.py:1193
  149.3 3.1 %collective-permute-done.33.b_ref = bf16[32,2048]{1,0:T(8,128)(2,1)S(1)} collective-permute-done((bf16[32,2048]{1,0:T(8,128)(2,1)}, bf16[32,2048]{1,0:T(8,128)(2,1)S(1)}, u32[]{:S(2)}, u32[]{:S(2)}) %collective-permute-start.33) | collective-permute-done | bytes 131104 | tf_op jit(solution)/shard_map/ppermute | solution.py:1193
  152.4 2.3 %collective-permute-done.34.c_ref = bf16[32,2048]{1,0:T(8,128)(2,1)S(1)} collective-permute-done((bf16[32,2048]{1,0:T(8,128)(2,1)}, bf16[32,2048]{1,0:T(8,128)(2,1)S(1)}, u32[]{:S(2)}, u32[]{:S(2)}) %collective-permute-start.34) | collective-permute-done | bytes 131104 | tf_op jit(solution)/shard_map/ppermute | solution.py:1193
  156.6 2.6 %collective-permute-start.38 = (bf16[32,2048]{1,0:T(8,128)(2,1)S(1)}, bf16[32,2048]{1,0:T(8,128)(2,1)S(1)}, u32[]{:S(2)}, u32[]{:S(2)}) collective-permute-start(bf16[32,2048]{1,0:T(8,128)(2,1)S(1)} %last_parts.1.a_ref), channel_id=1, source_target_pairs={{0,3},{1,2},{2,1},{3,0},{4,7},{5,6},{6,5},{7,4},{8,11},{9,10},{10,... | collective-permute-start | bytes 393224 | tf_op jit(solution)/shard_map/ppermute | solution.py:1198
  159.2 1.8 collective-permute-done.36.b_ref
  161.0 6.4 %collective-permute-done.37.c_ref = bf16[32,2048]{1,0:T(8,128)(2,1)S(1)} collective-permute-done((bf16[32,2048]{1,0:T(8,128)(2,1)S(1)}, bf16[32,2048]{1,0:T(8,128)(2,1)S(1)}, u32[]{:S(2)}, u32[]{:S(2)}) %collective-permute-start.37) | collective-permute-done | bytes 131104 | tf_op jit(solution)/shard_map/ppermute | solution.py:1198
  169.3 1.7 collective-permute-start.41
  172.9 2.2 %collective-permute-done.41.refs_3_ = bf16[32,2048]{1,0:T(8,128)(2,1)S(1)} collective-permute-done((bf16[32,2048]{1,0:T(8,128)(2,1)S(1)}, bf16[32,2048]{1,0:T(8,128)(2,1)S(1)}, u32[]{:S(2)}, u32[]{:S(2)}) %collective-permute-start.41) | collective-permute-done | bytes 131104 | tf_op jit(solution)/shard_map/ppermute | solution.py:1193
  (140 shorter events, 57.8 us)
Async XLA Ops:
  9.2 7.4 %collective-permute-start.1 = (bf16[272,256]{1,0:T(8,128)(2,1)}, bf16[272,256]{1,0:T(8,128)(2,1)S(1)}, u32[]{:S(2)}, u32[]{:S(2)}) collective-permute-start(bf16[272,256]{1,0:T(8,128)(2,1)} %get-tuple-element.94), channel_id=1, source_target_pairs={{0,8},{4,12},{8,0},{12,4},{16,24},{20,28},{24,16},{28,20},{1,9},{5... | collective-permute-start | bytes 417800 | tf_op jit(solution)/shard_map/ppermute | solution.py:1193
  12.2 8.6 %collective-permute-start.2 = (bf16[272,256]{1,0:T(8,128)(2,1)}, bf16[272,256]{1,0:T(8,128)(2,1)S(1)}, u32[]{:S(2)}, u32[]{:S(2)}) collective-permute-start(bf16[272,256]{1,0:T(8,128)(2,1)} %get-tuple-element.95), channel_id=1, source_target_pairs={{0,16},{4,20},{8,24},{12,28},{16,0},{20,4},{24,8},{28,12},{1,17},{... | collective-permute-start | bytes 417800 | tf_op jit(solution)/shard_map/ppermute | solution.py:1193
  13.7 7.1 %collective-permute-start.3 = (bf16[272,256]{1,0:T(8,128)(2,1)}, bf16[272,256]{1,0:T(8,128)(2,1)S(1)}, u32[]{:S(2)}, u32[]{:S(2)}) collective-permute-start(bf16[272,256]{1,0:T(8,128)(2,1)} %get-tuple-element.96), channel_id=1, source_target_pairs={{0,24},{4,28},{8,16},{12,20},{16,8},{20,12},{24,0},{28,4},{1,25},{... | collective-permute-start | bytes 417800 | tf_op jit(solution)/shard_map/ppermute | solution.py:1193
  21.6 8.5 %collective-permute-start.4 = (bf16[272,256]{1,0:T(8,128)(2,1)}, bf16[272,256]{1,0:T(8,128)(2,1)S(1)}, u32[]{:S(2)}, u32[]{:S(2)}) collective-permute-start(bf16[272,256]{1,0:T(8,128)(2,1)} %gather.1.a_hbm), channel_id=1, source_target_pairs={{0,1},{1,0},{2,3},{3,2},{4,5},{5,4},{6,7},{7,6},{8,9},{9,8},{10,11... | collective-permute-start | bytes 417800 | tf_op jit(solution)/shard_map/ppermute | solution.py:1198
  23.2 13.0 %collective-permute-start.5 = (bf16[272,256]{1,0:T(8,128)(2,1)}, bf16[272,256]{1,0:T(8,128)(2,1)S(1)}, u32[]{:S(2)}, u32[]{:S(2)}) collective-permute-start(bf16[272,256]{1,0:T(8,128)(2,1)} %gather.1.a_hbm), channel_id=1, source_target_pairs={{0,2},{1,3},{2,0},{3,1},{4,6},{5,7},{6,4},{7,5},{8,10},{9,11},{10,... | collective-permute-start | bytes 417800 | tf_op jit(solution)/shard_map/ppermute | solution.py:1198
  25.8 10.4 %collective-permute-start.6 = (bf16[272,256]{1,0:T(8,128)(2,1)}, bf16[272,256]{1,0:T(8,128)(2,1)S(1)}, u32[]{:S(2)}, u32[]{:S(2)}) collective-permute-start(bf16[272,256]{1,0:T(8,128)(2,1)} %gather.1.a_hbm), channel_id=1, source_target_pairs={{0,3},{1,2},{2,1},{3,0},{4,7},{5,6},{6,5},{7,4},{8,11},{9,10},{10,... | collective-permute-start | bytes 417800 | tf_op jit(solution)/shard_map/ppermute | solution.py:1198
  38.0 6.1 %collective-permute-start.11 = (bf16[4,256,256]{2,1,0:T(8,128)(2,1)S(1)}, bf16[4,256,256]{2,1,0:T(8,128)(2,1)S(1)}, u32[]{:S(2)}, u32[]{:S(2)}) collective-permute-start(bf16[4,256,256]{2,1,0:T(8,128)(2,1)S(1)} %project_units.4), channel_id=1, source_target_pairs={{0,4},{4,0},{8,12},{12,8},{16,20},{20,16},{24,28},{28,24},{1,5},{5... | collective-permute-start | bytes 1572872 | tf_op jit(solution)/shard_map/ppermute | solution.py:239
  40.5 8.0 %collective-permute-start.8 = (bf16[384,256]{1,0:T(8,128)(2,1)}, bf16[384,256]{1,0:T(8,128)(2,1)S(1)}, u32[]{:S(2)}, u32[]{:S(2)}) collective-permute-start(bf16[384,256]{1,0:T(8,128)(2,1)} %get-tuple-element.112), channel_id=1, source_target_pairs={{0,8},{4,12},{8,0},{12,4},{16,24},{20,28},{24,16},{28,20},{1,9},{5... | collective-permute-start | bytes 589832 | tf_op jit(solution)/shard_map/ppermute | solution.py:1193
  42.1 11.1 %collective-permute-start.9 = (bf16[384,256]{1,0:T(8,128)(2,1)}, bf16[384,256]{1,0:T(8,128)(2,1)S(1)}, u32[]{:S(2)}, u32[]{:S(2)}) collective-permute-start(bf16[384,256]{1,0:T(8,128)(2,1)} %get-tuple-element.113), channel_id=1, source_target_pairs={{0,16},{4,20},{8,24},{12,28},{16,0},{20,4},{24,8},{28,12},{1,17},{... | collective-permute-start | bytes 589832 | tf_op jit(solution)/shard_map/ppermute | solution.py:1193
  42.6 10.5 %collective-permute-start.10 = (bf16[384,256]{1,0:T(8,128)(2,1)}, bf16[384,256]{1,0:T(8,128)(2,1)S(1)}, u32[]{:S(2)}, u32[]{:S(2)}) collective-permute-start(bf16[384,256]{1,0:T(8,128)(2,1)} %get-tuple-element.114), channel_id=1, source_target_pairs={{0,24},{4,28},{8,16},{12,20},{16,8},{20,12},{24,0},{28,4},{1,25},{... | collective-permute-start | bytes 589832 | tf_op jit(solution)/shard_map/ppermute | solution.py:1193
  53.5 8.6 %collective-permute-start.13 = (bf16[256,256]{1,0:T(8,128)(2,1)S(1)}, bf16[256,256]{1,0:T(8,128)(2,1)S(1)}, u32[]{:S(2)}, u32[]{:S(2)}) collective-permute-start(bf16[256,256]{1,0:T(8,128)(2,1)S(1)} %get-tuple-element.128), channel_id=1, source_target_pairs={{0,8},{4,12},{8,0},{12,4},{16,24},{20,28},{24,16},{28,20},{1,9},{5... | collective-permute-start | bytes 393224 | tf_op jit(solution)/shard_map/ppermute | solution.py:1193
  54.1 8.4 %collective-permute-start.14 = (bf16[256,256]{1,0:T(8,128)(2,1)S(1)}, bf16[256,256]{1,0:T(8,128)(2,1)S(1)}, u32[]{:S(2)}, u32[]{:S(2)}) collective-permute-start(bf16[256,256]{1,0:T(8,128)(2,1)S(1)} %get-tuple-element.129), channel_id=1, source_target_pairs={{0,16},{4,20},{8,24},{12,28},{16,0},{20,4},{24,8},{28,12},{1,17},{... | collective-permute-start | bytes 393224 | tf_op jit(solution)/shard_map/ppermute | solution.py:1193
  55.5 6.9 %collective-permute-start.15 = (bf16[256,256]{1,0:T(8,128)(2,1)S(1)}, bf16[256,256]{1,0:T(8,128)(2,1)S(1)}, u32[]{:S(2)}, u32[]{:S(2)}) collective-permute-start(bf16[256,256]{1,0:T(8,128)(2,1)S(1)} %get-tuple-element.130), channel_id=1, source_target_pairs={{0,24},{4,28},{8,16},{12,20},{16,8},{20,12},{24,0},{28,4},{1,25},{... | collective-permute-start | bytes 393224 | tf_op jit(solution)/shard_map/ppermute | solution.py:1193
  76.4 6.6 %collective-permute-start.17 = (bf16[32,2048]{1,0:T(8,128)(2,1)}, bf16[32,2048]{1,0:T(8,128)(2,1)S(1)}, u32[]{:S(2)}, u32[]{:S(2)}) collective-permute-start(bf16[32,2048]{1,0:T(8,128)(2,1)} %get-tuple-element.138), channel_id=1, source_target_pairs={{0,8},{4,12},{8,0},{12,4},{16,24},{20,28},{24,16},{28,20},{1,9},{5... | collective-permute-start | bytes 393224 | tf_op jit(solution)/shard_map/ppermute | solution.py:1193
  77.0 8.3 %collective-permute-start.18 = (bf16[32,2048]{1,0:T(8,128)(2,1)}, bf16[32,2048]{1,0:T(8,128)(2,1)S(1)}, u32[]{:S(2)}, u32[]{:S(2)}) collective-permute-start(bf16[32,2048]{1,0:T(8,128)(2,1)} %get-tuple-element.139), channel_id=1, source_target_pairs={{0,16},{4,20},{8,24},{12,28},{16,0},{20,4},{24,8},{28,12},{1,17},{... | collective-permute-start | bytes 393224 | tf_op jit(solution)/shard_map/ppermute | solution.py:1193
  77.6 7.7 %collective-permute-start.19 = (bf16[32,2048]{1,0:T(8,128)(2,1)}, bf16[32,2048]{1,0:T(8,128)(2,1)S(1)}, u32[]{:S(2)}, u32[]{:S(2)}) collective-permute-start(bf16[32,2048]{1,0:T(8,128)(2,1)} %get-tuple-element.140), channel_id=1, source_target_pairs={{0,24},{4,28},{8,16},{12,20},{16,8},{20,12},{24,0},{28,4},{1,25},{... | collective-permute-start | bytes 393224 | tf_op jit(solution)/shard_map/ppermute | solution.py:1193
  88.6 5.7 %collective-permute-start.22 = (bf16[8,2048]{1,0:T(8,128)(2,1)S(1)}, bf16[8,2048]{1,0:T(8,128)(2,1)S(1)}, u32[]{:S(2)}, u32[]{:S(2)}) collective-permute-start(bf16[8,2048]{1,0:T(8,128)(2,1)S(1)} %get-tuple-element.144), channel_id=1, source_target_pairs={{0,3},{1,2},{2,1},{3,0},{4,7},{5,6},{6,5},{7,4},{8,11},{9,10},{10,... | collective-permute-start | bytes 98312 | tf_op jit(solution)/shard_map/ppermute | solution.py:1198
  95.8 11.1 %all-to-all-start.1 = ((bf16[32,8,256]{2,1,0:T(8,128)(2,1)}), bf16[32,8,256]{2,1,0:T(8,128)(2,1)S(1)}, u32[]{:S(2)}, u32[]{:S(2)}) async-start(bf16[32,8,256]{2,1,0:T(8,128)(2,1)} %get-tuple-element.145), calls=%async_computation.1 | async-start | bytes 262144 | tf_op jit(solution)/shard_map/all_to_all | solution.py:1221
  107.6 6.0 %collective-permute-start.27 = (bf16[4,256,256]{2,1,0:T(8,128)(2,1)S(1)}, bf16[4,256,256]{2,1,0:T(8,128)(2,1)S(1)}, u32[]{:S(2)}, u32[]{:S(2)}) collective-permute-start(bf16[4,256,256]{2,1,0:T(8,128)(2,1)S(1)} %project_units.6), channel_id=1, source_target_pairs={{0,4},{4,0},{8,12},{12,8},{16,20},{20,16},{24,28},{28,24},{1,5},{5... | collective-permute-start | bytes 1572872 | tf_op jit(solution)/shard_map/ppermute | solution.py:239
  110.1 8.0 %collective-permute-start.24 = (bf16[384,256]{1,0:T(8,128)(2,1)}, bf16[384,256]{1,0:T(8,128)(2,1)S(1)}, u32[]{:S(2)}, u32[]{:S(2)}) collective-permute-start(bf16[384,256]{1,0:T(8,128)(2,1)} %get-tuple-element.147), channel_id=1, source_target_pairs={{0,8},{4,12},{8,0},{12,4},{16,24},{20,28},{24,16},{28,20},{1,9},{5... | collective-permute-start | bytes 589832 | tf_op jit(solution)/shard_map/ppermute | solution.py:1193
  110.9 11.1 %collective-permute-start.25 = (bf16[384,256]{1,0:T(8,128)(2,1)}, bf16[384,256]{1,0:T(8,128)(2,1)S(1)}, u32[]{:S(2)}, u32[]{:S(2)}) collective-permute-start(bf16[384,256]{1,0:T(8,128)(2,1)} %get-tuple-element.148), channel_id=1, source_target_pairs={{0,16},{4,20},{8,24},{12,28},{16,0},{20,4},{24,8},{28,12},{1,17},{... | collective-permute-start | bytes 589832 | tf_op jit(solution)/shard_map/ppermute | solution.py:1193
  111.4 10.6 %collective-permute-start.26 = (bf16[384,256]{1,0:T(8,128)(2,1)}, bf16[384,256]{1,0:T(8,128)(2,1)S(1)}, u32[]{:S(2)}, u32[]{:S(2)}) collective-permute-start(bf16[384,256]{1,0:T(8,128)(2,1)} %get-tuple-element.149), channel_id=1, source_target_pairs={{0,24},{4,28},{8,16},{12,20},{16,8},{20,12},{24,0},{28,4},{1,25},{... | collective-permute-start | bytes 589832 | tf_op jit(solution)/shard_map/ppermute | solution.py:1193
  122.3 8.5 %collective-permute-start.29 = (bf16[256,256]{1,0:T(8,128)(2,1)S(1)}, bf16[256,256]{1,0:T(8,128)(2,1)S(1)}, u32[]{:S(2)}, u32[]{:S(2)}) collective-permute-start(bf16[256,256]{1,0:T(8,128)(2,1)S(1)} %get-tuple-element.162), channel_id=1, source_target_pairs={{0,8},{4,12},{8,0},{12,4},{16,24},{20,28},{24,16},{28,20},{1,9},{5... | collective-permute-start | bytes 393224 | tf_op jit(solution)/shard_map/ppermute | solution.py:1193
  123.7 8.4 %collective-permute-start.30 = (bf16[256,256]{1,0:T(8,128)(2,1)S(1)}, bf16[256,256]{1,0:T(8,128)(2,1)S(1)}, u32[]{:S(2)}, u32[]{:S(2)}) collective-permute-start(bf16[256,256]{1,0:T(8,128)(2,1)S(1)} %get-tuple-element.163), channel_id=1, source_target_pairs={{0,16},{4,20},{8,24},{12,28},{16,0},{20,4},{24,8},{28,12},{1,17},{... | collective-permute-start | bytes 393224 | tf_op jit(solution)/shard_map/ppermute | solution.py:1193
  124.4 7.6 %collective-permute-start.31 = (bf16[256,256]{1,0:T(8,128)(2,1)S(1)}, bf16[256,256]{1,0:T(8,128)(2,1)S(1)}, u32[]{:S(2)}, u32[]{:S(2)}) collective-permute-start(bf16[256,256]{1,0:T(8,128)(2,1)S(1)} %get-tuple-element.164), channel_id=1, source_target_pairs={{0,24},{4,28},{8,16},{12,20},{16,8},{20,12},{24,0},{28,4},{1,25},{... | collective-permute-start | bytes 393224 | tf_op jit(solution)/shard_map/ppermute | solution.py:1193
  145.7 6.6 %collective-permute-start.33 = (bf16[32,2048]{1,0:T(8,128)(2,1)}, bf16[32,2048]{1,0:T(8,128)(2,1)S(1)}, u32[]{:S(2)}, u32[]{:S(2)}) collective-permute-start(bf16[32,2048]{1,0:T(8,128)(2,1)} %get-tuple-element.171), channel_id=1, source_target_pairs={{0,8},{4,12},{8,0},{12,4},{16,24},{20,28},{24,16},{28,20},{1,9},{5... | collective-permute-start | bytes 393224 | tf_op jit(solution)/shard_map/ppermute | solution.py:1193
  146.4 8.3 %collective-permute-start.34 = (bf16[32,2048]{1,0:T(8,128)(2,1)}, bf16[32,2048]{1,0:T(8,128)(2,1)S(1)}, u32[]{:S(2)}, u32[]{:S(2)}) collective-permute-start(bf16[32,2048]{1,0:T(8,128)(2,1)} %get-tuple-element.172), channel_id=1, source_target_pairs={{0,16},{4,20},{8,24},{12,28},{16,0},{20,4},{24,8},{28,12},{1,17},{... | collective-permute-start | bytes 393224 | tf_op jit(solution)/shard_map/ppermute | solution.py:1193
  146.9 7.7 %collective-permute-start.35 = (bf16[32,2048]{1,0:T(8,128)(2,1)}, bf16[32,2048]{1,0:T(8,128)(2,1)S(1)}, u32[]{:S(2)}, u32[]{:S(2)}) collective-permute-start(bf16[32,2048]{1,0:T(8,128)(2,1)} %get-tuple-element.173), channel_id=1, source_target_pairs={{0,24},{4,28},{8,16},{12,20},{16,8},{20,12},{24,0},{28,4},{1,25},{... | collective-permute-start | bytes 393224 | tf_op jit(solution)/shard_map/ppermute | solution.py:1193
  154.7 6.2 %collective-permute-start.36 = (bf16[32,2048]{1,0:T(8,128)(2,1)S(1)}, bf16[32,2048]{1,0:T(8,128)(2,1)S(1)}, u32[]{:S(2)}, u32[]{:S(2)}) collective-permute-start(bf16[32,2048]{1,0:T(8,128)(2,1)S(1)} %last_parts.1.a_ref), channel_id=1, source_target_pairs={{0,1},{1,0},{2,3},{3,2},{4,5},{5,4},{6,7},{7,6},{8,9},{9,8},{10,11... | collective-permute-start | bytes 393224 | tf_op jit(solution)/shard_map/ppermute | solution.py:1198
  155.0 12.3 %collective-permute-start.37 = (bf16[32,2048]{1,0:T(8,128)(2,1)S(1)}, bf16[32,2048]{1,0:T(8,128)(2,1)S(1)}, u32[]{:S(2)}, u32[]{:S(2)}) collective-permute-start(bf16[32,2048]{1,0:T(8,128)(2,1)S(1)} %last_parts.1.a_ref), channel_id=1, source_target_pairs={{0,2},{1,3},{2,0},{3,1},{4,6},{5,7},{6,4},{7,5},{8,10},{9,11},{10,... | collective-permute-start | bytes 393224 | tf_op jit(solution)/shard_map/ppermute | solution.py:1198
  156.6 10.7 %collective-permute-start.38 = (bf16[32,2048]{1,0:T(8,128)(2,1)S(1)}, bf16[32,2048]{1,0:T(8,128)(2,1)S(1)}, u32[]{:S(2)}, u32[]{:S(2)}) collective-permute-start(bf16[32,2048]{1,0:T(8,128)(2,1)S(1)} %last_parts.1.a_ref), channel_id=1, source_target_pairs={{0,3},{1,2},{2,1},{3,0},{4,7},{5,6},{6,5},{7,4},{8,11},{9,10},{10,... | collective-permute-start | bytes 393224 | tf_op jit(solution)/shard_map/ppermute | solution.py:1198
  169.3 5.9 %collective-permute-start.41 = (bf16[32,2048]{1,0:T(8,128)(2,1)S(1)}, bf16[32,2048]{1,0:T(8,128)(2,1)S(1)}, u32[]{:S(2)}, u32[]{:S(2)}) collective-permute-start(bf16[32,2048]{1,0:T(8,128)(2,1)S(1)} %last_rows.1.refs_0_), channel_id=1, source_target_pairs={{0,24},{4,28},{8,16},{12,20},{16,8},{20,12},{24,0},{28,4},{1,25},{... | collective-permute-start | bytes 393224 | tf_op jit(solution)/shard_map/ppermute | solution.py:1193
  (32 other events, 334.9 us)

commit v7 on v6

--- a/solution.py
+++ b/solution.py
@@ -551,7 +551,7 @@
     return pl.pallas_call(
         functools.partial(norm_kernel, layer_index, tp_count),
         out_shape=(
-            jax.ShapeDtypeStruct((rows, width), jnp.float32),
+            pltpu.HBM((rows, width), jnp.float32),
             jax.ShapeDtypeStruct((devices, rows, cut), jnp.bfloat16),
         ),
         in_specs=[whole()] * len(operands),

time: 179 us -> 178 us (level)
    unnamed x36 -> x34, local copies, waits for them, and re-layouts: 4.24 us -> 3.62 us
where the time goes in v7:
time: 178 us
  waiting for transfers between devices  66.2 us (37%)
  starting transfers between devices  47.8 us (27%)
  Pallas kernels  34 us (19%)
  blocking collectives  20.2 us (11%)
  local copies, waits for them, and re-layouts  8.47 us (5%)
    ppermute x24, waiting for transfers between devices, to_distances(): lax.ppermute(parts[k], 'seq', [(i, i ^ 2 * k) for i in range(seq_count)])  37.5 us
    ppermute x24, starting transfers between devices, to_distances(): lax.ppermute(parts[k], 'seq', [(i, i ^ 2 * k) for i in range(seq_count)])  29.3 us
    all_to_all x2, blocking collectives, per_device(): parts = lax.all_to_all(parts, 'seq', 0, 0)  20.2 us
    ppermute x9, waiting for transfers between devices, over_tp(): lax.ppermute(part, 'tp', [(i, i ^ distance) for i in range(tp_count)])  18.5 us
    ppermute x9, starting transfers between devices, over_tp(): lax.ppermute(part, 'tp', [(i, i ^ distance) for i in range(tp_count)])  13.5 us
    pallas_call x2, Pallas kernels, attend(): pl.pallas_call(functools.partial(attend_kernel, layer_index, new_tokens),...  9.91 us
    pallas_call x1, Pallas kernels, embed(): pl.pallas_call(embed_kernel, out_shape=(jax.ShapeDtypeStruct((CHIPS, rows...  6.08 us
    ppermute x13, waiting for transfers between devices, swap_cores(): return lax.ppermute(values, 'seq', [(i, i ^ 1) for i in range(seq_count)])  5.66 us
  transfers between devices with their start and end apart: 47, of which 27 were waited for; matrix products, arithmetic and copies ran while one was open for 5% of the time, Pallas kernels for 10%

profile of v7, /device:TPU:0, one launch (start us, length us, event | category | flops | bytes accessed | tf_op | source)
XLA Modules:
  0.0 177.7 jit_solution(16817895546220984881)
XLA Ops:
  0.0 6.1 %embed.1 = (bf16[4,256,256]{2,1,0:T(8,128)(2,1)S(1)}, bf16[1040,256]{1,0:T(8,128)(2,1)}, f32[8,256]{1,0:T(8,128)S(1)}) custom-call(s32[4,64]{1,0:T(4,128)} %bitcast.15, s32[1,64]{1,0:T(1,128)} %bitcast.11, bf16[1600,2048]{1,0:T(8,128)(2,1)} %table_hbm.1), custom_call_target="tpu_custom_call" | custom-call | tf_op jit(solution)/shard_map/embed/pallas_call | solution.py:416
  9.2 2.9 %collective-permute-start.1 = (bf16[272,256]{1,0:T(8,128)(2,1)}, bf16[272,256]{1,0:T(8,128)(2,1)S(1)}, u32[]{:S(2)}, u32[]{:S(2)}) collective-permute-start(bf16[272,256]{1,0:T(8,128)(2,1)} %get-tuple-element.94), channel_id=1, source_target_pairs={{0,8},{4,12},{8,0},{12,4},{16,24},{20,28},{24,16},{28,20},{1,9},{5... | collective-permute-start | bytes 417800 | tf_op jit(solution)/shard_map/ppermute | solution.py:1193
  16.6 4.2 %collective-permute-done.2.c_ref = bf16[272,256]{1,0:T(8,128)(2,1)S(1)} collective-permute-done((bf16[272,256]{1,0:T(8,128)(2,1)}, bf16[272,256]{1,0:T(8,128)(2,1)S(1)}, u32[]{:S(2)}, u32[]{:S(2)}) %collective-permute-start.2) | collective-permute-done | bytes 139296 | tf_op jit(solution)/shard_map/ppermute | solution.py:1193
  21.5 1.6 collective-permute-start.4
  23.2 2.6 %collective-permute-start.5 = (bf16[272,256]{1,0:T(8,128)(2,1)}, bf16[272,256]{1,0:T(8,128)(2,1)S(1)}, u32[]{:S(2)}, u32[]{:S(2)}) collective-permute-start(bf16[272,256]{1,0:T(8,128)(2,1)} %gather.1.a_hbm), channel_id=1, source_target_pairs={{0,2},{1,3},{2,0},{3,1},{4,6},{5,7},{6,4},{7,5},{8,10},{9,11},{10,... | collective-permute-start | bytes 417800 | tf_op jit(solution)/shard_map/ppermute | solution.py:1198
  26.0 2.5 %order_requests.1 = (s32[64]{0:T(128)}, s32[256]{0:T(256)}, s32[64]{0:T(128)}) custom-call(s32[64]{0:T(128)} %group_ref, s32[8]{0:T(128)} %prefix_ref.1, s32[64]{0:T(128)} %tail_ref.1, s32[2,16]{1,0:T(2,128)} %bitcast.16), custom_call_target="tpu_custom_call" | custom-call | tf_op jit(solution)/shard_map/order_requests/pallas_call | solution.py:303
  30.1 6.1 %collective-permute-done.5.c_ref = bf16[272,256]{1,0:T(8,128)(2,1)S(1)} collective-permute-done((bf16[272,256]{1,0:T(8,128)(2,1)}, bf16[272,256]{1,0:T(8,128)(2,1)S(1)}, u32[]{:S(2)}, u32[]{:S(2)}) %collective-permute-start.5) | collective-permute-done | bytes 139296 | tf_op jit(solution)/shard_map/ppermute | solution.py:1198
  44.4 4.1 %collective-permute-done.8.b_ref = bf16[384,256]{1,0:T(8,128)(2,1)S(1)} collective-permute-done((bf16[384,256]{1,0:T(8,128)(2,1)}, bf16[384,256]{1,0:T(8,128)(2,1)S(1)}, u32[]{:S(2)}, u32[]{:S(2)}) %collective-permute-start.8) | collective-permute-done | bytes 196640 | tf_op jit(solution)/shard_map/ppermute | solution.py:1193
  48.5 4.6 %collective-permute-done.9.c_ref = bf16[384,256]{1,0:T(8,128)(2,1)S(1)} collective-permute-done((bf16[384,256]{1,0:T(8,128)(2,1)}, bf16[384,256]{1,0:T(8,128)(2,1)S(1)}, u32[]{:S(2)}, u32[]{:S(2)}) %collective-permute-start.9) | collective-permute-done | bytes 196640 | tf_op jit(solution)/shard_map/ppermute | solution.py:1193
  57.0 5.0 %attend.2 = bf16[8,160,128]{2,1,0:T(8,128)(2,1)S(1)} custom-call(s32[64]{0:T(128)} %get-tuple-element.105.visit_hbm, bf16[128,512]{1,0:T(8,128)(2,1)S(1)} %get-tuple-element.124.query_ref, bf16[128,512]{1,0:T(8,128)(2,1)S(1)} %collective-permute-done.12.far_query_ref, bf16[32,512]{1,0:T(8,128)(2,1)S(1)} %get-tuple-element.125.new_key_ref, ...), custom_call_target="tpu_custom_call" | custom-call | tf_op jit(solution)/shard_map/attend/pallas_call | solution.py:1061
  62.4 10.2 %all_to_all.15.part_ref = bf16[8,160,128]{2,1,0:T(8,128)(2,1)S(1)} all-to-all(bf16[8,160,128]{2,1,0:T(8,128)(2,1)S(1)} %attend.2), channel_id=1, replica_groups=mesh['seq'=8,'tp'=4] {'seq'}, dimensions={0} | all-to-all | bytes 655360 | tf_op jit(solution)/shard_map/all_to_all | solution.py:1234
  77.6 2.4 %collective-permute-start.19 = (bf16[32,2048]{1,0:T(8,128)(2,1)}, bf16[32,2048]{1,0:T(8,128)(2,1)S(1)}, u32[]{:S(2)}, u32[]{:S(2)}) collective-permute-start(bf16[32,2048]{1,0:T(8,128)(2,1)} %get-tuple-element.140), channel_id=1, source_target_pairs={{0,24},{4,28},{8,16},{12,20},{16,8},{20,12},{24,0},{28,4},{1,25},{... | collective-permute-start | bytes 393224 | tf_op jit(solution)/shard_map/ppermute | solution.py:1193
  79.9 3.1 %collective-permute-done.17.b_ref = bf16[32,2048]{1,0:T(8,128)(2,1)S(1)} collective-permute-done((bf16[32,2048]{1,0:T(8,128)(2,1)}, bf16[32,2048]{1,0:T(8,128)(2,1)S(1)}, u32[]{:S(2)}, u32[]{:S(2)}) %collective-permute-start.17) | collective-permute-done | bytes 131104 | tf_op jit(solution)/shard_map/ppermute | solution.py:1193
  83.0 2.3 %collective-permute-done.18.c_ref = bf16[32,2048]{1,0:T(8,128)(2,1)S(1)} collective-permute-done((bf16[32,2048]{1,0:T(8,128)(2,1)}, bf16[32,2048]{1,0:T(8,128)(2,1)S(1)}, u32[]{:S(2)}, u32[]{:S(2)}) %collective-permute-start.18) | collective-permute-done | bytes 131104 | tf_op jit(solution)/shard_map/ppermute | solution.py:1193
  85.4 2.1 %collective-permute-start.20 = (bf16[8,2048]{1,0:T(8,128)(2,1)S(1)}, bf16[8,2048]{1,0:T(8,128)(2,1)S(1)}, u32[]{:S(2)}, u32[]{:S(2)}) collective-permute-start(bf16[8,2048]{1,0:T(8,128)(2,1)S(1)} %get-tuple-element.142), channel_id=1, source_target_pairs={{0,1},{1,0},{2,3},{3,2},{4,5},{5,4},{6,7},{7,6},{8,9},{9,8},{10,11... | collective-permute-start | bytes 98312 | tf_op jit(solution)/shard_map/ppermute | solution.py:1198
  90.0 2.9 %collective-permute-done.21.refs_2_ = bf16[8,2048]{1,0:T(8,128)(2,1)S(1)} collective-permute-done((bf16[8,2048]{1,0:T(8,128)(2,1)S(1)}, bf16[8,2048]{1,0:T(8,128)(2,1)S(1)}, u32[]{:S(2)}, u32[]{:S(2)}) %collective-permute-start.21) | collective-permute-done | bytes 32800 | tf_op jit(solution)/shard_map/ppermute | solution.py:1198
  95.2 2.8 %all-to-all-start.1 = ((bf16[32,8,256]{2,1,0:T(8,128)(2,1)}), bf16[32,8,256]{2,1,0:T(8,128)(2,1)S(1)}, u32[]{:S(2)}, u32[]{:S(2)}) async-start(bf16[32,8,256]{2,1,0:T(8,128)(2,1)} %get-tuple-element.145), calls=%async_computation.1 | async-start | bytes 262144 | tf_op jit(solution)/shard_map/all_to_all | solution.py:1221
  98.0 2.3 %copy.25 = bf16[1,256,3,512]{1,3,2,0:T(8,128)(2,1)} copy(bf16[1,256,3,512]{3,1,2,0:T(8,128)(2,1)} %get-tuple-element.175) | data formatting | bytes 1572864
  101.8 4.5 %all-to-all-done.1 = bf16[32,8,256]{2,1,0:T(8,128)(2,1)S(1)} async-done(((bf16[32,8,256]{2,1,0:T(8,128)(2,1)}), bf16[32,8,256]{2,1,0:T(8,128)(2,1)S(1)}, u32[]{:S(2)}, u32[]{:S(2)}) %all-to-all-start.1) | async-done | bytes 131104 | tf_op jit(solution)/shard_map/all_to_all | solution.py:1221
  110.8 2.2 %collective-permute-start.26 = (bf16[384,256]{1,0:T(8,128)(2,1)}, bf16[384,256]{1,0:T(8,128)(2,1)S(1)}, u32[]{:S(2)}, u32[]{:S(2)}) collective-permute-start(bf16[384,256]{1,0:T(8,128)(2,1)} %get-tuple-element.149), channel_id=1, source_target_pairs={{0,24},{4,28},{8,16},{12,20},{16,8},{20,12},{24,0},{28,4},{1,25},{... | collective-permute-start | bytes 589832 | tf_op jit(solution)/shard_map/ppermute | solution.py:1193
  113.3 4.1 %collective-permute-done.24.b_ref = bf16[384,256]{1,0:T(8,128)(2,1)S(1)} collective-permute-done((bf16[384,256]{1,0:T(8,128)(2,1)}, bf16[384,256]{1,0:T(8,128)(2,1)S(1)}, u32[]{:S(2)}, u32[]{:S(2)}) %collective-permute-start.24) | collective-permute-done | bytes 196640 | tf_op jit(solution)/shard_map/ppermute | solution.py:1193
  117.5 3.9 %collective-permute-done.25.c_ref = bf16[384,256]{1,0:T(8,128)(2,1)S(1)} collective-permute-done((bf16[384,256]{1,0:T(8,128)(2,1)}, bf16[384,256]{1,0:T(8,128)(2,1)S(1)}, u32[]{:S(2)}, u32[]{:S(2)}) %collective-permute-start.25) | collective-permute-done | bytes 196640 | tf_op jit(solution)/shard_map/ppermute | solution.py:1193
  125.3 4.9 %attend.3 = bf16[8,160,128]{2,1,0:T(8,128)(2,1)S(1)} custom-call(s32[64]{0:T(128)} %get-tuple-element.105.visit_hbm, bf16[128,512]{1,0:T(8,128)(2,1)S(1)} %get-tuple-element.158.query_ref, bf16[128,512]{1,0:T(8,128)(2,1)S(1)} %collective-permute-done.28.far_query_ref, bf16[32,512]{1,0:T(8,128)(2,1)S(1)} %get-tuple-element.159.new_key_ref, ...), custom_call_target="tpu_custom_call" | custom-call | tf_op jit(solution)/shard_map/attend/pallas_call | solution.py:1061
  131.4 10.0 %all_to_all.16.part_ref = bf16[8,160,128]{2,1,0:T(8,128)(2,1)S(1)} all-to-all(bf16[8,160,128]{2,1,0:T(8,128)(2,1)S(1)} %attend.3), channel_id=1, replica_groups=mesh['seq'=8,'tp'=4] {'seq'}, dimensions={0} | all-to-all | bytes 655360 | tf_op jit(solution)/shard_map/all_to_all | solution.py:1234
  146.3 2.4 %collective-permute-start.35 = (bf16[32,2048]{1,0:T(8,128)(2,1)}, bf16[32,2048]{1,0:T(8,128)(2,1)S(1)}, u32[]{:S(2)}, u32[]{:S(2)}) collective-permute-start(bf16[32,2048]{1,0:T(8,128)(2,1)} %get-tuple-element.173), channel_id=1, source_target_pairs={{0,24},{4,28},{8,16},{12,20},{16,8},{20,12},{24,0},{28,4},{1,25},{... | collective-permute-start | bytes 393224 | tf_op jit(solution)/shard_map/ppermute | solution.py:1193
  148.7 3.1 %collective-permute-done.33.b_ref = bf16[32,2048]{1,0:T(8,128)(2,1)S(1)} collective-permute-done((bf16[32,2048]{1,0:T(8,128)(2,1)}, bf16[32,2048]{1,0:T(8,128)(2,1)S(1)}, u32[]{:S(2)}, u32[]{:S(2)}) %collective-permute-start.33) | collective-permute-done | bytes 131104 | tf_op jit(solution)/shard_map/ppermute | solution.py:1193
  151.7 2.3 %collective-permute-done.34.c_ref = bf16[32,2048]{1,0:T(8,128)(2,1)S(1)} collective-permute-done((bf16[32,2048]{1,0:T(8,128)(2,1)}, bf16[32,2048]{1,0:T(8,128)(2,1)S(1)}, u32[]{:S(2)}, u32[]{:S(2)}) %collective-permute-start.34) | collective-permute-done | bytes 131104 | tf_op jit(solution)/shard_map/ppermute | solution.py:1193
  155.9 2.6 %collective-permute-start.38 = (bf16[32,2048]{1,0:T(8,128)(2,1)S(1)}, bf16[32,2048]{1,0:T(8,128)(2,1)S(1)}, u32[]{:S(2)}, u32[]{:S(2)}) collective-permute-start(bf16[32,2048]{1,0:T(8,128)(2,1)S(1)} %last_parts.1.a_ref), channel_id=1, source_target_pairs={{0,3},{1,2},{2,1},{3,0},{4,7},{5,6},{6,5},{7,4},{8,11},{9,10},{10,... | collective-permute-start | bytes 393224 | tf_op jit(solution)/shard_map/ppermute | solution.py:1198
  158.5 1.8 collective-permute-done.36.b_ref
  160.3 6.4 %collective-permute-done.37.c_ref = bf16[32,2048]{1,0:T(8,128)(2,1)S(1)} collective-permute-done((bf16[32,2048]{1,0:T(8,128)(2,1)S(1)}, bf16[32,2048]{1,0:T(8,128)(2,1)S(1)}, u32[]{:S(2)}, u32[]{:S(2)}) %collective-permute-start.37) | collective-permute-done | bytes 131104 | tf_op jit(solution)/shard_map/ppermute | solution.py:1198
  168.6 1.7 collective-permute-start.41
  172.3 2.2 %collective-permute-done.41.refs_3_ = bf16[32,2048]{1,0:T(8,128)(2,1)S(1)} collective-permute-done((bf16[32,2048]{1,0:T(8,128)(2,1)S(1)}, bf16[32,2048]{1,0:T(8,128)(2,1)S(1)}, u32[]{:S(2)}, u32[]{:S(2)}) %collective-permute-start.41) | collective-permute-done | bytes 131104 | tf_op jit(solution)/shard_map/ppermute | solution.py:1193
  (138 shorter events, 57.1 us)
Async XLA Ops:
  9.2 7.4 %collective-permute-start.1 = (bf16[272,256]{1,0:T(8,128)(2,1)}, bf16[272,256]{1,0:T(8,128)(2,1)S(1)}, u32[]{:S(2)}, u32[]{:S(2)}) collective-permute-start(bf16[272,256]{1,0:T(8,128)(2,1)} %get-tuple-element.94), channel_id=1, source_target_pairs={{0,8},{4,12},{8,0},{12,4},{16,24},{20,28},{24,16},{28,20},{1,9},{5... | collective-permute-start | bytes 417800 | tf_op jit(solution)/shard_map/ppermute | solution.py:1193
  12.2 8.6 %collective-permute-start.2 = (bf16[272,256]{1,0:T(8,128)(2,1)}, bf16[272,256]{1,0:T(8,128)(2,1)S(1)}, u32[]{:S(2)}, u32[]{:S(2)}) collective-permute-start(bf16[272,256]{1,0:T(8,128)(2,1)} %get-tuple-element.95), channel_id=1, source_target_pairs={{0,16},{4,20},{8,24},{12,28},{16,0},{20,4},{24,8},{28,12},{1,17},{... | collective-permute-start | bytes 417800 | tf_op jit(solution)/shard_map/ppermute | solution.py:1193
  13.7 7.1 %collective-permute-start.3 = (bf16[272,256]{1,0:T(8,128)(2,1)}, bf16[272,256]{1,0:T(8,128)(2,1)S(1)}, u32[]{:S(2)}, u32[]{:S(2)}) collective-permute-start(bf16[272,256]{1,0:T(8,128)(2,1)} %get-tuple-element.96), channel_id=1, source_target_pairs={{0,24},{4,28},{8,16},{12,20},{16,8},{20,12},{24,0},{28,4},{1,25},{... | collective-permute-start | bytes 417800 | tf_op jit(solution)/shard_map/ppermute | solution.py:1193
  21.5 8.5 %collective-permute-start.4 = (bf16[272,256]{1,0:T(8,128)(2,1)}, bf16[272,256]{1,0:T(8,128)(2,1)S(1)}, u32[]{:S(2)}, u32[]{:S(2)}) collective-permute-start(bf16[272,256]{1,0:T(8,128)(2,1)} %gather.1.a_hbm), channel_id=1, source_target_pairs={{0,1},{1,0},{2,3},{3,2},{4,5},{5,4},{6,7},{7,6},{8,9},{9,8},{10,11... | collective-permute-start | bytes 417800 | tf_op jit(solution)/shard_map/ppermute | solution.py:1198
  23.2 13.0 %collective-permute-start.5 = (bf16[272,256]{1,0:T(8,128)(2,1)}, bf16[272,256]{1,0:T(8,128)(2,1)S(1)}, u32[]{:S(2)}, u32[]{:S(2)}) collective-permute-start(bf16[272,256]{1,0:T(8,128)(2,1)} %gather.1.a_hbm), channel_id=1, source_target_pairs={{0,2},{1,3},{2,0},{3,1},{4,6},{5,7},{6,4},{7,5},{8,10},{9,11},{10,... | collective-permute-start | bytes 417800 | tf_op jit(solution)/shard_map/ppermute | solution.py:1198
  25.8 10.4 %collective-permute-start.6 = (bf16[272,256]{1,0:T(8,128)(2,1)}, bf16[272,256]{1,0:T(8,128)(2,1)S(1)}, u32[]{:S(2)}, u32[]{:S(2)}) collective-permute-start(bf16[272,256]{1,0:T(8,128)(2,1)} %gather.1.a_hbm), channel_id=1, source_target_pairs={{0,3},{1,2},{2,1},{3,0},{4,7},{5,6},{6,5},{7,4},{8,11},{9,10},{10,... | collective-permute-start | bytes 417800 | tf_op jit(solution)/shard_map/ppermute | solution.py:1198
  38.0 6.1 %collective-permute-start.11 = (bf16[4,256,256]{2,1,0:T(8,128)(2,1)S(1)}, bf16[4,256,256]{2,1,0:T(8,128)(2,1)S(1)}, u32[]{:S(2)}, u32[]{:S(2)}) collective-permute-start(bf16[4,256,256]{2,1,0:T(8,128)(2,1)S(1)} %project_units.4), channel_id=1, source_target_pairs={{0,4},{4,0},{8,12},{12,8},{16,20},{20,16},{24,28},{28,24},{1,5},{5... | collective-permute-start | bytes 1572872 | tf_op jit(solution)/shard_map/ppermute | solution.py:239
  40.5 8.0 %collective-permute-start.8 = (bf16[384,256]{1,0:T(8,128)(2,1)}, bf16[384,256]{1,0:T(8,128)(2,1)S(1)}, u32[]{:S(2)}, u32[]{:S(2)}) collective-permute-start(bf16[384,256]{1,0:T(8,128)(2,1)} %get-tuple-element.112), channel_id=1, source_target_pairs={{0,8},{4,12},{8,0},{12,4},{16,24},{20,28},{24,16},{28,20},{1,9},{5... | collective-permute-start | bytes 589832 | tf_op jit(solution)/shard_map/ppermute | solution.py:1193
  42.0 11.1 %collective-permute-start.9 = (bf16[384,256]{1,0:T(8,128)(2,1)}, bf16[384,256]{1,0:T(8,128)(2,1)S(1)}, u32[]{:S(2)}, u32[]{:S(2)}) collective-permute-start(bf16[384,256]{1,0:T(8,128)(2,1)} %get-tuple-element.113), channel_id=1, source_target_pairs={{0,16},{4,20},{8,24},{12,28},{16,0},{20,4},{24,8},{28,12},{1,17},{... | collective-permute-start | bytes 589832 | tf_op jit(solution)/shard_map/ppermute | solution.py:1193
  42.6 10.5 %collective-permute-start.10 = (bf16[384,256]{1,0:T(8,128)(2,1)}, bf16[384,256]{1,0:T(8,128)(2,1)S(1)}, u32[]{:S(2)}, u32[]{:S(2)}) collective-permute-start(bf16[384,256]{1,0:T(8,128)(2,1)} %get-tuple-element.114), channel_id=1, source_target_pairs={{0,24},{4,28},{8,16},{12,20},{16,8},{20,12},{24,0},{28,4},{1,25},{... | collective-permute-start | bytes 589832 | tf_op jit(solution)/shard_map/ppermute | solution.py:1193
  53.5 8.6 %collective-permute-start.13 = (bf16[256,256]{1,0:T(8,128)(2,1)S(1)}, bf16[256,256]{1,0:T(8,128)(2,1)S(1)}, u32[]{:S(2)}, u32[]{:S(2)}) collective-permute-start(bf16[256,256]{1,0:T(8,128)(2,1)S(1)} %get-tuple-element.128), channel_id=1, source_target_pairs={{0,8},{4,12},{8,0},{12,4},{16,24},{20,28},{24,16},{28,20},{1,9},{5... | collective-permute-start | bytes 393224 | tf_op jit(solution)/shard_map/ppermute | solution.py:1193
  54.1 8.4 %collective-permute-start.14 = (bf16[256,256]{1,0:T(8,128)(2,1)S(1)}, bf16[256,256]{1,0:T(8,128)(2,1)S(1)}, u32[]{:S(2)}, u32[]{:S(2)}) collective-permute-start(bf16[256,256]{1,0:T(8,128)(2,1)S(1)} %get-tuple-element.129), channel_id=1, source_target_pairs={{0,16},{4,20},{8,24},{12,28},{16,0},{20,4},{24,8},{28,12},{1,17},{... | collective-permute-start | bytes 393224 | tf_op jit(solution)/shard_map/ppermute | solution.py:1193
  55.5 6.9 %collective-permute-start.15 = (bf16[256,256]{1,0:T(8,128)(2,1)S(1)}, bf16[256,256]{1,0:T(8,128)(2,1)S(1)}, u32[]{:S(2)}, u32[]{:S(2)}) collective-permute-start(bf16[256,256]{1,0:T(8,128)(2,1)S(1)} %get-tuple-element.130), channel_id=1, source_target_pairs={{0,24},{4,28},{8,16},{12,20},{16,8},{20,12},{24,0},{28,4},{1,25},{... | collective-permute-start | bytes 393224 | tf_op jit(solution)/shard_map/ppermute | solution.py:1193
  76.4 6.6 %collective-permute-start.17 = (bf16[32,2048]{1,0:T(8,128)(2,1)}, bf16[32,2048]{1,0:T(8,128)(2,1)S(1)}, u32[]{:S(2)}, u32[]{:S(2)}) collective-permute-start(bf16[32,2048]{1,0:T(8,128)(2,1)} %get-tuple-element.138), channel_id=1, source_target_pairs={{0,8},{4,12},{8,0},{12,4},{16,24},{20,28},{24,16},{28,20},{1,9},{5... | collective-permute-start | bytes 393224 | tf_op jit(solution)/shard_map/ppermute | solution.py:1193
  77.0 8.3 %collective-permute-start.18 = (bf16[32,2048]{1,0:T(8,128)(2,1)}, bf16[32,2048]{1,0:T(8,128)(2,1)S(1)}, u32[]{:S(2)}, u32[]{:S(2)}) collective-permute-start(bf16[32,2048]{1,0:T(8,128)(2,1)} %get-tuple-element.139), channel_id=1, source_target_pairs={{0,16},{4,20},{8,24},{12,28},{16,0},{20,4},{24,8},{28,12},{1,17},{... | collective-permute-start | bytes 393224 | tf_op jit(solution)/shard_map/ppermute | solution.py:1193
  77.6 7.7 %collective-permute-start.19 = (bf16[32,2048]{1,0:T(8,128)(2,1)}, bf16[32,2048]{1,0:T(8,128)(2,1)S(1)}, u32[]{:S(2)}, u32[]{:S(2)}) collective-permute-start(bf16[32,2048]{1,0:T(8,128)(2,1)} %get-tuple-element.140), channel_id=1, source_target_pairs={{0,24},{4,28},{8,16},{12,20},{16,8},{20,12},{24,0},{28,4},{1,25},{... | collective-permute-start | bytes 393224 | tf_op jit(solution)/shard_map/ppermute | solution.py:1193
  88.6 5.7 %collective-permute-start.22 = (bf16[8,2048]{1,0:T(8,128)(2,1)S(1)}, bf16[8,2048]{1,0:T(8,128)(2,1)S(1)}, u32[]{:S(2)}, u32[]{:S(2)}) collective-permute-start(bf16[8,2048]{1,0:T(8,128)(2,1)S(1)} %get-tuple-element.144), channel_id=1, source_target_pairs={{0,3},{1,2},{2,1},{3,0},{4,7},{5,6},{6,5},{7,4},{8,11},{9,10},{10,... | collective-permute-start | bytes 98312 | tf_op jit(solution)/shard_map/ppermute | solution.py:1198
  95.2 11.1 %all-to-all-start.1 = ((bf16[32,8,256]{2,1,0:T(8,128)(2,1)}), bf16[32,8,256]{2,1,0:T(8,128)(2,1)S(1)}, u32[]{:S(2)}, u32[]{:S(2)}) async-start(bf16[32,8,256]{2,1,0:T(8,128)(2,1)} %get-tuple-element.145), calls=%async_computation.1 | async-start | bytes 262144 | tf_op jit(solution)/shard_map/all_to_all | solution.py:1221
  107.0 6.0 %collective-permute-start.27 = (bf16[4,256,256]{2,1,0:T(8,128)(2,1)S(1)}, bf16[4,256,256]{2,1,0:T(8,128)(2,1)S(1)}, u32[]{:S(2)}, u32[]{:S(2)}) collective-permute-start(bf16[4,256,256]{2,1,0:T(8,128)(2,1)S(1)} %project_units.6), channel_id=1, source_target_pairs={{0,4},{4,0},{8,12},{12,8},{16,20},{20,16},{24,28},{28,24},{1,5},{5... | collective-permute-start | bytes 1572872 | tf_op jit(solution)/shard_map/ppermute | solution.py:239
  109.4 8.0 %collective-permute-start.24 = (bf16[384,256]{1,0:T(8,128)(2,1)}, bf16[384,256]{1,0:T(8,128)(2,1)S(1)}, u32[]{:S(2)}, u32[]{:S(2)}) collective-permute-start(bf16[384,256]{1,0:T(8,128)(2,1)} %get-tuple-element.147), channel_id=1, source_target_pairs={{0,8},{4,12},{8,0},{12,4},{16,24},{20,28},{24,16},{28,20},{1,9},{5... | collective-permute-start | bytes 589832 | tf_op jit(solution)/shard_map/ppermute | solution.py:1193
  110.3 11.1 %collective-permute-start.25 = (bf16[384,256]{1,0:T(8,128)(2,1)}, bf16[384,256]{1,0:T(8,128)(2,1)S(1)}, u32[]{:S(2)}, u32[]{:S(2)}) collective-permute-start(bf16[384,256]{1,0:T(8,128)(2,1)} %get-tuple-element.148), channel_id=1, source_target_pairs={{0,16},{4,20},{8,24},{12,28},{16,0},{20,4},{24,8},{28,12},{1,17},{... | collective-permute-start | bytes 589832 | tf_op jit(solution)/shard_map/ppermute | solution.py:1193
  110.8 10.6 %collective-permute-start.26 = (bf16[384,256]{1,0:T(8,128)(2,1)}, bf16[384,256]{1,0:T(8,128)(2,1)S(1)}, u32[]{:S(2)}, u32[]{:S(2)}) collective-permute-start(bf16[384,256]{1,0:T(8,128)(2,1)} %get-tuple-element.149), channel_id=1, source_target_pairs={{0,24},{4,28},{8,16},{12,20},{16,8},{20,12},{24,0},{28,4},{1,25},{... | collective-permute-start | bytes 589832 | tf_op jit(solution)/shard_map/ppermute | solution.py:1193
  121.7 8.5 %collective-permute-start.29 = (bf16[256,256]{1,0:T(8,128)(2,1)S(1)}, bf16[256,256]{1,0:T(8,128)(2,1)S(1)}, u32[]{:S(2)}, u32[]{:S(2)}) collective-permute-start(bf16[256,256]{1,0:T(8,128)(2,1)S(1)} %get-tuple-element.162), channel_id=1, source_target_pairs={{0,8},{4,12},{8,0},{12,4},{16,24},{20,28},{24,16},{28,20},{1,9},{5... | collective-permute-start | bytes 393224 | tf_op jit(solution)/shard_map/ppermute | solution.py:1193
  123.0 8.4 %collective-permute-start.30 = (bf16[256,256]{1,0:T(8,128)(2,1)S(1)}, bf16[256,256]{1,0:T(8,128)(2,1)S(1)}, u32[]{:S(2)}, u32[]{:S(2)}) collective-permute-start(bf16[256,256]{1,0:T(8,128)(2,1)S(1)} %get-tuple-element.163), channel_id=1, source_target_pairs={{0,16},{4,20},{8,24},{12,28},{16,0},{20,4},{24,8},{28,12},{1,17},{... | collective-permute-start | bytes 393224 | tf_op jit(solution)/shard_map/ppermute | solution.py:1193
  123.8 7.6 %collective-permute-start.31 = (bf16[256,256]{1,0:T(8,128)(2,1)S(1)}, bf16[256,256]{1,0:T(8,128)(2,1)S(1)}, u32[]{:S(2)}, u32[]{:S(2)}) collective-permute-start(bf16[256,256]{1,0:T(8,128)(2,1)S(1)} %get-tuple-element.164), channel_id=1, source_target_pairs={{0,24},{4,28},{8,16},{12,20},{16,8},{20,12},{24,0},{28,4},{1,25},{... | collective-permute-start | bytes 393224 | tf_op jit(solution)/shard_map/ppermute | solution.py:1193
  145.1 6.6 %collective-permute-start.33 = (bf16[32,2048]{1,0:T(8,128)(2,1)}, bf16[32,2048]{1,0:T(8,128)(2,1)S(1)}, u32[]{:S(2)}, u32[]{:S(2)}) collective-permute-start(bf16[32,2048]{1,0:T(8,128)(2,1)} %get-tuple-element.171), channel_id=1, source_target_pairs={{0,8},{4,12},{8,0},{12,4},{16,24},{20,28},{24,16},{28,20},{1,9},{5... | collective-permute-start | bytes 393224 | tf_op jit(solution)/shard_map/ppermute | solution.py:1193
  145.7 8.3 %collective-permute-start.34 = (bf16[32,2048]{1,0:T(8,128)(2,1)}, bf16[32,2048]{1,0:T(8,128)(2,1)S(1)}, u32[]{:S(2)}, u32[]{:S(2)}) collective-permute-start(bf16[32,2048]{1,0:T(8,128)(2,1)} %get-tuple-element.172), channel_id=1, source_target_pairs={{0,16},{4,20},{8,24},{12,28},{16,0},{20,4},{24,8},{28,12},{1,17},{... | collective-permute-start | bytes 393224 | tf_op jit(solution)/shard_map/ppermute | solution.py:1193
  146.3 7.7 %collective-permute-start.35 = (bf16[32,2048]{1,0:T(8,128)(2,1)}, bf16[32,2048]{1,0:T(8,128)(2,1)S(1)}, u32[]{:S(2)}, u32[]{:S(2)}) collective-permute-start(bf16[32,2048]{1,0:T(8,128)(2,1)} %get-tuple-element.173), channel_id=1, source_target_pairs={{0,24},{4,28},{8,16},{12,20},{16,8},{20,12},{24,0},{28,4},{1,25},{... | collective-permute-start | bytes 393224 | tf_op jit(solution)/shard_map/ppermute | solution.py:1193
  154.1 6.2 %collective-permute-start.36 = (bf16[32,2048]{1,0:T(8,128)(2,1)S(1)}, bf16[32,2048]{1,0:T(8,128)(2,1)S(1)}, u32[]{:S(2)}, u32[]{:S(2)}) collective-permute-start(bf16[32,2048]{1,0:T(8,128)(2,1)S(1)} %last_parts.1.a_ref), channel_id=1, source_target_pairs={{0,1},{1,0},{2,3},{3,2},{4,5},{5,4},{6,7},{7,6},{8,9},{9,8},{10,11... | collective-permute-start | bytes 393224 | tf_op jit(solution)/shard_map/ppermute | solution.py:1198
  154.3 12.3 %collective-permute-start.37 = (bf16[32,2048]{1,0:T(8,128)(2,1)S(1)}, bf16[32,2048]{1,0:T(8,128)(2,1)S(1)}, u32[]{:S(2)}, u32[]{:S(2)}) collective-permute-start(bf16[32,2048]{1,0:T(8,128)(2,1)S(1)} %last_parts.1.a_ref), channel_id=1, source_target_pairs={{0,2},{1,3},{2,0},{3,1},{4,6},{5,7},{6,4},{7,5},{8,10},{9,11},{10,... | collective-permute-start | bytes 393224 | tf_op jit(solution)/shard_map/ppermute | solution.py:1198
  155.9 10.7 %collective-permute-start.38 = (bf16[32,2048]{1,0:T(8,128)(2,1)S(1)}, bf16[32,2048]{1,0:T(8,128)(2,1)S(1)}, u32[]{:S(2)}, u32[]{:S(2)}) collective-permute-start(bf16[32,2048]{1,0:T(8,128)(2,1)S(1)} %last_parts.1.a_ref), channel_id=1, source_target_pairs={{0,3},{1,2},{2,1},{3,0},{4,7},{5,6},{6,5},{7,4},{8,11},{9,10},{10,... | collective-permute-start | bytes 393224 | tf_op jit(solution)/shard_map/ppermute | solution.py:1198
  168.6 5.9 %collective-permute-start.41 = (bf16[32,2048]{1,0:T(8,128)(2,1)S(1)}, bf16[32,2048]{1,0:T(8,128)(2,1)S(1)}, u32[]{:S(2)}, u32[]{:S(2)}) collective-permute-start(bf16[32,2048]{1,0:T(8,128)(2,1)S(1)} %last_rows.1.refs_0_), channel_id=1, source_target_pairs={{0,24},{4,28},{8,16},{12,20},{16,8},{20,12},{24,0},{28,4},{1,25},{... | collective-permute-start | bytes 393224 | tf_op jit(solution)/shard_map/ppermute | solution.py:1193
  (31 other events, 334.3 us)
